TPU v7x, 32 devices: a whole 2x2x4 slice. The times are simulated.
32 devices in a mesh: section: 2 (over x), tensor: 2 (over core), dp: 8 (over z, y).
Axes of the slice: x: 2, y: 2, z: 4, core: 2. Of those that a mesh axis runs over, the one named last changes fastest.
Arguments:
- tokens: bfloat16 [2048, 2048], P('dp'), may hold values from -6 to 6
- segments: int32 [16, 128], P('dp'), may hold values from 0 to 3, never falling along the last dimension, each value on 1 to 64 neighbouring positions
- cotangent: bfloat16 [2048, 2048], P('dp'), may hold values from -6 to 6
- norm_gain: bfloat16 [2, 2, 2048], P('section'), may hold values from 0.5 to 1.5
- norm_bias: bfloat16 [2, 2, 2048], P('section'), may hold values from -1 to 1
- qkv_weight: bfloat16 [2, 2048, 8, 768], P('section', 'dp', 'tensor'), may hold values from -0.125 to 0.125
- qkv_bias: bfloat16 [2, 8, 768], P('section', 'tensor'), may hold values from -1.5 to 1.5
- out_weight: bfloat16 [2, 8, 256, 2048], P('section', 'tensor', 'dp'), may hold values from -0.5 to 0.5
- out_bias: bfloat16 [2, 2048], P('section'), may hold values from -1 to 1
- up_weight: bfloat16 [2, 2048, 8192], P('section', 'dp', 'tensor'), may hold values from -0.125 to 0.125
- up_bias: bfloat16 [2, 8192], P('section', 'tensor'), may hold values from -1.5 to 1.5
- down_weight: bfloat16 [2, 8192, 2048], P('section', ('tensor', 'dp')), may hold values from -0.0625 to 0.0625
- down_bias: bfloat16 [2, 2048], P('section'), may hold values from -1 to 1
Outputs:
- layer_outputs: bfloat16 [2, 2048, 2048], P('section', 'dp')
- input_gradients: float32 [2, 2048, 2048], P('section', 'dp')
- norm_gain_grad: float32 [2, 2, 2048], P('section')
- norm_bias_grad: float32 [2, 2, 2048], P('section')
- qkv_weight_grad: float32 [2, 2048, 8, 768], P('section', 'dp', 'tensor')
- qkv_bias_grad: float32 [2, 8, 768], P('section', 'tensor')
- out_weight_grad: float32 [2, 8, 256, 2048], P('section', 'tensor', 'dp')
- out_bias_grad: float32 [2, 2048], P('section')
- up_weight_grad: float32 [2, 2048, 8192], P('section', 'dp', 'tensor')
- up_bias_grad: float32 [2, 8192], P('section', 'tensor')
- down_weight_grad: float32 [2, 8192, 2048], P('section', ('tensor', 'dp'))
- down_bias_grad: float32 [2, 2048], P('section')
Inputs may be any that keep to these rules, and one draw needn't show every extreme that they name: `segments`: each row is one packed sequence: its segment numbers never fall along the row, a document holds 1 to 64 positions, and some document holds exactly 64.
All inputs are finite; a program needn't handle non-finite values.
Results may differ from a plain program's by a relative error of at most 0.018.
Values may be sent and summed in bfloat16 or wider, within the bound.
No kernel may reach another device: no remote copies, remote signals or barrier semaphores. Data moves between devices by JAX's collectives and lax.ppermute only.
A program may use at most 320 MiB of HBM per device.

v0:
```python
import math

import jax
import jax.numpy as jnp
from jax import lax
from jax.sharding import PartitionSpec as P

HD = 256
ROT = 64


NORM_EPSILON = 1e-05
MASK_VALUE = -1e30
ROOT_HALF = 0.7071067811865476
DENSITY_SCALE = 0.3989422804014327


def from_behind(block, axis, distance):
    devices = range(lax.axis_size(axis))
    route = [(i - distance, i) for i in devices if i - distance in devices]
    return lax.ppermute(block, axis, route)


def as_sent(x):
    return jax.tree.map(lambda a: a.astype(jnp.bfloat16) if a.dtype == jnp.float32 else a, x)


def contract_rows(left_side, right_side):
    return lax.dot_general(
        left_side, right_side, (((0,), (0,)), ((), ())), preferred_element_type=jnp.float32
    )


def contract_cols(left_side, right_side):
    return lax.dot_general(
        left_side, right_side, (((1,), (1,)), ((), ())), preferred_element_type=jnp.float32
    )


def normalize(values):
    centered = values - jnp.mean(values, axis=-1, keepdims=True)
    inverse = lax.rsqrt(jnp.mean(centered * centered, axis=-1, keepdims=True) + NORM_EPSILON)
    return (centered * inverse, inverse)


def norm_back(upstream, normed, inverse, norm_gain):
    scaled = upstream * norm_gain
    return inverse * (
        scaled
        - jnp.mean(scaled, axis=-1, keepdims=True)
        - normed * jnp.mean(scaled * normed, axis=-1, keepdims=True)
    )


def document_tables(segment):
    places = jnp.arange(segment.shape[0], dtype=jnp.int32)
    same_doc = segment[:, None] == segment[None, :]
    earlier = places[None, :] < places[:, None]
    position = jnp.sum(jnp.where(same_doc & earlier, 1, 0).astype(jnp.int32), axis=1)
    allowed = same_doc & (places[None, :] <= places[:, None])
    return (position, allowed)


def rotary_tables(position):
    half_width = ROT // 2
    exponent = jnp.arange(half_width, dtype=jnp.float32) * (2.0 / ROT)
    frequency = 10000.0 ** (-exponent)
    angles = position.astype(jnp.float32)[:, None] * frequency[None, :]
    cosine_table = jnp.cos(angles)
    sine_table = jnp.sin(angles)
    return (
        jnp.concatenate([cosine_table, cosine_table], axis=1),
        jnp.concatenate([sine_table, sine_table], axis=1),
    )


def rotate(values, cosine_table, sine_table):
    half_width = ROT // 2
    turned = values[..., :ROT]
    swapped = jnp.concatenate([-turned[..., half_width:], turned[..., :half_width]], axis=-1)
    turned = turned * cosine_table[:, None, :] + swapped * sine_table[:, None, :]
    return jnp.concatenate([turned, values[..., ROT:]], axis=-1)


def forward_layer(inputs, segment, vectors, matrices):
    norm_gain, norm_bias, joined_bias, out_bias, up_bias, down_bias = vectors
    joined_weight, out_weight, up_weight, down_weight = matrices
    row_count = inputs.shape[0]
    heads_here = joined_bias.shape[0]
    score_scale = 1.0 / math.sqrt(HD)
    normed, inverse = normalize(inputs)
    first_norm = (normed * norm_gain[0] + norm_bias[0]).astype(jnp.bfloat16)
    second_norm = (normed * norm_gain[1] + norm_bias[1]).astype(jnp.bfloat16)
    joined = jnp.dot(
        first_norm,
        joined_weight.reshape(joined_weight.shape[0], -1),
        preferred_element_type=jnp.float32,
    ) + joined_bias.reshape(-1)
    joined = joined.reshape(row_count, heads_here, 3, HD)
    position, allowed = document_tables(segment)
    cosine_table, sine_table = rotary_tables(position)
    queries = rotate(joined[:, :, 0], cosine_table, sine_table).astype(jnp.bfloat16)
    key_rows = rotate(joined[:, :, 1], cosine_table, sine_table).astype(jnp.bfloat16)
    values = joined[:, :, 2].astype(jnp.bfloat16)
    scores = (
        jnp.einsum("qhd,khd->hqk", queries, key_rows, preferred_element_type=jnp.float32)
        * score_scale
    )
    scores = jnp.where(allowed[None], scores, MASK_VALUE)
    largest = jnp.max(scores, axis=-1, keepdims=True)
    powered = jnp.exp(scores - largest)
    row_total = jnp.sum(powered, axis=-1, keepdims=True)
    attention = (powered / row_total).astype(jnp.bfloat16)
    log_total = largest + jnp.log(row_total)
    attended = (
        jnp.einsum("hqk,khd->qhd", attention, values, preferred_element_type=jnp.float32)
        .astype(jnp.bfloat16)
        .reshape(row_count, -1)
    )
    hidden = jnp.dot(second_norm, up_weight, preferred_element_type=jnp.float32) + up_bias
    active = jax.nn.gelu(hidden, approximate=False).astype(jnp.bfloat16)
    local_sum = jnp.dot(
        attended, out_weight.reshape(-1, out_weight.shape[-1]), preferred_element_type=jnp.float32
    )
    local_sum = local_sum + jnp.dot(active, down_weight, preferred_element_type=jnp.float32)
    branch = lax.psum(local_sum, "tensor")
    output = inputs + branch + out_bias + down_bias
    stored = (
        normed,
        inverse,
        first_norm,
        second_norm,
        queries,
        key_rows,
        values,
        log_total,
        attended,
        hidden,
        active,
        cosine_table,
        sine_table,
        allowed,
    )
    return (output, stored)


def backward_layer(upstream, stored, vectors, matrices):
    (
        normed,
        inverse,
        first_norm,
        second_norm,
        queries,
        key_rows,
        values,
        log_total,
        attended,
        hidden,
        active,
        cosine_table,
        sine_table,
        allowed,
    ) = stored
    norm_gain = vectors[0]
    joined_weight, out_weight, up_weight, down_weight = matrices
    row_count = upstream.shape[0]
    heads_here = queries.shape[1]
    score_scale = 1.0 / math.sqrt(HD)
    upstream_low = upstream.astype(jnp.bfloat16)
    out_bias_grad = jnp.sum(upstream, axis=0)
    out_weight_grad = contract_rows(attended, upstream_low).reshape(heads_here, HD, -1)
    down_weight_grad = contract_rows(active, upstream_low)
    attended_grad = contract_cols(
        upstream_low, out_weight.reshape(-1, out_weight.shape[-1])
    ).astype(jnp.bfloat16)
    attended_grad = attended_grad.reshape(row_count, heads_here, HD)
    active_grad = contract_cols(upstream_low, down_weight)
    normal_cdf = 0.5 * (1.0 + lax.erf(hidden * ROOT_HALF))
    normal_pdf = jnp.exp(-0.5 * hidden * hidden) * DENSITY_SCALE
    hidden_grad = (active_grad * (normal_cdf + hidden * normal_pdf)).astype(jnp.bfloat16)
    up_weight_grad = contract_rows(second_norm, hidden_grad)
    up_bias_grad = jnp.sum(hidden_grad, axis=0, dtype=jnp.float32)
    second_local = contract_cols(hidden_grad, up_weight)
    scores = (
        jnp.einsum("qhd,khd->hqk", queries, key_rows, preferred_element_type=jnp.float32)
        * score_scale
    )
    scores = jnp.where(allowed[None], scores, MASK_VALUE)
    attention = jnp.exp(scores - log_total)
    values_grad = jnp.einsum(
        "hqk,qhd->khd",
        attention.astype(jnp.bfloat16),
        attended_grad,
        preferred_element_type=jnp.float32,
    )
    attention_grad = jnp.einsum(
        "qhd,khd->hqk", attended_grad, values, preferred_element_type=jnp.float32
    )
    row_dots = jnp.sum(attention_grad * attention, axis=-1, keepdims=True)
    scores_grad = (attention * (attention_grad - row_dots)).astype(jnp.bfloat16)
    queries_grad = (
        jnp.einsum("hqk,khd->qhd", scores_grad, key_rows, preferred_element_type=jnp.float32)
        * score_scale
    )
    keys_grad = (
        jnp.einsum("hqk,qhd->khd", scores_grad, queries, preferred_element_type=jnp.float32)
        * score_scale
    )
    queries_grad = rotate(queries_grad, cosine_table, -sine_table)
    keys_grad = rotate(keys_grad, cosine_table, -sine_table)
    joined_grad = (
        jnp.stack([queries_grad, keys_grad, values_grad], axis=2)
        .reshape(row_count, -1)
        .astype(jnp.bfloat16)
    )
    joined_weight_grad = contract_rows(first_norm, joined_grad).reshape(-1, heads_here, 3 * HD)
    joined_bias_grad = jnp.sum(joined_grad, axis=0, dtype=jnp.float32).reshape(heads_here, 3 * HD)
    first_local = contract_cols(joined_grad, joined_weight.reshape(joined_weight.shape[0], -1))
    first_grad, second_grad = (
        lax.psum(first_local.astype(jnp.bfloat16), "tensor").astype(jnp.float32),
        lax.psum(second_local.astype(jnp.bfloat16), "tensor").astype(jnp.float32),
    )
    gain_grad = jnp.stack(
        [jnp.sum(first_grad * normed, axis=0), jnp.sum(second_grad * normed, axis=0)]
    )
    bias_grad = jnp.stack([jnp.sum(first_grad, axis=0), jnp.sum(second_grad, axis=0)])
    input_grad = (
        upstream
        + norm_back(first_grad, normed, inverse, norm_gain[0])
        + norm_back(second_grad, normed, inverse, norm_gain[1])
    )
    matrix_grads = (joined_weight_grad, out_weight_grad, up_weight_grad, down_weight_grad)
    vector_grads = (
        gain_grad,
        bias_grad,
        joined_bias_grad,
        out_bias_grad,
        up_bias_grad,
        out_bias_grad,
    )
    return (input_grad, matrix_grads, vector_grads)


def on_device(
    tokens,
    segments,
    cotangent,
    norm_gain,
    norm_bias,
    qkv_weight,
    qkv_bias,
    out_weight,
    out_bias,
    up_weight,
    up_bias,
    down_weight,
    down_bias,
):
    first_section = lax.axis_index("section") == 0
    micro_count = segments.shape[0]
    length = segments.shape[1]
    width = tokens.shape[1]
    matrices = (
        lax.all_gather(qkv_weight[0], "dp", axis=0, tiled=True),
        lax.all_gather(out_weight[0], "dp", axis=1, tiled=True),
        lax.all_gather(up_weight[0], "dp", axis=0, tiled=True),
        lax.all_gather(down_weight[0], "dp", axis=0, tiled=True),
    )
    vectors = tuple(
        (
            item[0].astype(jnp.float32)
            for item in (norm_gain, norm_bias, qkv_bias, out_bias, up_bias, down_bias)
        )
    )
    arriving = jnp.zeros((length, width), jnp.bfloat16)
    outputs = []
    stored_all = []
    for step_index in range(micro_count + 1):
        own_index = min(step_index, micro_count - 1)
        own_rows = tokens[own_index * length : (own_index + 1) * length]
        layer_input = jnp.where(first_section, own_rows, arriving).astype(jnp.float32)
        segment_index = jnp.clip(step_index - jnp.where(first_section, 0, 1), 0, micro_count - 1)
        segment = lax.dynamic_index_in_dim(segments, segment_index, 0, keepdims=False)
        output, stored = forward_layer(layer_input, segment, vectors, matrices)
        output_low = output.astype(jnp.bfloat16)
        outputs.append(output_low)
        stored_all.append(stored)
        if step_index < micro_count:
            arriving = from_behind(output_low, "section", 1)
    layer_outputs = jnp.where(
        first_section,
        jnp.concatenate(outputs[:micro_count], axis=0),
        jnp.concatenate(outputs[1:], axis=0),
    )
    back_matrices = (
        lax.all_gather(qkv_weight[0], "dp", axis=0, tiled=True),
        lax.all_gather(out_weight[0], "dp", axis=1, tiled=True),
        lax.all_gather(up_weight[0], "dp", axis=0, tiled=True),
        lax.all_gather(down_weight[0], "dp", axis=0, tiled=True),
    )
    back_arriving = jnp.zeros((length, width), jnp.bfloat16)
    input_grads = []
    matrix_totals = None
    vector_totals = None
    for step_index in range(micro_count + 1):
        if step_index < micro_count:
            given_rows = cotangent[step_index * length : (step_index + 1) * length]
        else:
            given_rows = jnp.zeros((length, width), jnp.bfloat16)
        upstream = jnp.where(first_section, back_arriving, given_rows).astype(jnp.float32)
        lower_stored = stored_all[max(step_index - 1, 0)]
        upper_stored = stored_all[min(step_index + 1, micro_count)]
        stored = jax.tree.map(
            lambda earlier, further: jnp.where(first_section, earlier, further),
            lower_stored,
            upper_stored,
        )
        input_grad, matrix_grads, vector_grads = backward_layer(
            upstream, stored, vectors, back_matrices
        )
        input_grads.append(input_grad)
        if step_index < micro_count:
            back_arriving = from_behind(input_grad.astype(jnp.bfloat16), "section", -1)
        if matrix_totals is None:
            matrix_totals = matrix_grads
            vector_totals = vector_grads
        else:
            matrix_totals = jax.tree.map(jnp.add, matrix_totals, matrix_grads)
            vector_totals = jax.tree.map(jnp.add, vector_totals, vector_grads)
    matrix_totals = (
        lax.psum_scatter(
            matrix_totals[0].astype(jnp.bfloat16), "dp", scatter_dimension=0, tiled=True
        ).astype(jnp.float32),
        lax.psum_scatter(
            matrix_totals[1].astype(jnp.bfloat16), "dp", scatter_dimension=1, tiled=True
        ).astype(jnp.float32),
        lax.psum_scatter(
            matrix_totals[2].astype(jnp.bfloat16), "dp", scatter_dimension=0, tiled=True
        ).astype(jnp.float32),
        lax.psum_scatter(
            matrix_totals[3].astype(jnp.bfloat16), "dp", scatter_dimension=0, tiled=True
        ).astype(jnp.float32),
    )
    vector_totals = jax.tree.map(
        lambda part: part.astype(jnp.float32), lax.psum(as_sent(vector_totals), "dp")
    )
    input_gradients = jnp.where(
        first_section,
        jnp.concatenate(input_grads[1:], axis=0),
        jnp.concatenate(input_grads[:micro_count], axis=0),
    )
    joined_weight_grad, out_weight_grad, up_weight_grad, down_weight_grad = matrix_totals
    gain_grad, bias_grad, joined_bias_grad, out_bias_grad, up_bias_grad, down_bias_grad = (
        vector_totals
    )
    return (
        layer_outputs[None],
        input_gradients[None],
        gain_grad[None],
        bias_grad[None],
        joined_weight_grad[None],
        joined_bias_grad[None],
        out_weight_grad[None],
        out_bias_grad[None],
        up_weight_grad[None],
        up_bias_grad[None],
        down_weight_grad[None],
        down_bias_grad[None],
    )


def solution(mesh):
    return jax.shard_map(
        on_device,
        mesh=mesh,
        in_specs=(
            P("dp", None),
            P("dp", None),
            P("dp", None),
            P("section", None, None),
            P("section", None, None),
            P("section", "dp", "tensor", None),
            P("section", "tensor", None),
            P("section", "tensor", "dp", None),
            P("section", None),
            P("section", "dp", "tensor"),
            P("section", "tensor"),
            P("section", ("tensor", "dp"), None),
            P("section", None),
        ),
        out_specs=(
            P("section", "dp", None),
            P("section", "dp", None),
            P("section", None, None),
            P("section", None, None),
            P("section", "dp", "tensor", None),
            P("section", "tensor", None),
            P("section", "tensor", "dp", None),
            P("section", None),
            P("section", "dp", "tensor"),
            P("section", "tensor"),
            P("section", ("tensor", "dp"), None),
            P("section", None),
        ),
        check_vma=False,
    )
```

profile of v0, /device:TPU:10, one launch (start us, length us, event | category | flops | bytes accessed | tf_op | source)
XLA Modules:
  0.0 1956.1 jit_solution(14163988119017222674)
XLA Ops:
  14.2 171.8 %all-gather.9.cloned.1.call-done = bf16[1,2048,4,768]{3,2,0,1:T(4,128)(2,1)} async-done(((bf16[1,256,4,768]{3,2,0,1:T(4,128)(2,1)}), bf16[1,2048,4,768]{3,2,0,1:T(4,128)(2,1)}) %all-gather.9.cloned.1.call-update) | async-done | bytes 12582928 | tf_op jit(solution)/shard_map/all_gather | solution.py:264
  186.0 9.4 copy.292
  195.4 5.9 copy-done
  212.8 201.1 %all-gather.13.cloned.1.call-done = bf16[1,2048,4096]{2,1,0:T(8,128)(2,1)} async-done(((bf16[1,256,4096]{2,1,0:T(8,128)(2,1)}), bf16[1,2048,4096]{2,1,0:T(8,128)(2,1)}) %all-gather.13.cloned.1.call-update) | async-done | bytes 16777232 | tf_op jit(solution)/shard_map/all_gather | solution.py:266
  413.9 9.6 fusion.24
  423.5 218.4 %all-gather.15.cloned.1.call-done = bf16[1,4096,2048]{2,1,0:T(8,128)(2,1)} async-done(((bf16[1,512,2048]{2,1,0:T(8,128)(2,1)}), bf16[1,4096,2048]{2,1,0:T(8,128)(2,1)}) %all-gather.15.cloned.1.call-update) | async-done | bytes 16777232 | tf_op jit(solution)/shard_map/all_gather | solution.py:267
  641.9 13.1 fusion.10
  655.0 61.7 %all-gather.11.cloned.1.call-done = bf16[1,4,256,2048]{3,2,1,0:T(8,128)(2,1)} async-done(((bf16[1,4,32,2048]{3,2,1,0:T(8,128)(2,1)}), bf16[1,4,256,2048]{3,2,1,0:T(8,128)(2,1)}) %all-gather.11.cloned.1.call-update) | async-done | bytes 4194320 | tf_op jit(solution)/shard_map/all_gather | solution.py:265
  716.7 3.9 fusion.72
  720.7 18.8 all-reduce.11.cloned.1.call-done
  743.2 3.7 convolution_convert_fusion.8
  747.1 10.1 collective-permute-done
  758.7 7.7 convolution_add_fusion.1
  787.2 8.4 fusion.27
  796.6 7.0 fusion.8
  808.5 14.7 convert_reduce_fusion.2
  823.2 10.0 convolution_convert_fusion.2
  833.2 12.5 fusion.75
  849.6 17.2 all-reduce.21.cloned.1.call-done
  866.8 4.0 fusion.226
  871.7 7.7 convolution_add_fusion
  902.6 9.7 fusion.30
  924.5 9.7 convolution_convert_fusion.1
  934.3 14.2 convert_reduce_fusion.1
  948.5 12.6 fusion.78
  961.2 13.0 fusion.6
  977.3 4.8 all-reduce.19.cloned.1.call-done
  996.0 5.7 fusion.244
  1010.9 13.8 convert_reduce_fusion
  1024.7 9.9 convolution_convert_fusion
  1034.6 12.6 fusion.81
  1049.5 6.6 add_convert_fusion.3
  1056.8 13.9 fusion.249
  1070.7 12.4 fusion.247
  1083.1 22.9 %add_convert_fusion.2 = bf16[2048,4,768]{2,0,1:T(8,128)(2,1)} fusion(f32[2048,4,768]{2,0,1:T(8,128)} %fusion.249, f32[2048,4,768]{2,0,1:T(8,128)} %fusion.247, bf16[4,768,128]{2,1,0:T(8,128)(2,1)S(1)} %bitcast.344, pred[]{:T(512)S(6)} %eq.78, bf16[128,2048]{1,0:T(8,128)(2,1)S(1)} %get-tuple-element.119, f32[128]{0:T(128)S(1)} %copy-done.106, ...), kind=kOutput, calls=%fused_computation.2 | convolution fusion | flops 1632894976 | bytes 64768000 | tf_op jit(solution)/shard_map/dot_general | solution.py:29
  1106.6 15.0 fusion.254
  1121.6 13.5 fusion.252
  1135.1 29.2 %add_convert_fusion.1 = bf16[2048,4096]{1,0:T(8,128)(2,1)} fusion(f32[2048,4096]{1,0:T(8,128)} %fusion.254, f32[2048,4096]{1,0:T(8,128)} %fusion.252, bf16[128,4096]{1,0:T(8,128)(2,1)} %get-tuple-element.225, pred[]{:T(512)S(6)} %eq.78, bf16[128,2048]{1,0:T(8,128)(2,1)S(1)} %get-tuple-element.119, f32[128]{0:T(128)S(1)} %copy-done.106, ...), kind=kOutput, calls=%fused_computation.1 | convolution fusion | flops 2176057344 | bytes 86001664 | tf_op jit(solution)/shard_map/dot_general | solution.py:29
  1165.5 20.8 %fusion.235 = f32[4096,2048]{1,0:T(8,128)} fusion(pred[]{:T(512)S(6)} %eq.78, bf16[256,2048]{1,0:T(8,128)(2,1)S(1)} %copy-done.18, f32[128,4096]{1,0:T(8,128)} %copy-done.51, f32[128,4096]{1,0:T(8,128)} %fusion.24), kind=kOutput, calls=%fused_computation.307 | convolution fusion | flops 2216427520 | bytes 38274048 | tf_op jit(solution)/shard_map/dot_general | solution.py:29
  1186.3 16.9 fusion.233
  1203.2 32.8 %add_convert_fusion = bf16[4096,2048]{1,0:T(8,128)(2,1)} fusion(f32[4096,2048]{1,0:T(8,128)} %fusion.235, f32[4096,2048]{1,0:T(8,128)} %fusion.233, pred[]{:T(512)S(6)} %eq.78, bf16[128,2048]{1,0:T(8,128)(2,1)S(1)} %copy-done.14, f32[128,4096]{1,0:T(8,128)} %fusion.30, f32[128,4096]{1,0:T(8,128)} %copy-done.51), kind=kOutput, calls=%fused_computation | convolution fusion | flops 2241593344 | bytes 88604672 | tf_op jit(solution)/shard_map/dot_general | solution.py:29
  1242.3 37.7 %all-reduce = (bf16[1,2,2048]{2,1,0:T(2,128)(2,1)S(1)}, bf16[1,2,2048]{2,1,0:T(2,128)(2,1)S(1)}, bf16[1,4,768]{2,1,0:T(4,128)(2,1)S(1)}, bf16[1,2048]{1,0:T(2,128)(2,1)S(1)}, bf16[1,4096]{1,0:T(2,128)(2,1)S(1)}) all-reduce(bf16[1,2,2048]{2,1,0:T(2,128)(2,1)S(1)} %fusion.315, ...), channel_id=1, replica_groups=mesh['section'=2,'tensor'=2,'dp'=8] {'dp'}, use_global_device_ids=true, to_apply=%region_45.46 | all-reduce | flops 17408 | bytes 69632 | tf_op jit(solution)/shard_map/psum | solution.py:345
  1290.1 82.8 %reduce-scatter.5.cloned.1.call-done = bf16[256,4,768]{2,0,1:T(8,128)(2,1)} async-done(((bf16[2048,4,768]{2,0,1:T(8,128)(2,1)}), bf16[256,4,768]{2,0,1:T(8,128)(2,1)}) %reduce-scatter.5.cloned.1.call-update) | async-done | bytes 1572880 | tf_op jit(solution)/shard_map/reduce_scatter | solution.py:331
  1374.6 3.7 copy.249
  1378.3 280.9 %reduce-scatter.9.cloned.1.call-done = bf16[256,4096]{1,0:T(8,128)(2,1)} async-done(((bf16[2048,4096]{1,0:T(8,128)(2,1)}), bf16[256,4096]{1,0:T(8,128)(2,1)}) %reduce-scatter.9.cloned.1.call-update) | async-done | bytes 2097168 | tf_op jit(solution)/shard_map/reduce_scatter | solution.py:337
  1659.2 4.1 bitcast_convert_fusion.1
  1663.3 281.3 %reduce-scatter.11.cloned.1.call-done = bf16[512,2048]{1,0:T(8,128)(2,1)} async-done(((bf16[4096,2048]{1,0:T(8,128)(2,1)}), bf16[512,2048]{1,0:T(8,128)(2,1)}) %reduce-scatter.11.cloned.1.call-update) | async-done | bytes 2097168 | tf_op jit(solution)/shard_map/reduce_scatter | solution.py:340
  1944.6 4.1 bitcast_convert_fusion
  (542 shorter events, 137.9 us)
Async XLA Ops:
  7.2 178.8 %all-gather.9.cloned.1.call-start = ((), (), s32[]{:S(2)}) async-start(), calls=%async_computation.11 | async-start | bytes 14155776 | tf_op jit(solution)/shard_map/all_gather | solution.py:264
  7.9 406.0 %all-gather.13.cloned.1.call-start = ((), (), s32[]{:S(2)}) async-start(), calls=%async_computation.13 | async-start | bytes 18874368 | tf_op jit(solution)/shard_map/all_gather | solution.py:266
  8.7 633.1 %all-gather.15.cloned.1.call-start = ((), (), s32[]{:S(2)}) async-start(), calls=%async_computation.14 | async-start | bytes 18874368 | tf_op jit(solution)/shard_map/all_gather | solution.py:267
  9.5 707.2 %all-gather.11.cloned.1.call-start = ((), (), s32[]{:S(2)}) async-start(), calls=%async_computation.12 | async-start | bytes 4718592 | tf_op jit(solution)/shard_map/all_gather | solution.py:265
  10.0 729.5 %all-reduce.11.cloned.1.call-start = ((), (), s32[]{:S(2)}) async-start(), calls=%async_computation.4 | async-start | bytes 2097152 | tf_op jit(solution)/shard_map/psum | solution.py:126
  13.0 400.9 %copy-start.107 = (f32[128]{0:T(128)}, f32[128]{0:T(128)S(1)}, u32[]{:S(2)}) copy-start(f32[128]{0:T(128)S(1)} %broadcast_multiply_fusion.14) | copy-start | bytes 1540
  13.3 182.1 %copy-start.152 = (f32[128]{0:T(128)}, f32[128]{0:T(128)S(1)}, u32[]{:S(2)}) copy-start(f32[128]{0:T(128)S(1)} %fusion.194) | copy-start | bytes 1540
  13.3 400.6 %copy-start.110 = (f32[128]{0:T(128)}, f32[128]{0:T(128)S(1)}, u32[]{:S(2)}) copy-start(f32[128]{0:T(128)S(1)} %add_rsqrt_fusion.2) | copy-start | bytes 1540
  14.2 1068.9 %copy-start.49 = (f32[1,1,2048]{2,1,0:T(1,128)}, f32[1,1,2048]{2,1,0:T(1,128)S(1)}, u32[]{:S(2)}) copy-start(f32[1,1,2048]{2,1,0:T(1,128)S(1)} %get-tuple-element.183) | copy-start | bytes 24580
  212.0 211.5 %copy-start.65 = (bf16[128,4,64]{2,0,1:T(8,128)(2,1)}, bf16[128,4,64]{2,0,1:T(8,128)(2,1)S(1)}, u32[]{:S(2)}) copy-start(bf16[128,4,64]{2,0,1:T(8,128)(2,1)S(1)} %get-tuple-element.164) | copy-start | bytes 196612
  212.0 211.4 %copy-start.69 = (bf16[128,4,64]{2,0,1:T(8,128)(2,1)}, bf16[128,4,64]{2,0,1:T(8,128)(2,1)S(1)}, u32[]{:S(2)}) copy-start(bf16[128,4,64]{2,0,1:T(8,128)(2,1)S(1)} %get-tuple-element.163) | copy-start | bytes 196612
  212.4 211.0 %copy-start.130 = (f32[4,128]{1,0:T(4,128)}, f32[4,128]{1,0:T(4,128)S(1)}, u32[]{:S(2)}) copy-start(f32[4,128]{1,0:T(4,128)S(1)} %get-tuple-element.212) | copy-start | bytes 6148
  212.5 211.0 %copy-start.133 = (f32[4,128]{1,0:T(4,128)}, f32[4,128]{1,0:T(4,128)S(1)}, u32[]{:S(2)}) copy-start(f32[4,128]{1,0:T(4,128)S(1)} %fusion.292) | copy-start | bytes 6148
  212.8 503.9 %copy-start.83 = (bf16[128,4,256]{2,0,1:T(8,128)(2,1)}, bf16[128,4,256]{2,0,1:T(8,128)(2,1)S(1)}, u32[]{:S(2)}) copy-start(bf16[128,4,256]{2,0,1:T(8,128)(2,1)S(1)} %fusion.165) | copy-start | bytes 786436
  655.0 65.7 %copy-start.148 = (bf16[1,2048]{1,0:T(2,128)(2,1)S(1)}, bf16[1,2048]{1,0:T(2,128)(2,1)}, u32[]{:S(2)}) copy-start(bf16[1,2048]{1,0:T(2,128)(2,1)} %param.25) | copy-start | bytes 12292
  655.0 65.7 %copy-start.149 = (bf16[1,2048]{1,0:T(2,128)(2,1)S(1)}, bf16[1,2048]{1,0:T(2,128)(2,1)}, u32[]{:S(2)}) copy-start(bf16[1,2048]{1,0:T(2,128)(2,1)} %param.21) | copy-start | bytes 12292
  720.6 21.7 %copy-start.101 = (f32[128,64]{0,1:T(8,128)S(1)}, f32[128,64]{0,1:T(8,128)}, u32[]{:S(2)}) copy-start(f32[128,64]{0,1:T(8,128)} %get-tuple-element.178) | copy-start | bytes 98308
  720.6 21.8 %copy-start.102 = (f32[128,64]{0,1:T(8,128)S(1)}, f32[128,64]{0,1:T(8,128)}, u32[]{:S(2)}) copy-start(f32[128,64]{0,1:T(8,128)} %get-tuple-element.172) | copy-start | bytes 98308
  720.6 22.6 %copy-start.15 = (bf16[256,2048]{1,0:T(8,128)(2,1)S(1)}, bf16[256,2048]{1,0:T(8,128)(2,1)}, u32[]{:S(2)}) copy-start(bf16[256,2048]{1,0:T(8,128)(2,1)} %param.15) | copy-start | bytes 3145732
  720.6 125.2 %all-reduce.13.cloned.1.call-start = ((), (), s32[]{:S(2)}) async-start(), calls=%async_computation.5 | async-start | bytes 2097152 | tf_op jit(solution)/shard_map/psum | solution.py:126
  720.7 125.1 %copy-start.89 = (f32[1,2048]{1,0:T(1,128)}, f32[1,2048]{1,0:T(1,128)S(1)}, u32[]{:S(2)}) copy-start(f32[1,2048]{1,0:T(1,128)S(1)} %add.491) | copy-start | bytes 24580
  720.7 125.1 %copy-start.91 = (f32[1,2048]{1,0:T(1,128)}, f32[1,2048]{1,0:T(1,128)S(1)}, u32[]{:S(2)}) copy-start(f32[1,2048]{1,0:T(1,128)S(1)} %add.490) | copy-start | bytes 24580
  741.0 16.1 collective-permute-start
  782.8 20.9 %copy-start.85 = (bf16[128,4,256]{2,0,1:T(8,128)(2,1)}, bf16[128,4,256]{2,0,1:T(8,128)(2,1)S(1)}, u32[]{:S(2)}) copy-start(bf16[128,4,256]{2,0,1:T(8,128)(2,1)S(1)} %fusion.166) | copy-start | bytes 786436
  805.4 61.3 %all-reduce.21.cloned.1.call-start = ((), (), s32[]{:S(2)}) async-start(), calls=%async_computation.17 | async-start | bytes 2097152 | tf_op jit(solution)/shard_map/psum | solution.py:221
  808.5 14.7 copy-start.9
  845.7 21.0 %copy-start.105 = (f32[128]{0:T(128)S(1)}, f32[128]{0:T(128)}, u32[]{:S(2)}) copy-start(f32[128]{0:T(128)} %copy-done.103) | copy-start | bytes 1540
  845.7 21.0 %copy-start.108 = (f32[128]{0:T(128)S(1)}, f32[128]{0:T(128)}, u32[]{:S(2)}) copy-start(f32[128]{0:T(128)} %copy-done.107) | copy-start | bytes 1540
  845.7 21.0 %copy-start.111 = (f32[128]{0:T(128)S(1)}, f32[128]{0:T(128)}, u32[]{:S(2)}) copy-start(f32[128]{0:T(128)} %copy-done.110) | copy-start | bytes 1540
  845.8 136.3 %all-reduce.19.cloned.1.call-start = ((), (), s32[]{:S(2)}) async-start(), calls=%async_computation.16 | async-start | bytes 2097152 | tf_op jit(solution)/shard_map/psum | solution.py:221
  847.3 19.5 copy-start.54
  847.3 19.5 collective-permute-start.1
  894.4 18.8 collective-permute-start.2
  961.1 275.7 %all-reduce.15.cloned.1.call-start = ((), (), s32[]{:S(2)}) async-start(), calls=%async_computation.6 | async-start | bytes 2097152 | tf_op jit(solution)/shard_map/psum | solution.py:126
  977.2 259.7 %all-reduce.17.cloned.1.call-start = ((), (), s32[]{:S(2)}) async-start(), calls=%async_computation.15 | async-start | bytes 2097152 | tf_op jit(solution)/shard_map/psum | solution.py:221
  987.2 14.5 collective-permute-start.3
  1047.2 240.8 %reduce-scatter.7.cloned.1.call-start = ((), (), s32[]{:S(2)}) async-start(), calls=%async_computation.8 | async-start | bytes 4718592 | tf_op jit(solution)/shard_map/reduce_scatter | solution.py:334
  1056.2 316.8 %reduce-scatter.5.cloned.1.call-start = ((), (), s32[]{:S(2)}) async-start(), calls=%async_computation.7 | async-start | bytes 14155776 | tf_op jit(solution)/shard_map/reduce_scatter | solution.py:331
  1106.0 553.1 %reduce-scatter.9.cloned.1.call-start = ((), (), s32[]{:S(2)}) async-start(), calls=%async_computation.9 | async-start | bytes 18874368 | tf_op jit(solution)/shard_map/reduce_scatter | solution.py:337
  1106.6 15.0 copy-start.6
  1164.3 780.3 %reduce-scatter.11.cloned.1.call-start = ((), (), s32[]{:S(2)}) async-start(), calls=%async_computation.10 | async-start | bytes 18874368 | tf_op jit(solution)/shard_map/reduce_scatter | solution.py:340
  1165.5 20.8 %copy-start.7 = (f32[128,4096]{1,0:T(8,128)S(1)}, f32[128,4096]{1,0:T(8,128)}, u32[]{:S(2)}) copy-start(f32[128,4096]{1,0:T(8,128)} %fusion.30) | copy-start | bytes 6291460
  1165.5 20.8 %copy-start.8 = (f32[128,4096]{1,0:T(8,128)S(1)}, f32[128,4096]{1,0:T(8,128)}, u32[]{:S(2)}) copy-start(f32[128,4096]{1,0:T(8,128)} %fusion.24) | copy-start | bytes 6291460
  1186.3 16.9 copy-start.14
  1240.3 42.2 %copy-start.53 = (bf16[128,2048]{1,0:T(8,128)(2,1)S(1)}, bf16[128,2048]{1,0:T(8,128)(2,1)}, u32[]{:S(2)}) copy-start(bf16[128,2048]{1,0:T(8,128)(2,1)} %copy-done.52) | copy-start | bytes 1572868
  1242.1 43.1 %copy-start.19 = (f32[128,2048]{1,0:T(8,128)S(1)}, f32[128,2048]{1,0:T(8,128)}, u32[]{:S(2)}) copy-start(f32[128,2048]{1,0:T(8,128)} %get-tuple-element.114) | copy-start | bytes 3145732
  1242.1 43.1 %copy-start.20 = (f32[128,2048]{1,0:T(8,128)S(1)}, f32[128,2048]{1,0:T(8,128)}, u32[]{:S(2)}) copy-start(f32[128,2048]{1,0:T(8,128)} %get-tuple-element.111) | copy-start | bytes 3145732
  1281.8 666.9 %copy-start.129 = (f32[1,2048]{1,0:T(1,128)}, f32[1,2048]{1,0:T(1,128)S(1)}, u32[]{:S(2)}) copy-start(f32[1,2048]{1,0:T(1,128)S(1)} %broadcast_in_dim.221) | copy-start | bytes 24580
  (136 other events, 636.5 us)
Sparse Core Ops, SparseCore 0:
  10.2 175.7 all-gather.8
  188.1 225.7 all-gather.12
  416.0 225.7 all-gather.14
  643.9 72.7 all-gather.10
  720.7 18.7 all-reduce.10
  805.6 20.7 all-reduce.12
  845.9 20.8 all-reduce.20
  961.2 20.8 all-reduce.18
  984.4 20.7 all-reduce.14
  1047.3 21.8 all-reduce.16
  1073.3 89.3 reduce-scatter.6
  1166.7 206.2 reduce-scatter.4
  1377.2 281.9 reduce-scatter.8
  1662.8 281.7 reduce-scatter.10
where the time goes:
time: 1960 us
  waiting for transfers between devices  1350 us (69%)
  matrix products  414 us (21%)
  local copies, waits for them, and re-layouts  66.6 us (3%)
  other arithmetic  59.4 us (3%)
  blocking collectives  37.7 us (2%)
    reduce_scatter x1, waiting for transfers between devices, on_device(): lax.psum_scatter(matrix_totals[3].astype(jnp.bfloat16), 'dp', scatter_dim...  281 us
    reduce_scatter x1, waiting for transfers between devices, on_device(): lax.psum_scatter(matrix_totals[2].astype(jnp.bfloat16), 'dp', scatter_dim...  281 us
    all_gather x1, waiting for transfers between devices, on_device(): lax.all_gather(down_weight[0], 'dp', axis=0, tiled=True)  218 us
    all_gather x1, waiting for transfers between devices, on_device(): lax.all_gather(up_weight[0], 'dp', axis=0, tiled=True)  201 us
    dot_general x12, matrix products, contract_rows(): lax.dot_general(left_side, right_side, (((0,), (0,)), ((), ())), preferre...  192 us
    all_gather x1, waiting for transfers between devices, on_device(): lax.all_gather(qkv_weight[0], 'dp', axis=0, tiled=True)  172 us
    dot_general x12, matrix products, contract_cols(): lax.dot_general(left_side, right_side, (((1,), (1,)), ((), ())), preferre...  118 us
    reduce_scatter x1, waiting for transfers between devices, on_device(): lax.psum_scatter(matrix_totals[0].astype(jnp.bfloat16), 'dp', scatter_dim...  82.8 us
  transfers between devices with their start and end apart: 18, of which 11 were waited for; matrix products, arithmetic and copies ran while one was open for 20% of the time, Pallas kernels for 0%

commit v1 on v0

v1 whole, which is shorter than its diff:
```python
import math

import jax
import jax.numpy as jnp
from jax import lax
from jax.sharding import PartitionSpec as P

ROT = 64
NORM_EPSILON = 1e-05
MASK_VALUE = -1e30
ROOT_HALF = 0.7071067811865476
DENSITY_SCALE = 0.3989422804014327
F32 = jnp.float32
BF16 = jnp.bfloat16


def contract_rows(left_side, right_side):
    return lax.dot_general(
        left_side, right_side, (((0,), (0,)), ((), ())), preferred_element_type=F32
    )


def contract_cols(left_side, right_side):
    return lax.dot_general(
        left_side, right_side, (((1,), (1,)), ((), ())), preferred_element_type=F32
    )


def matmul(left_side, right_side):
    return jnp.dot(left_side, right_side, preferred_element_type=F32)


def normalize(values):
    centered = values - jnp.mean(values, axis=-1, keepdims=True)
    inverse = lax.rsqrt(jnp.mean(centered * centered, axis=-1, keepdims=True) + NORM_EPSILON)
    return (centered * inverse, inverse)


def document_tables(segments):
    places = jnp.arange(segments.shape[1], dtype=jnp.int32)
    same_doc = segments[:, :, None] == segments[:, None, :]
    earlier = places[None, :] < places[:, None]
    position = jnp.sum(jnp.where(same_doc & earlier, 1, 0).astype(jnp.int32), axis=2)
    allowed = same_doc & (places[None, :] <= places[:, None])
    return (position, allowed)


def rotary_tables(position):
    exponent = jnp.arange(ROT // 2, dtype=F32) * (2.0 / ROT)
    frequency = 10000.0 ** (-exponent)
    angles = position.astype(F32)[..., None] * frequency
    return (jnp.cos(angles), jnp.sin(angles))


def rotate(values, cosine, sine):
    half = ROT // 2
    first, second = values[..., :half], values[..., half:ROT]
    return jnp.concatenate(
        [first * cosine - second * sine, second * cosine + first * sine, values[..., ROT:]],
        axis=-1,
    )


class Layout:
    def __init__(self, mesh, heads):
        self.sections = mesh.shape["section"]
        self.cores = mesh.shape["tensor"]
        self.dp = mesh.shape["dp"]
        self.chips = heads
        self.groups = self.dp // heads
        self.core_heads = heads // self.cores
        self.ring = list(range(0, heads, 2)) + list(range(heads - 1, 0, -2))

    def place(self):
        dp_index = lax.axis_index("dp")
        self.core = lax.axis_index("tensor")
        self.chip = dp_index // self.groups
        self.group = dp_index % self.groups

    def between_chips(self, block, target_of, sections=None):
        if sections is None:
            pairs = [
                (chip * self.groups + group, target_of(chip) * self.groups + group)
                for chip in range(self.chips)
                for group in range(self.groups)
            ]
            return lax.ppermute(block, "dp", pairs)
        pairs = [
            (
                section * self.dp + chip * self.groups + group,
                section * self.dp + target_of(chip) * self.groups + group,
            )
            for section in sections
            for chip in range(self.chips)
            for group in range(self.groups)
        ]
        return lax.ppermute(block, ("section", "dp"), pairs)

    def ring_step(self, block, distance, sections=None):
        size = len(self.ring)

        def target_of(chip):
            return self.ring[(self.ring.index(chip) + distance) % size]

        return self.between_chips(block, target_of, sections)

    def between_groups(self, block, distance):
        pairs = [
            (chip * self.groups + group, chip * self.groups + (group + distance) % self.groups)
            for chip in range(self.chips)
            for group in range(self.groups)
        ]
        return lax.ppermute(block, "dp", pairs)

    def other_core(self, block):
        return lax.ppermute(block, "tensor", [(0, 1), (1, 0)])

    def gather_groups(self, block, axis):
        if self.groups == 1:
            return block
        size = block.shape[axis]
        shape = list(block.shape)
        shape[axis] = size * self.groups
        total = jnp.zeros(shape, block.dtype)
        for distance in range(self.groups):
            part = self.between_groups(block, distance) if distance else block
            source = (self.group - distance) % self.groups
            total = lax.dynamic_update_slice_in_dim(total, part, source * size, axis)
        return total

    def scatter_groups(self, block, axis):
        if self.groups == 1:
            return block.astype(F32)
        size = block.shape[axis] // self.groups
        total = lax.dynamic_slice_in_dim(block, self.group * size, size, axis).astype(F32)
        for distance in range(1, self.groups):
            target = (self.group + distance) % self.groups
            part = lax.dynamic_slice_in_dim(block, target * size, size, axis)
            total = total + self.between_groups(part.astype(BF16), distance).astype(F32)
        return total

    def ring_gather(self, block, sections=None):
        half = self.chips // 2
        below, above = [block], []
        for _ in range(half):
            below.append(self.ring_step(below[-1], -1, sections))
        moving = block
        for _ in range(self.chips - 1 - half):
            moving = self.ring_step(moving, 1, sections)
            above.append(moving)
        return jnp.concatenate(below + above[::-1], axis=0)

    def ring_scatter(self, partial, sections=None):
        half = self.chips // 2
        rows = partial.shape[0] // self.chips
        pieces = [partial[k * rows : (k + 1) * rows] for k in range(self.chips)]
        total = pieces[0].astype(F32)
        moving = pieces[half].astype(BF16)
        for k in range(half - 1, -1, -1):
            arrived = self.ring_step(moving, 1, sections).astype(F32)
            if k == 0:
                total = total + arrived
            else:
                moving = (arrived + pieces[k].astype(F32)).astype(BF16)
        moving = pieces[half + 1].astype(BF16)
        for k in range(half + 2, self.chips + 1):
            arrived = self.ring_step(moving, -1, sections).astype(F32)
            if k == self.chips:
                total = total + arrived
            else:
                moving = (arrived + pieces[k].astype(F32)).astype(BF16)
        return total

    def head_route(self, turn):
        pairs = []
        for core in range(self.cores):
            for chip in range(self.chips):
                head = (chip // self.cores + turn) % self.core_heads
                target_core, target = chip % self.cores, core * self.core_heads + head
                for group in range(self.groups):
                    pairs.append(
                        (
                            core * self.dp + chip * self.groups + group,
                            target_core * self.dp + target * self.groups + group,
                        )
                    )
        return pairs

    def heads_out(self, blocks):
        rows, cols = blocks.shape[1:]
        held = jnp.zeros((self.core_heads, rows, cols), blocks.dtype)
        for turn in range(self.core_heads):
            head = (self.chip // self.cores + turn) % self.core_heads
            block = lax.dynamic_index_in_dim(blocks, head, 0, keepdims=True)
            block = lax.ppermute(block, ("tensor", "dp"), self.head_route(turn))
            slot = (self.chip - turn) % self.core_heads
            held = lax.dynamic_update_slice_in_dim(held, block, slot, 0)
        other = self.other_core(held)
        first = self.core == 0
        whole = jnp.stack(
            [jnp.where(first, held, other), jnp.where(first, other, held)], axis=1
        )
        return whole.reshape(self.chips * rows, cols)

    def heads_back(self, whole):
        rows = whole.shape[0] // self.chips
        cols = whole.shape[1]
        split = whole.reshape(self.core_heads, self.cores, rows, cols)
        first = self.core == 0
        own = jnp.where(first, split[:, 0], split[:, 1])
        given = jnp.where(first, split[:, 1], split[:, 0]).astype(BF16)
        held = (own + self.other_core(given).astype(F32)).astype(BF16)
        blocks = jnp.zeros((self.core_heads, rows, cols), BF16)
        for turn in range(self.core_heads):
            slot = (self.chip - turn) % self.core_heads
            block = lax.dynamic_index_in_dim(held, slot, 0, keepdims=True)
            pairs = [(target, source) for source, target in self.head_route(turn)]
            block = lax.ppermute(block, ("tensor", "dp"), pairs)
            head = (self.chip // self.cores + turn) % self.core_heads
            blocks = lax.dynamic_update_slice_in_dim(blocks, block, head, 0)
        return blocks

    def columns_out(self, block):
        rows = block.shape[0]
        width = block.shape[1] // self.chips
        whole = jnp.zeros((rows * self.chips, width), block.dtype)
        for mask in range(self.chips):
            source = self.chip ^ mask
            part = lax.dynamic_slice_in_dim(block, source * width, width, 1)
            if mask:
                part = self.between_chips(part, lambda chip: chip ^ mask)
            whole = lax.dynamic_update_slice_in_dim(whole, part, source * rows, 0)
        return jnp.concatenate([whole, self.other_core(whole)], axis=1)

    def columns_back(self, whole):
        rows = whole.shape[0] // self.chips
        width = whole.shape[1] // self.cores
        held = whole[:, :width] + self.other_core(whole[:, width:].astype(BF16)).astype(F32)
        held = held.astype(BF16)
        block = jnp.zeros((rows, width * self.chips), BF16)
        for mask in range(self.chips):
            source = self.chip ^ mask
            part = lax.dynamic_slice_in_dim(held, source * rows, rows, 0)
            if mask:
                part = self.between_chips(part, lambda chip: chip ^ mask)
            block = lax.dynamic_update_slice_in_dim(block, part, source * width, 1)
        return block


def attention_parts(joined, tables):
    cosine, sine, allowed = tables
    sequences, length = allowed.shape[:2]
    head_size = joined.shape[1] // 3
    joined = joined.reshape(sequences, length, 3, head_size)
    queries = rotate(joined[:, :, 0], cosine, sine).astype(BF16)
    key_rows = rotate(joined[:, :, 1], cosine, sine).astype(BF16)
    values = joined[:, :, 2].astype(BF16)
    scores = jnp.einsum("sqd,skd->sqk", queries, key_rows, preferred_element_type=F32)
    scores = jnp.where(allowed, scores * (1.0 / math.sqrt(head_size)), MASK_VALUE)
    powered = jnp.exp(scores - jnp.max(scores, axis=-1, keepdims=True))
    attention = powered / jnp.sum(powered, axis=-1, keepdims=True)
    attended = jnp.einsum(
        "sqk,skd->sqd", attention.astype(BF16), values, preferred_element_type=F32
    ).astype(BF16)
    return (queries, key_rows, values, attention, attended.reshape(sequences * length, head_size))


def attention_back(parts, attended_grad, tables):
    queries, key_rows, values, attention, _ = parts
    cosine, sine, _ = tables
    sequences, length, head_size = queries.shape
    scale = 1.0 / math.sqrt(head_size)
    attended_grad = attended_grad.reshape(sequences, length, head_size)
    values_grad = jnp.einsum(
        "sqk,sqd->skd", attention.astype(BF16), attended_grad, preferred_element_type=F32
    )
    attention_grad = jnp.einsum(
        "sqd,skd->sqk", attended_grad, values, preferred_element_type=F32
    )
    row_dots = jnp.sum(attention_grad * attention, axis=-1, keepdims=True)
    scores_grad = (attention * (attention_grad - row_dots)).astype(BF16)
    queries_grad = scale * jnp.einsum(
        "sqk,skd->sqd", scores_grad, key_rows, preferred_element_type=F32
    )
    keys_grad = scale * jnp.einsum(
        "sqk,sqd->skd", scores_grad, queries, preferred_element_type=F32
    )
    return (
        jnp.stack(
            [rotate(queries_grad, cosine, -sine), rotate(keys_grad, cosine, -sine), values_grad],
            axis=2,
        )
        .reshape(sequences * length, 3 * head_size)
        .astype(BF16)
    )


def on_device(
    layout,
    tokens,
    segments,
    cotangent,
    norm_gain,
    norm_bias,
    qkv_weight,
    qkv_bias,
    out_weight,
    out_bias,
    up_weight,
    up_bias,
    down_weight,
    down_bias,
):
    layout.place()
    first_section = lax.axis_index("section") == 0
    cores, chips, chip, core = layout.cores, layout.chips, layout.chip, layout.core
    length = segments.shape[1]
    width = tokens.shape[1]
    core_heads, joined_size = qkv_weight.shape[2:]
    head_size = joined_size // 3
    hidden_part = up_weight.shape[2] // chips

    def core_rows(block):
        return lax.dynamic_slice_in_dim(block, core * length, length, 0)

    def both_cores(rows):
        other = layout.other_core(rows)
        return jnp.concatenate(
            [jnp.where(core == 0, rows, other), jnp.where(core == 0, other, rows)], axis=0
        )

    gains = norm_gain[0].astype(F32)
    shifts = norm_bias[0].astype(F32)
    own_tokens = core_rows(tokens).astype(F32)
    own_cotangent = core_rows(cotangent)
    own_normed, own_inverse = normalize(own_tokens)
    gathered = layout.ring_gather(
        jnp.where(first_section, own_normed.astype(BF16), own_cotangent)
    )

    ring = jnp.array(layout.ring, jnp.int32)
    ring_place = jnp.array([layout.ring.index(c) for c in range(chips)], jnp.int32)
    chip_of = ring[(ring_place[chip] + jnp.arange(chips)) % chips]
    all_segments = lax.all_gather(segments, "dp", axis=0, tiled=True)
    own_segments = all_segments[(chip_of * layout.groups + layout.group) * cores + core]
    position, allowed = document_tables(own_segments)
    tables = rotary_tables(position) + (allowed,)

    shard = qkv_weight.shape[1]
    at = lax.axis_index("dp") * shard
    qkv_scaled = qkv_weight[0].astype(F32) * lax.dynamic_slice_in_dim(gains[0], at, shard)[:, None, None]
    up_scaled = up_weight[0].astype(F32) * lax.dynamic_slice_in_dim(gains[1], at, shard)[:, None]
    joined_weight = layout.heads_out(
        layout.gather_groups(qkv_scaled.astype(BF16).transpose(1, 0, 2), 1)
    )
    out_matrix = layout.heads_out(layout.gather_groups(out_weight[0], 1))
    hidden_weight = layout.columns_out(layout.gather_groups(up_scaled.astype(BF16), 0))
    down_own = layout.gather_groups(down_weight[0], 0)
    down_matrix = jnp.concatenate([down_own, layout.other_core(down_own)], axis=0)

    all_joined_bias = lax.all_gather(qkv_bias[0].astype(F32), "tensor", axis=0, tiled=True)
    all_up_bias = lax.all_gather(up_bias[0].astype(F32), "tensor", axis=0)
    joined_bias = lax.dynamic_index_in_dim(all_joined_bias, chip, 0, keepdims=False)
    hidden_bias = lax.dynamic_slice_in_dim(all_up_bias, chip * hidden_part, hidden_part, 1)
    hidden_bias = jnp.concatenate(
        [
            lax.dynamic_index_in_dim(hidden_bias, core, 0, keepdims=False),
            lax.dynamic_index_in_dim(hidden_bias, 1 - core, 0, keepdims=False),
        ]
    )
    ratio = (shifts / gains).astype(BF16)
    joined_bias = joined_bias + matmul(ratio[:1], joined_weight)[0]
    hidden_bias = hidden_bias + matmul(ratio[1:], hidden_weight)[0]
    row_bias = (out_bias[0].astype(F32) + down_bias[0].astype(F32))[None]

    def forward(normed):
        joined = matmul(normed, joined_weight) + joined_bias
        parts = attention_parts(joined, tables)
        hidden = matmul(normed, hidden_weight) + hidden_bias
        active = jax.nn.gelu(hidden, approximate=False).astype(BF16)
        return (parts, hidden, active)

    def branch(parts, active):
        return matmul(parts[-1], out_matrix) + matmul(active, down_matrix)

    def backward(upstream, parts, hidden):
        attended_grad = contract_cols(upstream, out_matrix).astype(BF16)
        active_grad = contract_cols(upstream, down_matrix)
        normal_cdf = 0.5 * (1.0 + lax.erf(hidden * ROOT_HALF))
        normal_pdf = jnp.exp(-0.5 * hidden * hidden) * DENSITY_SCALE
        hidden_grad = (active_grad * (normal_cdf + hidden * normal_pdf)).astype(BF16)
        joined_grad = attention_back(parts, attended_grad, tables)
        scaled = contract_cols(joined_grad, joined_weight) + contract_cols(
            hidden_grad, hidden_weight
        )
        return (scaled, joined_grad, hidden_grad)

    def norm_back(upstream, scaled, normed, inverse):
        return upstream.astype(F32) + inverse * (
            scaled
            - jnp.mean(scaled, axis=-1, keepdims=True)
            - normed * jnp.mean(scaled * normed, axis=-1, keepdims=True)
        )

    parts, _, active = forward(gathered)
    branch_rows = layout.ring_scatter(branch(parts, active), (0,))
    first_out = (own_tokens + branch_rows + row_bias).astype(BF16)

    arrived = lax.ppermute(first_out, "section", [(0, 1)])
    layer_input = jnp.where(first_section, own_tokens, arrived.astype(F32))
    own_normed, own_inverse = normalize(layer_input)
    normed = layout.ring_gather(own_normed.astype(BF16))
    parts, hidden, active = forward(normed)

    scaled, _, _ = backward(gathered, parts, hidden)
    scaled_rows = layout.ring_scatter(scaled, (1,))
    second_grad = norm_back(own_cotangent, scaled_rows, own_normed, own_inverse)

    arrived_grad = lax.ppermute(second_grad.astype(BF16), "section", [(1, 0)])
    own_upstream = jnp.where(first_section, arrived_grad, own_cotangent)
    upstream = layout.ring_gather(own_upstream)
    scaled, joined_grad, hidden_grad = backward(upstream, parts, hidden)

    branch_rows = layout.ring_scatter(branch(parts, active), (1,))
    second_out = (layer_input + branch_rows + row_bias).astype(BF16)
    layer_outputs = both_cores(jnp.where(first_section, first_out, second_out))

    scaled_rows = layout.ring_scatter(scaled, (0,))
    first_grad = norm_back(own_upstream, scaled_rows, own_normed, own_inverse)
    input_gradients = both_cores(jnp.where(first_section, first_grad, second_grad))

    out_grad = contract_rows(parts[-1], upstream)
    down_grad = contract_rows(active, upstream)
    hidden_weight_grad = contract_rows(normed, hidden_grad)
    joined_weight_grad = contract_rows(normed, joined_grad)
    joined_bias_part = jnp.sum(joined_grad, axis=0, dtype=F32)
    hidden_bias_part = jnp.sum(hidden_grad, axis=0, dtype=F32)

    gain_part = jnp.stack(
        [
            jnp.sum(joined_weight_grad * joined_weight, axis=1),
            jnp.sum(hidden_weight_grad * hidden_weight, axis=1),
        ]
    ) / gains
    shift_part = jnp.stack(
        [
            jnp.sum(joined_weight * joined_bias_part, axis=1),
            jnp.sum(hidden_weight * hidden_bias_part, axis=1),
        ]
    ) / gains
    joined_bias_all = lax.dynamic_update_slice(
        jnp.zeros((chips, joined_size), F32), joined_bias_part[None], (chip, 0)
    )
    hidden_bias_all = jnp.zeros((cores, chips, hidden_part), F32)
    hidden_bias_all = lax.dynamic_update_slice(
        hidden_bias_all, hidden_bias_part[None, None, :hidden_part], (core, chip, 0)
    )
    hidden_bias_all = lax.dynamic_update_slice(
        hidden_bias_all, hidden_bias_part[None, None, hidden_part:], (1 - core, chip, 0)
    )
    vectors = (
        gain_part,
        shift_part,
        joined_bias_all,
        jnp.sum(own_upstream, axis=0, dtype=F32),
        hidden_bias_all,
    )
    sizes = [item.size for item in vectors]
    joint = jnp.concatenate([item.reshape(-1) for item in vectors])
    joint = lax.psum(joint, ("tensor", "dp"))
    summed, start = [], 0
    for item, size in zip(vectors, sizes):
        summed.append(joint[start : start + size].reshape(item.shape))
        start += size
    gain_grad, shift_grad, joined_bias_all, out_bias_grad, hidden_bias_all = summed
    joined_bias_grad = lax.dynamic_slice_in_dim(joined_bias_all, core * core_heads, core_heads, 0)
    up_bias_grad = lax.dynamic_index_in_dim(hidden_bias_all, core, 0, keepdims=False).reshape(-1)

    out_weight_grad = layout.scatter_groups(layout.heads_back(out_grad), 1)
    own_half = down_grad.shape[0] // cores
    down_weight_grad = down_grad[:own_half] + layout.other_core(
        down_grad[own_half:].astype(BF16)
    ).astype(F32)
    if layout.groups > 1:
        down_weight_grad = layout.scatter_groups(down_weight_grad, 0)
    up_plain = layout.scatter_groups(layout.columns_back(hidden_weight_grad), 0)
    joined_plain = layout.scatter_groups(layout.heads_back(joined_weight_grad), 1)
    gain_rows = lax.dynamic_slice_in_dim(gains, at, shard, 1)
    shift_rows = lax.dynamic_slice_in_dim(shifts, at, shard, 1)
    up_weight_grad = up_plain * gain_rows[1][:, None] + shift_rows[1][:, None] * up_bias_grad
    joined_weight_grad = (
        joined_plain.transpose(1, 0, 2) * gain_rows[0][:, None, None]
        + shift_rows[0][:, None, None] * joined_bias_grad
    )

    return (
        layer_outputs[None],
        input_gradients[None],
        gain_grad[None],
        shift_grad[None],
        joined_weight_grad[None],
        joined_bias_grad[None],
        out_weight_grad[None],
        out_bias_grad[None],
        up_weight_grad[None],
        up_bias_grad[None],
        down_weight_grad[None],
        out_bias_grad[None],
    )


def solution(mesh):
    def whole(*arrays):
        layout = Layout(mesh, arrays[5].shape[2])

        def local(*blocks):
            return on_device(layout, *blocks)

        return jax.shard_map(
            local,
            mesh=mesh,
            in_specs=(
                P("dp", None),
                P("dp", None),
                P("dp", None),
                P("section", None, None),
                P("section", None, None),
                P("section", "dp", "tensor", None),
                P("section", "tensor", None),
                P("section", "tensor", "dp", None),
                P("section", None),
                P("section", "dp", "tensor"),
                P("section", "tensor"),
                P("section", ("tensor", "dp"), None),
                P("section", None),
            ),
            out_specs=(
                P("section", "dp", None),
                P("section", "dp", None),
                P("section", None, None),
                P("section", None, None),
                P("section", "dp", "tensor", None),
                P("section", "tensor", None),
                P("section", "tensor", "dp", None),
                P("section", None),
                P("section", "dp", "tensor"),
                P("section", "tensor"),
                P("section", ("tensor", "dp"), None),
                P("section", None),
            ),
            check_vma=False,
        )(*arrays)

    return whole
```

time: 1960 us -> 1070 us (0.55)
  the two profiles are of different devices: /device:TPU:10 before, /device:TPU:16 now
where the time goes in v1:
time: 1070 us; the launch traced here: 1050 us
  waiting for transfers between devices  362 us (34%)
  local copies, waits for them, and re-layouts  230 us (21%)
  starting transfers between devices  173 us (16%)
  matrix products  164 us (15%)
  other arithmetic  84.9 us (8%)
  blocking collectives  18.6 us (2%)
  between operations  17.5 us (2%)
    ppermute x35, waiting for transfers between devices, between_chips(): return lax.ppermute(block, 'dp', pairs)  152 us
    psum x1, waiting for transfers between devices, on_device(): joint = lax.psum(joint, ('tensor', 'dp'))  78.6 us
    dot_general x9, matrix products, matmul(): return jnp.dot(left_side, right_side, preferred_element_type=F32)  74.3 us
    dynamic_update_slice x8, local copies, waits for them, and re-layouts, heads_out(): held = lax.dynamic_update_slice_in_dim(held, block, slot, 0)  62.3 us
    ppermute x28, starting transfers between devices, between_chips(): return lax.ppermute(block, ('section', 'dp'), pairs)  58.4 us
    dynamic_update_slice x8, local copies, waits for them, and re-layouts, heads_back(): blocks = lax.dynamic_update_slice_in_dim(blocks, block, head, 0)  57.6 us
    dot_general x7, matrix products, contract_cols(): lax.dot_general(left_side, right_side, (((1,), (1,)), ((), ())), preferre...  53.2 us
    ppermute x1, waiting for transfers between devices, on_device(): arrived_grad = lax.ppermute(second_grad.astype(BF16), 'section', [(1, 0)])  51.8 us
  transfers between devices with their start and end apart: 92, of which 40 were waited for; matrix products, arithmetic and copies ran while one was open for 30% of the time, Pallas kernels for 0%

profile of v1, /device:TPU:16, one launch (start us, length us, event | category | flops | bytes accessed | tf_op | source)
XLA Modules:
  0.0 1049.6 jit_solution(1312335728201972581)
XLA Ops:
  15.0 6.4 collective-permute-start.15
  34.8 14.8 %all-gather.1 = s32[8,2,128]{2,1,0:T(2,128)S(1)} all-gather(s32[1,2,128]{2,1,0:T(2,128)S(1)} %bitcast.337), channel_id=1, replica_groups=mesh['section'=2,'tensor'=2,'dp'=8] {'dp'}, dimensions={0}, use_global_device_ids=true | all-gather | bytes 9216 | tf_op jit(solution)/shard_map/all_gather | solution.py:344
  91.9 23.6 %collective-permute-start.9 = (bf16[1,256,768]{2,1,0:T(8,128)(2,1)S(1)}, bf16[1,256,768]{2,1,0:T(8,128)(2,1)S(1)}, u32[]{:S(2)}, u32[]{:S(2)}) collective-permute-start(bf16[1,256,768]{2,1,0:T(8,128)(2,1)S(1)} %get-tuple-element.80), channel_id=1, source_target_pairs={{0,2},{1,10},{2,3},{3,11},{4,0},{5,8},{6,1},{7,9},{8,6},{9,14},{10... | collective-permute-start | bytes 1179656 | tf_op jit(solution)/shard_map/ppermute | solution.py:195
  117.9 14.7 %collective-permute-done.22 = bf16[256,512]{0,1:T(8,128)(2,1)S(1)} collective-permute-done((bf16[256,512]{0,1:T(8,128)(2,1)S(1)}, bf16[256,512]{0,1:T(8,128)(2,1)S(1)}, u32[]{:S(2)}, u32[]{:S(2)}) %collective-permute-start.22) | collective-permute-done | bytes 262176 | tf_op jit(solution)/shard_map/ppermute | solution.py:87
  137.9 6.1 collective-permute-start.4
  144.0 5.8 collective-permute-done.9
  153.5 14.6 %dynamic_update_slice.109 = bf16[4,256,768]{2,0,1:T(4,128)(2,1)} dynamic-update-slice(bf16[4,256,768]{2,0,1:T(4,128)(2,1)} %broadcast.332.clone, bf16[1,256,768]{2,0,1:T(2,128)(2,1)S(1)} %copy.171, s32[]{:T(128)S(6)} %select_n.414, s32[]{:T(128)} %constant.327.clone.1, s32[]{:T(128)} %constant.327.clone.1) | dynamic-update-slice | bytes 786436 | tf_op jit(solution)/shard_map/dynamic_update_slice | solution.py:197
  169.8 14.7 %dynamic_update_slice.110 = bf16[4,256,768]{2,0,1:T(4,128)(2,1)} dynamic-update-slice(bf16[4,256,768]{2,0,1:T(4,128)(2,1)} %dynamic_update_slice.109, bf16[1,256,768]{2,0,1:T(2,128)(2,1)S(1)} %copy.172, s32[]{:T(128)S(6)} %select_n.418, s32[]{:T(128)} %constant.327.clone.1, s32[]{:T(128)} %constant.327.clone.1) | dynamic-update-slice | bytes 786436 | tf_op jit(solution)/shard_map/dynamic_update_slice | solution.py:197
  186.0 14.7 %dynamic_update_slice.111 = bf16[4,256,768]{2,0,1:T(4,128)(2,1)} dynamic-update-slice(bf16[4,256,768]{2,0,1:T(4,128)(2,1)} %dynamic_update_slice.110, bf16[1,256,768]{2,0,1:T(2,128)(2,1)S(1)} %copy.173, s32[]{:T(128)S(6)} %select_n.422, s32[]{:T(128)} %constant.327.clone.1, s32[]{:T(128)} %constant.327.clone.1) | dynamic-update-slice | bytes 786436 | tf_op jit(solution)/shard_map/dynamic_update_slice | solution.py:197
  202.7 14.7 %dynamic_update_slice.112 = bf16[4,256,768]{2,0,1:T(4,128)(2,1)} dynamic-update-slice(bf16[4,256,768]{2,0,1:T(4,128)(2,1)} %dynamic_update_slice.111, bf16[1,256,768]{2,0,1:T(2,128)(2,1)S(1)} %copy.174, s32[]{:T(128)S(6)} %select_n.426, s32[]{:T(128)} %constant.327.clone.1, s32[]{:T(128)} %constant.327.clone.1) | dynamic-update-slice | bytes 786436 | tf_op jit(solution)/shard_map/dynamic_update_slice | solution.py:197
  225.4 12.4 %collective-permute-done.5 = bf16[128,2048]{1,0:T(8,128)(2,1)S(1)} collective-permute-done((bf16[128,2048]{1,0:T(8,128)(2,1)}, bf16[128,2048]{1,0:T(8,128)(2,1)S(1)}, u32[]{:S(2)}, u32[]{:S(2)}) %collective-permute-start.5) | collective-permute-done | bytes 524320 | tf_op jit(solution)/shard_map/ppermute | solution.py:87
  285.4 29.7 %fusion.305 = (bf16[1024,2048]{1,0:T(8,128)(2,1)}, f32[1024,2048]{1,0:T(8,128)}) fusion(f32[1024,2048]{1,0:T(8,128)} %fusion.310, bf16[512,2048]{1,0:T(8,128)(2,1)} %collective-permute-done.25, bf16[512,2048]{1,0:T(8,128)(2,1)} %bitcast.339, f32[1024]{0:T(1024)S(1)} %maximum_add_fusion, bf16[1024,2048]{1,0:T(8,128)(2,1)} %copy-done.41, ...), kind=kOutput, calls=%fused_computation.537 | convolution fusion | flops 8680112128 | bytes 33558528 | tf_op jit(solution)/shard_map/dot_general | solution.py:30
  322.2 8.6 collective-permute-done.26
  336.1 9.6 collective-permute-done.27
  353.4 6.8 collective-permute-done.28
  371.9 5.5 collective-permute-done.32
  382.5 6.6 collective-permute-done.33
  390.8 12.7 %collective-permute-done.34 = bf16[128,2048]{1,0:T(8,128)(2,1)S(1)} collective-permute-done((bf16[128,2048]{1,0:T(8,128)(2,1)S(1)}, bf16[128,2048]{1,0:T(8,128)(2,1)S(1)}, u32[]{:S(2)}, u32[]{:S(2)}) %collective-permute-start.34) | collective-permute-done | bytes 524320 | tf_op jit(solution)/shard_map/ppermute | solution.py:87
  405.5 12.3 %collective-permute-done.35 = bf16[128,2048]{1,0:T(8,128)(2,1)S(1)} collective-permute-done((bf16[128,2048]{1,0:T(8,128)(2,1)S(1)}, bf16[128,2048]{1,0:T(8,128)(2,1)S(1)}, u32[]{:S(2)}, u32[]{:S(2)}) %collective-permute-start.35) | collective-permute-done | bytes 524320 | tf_op jit(solution)/shard_map/ppermute | solution.py:87
  422.3 9.9 collective-permute-done.36
  434.4 7.0 collective-permute-done.37
  468.7 5.6 fusion.73
  474.3 15.2 %fusion.9 = (bf16[1024,1024]{1,0:T(8,128)(2,1)}, f32[1024,1024]{1,0:T(8,128)}) fusion(f32[1024]{0:T(1024)S(1)} %copy-done.85, bf16[1024,2048]{1,0:T(8,128)(2,1)S(1)} %copy-done.44, bf16[2048,512]{0,1:T(8,128)(2,1)} %collective-permute-done.24, bf16[2048,512]{0,1:T(8,128)(2,1)S(1)} %copy-done.23), kind=kOutput, calls=%fused_computation.18 | convolution fusion | flops 4372561920 | bytes 14684160 | tf_op jit(solution)/shard_map/dot_general | solution.py:30
  489.5 22.8 %fusion.308 = (bf16[1024,2048]{1,0:T(8,128)(2,1)}, f32[1024,2048]{1,0:T(8,128)}) fusion(f32[1024,2048]{1,0:T(8,128)} %fusion.73, bf16[2048,512]{0,1:T(8,128)(2,1)} %collective-permute-done.24, bf16[2048,512]{0,1:T(8,128)(2,1)} %constant_dynamic-update-slice_fusion.33, bf16[1024,2048]{1,0:T(8,128)(2,1)} %copy-done.41, ...), kind=kOutput, calls=%fused_computation.540 | convolution fusion | flops 8622440448 | bytes 37752832 | tf_op jit(solution)/shard_map/dot_general | solution.py:24
  520.5 9.5 fusion.307
  552.7 51.8 %collective-permute-done.56 = bf16[128,2048]{1,0:T(8,128)(2,1)} collective-permute-done((bf16[128,2048]{1,0:T(8,128)(2,1)S(1)}, bf16[128,2048]{1,0:T(8,128)(2,1)}, u32[]{:S(2)}, u32[]{:S(2)}) %collective-permute-start.56) | collective-permute-done | bytes 524320 | tf_op jit(solution)/shard_map/ppermute | solution.py:419
  610.0 8.1 collective-permute-done.57
  625.0 6.0 collective-permute-done.58
  635.5 9.8 collective-permute-done.59
  666.8 6.0 multiply_reduce_fusion.1
  672.8 6.9 fusion.312
  679.7 7.8 convert_reduce_fusion
  687.6 10.1 fusion.309
  704.8 10.1 fusion.3
  735.3 78.6 %all-reduce.2.cloned.1.call-done = f32[24576]{0:T(1024)} async-done(((f32[24576]{0:T(1024)}), f32[24576]{0:T(1024)}) %all-reduce.2.cloned.1.call-update) | async-done | bytes 98320 | tf_op jit(solution)/shard_map/psum | solution.py:470
  832.4 10.3 collective-permute-done.79
  844.1 5.3 collective-permute-done.80
  849.4 5.7 collective-permute-start.81
  857.1 5.7 collective-permute-start.66
  871.6 5.3 collective-permute-done.66
  888.3 6.5 collective-permute-done.73
  902.2 14.6 %dynamic_update_slice.128 = bf16[4,256,768]{2,0,1:T(4,128)(2,1)S(1)} dynamic-update-slice(bf16[4,256,768]{2,0,1:T(4,128)(2,1)S(1)} %broadcast.332, bf16[1,256,768]{2,0,1:T(2,128)(2,1)} %copy.210, s32[]{:T(128)S(6)} %select_n.412, s32[]{:T(128)} %constant.327.clone.1, s32[]{:T(128)} %constant.327.clone.1) | dynamic-update-slice | bytes 786436 | tf_op jit(solution)/shard_map/dynamic_update_slice | solution.py:220
  918.3 14.3 %dynamic_update_slice.129 = bf16[4,256,768]{2,0,1:T(4,128)(2,1)S(1)} dynamic-update-slice(bf16[4,256,768]{2,0,1:T(4,128)(2,1)S(1)} %dynamic_update_slice.128, bf16[1,256,768]{2,0,1:T(2,128)(2,1)} %copy.211, s32[]{:T(128)S(6)} %select_n.416, s32[]{:T(128)} %constant.327.clone.1, s32[]{:T(128)} %constant.327.clone.1) | dynamic-update-slice | bytes 786436 | tf_op jit(solution)/shard_map/dynamic_update_slice | solution.py:220
  935.2 14.3 %dynamic_update_slice.130 = bf16[4,256,768]{2,0,1:T(4,128)(2,1)S(1)} dynamic-update-slice(bf16[4,256,768]{2,0,1:T(4,128)(2,1)S(1)} %dynamic_update_slice.129, bf16[1,256,768]{2,0,1:T(2,128)(2,1)} %copy.212, s32[]{:T(128)S(6)} %select_n.420, s32[]{:T(128)} %constant.327.clone.1, s32[]{:T(128)} %constant.327.clone.1) | dynamic-update-slice | bytes 786436 | tf_op jit(solution)/shard_map/dynamic_update_slice | solution.py:220
  952.0 14.3 %dynamic_update_slice.131 = bf16[4,256,768]{2,0,1:T(4,128)(2,1)S(1)} dynamic-update-slice(bf16[4,256,768]{2,0,1:T(4,128)(2,1)S(1)} %dynamic_update_slice.130, bf16[1,256,768]{2,0,1:T(2,128)(2,1)} %copy.213, s32[]{:T(128)S(6)} %select_n.424, s32[]{:T(128)} %constant.327.clone.1, s32[]{:T(128)} %constant.327.clone.1) | dynamic-update-slice | bytes 786436 | tf_op jit(solution)/shard_map/dynamic_update_slice | solution.py:220
  993.3 6.0 collective-permute-done.84
  1007.3 14.2 %collective-permute-done.87 = bf16[256,512]{0,1:T(8,128)(2,1)} collective-permute-done((bf16[256,512]{0,1:T(8,128)(2,1)S(1)}, bf16[256,512]{0,1:T(8,128)(2,1)}, u32[]{:S(2)}, u32[]{:S(2)}) %collective-permute-start.87) | collective-permute-done | bytes 262176 | tf_op jit(solution)/shard_map/ppermute | solution.py:87
  1022.6 7.1 collective-permute-done.88
  (612 shorter events, 409.2 us)
Async XLA Ops:
  7.2 806.7 %all-reduce.2.cloned.1.call-start = ((), (), s32[]{:S(2)}) async-start(), calls=%async_computation | async-start | bytes 196608 | tf_op jit(solution)/shard_map/psum | solution.py:470
  9.2 49.9 %collective-permute-start.12 = (bf16[1,32,2048]{2,1,0:T(8,128)(2,1)}, bf16[1,32,2048]{2,1,0:T(8,128)(2,1)}, u32[]{:S(2)}, u32[]{:S(2)}) collective-permute-start(bf16[1,32,2048]{2,1,0:T(8,128)(2,1)} %get-tuple-element.109), channel_id=1, source_target_pairs={{0,0},{1,8},{2,1},{3,9},{4,2},{5,10},{6,3},{7,11},{8,4},{9,12},{10... | collective-permute-start | bytes 393224 | tf_op jit(solution)/shard_map/ppermute | solution.py:195
  11.6 50.9 %collective-permute-start.13 = (bf16[1,32,2048]{2,1,0:T(8,128)(2,1)}, bf16[1,32,2048]{2,1,0:T(8,128)(2,1)}, u32[]{:S(2)}, u32[]{:S(2)}) collective-permute-start(bf16[1,32,2048]{2,1,0:T(8,128)(2,1)} %get-tuple-element.108), channel_id=1, source_target_pairs={{0,1},{1,9},{2,2},{3,10},{4,3},{5,11},{6,0},{7,8},{8,5},{9,13},{10... | collective-permute-start | bytes 393224 | tf_op jit(solution)/shard_map/ppermute | solution.py:195
  14.5 50.0 %collective-permute-start.14 = (bf16[1,32,2048]{2,1,0:T(8,128)(2,1)}, bf16[1,32,2048]{2,1,0:T(8,128)(2,1)}, u32[]{:S(2)}, u32[]{:S(2)}) collective-permute-start(bf16[1,32,2048]{2,1,0:T(8,128)(2,1)} %get-tuple-element.110), channel_id=1, source_target_pairs={{0,2},{1,10},{2,3},{3,11},{4,0},{5,8},{6,1},{7,9},{8,6},{9,14},{10... | collective-permute-start | bytes 393224 | tf_op jit(solution)/shard_map/ppermute | solution.py:195
  15.0 52.9 %collective-permute-start.15 = (bf16[1,32,2048]{2,1,0:T(8,128)(2,1)}, bf16[1,32,2048]{2,1,0:T(8,128)(2,1)}, u32[]{:S(2)}, u32[]{:S(2)}) collective-permute-start(bf16[1,32,2048]{2,1,0:T(8,128)(2,1)} %get-tuple-element.107), channel_id=1, source_target_pairs={{0,3},{1,11},{2,0},{3,8},{4,1},{5,9},{6,2},{7,10},{8,7},{9,15},{10... | collective-permute-start | bytes 393224 | tf_op jit(solution)/shard_map/ppermute | solution.py:195
  31.2 39.9 %collective-permute-start.17 = (bf16[256,512]{0,1:T(8,128)(2,1)}, bf16[256,512]{0,1:T(8,128)(2,1)}, u32[]{:S(2)}, u32[]{:S(2)}) collective-permute-start(bf16[256,512]{0,1:T(8,128)(2,1)} %get-tuple-element.73), channel_id=1, source_target_pairs={{0,1},{1,0},{2,3},{3,2},{4,5},{5,4},{6,7},{7,6},{8,9},{9,8},{10,11... | collective-permute-start | bytes 786440 | tf_op jit(solution)/shard_map/ppermute | solution.py:87
  62.5 19.8 %collective-permute-start.19 = (bf16[256,512]{0,1:T(8,128)(2,1)}, bf16[256,512]{0,1:T(8,128)(2,1)S(1)}, u32[]{:S(2)}, u32[]{:S(2)}) collective-permute-start(bf16[256,512]{0,1:T(8,128)(2,1)} %get-tuple-element.71), channel_id=1, source_target_pairs={{0,3},{1,2},{2,1},{3,0},{4,7},{5,6},{6,5},{7,4},{8,11},{9,10},{10,... | collective-permute-start | bytes 786440 | tf_op jit(solution)/shard_map/ppermute | solution.py:87
  64.5 21.8 %collective-permute-start.20 = (bf16[256,512]{0,1:T(8,128)(2,1)}, bf16[256,512]{0,1:T(8,128)(2,1)S(1)}, u32[]{:S(2)}, u32[]{:S(2)}) collective-permute-start(bf16[256,512]{0,1:T(8,128)(2,1)} %get-tuple-element.70), channel_id=1, source_target_pairs={{0,4},{1,5},{2,6},{3,7},{4,0},{5,1},{6,2},{7,3},{8,12},{9,13},{10,... | collective-permute-start | bytes 786440 | tf_op jit(solution)/shard_map/ppermute | solution.py:87
  67.9 24.0 %collective-permute-start.21 = (bf16[256,512]{0,1:T(8,128)(2,1)}, bf16[256,512]{0,1:T(8,128)(2,1)S(1)}, u32[]{:S(2)}, u32[]{:S(2)}) collective-permute-start(bf16[256,512]{0,1:T(8,128)(2,1)} %get-tuple-element.69), channel_id=1, source_target_pairs={{0,5},{1,4},{2,7},{3,6},{4,1},{5,0},{6,3},{7,2},{8,13},{9,12},{10,... | collective-permute-start | bytes 786440 | tf_op jit(solution)/shard_map/ppermute | solution.py:87
  71.1 78.8 %collective-permute-start = (bf16[128,2048]{1,0:T(8,128)(2,1)S(1)}, bf16[128,2048]{1,0:T(8,128)(2,1)}, u32[]{:S(2)}, u32[]{:S(2)}) collective-permute-start(bf16[128,2048]{1,0:T(8,128)(2,1)S(1)} %get-tuple-element.26), channel_id=1, source_target_pairs={{0,1},{1,3},{2,0},{3,5},{4,2},{5,7},{6,4},{7,6},{8,9},{9,11},{10,8... | collective-permute-start | bytes 1572872 | tf_op jit(solution)/shard_map/ppermute | solution.py:87
  77.0 58.2 %collective-permute-start.7 = (bf16[1,256,768]{2,1,0:T(8,128)(2,1)}, bf16[1,256,768]{2,1,0:T(8,128)(2,1)S(1)}, u32[]{:S(2)}, u32[]{:S(2)}) collective-permute-start(bf16[1,256,768]{2,1,0:T(8,128)(2,1)} %get-tuple-element.82), channel_id=1, source_target_pairs={{0,0},{1,8},{2,1},{3,9},{4,2},{5,10},{6,3},{7,11},{8,4},{9,12},{10... | collective-permute-start | bytes 1179656 | tf_op jit(solution)/shard_map/ppermute | solution.py:195
  82.3 50.3 %collective-permute-start.22 = (bf16[256,512]{0,1:T(8,128)(2,1)S(1)}, bf16[256,512]{0,1:T(8,128)(2,1)S(1)}, u32[]{:S(2)}, u32[]{:S(2)}) collective-permute-start(bf16[256,512]{0,1:T(8,128)(2,1)S(1)} %get-tuple-element.68), channel_id=1, source_target_pairs={{0,6},{1,7},{2,4},{3,5},{4,2},{5,3},{6,0},{7,1},{8,14},{9,15},{10,... | collective-permute-start | bytes 786440 | tf_op jit(solution)/shard_map/ppermute | solution.py:87
  86.2 51.7 %collective-permute-start.8 = (bf16[1,256,768]{2,1,0:T(8,128)(2,1)}, bf16[1,256,768]{2,1,0:T(8,128)(2,1)S(1)}, u32[]{:S(2)}, u32[]{:S(2)}) collective-permute-start(bf16[1,256,768]{2,1,0:T(8,128)(2,1)} %get-tuple-element.81), channel_id=1, source_target_pairs={{0,1},{1,9},{2,2},{3,10},{4,3},{5,11},{6,0},{7,8},{8,5},{9,13},{10... | collective-permute-start | bytes 1179656 | tf_op jit(solution)/shard_map/ppermute | solution.py:195
  91.9 57.9 %collective-permute-start.9 = (bf16[1,256,768]{2,1,0:T(8,128)(2,1)S(1)}, bf16[1,256,768]{2,1,0:T(8,128)(2,1)S(1)}, u32[]{:S(2)}, u32[]{:S(2)}) collective-permute-start(bf16[1,256,768]{2,1,0:T(8,128)(2,1)S(1)} %get-tuple-element.80), channel_id=1, source_target_pairs={{0,2},{1,10},{2,3},{3,11},{4,0},{5,8},{6,1},{7,9},{8,6},{9,14},{10... | collective-permute-start | bytes 1179656 | tf_op jit(solution)/shard_map/ppermute | solution.py:195
  132.6 68.1 %collective-permute-start.10 = (bf16[1,256,768]{2,1,0:T(8,128)(2,1)}, bf16[1,256,768]{2,1,0:T(8,128)(2,1)}, u32[]{:S(2)}, u32[]{:S(2)}) collective-permute-start(bf16[1,256,768]{2,1,0:T(8,128)(2,1)} %get-tuple-element.79), channel_id=1, source_target_pairs={{0,3},{1,11},{2,0},{3,8},{4,1},{5,9},{6,2},{7,10},{8,7},{9,15},{10... | collective-permute-start | bytes 1179656 | tf_op jit(solution)/shard_map/ppermute | solution.py:195
  135.2 82.2 %collective-permute-start.23 = (bf16[256,512]{0,1:T(8,128)(2,1)}, bf16[256,512]{0,1:T(8,128)(2,1)}, u32[]{:S(2)}, u32[]{:S(2)}) collective-permute-start(bf16[256,512]{0,1:T(8,128)(2,1)} %get-tuple-element.67), channel_id=1, source_target_pairs={{0,7},{1,6},{2,5},{3,4},{4,3},{5,2},{6,1},{7,0},{8,15},{9,14},{10,... | collective-permute-start | bytes 786440 | tf_op jit(solution)/shard_map/ppermute | solution.py:87
  137.9 83.1 %collective-permute-start.4 = (bf16[128,2048]{1,0:T(8,128)(2,1)S(1)}, bf16[128,2048]{1,0:T(8,128)(2,1)}, u32[]{:S(2)}, u32[]{:S(2)}) collective-permute-start(bf16[128,2048]{1,0:T(8,128)(2,1)S(1)} %get-tuple-element.26), channel_id=1, source_target_pairs={{0,2},{1,0},{2,4},{3,1},{4,6},{5,3},{6,7},{7,5},{8,10},{9,8},{10,1... | collective-permute-start | bytes 1572872 | tf_op jit(solution)/shard_map/ppermute | solution.py:87
  149.8 71.6 %collective-permute-start.16 = (bf16[4,32,2048]{2,1,0:T(8,128)(2,1)S(1)}, bf16[4,32,2048]{2,1,0:T(8,128)(2,1)S(1)}, u32[]{:S(2)}, u32[]{:S(2)}) collective-permute-start(bf16[4,32,2048]{2,1,0:T(8,128)(2,1)S(1)} %constant_dynamic-update-slice_fusion.40), channel_id=1, source_target_pairs={{0,8},{8,0},{1,9},{9,1},{2,10},{10,2},{3,11},{11,3},{4,12},{12,4},... | collective-permute-start | bytes 1572872 | tf_op jit(solution)/shard_map/ppermute | solution.py:116
  149.8 73.4 %collective-permute-start.1 = (bf16[128,2048]{1,0:T(8,128)(2,1)}, bf16[128,2048]{1,0:T(8,128)(2,1)}, u32[]{:S(2)}, u32[]{:S(2)}) collective-permute-start(bf16[128,2048]{1,0:T(8,128)(2,1)} %collective-permute-done), channel_id=1, source_target_pairs={{0,1},{1,3},{2,0},{3,5},{4,2},{5,7},{6,4},{7,6},{8,9},{9,11},{10,8... | collective-permute-start | bytes 1572872 | tf_op jit(solution)/shard_map/ppermute | solution.py:87
  200.7 84.6 %collective-permute-start.25 = (bf16[512,2048]{1,0:T(8,128)(2,1)}, bf16[512,2048]{1,0:T(8,128)(2,1)}, u32[]{:S(2)}, u32[]{:S(2)}) collective-permute-start(bf16[512,2048]{1,0:T(8,128)(2,1)} %bitcast.338), channel_id=1, source_target_pairs={{0,8},{8,0},{1,9},{9,1},{2,10},{10,2},{3,11},{11,3},{4,12},{12,4},... | collective-permute-start | bytes 6291464 | tf_op jit(solution)/shard_map/ppermute | solution.py:116
  217.4 23.8 %collective-permute-start.11 = (bf16[4,256,768]{2,0,1:T(4,128)(2,1)}, bf16[4,256,768]{2,0,1:T(4,128)(2,1)S(1)}, u32[]{:S(2)}, u32[]{:S(2)}) collective-permute-start(bf16[4,256,768]{2,0,1:T(4,128)(2,1)} %dynamic_update_slice.112), channel_id=1, source_target_pairs={{0,8},{8,0},{1,9},{9,1},{2,10},{10,2},{3,11},{11,3},{4,12},{12,4},... | collective-permute-start | bytes 4718600 | tf_op jit(solution)/shard_map/ppermute | solution.py:116
  221.0 61.5 %collective-permute-start.24 = (bf16[2048,512]{0,1:T(8,128)(2,1)}, bf16[2048,512]{0,1:T(8,128)(2,1)}, u32[]{:S(2)}, u32[]{:S(2)}) collective-permute-start(bf16[2048,512]{0,1:T(8,128)(2,1)} %constant_dynamic-update-slice_fusion.33), channel_id=1, source_target_pairs={{0,8},{8,0},{1,9},{9,1},{2,10},{10,2},{3,11},{11,3},{4,12},{12,4},... | collective-permute-start | bytes 6291464 | tf_op jit(solution)/shard_map/ppermute | solution.py:116
  546.6 58.0 %collective-permute-start.56 = (bf16[128,2048]{1,0:T(8,128)(2,1)S(1)}, bf16[128,2048]{1,0:T(8,128)(2,1)}, u32[]{:S(2)}, u32[]{:S(2)}) collective-permute-start(bf16[128,2048]{1,0:T(8,128)(2,1)S(1)} %fusion.281), channel_id=1, source_target_pairs={{16,0},{17,1},{18,2},{19,3},{20,4},{21,5},{22,6},{23,7},{24,8},{25... | collective-permute-start | bytes 1572872 | tf_op jit(solution)/shard_map/ppermute | solution.py:419
  549.2 57.9 %collective-permute-start.47 = (bf16[128,2048]{1,0:T(8,128)(2,1)}, bf16[128,2048]{1,0:T(8,128)(2,1)}, u32[]{:S(2)}, u32[]{:S(2)}) collective-permute-start(bf16[128,2048]{1,0:T(8,128)(2,1)} %get-tuple-element.36), channel_id=1, source_target_pairs={{16,17},{17,19},{18,16},{19,21},{20,18},{21,23},{22,20},{23,22},{2... | collective-permute-start | bytes 1572872 | tf_op jit(solution)/shard_map/ppermute | solution.py:97
  550.7 56.4 %collective-permute-start.44 = (bf16[128,2048]{1,0:T(8,128)(2,1)}, bf16[128,2048]{1,0:T(8,128)(2,1)}, u32[]{:S(2)}, u32[]{:S(2)}) collective-permute-start(bf16[128,2048]{1,0:T(8,128)(2,1)} %get-tuple-element.35), channel_id=1, source_target_pairs={{16,18},{17,16},{18,20},{19,17},{20,22},{21,19},{22,23},{23,21},{2... | collective-permute-start | bytes 1572872 | tf_op jit(solution)/shard_map/ppermute | solution.py:97
  610.0 21.0 %collective-permute-start.48 = (bf16[128,2048]{1,0:T(8,128)(2,1)}, bf16[128,2048]{1,0:T(8,128)(2,1)}, u32[]{:S(2)}, u32[]{:S(2)}) collective-permute-start(bf16[128,2048]{1,0:T(8,128)(2,1)} %fusion.125), channel_id=1, source_target_pairs={{0,8},{8,0},{1,9},{9,1},{2,10},{10,2},{3,11},{11,3},{4,12},{12,4},... | collective-permute-start | bytes 1572872 | tf_op jit(solution)/shard_map/ppermute | solution.py:116
  698.7 125.9 %collective-permute-start.64 = (bf16[128,2048]{1,0:T(8,128)(2,1)}, bf16[128,2048]{1,0:T(8,128)(2,1)}, u32[]{:S(2)}, u32[]{:S(2)}) collective-permute-start(bf16[128,2048]{1,0:T(8,128)(2,1)} %get-tuple-element.43), channel_id=1, source_target_pairs={{0,2},{1,0},{2,4},{3,1},{4,6},{5,3},{6,7},{7,5},{8,10},{9,8},{10,1... | collective-permute-start | bytes 1572872 | tf_op jit(solution)/shard_map/ppermute | solution.py:97
  702.8 152.2 %collective-permute-start.68 = (bf16[128,2048]{1,0:T(8,128)(2,1)}, bf16[128,2048]{1,0:T(8,128)(2,1)}, u32[]{:S(2)}, u32[]{:S(2)}) collective-permute-start(bf16[128,2048]{1,0:T(8,128)(2,1)} %get-tuple-element.44), channel_id=1, source_target_pairs={{0,1},{1,3},{2,0},{3,5},{4,2},{5,7},{6,4},{7,6},{8,9},{9,11},{10,8... | collective-permute-start | bytes 1572872 | tf_op jit(solution)/shard_map/ppermute | solution.py:97
  724.3 141.8 %collective-permute-start.72 = (bf16[4,256,768]{2,1,0:T(8,128)(2,1)}, bf16[4,256,768]{2,1,0:T(8,128)(2,1)}, u32[]{:S(2)}, u32[]{:S(2)}) collective-permute-start(bf16[4,256,768]{2,1,0:T(8,128)(2,1)} %fusion.68), channel_id=1, source_target_pairs={{0,8},{8,0},{1,9},{9,1},{2,10},{10,2},{3,11},{11,3},{4,12},{12,4},... | collective-permute-start | bytes 4718600 | tf_op jit(solution)/shard_map/ppermute | solution.py:116
  727.0 93.5 %collective-permute-start.77 = (bf16[4,32,2048]{2,1,0:T(8,128)(2,1)S(1)}, bf16[4,32,2048]{2,1,0:T(8,128)(2,1)S(1)}, u32[]{:S(2)}, u32[]{:S(2)}) collective-permute-start(bf16[4,32,2048]{2,1,0:T(8,128)(2,1)S(1)} %fusion.124), channel_id=1, source_target_pairs={{0,8},{8,0},{1,9},{9,1},{2,10},{10,2},{3,11},{11,3},{4,12},{12,4},... | collective-permute-start | bytes 1572872 | tf_op jit(solution)/shard_map/ppermute | solution.py:116
  731.4 243.4 %collective-permute-start.82 = (bf16[2048,512]{0,1:T(8,128)(2,1)}, bf16[2048,512]{0,1:T(8,128)(2,1)}, u32[]{:S(2)}, u32[]{:S(2)}) collective-permute-start(bf16[2048,512]{0,1:T(8,128)(2,1)} %slice.647), channel_id=1, source_target_pairs={{0,8},{8,0},{1,9},{9,1},{2,10},{10,2},{3,11},{11,3},{4,12},{12,4},... | collective-permute-start | bytes 6291464 | tf_op jit(solution)/shard_map/ppermute | solution.py:116
  826.2 28.9 %collective-permute-start.65 = (bf16[128,2048]{1,0:T(8,128)(2,1)S(1)}, bf16[128,2048]{1,0:T(8,128)(2,1)S(1)}, u32[]{:S(2)}, u32[]{:S(2)}) collective-permute-start(bf16[128,2048]{1,0:T(8,128)(2,1)S(1)} %fusion.97), channel_id=1, source_target_pairs={{0,2},{1,0},{2,4},{3,1},{4,6},{5,3},{6,7},{7,5},{8,10},{9,8},{10,1... | collective-permute-start | bytes 1572872 | tf_op jit(solution)/shard_map/ppermute | solution.py:97
  849.4 36.4 %collective-permute-start.81 = (bf16[1,32,2048]{2,1,0:T(8,128)(2,1)S(1)}, bf16[1,32,2048]{2,1,0:T(8,128)(2,1)S(1)}, u32[]{:S(2)}, u32[]{:S(2)}) collective-permute-start(bf16[1,32,2048]{2,1,0:T(8,128)(2,1)S(1)} %get-tuple-element.103), channel_id=1, source_target_pairs={{3,0},{11,1},{0,2},{8,3},{1,4},{9,5},{2,6},{10,7},{7,8},{15,9},{4,... | collective-permute-start | bytes 393224 | tf_op jit(solution)/shard_map/ppermute | solution.py:218
  857.1 19.9 %collective-permute-start.66 = (bf16[128,2048]{1,0:T(8,128)(2,1)S(1)}, bf16[128,2048]{1,0:T(8,128)(2,1)S(1)}, u32[]{:S(2)}, u32[]{:S(2)}) collective-permute-start(bf16[128,2048]{1,0:T(8,128)(2,1)S(1)} %get-tuple-element.29), channel_id=1, source_target_pairs={{0,2},{1,0},{2,4},{3,1},{4,6},{5,3},{6,7},{7,5},{8,10},{9,8},{10,1... | collective-permute-start | bytes 1572872 | tf_op jit(solution)/shard_map/ppermute | solution.py:97
  869.3 25.6 %collective-permute-start.73 = (bf16[1,256,768]{2,1,0:T(8,128)(2,1)S(1)}, bf16[1,256,768]{2,1,0:T(8,128)(2,1)S(1)}, u32[]{:S(2)}, u32[]{:S(2)}) collective-permute-start(bf16[1,256,768]{2,1,0:T(8,128)(2,1)S(1)} %get-tuple-element.78), channel_id=1, source_target_pairs={{0,0},{8,1},{1,2},{9,3},{2,4},{10,5},{3,6},{11,7},{4,8},{12,9},{5,... | collective-permute-start | bytes 1179656 | tf_op jit(solution)/shard_map/ppermute | solution.py:218
  877.0 19.2 %collective-permute-start.74 = (bf16[1,256,768]{2,1,0:T(8,128)(2,1)S(1)}, bf16[1,256,768]{2,1,0:T(8,128)(2,1)S(1)}, u32[]{:S(2)}, u32[]{:S(2)}) collective-permute-start(bf16[1,256,768]{2,1,0:T(8,128)(2,1)S(1)} %get-tuple-element.77), channel_id=1, source_target_pairs={{1,0},{9,1},{2,2},{10,3},{3,4},{11,5},{0,6},{8,7},{5,8},{13,9},{6,... | collective-permute-start | bytes 1179656 | tf_op jit(solution)/shard_map/ppermute | solution.py:218
  882.5 86.2 %collective-permute-start.70 = (bf16[128,2048]{1,0:T(8,128)(2,1)}, bf16[128,2048]{1,0:T(8,128)(2,1)}, u32[]{:S(2)}, u32[]{:S(2)}) collective-permute-start(bf16[128,2048]{1,0:T(8,128)(2,1)} %get-tuple-element.28), channel_id=1, source_target_pairs={{0,1},{1,3},{2,0},{3,5},{4,2},{5,7},{6,4},{7,6},{8,9},{9,11},{10,8... | collective-permute-start | bytes 1572872 | tf_op jit(solution)/shard_map/ppermute | solution.py:97
  885.8 82.9 %collective-permute-start.67 = (bf16[128,2048]{1,0:T(8,128)(2,1)}, bf16[128,2048]{1,0:T(8,128)(2,1)}, u32[]{:S(2)}, u32[]{:S(2)}) collective-permute-start(bf16[128,2048]{1,0:T(8,128)(2,1)} %get-tuple-element.27), channel_id=1, source_target_pairs={{0,2},{1,0},{2,4},{3,1},{4,6},{5,3},{6,7},{7,5},{8,10},{9,8},{10,1... | collective-permute-start | bytes 1572872 | tf_op jit(solution)/shard_map/ppermute | solution.py:97
  894.8 37.8 %collective-permute-start.75 = (bf16[1,256,768]{2,1,0:T(8,128)(2,1)}, bf16[1,256,768]{2,1,0:T(8,128)(2,1)}, u32[]{:S(2)}, u32[]{:S(2)}) collective-permute-start(bf16[1,256,768]{2,1,0:T(8,128)(2,1)} %get-tuple-element.76), channel_id=1, source_target_pairs={{2,0},{10,1},{3,2},{11,3},{0,4},{8,5},{1,6},{9,7},{6,8},{14,9},{7,... | collective-permute-start | bytes 1179656 | tf_op jit(solution)/shard_map/ppermute | solution.py:218
  896.1 53.4 %collective-permute-start.76 = (bf16[1,256,768]{2,1,0:T(8,128)(2,1)}, bf16[1,256,768]{2,1,0:T(8,128)(2,1)}, u32[]{:S(2)}, u32[]{:S(2)}) collective-permute-start(bf16[1,256,768]{2,1,0:T(8,128)(2,1)} %get-tuple-element.75), channel_id=1, source_target_pairs={{3,0},{11,1},{0,2},{8,3},{1,4},{9,5},{2,6},{10,7},{7,8},{15,9},{4,... | collective-permute-start | bytes 1179656 | tf_op jit(solution)/shard_map/ppermute | solution.py:218
  932.7 50.9 %collective-permute-start.90 = (bf16[512,2048]{1,0:T(8,128)(2,1)}, bf16[512,2048]{1,0:T(8,128)(2,1)}, u32[]{:S(2)}, u32[]{:S(2)}) collective-permute-start(bf16[512,2048]{1,0:T(8,128)(2,1)} %slice.646), channel_id=1, source_target_pairs={{0,8},{8,0},{1,9},{9,1},{2,10},{10,2},{3,11},{11,3},{4,12},{12,4},... | collective-permute-start | bytes 6291464 | tf_op jit(solution)/shard_map/ppermute | solution.py:116
  974.4 64.2 %collective-permute-start.71 = (f32[128,2048]{1,0:T(8,128)}, f32[128,2048]{1,0:T(8,128)}, u32[]{:S(2)}, u32[]{:S(2)}) collective-permute-start(f32[128,2048]{1,0:T(8,128)} %fusion.90), channel_id=1, source_target_pairs={{0,8},{8,0},{1,9},{9,1},{2,10},{10,2},{3,11},{11,3},{4,12},{12,4},... | collective-permute-start | bytes 3145736 | tf_op jit(solution)/shard_map/ppermute | solution.py:116
  979.8 19.6 %collective-permute-start.84 = (bf16[256,512]{0,1:T(8,128)(2,1)}, bf16[256,512]{0,1:T(8,128)(2,1)}, u32[]{:S(2)}, u32[]{:S(2)}) collective-permute-start(bf16[256,512]{0,1:T(8,128)(2,1)} %get-tuple-element.62), channel_id=1, source_target_pairs={{0,2},{1,3},{2,0},{3,1},{4,6},{5,7},{6,4},{7,5},{8,10},{9,11},{10,... | collective-permute-start | bytes 786440 | tf_op jit(solution)/shard_map/ppermute | solution.py:87
  983.6 20.0 %collective-permute-start.85 = (bf16[256,512]{0,1:T(8,128)(2,1)}, bf16[256,512]{0,1:T(8,128)(2,1)}, u32[]{:S(2)}, u32[]{:S(2)}) collective-permute-start(bf16[256,512]{0,1:T(8,128)(2,1)} %get-tuple-element.61), channel_id=1, source_target_pairs={{0,3},{1,2},{2,1},{3,0},{4,7},{5,6},{6,5},{7,4},{8,11},{9,10},{10,... | collective-permute-start | bytes 786440 | tf_op jit(solution)/shard_map/ppermute | solution.py:87
  983.6 22.5 %collective-permute-start.86 = (bf16[256,512]{0,1:T(8,128)(2,1)}, bf16[256,512]{0,1:T(8,128)(2,1)}, u32[]{:S(2)}, u32[]{:S(2)}) collective-permute-start(bf16[256,512]{0,1:T(8,128)(2,1)} %get-tuple-element.60), channel_id=1, source_target_pairs={{0,4},{1,5},{2,6},{3,7},{4,0},{5,1},{6,2},{7,3},{8,12},{9,13},{10,... | collective-permute-start | bytes 786440 | tf_op jit(solution)/shard_map/ppermute | solution.py:87
  991.3 30.2 %collective-permute-start.87 = (bf16[256,512]{0,1:T(8,128)(2,1)S(1)}, bf16[256,512]{0,1:T(8,128)(2,1)}, u32[]{:S(2)}, u32[]{:S(2)}) collective-permute-start(bf16[256,512]{0,1:T(8,128)(2,1)S(1)} %get-tuple-element.59), channel_id=1, source_target_pairs={{0,5},{1,4},{2,7},{3,6},{4,1},{5,0},{6,3},{7,2},{8,13},{9,12},{10,... | collective-permute-start | bytes 786440 | tf_op jit(solution)/shard_map/ppermute | solution.py:87
  999.4 30.3 %collective-permute-start.88 = (bf16[256,512]{0,1:T(8,128)(2,1)S(1)}, bf16[256,512]{0,1:T(8,128)(2,1)}, u32[]{:S(2)}, u32[]{:S(2)}) collective-permute-start(bf16[256,512]{0,1:T(8,128)(2,1)S(1)} %get-tuple-element.58), channel_id=1, source_target_pairs={{0,6},{1,7},{2,4},{3,5},{4,2},{5,3},{6,0},{7,1},{8,14},{9,15},{10,... | collective-permute-start | bytes 786440 | tf_op jit(solution)/shard_map/ppermute | solution.py:87
  1003.6 30.9 %collective-permute-start.89 = (bf16[256,512]{0,1:T(8,128)(2,1)S(1)}, bf16[256,512]{0,1:T(8,128)(2,1)}, u32[]{:S(2)}, u32[]{:S(2)}) collective-permute-start(bf16[256,512]{0,1:T(8,128)(2,1)S(1)} %get-tuple-element.57), channel_id=1, source_target_pairs={{0,7},{1,6},{2,5},{3,4},{4,3},{5,2},{6,1},{7,0},{8,15},{9,14},{10,... | collective-permute-start | bytes 786440 | tf_op jit(solution)/shard_map/ppermute | solution.py:87
  (144 other events, 2160.3 us)
Sparse Core Ops, SparseCore 0:
  720.0 93.7 all-reduce.1

commit v2 on v1

v2 whole, which is shorter than its diff:
```python
import functools
import math

import jax
import jax.numpy as jnp
from jax import lax
from jax.experimental import pallas as pl
from jax.experimental.pallas import tpu as pltpu
from jax.sharding import PartitionSpec as P

ROT = 64
LANES = 128
NORM_EPSILON = 1e-05
MASK_VALUE = -1e30
ROOT_HALF = 0.7071067811865476
DENSITY_SCALE = 0.3989422804014327
F32 = jnp.float32
BF16 = jnp.bfloat16


def contract_rows(left_side, right_side):
    return lax.dot_general(
        left_side, right_side, (((0,), (0,)), ((), ())), preferred_element_type=F32
    )


def contract_cols(left_side, right_side):
    return lax.dot_general(
        left_side, right_side, (((1,), (1,)), ((), ())), preferred_element_type=F32
    )


def matmul(left_side, right_side):
    return jnp.dot(left_side, right_side, preferred_element_type=F32)


def normalize(values):
    centered = values - jnp.mean(values, axis=-1, keepdims=True)
    inverse = lax.rsqrt(jnp.mean(centered * centered, axis=-1, keepdims=True) + NORM_EPSILON)
    return (centered * inverse, inverse)


def sequence_tables(segments):
    places = jnp.arange(segments.shape[1], dtype=jnp.int32)
    same_doc = segments[:, :, None] == segments[:, None, :]
    earlier = places[None, :] < places[:, None]
    position = jnp.sum(jnp.where(same_doc & earlier, 1, 0).astype(jnp.int32), axis=2)
    allowed = same_doc & (places[None, :] <= places[:, None])
    exponent = jnp.arange(ROT // 2, dtype=F32) * (2.0 / ROT)
    frequency = 10000.0 ** (-exponent)
    angles = position.astype(F32)[..., None] * frequency
    cosine, sine = jnp.cos(angles), jnp.sin(angles)
    rest = jnp.zeros(angles.shape[:2] + (LANES - ROT,), F32)
    count = segments.shape[0] * segments.shape[1]
    return (
        jnp.concatenate([cosine, cosine, rest + 1.0], axis=-1).reshape(count, LANES),
        jnp.concatenate([-sine, sine, rest], axis=-1).reshape(count, LANES),
        jnp.where(allowed, 0.0, MASK_VALUE).astype(F32).reshape(count, segments.shape[1]),
    )


class Layout:
    def __init__(self, mesh, heads):
        self.cores = mesh.shape["tensor"]
        self.dp = mesh.shape["dp"]
        self.chips = heads
        self.groups = self.dp // heads
        self.core_heads = heads // self.cores
        self.ring = list(range(0, heads, 2)) + list(range(heads - 1, 0, -2))
        self.slots = []
        for k in range(heads // 2):
            self.slots += [-k % heads, k + 1]

    def place(self):
        dp_index = lax.axis_index("dp")
        self.core = lax.axis_index("tensor")
        self.chip = dp_index // self.groups
        self.group = dp_index % self.groups

    def between_chips(self, block, target_of, sections=None):
        pairs = [
            (chip * self.groups + group, target_of(chip) * self.groups + group)
            for chip in range(self.chips)
            for group in range(self.groups)
        ]
        if sections is None:
            return lax.ppermute(block, "dp", pairs)
        pairs = [
            (section * self.dp + source, section * self.dp + target)
            for section in sections
            for source, target in pairs
        ]
        return lax.ppermute(block, ("section", "dp"), pairs)

    def ring_step(self, block, distance, sections=None):
        size = len(self.ring)

        def target_of(chip):
            return self.ring[(self.ring.index(chip) + distance) % size]

        return self.between_chips(block, target_of, sections)

    def between_groups(self, block, distance):
        pairs = [
            (chip * self.groups + group, chip * self.groups + (group + distance) % self.groups)
            for chip in range(self.chips)
            for group in range(self.groups)
        ]
        return lax.ppermute(block, "dp", pairs)

    def other_core(self, block):
        return lax.ppermute(block, "tensor", [(0, 1), (1, 0)])

    def by_core(self, own, other):
        first = self.core == 0
        return jnp.concatenate(
            [jnp.where(first, own, other), jnp.where(first, other, own)], axis=0
        )

    def gather_groups(self, block, axis):
        if self.groups == 1:
            return block
        size = block.shape[axis]
        shape = list(block.shape)
        shape[axis] = size * self.groups
        total = jnp.zeros(shape, block.dtype)
        for distance in range(self.groups):
            part = self.between_groups(block, distance) if distance else block
            source = (self.group - distance) % self.groups
            total = lax.dynamic_update_slice_in_dim(total, part, source * size, axis)
        return total

    def scatter_groups(self, block, axis):
        if self.groups == 1:
            return block.astype(F32)
        size = block.shape[axis] // self.groups
        total = lax.dynamic_slice_in_dim(block, self.group * size, size, axis).astype(F32)
        for distance in range(1, self.groups):
            target = (self.group + distance) % self.groups
            part = lax.dynamic_slice_in_dim(block, target * size, size, axis)
            total = total + self.between_groups(part.astype(BF16), distance).astype(F32)
        return total

    def gather_chips(self, block):
        held = block[None]
        mask = 1
        while mask < self.chips:
            held = jnp.concatenate(
                [held, self.between_chips(held, lambda chip: chip ^ mask)], axis=0
            )
            mask *= 2
        return held

    def sum_all(self, block):
        block = block + self.other_core(block)
        mask = 1
        while mask < self.chips:
            block = block + self.between_chips(block, lambda chip: chip ^ mask)
            mask *= 2
        total = block
        for distance in range(1, self.groups):
            total = total + self.between_groups(block, distance)
        return total

    def ring_gather(self, block):
        half = self.chips // 2
        held = {0: block}
        for k in range(1, half + 1):
            held[k] = self.ring_step(held[k - 1], -1)
            if k < half:
                held[self.chips - k] = self.ring_step(held[(self.chips - k + 1) % self.chips], 1)
        return held

    def ring_scatter(self, pieces, sections):
        half = self.chips // 2
        total = pieces[0].astype(F32)
        moving = pieces[half]
        for k in range(half - 1, -1, -1):
            arrived = self.ring_step(moving, 1, sections).astype(F32)
            if k == 0:
                total = total + arrived
            else:
                moving = (arrived + pieces[k].astype(F32)).astype(BF16)
        moving = pieces[half + 1]
        for k in range(half + 2, self.chips + 1):
            arrived = self.ring_step(moving, -1, sections).astype(F32)
            if k == self.chips:
                total = total + arrived
            else:
                moving = (arrived + pieces[k].astype(F32)).astype(BF16)
        return total

    def head_turn(self, chip, turn):
        return (chip % self.core_heads + turn) % self.core_heads

    def head_route(self, turn):
        pairs = []
        for core in range(self.cores):
            for chip in range(self.chips):
                target_core = chip // self.core_heads
                target = core * self.core_heads + self.head_turn(chip, turn)
                for group in range(self.groups):
                    pairs.append(
                        (
                            core * self.dp + chip * self.groups + group,
                            target_core * self.dp + target * self.groups + group,
                        )
                    )
        return pairs

    def heads_out(self, take):
        held = None
        for turn in range(self.core_heads):
            block = take(self.head_turn(self.chip, turn))
            block = lax.ppermute(block, ("tensor", "dp"), self.head_route(turn))
            rows, cols = block.shape
            if held is None:
                held = jnp.zeros((self.core_heads * rows, cols), block.dtype)
            slot = (self.chip - turn) % self.core_heads
            held = lax.dynamic_update_slice_in_dim(held, block, slot * rows, 0)
        return self.by_core(held, self.other_core(held))

    def heads_back(self, held, put, blocks):
        rows = held.shape[0] // self.core_heads
        for turn in range(self.core_heads):
            slot = (self.chip - turn) % self.core_heads
            block = lax.dynamic_slice_in_dim(held, slot * rows, rows, 0)
            pairs = [(target, source) for source, target in self.head_route(turn)]
            block = lax.ppermute(block, ("tensor", "dp"), pairs)
            blocks = put(blocks, self.head_turn(self.chip, turn), block)
        return blocks

    def columns_out(self, block):
        rows = block.shape[0]
        width = block.shape[1] // self.chips
        whole = jnp.zeros((rows * self.chips, width), block.dtype)
        for mask in range(self.chips):
            source = self.chip ^ mask
            part = lax.dynamic_slice_in_dim(block, source * width, width, 1)
            if mask:
                part = self.between_chips(part, lambda chip: chip ^ mask)
            whole = lax.dynamic_update_slice_in_dim(whole, part, source * rows, 0)
        return jnp.concatenate([whole, self.other_core(whole)], axis=1)

    def columns_back(self, held):
        rows = held.shape[0] // self.chips
        width = held.shape[1]
        block = jnp.zeros((rows, width * self.chips), BF16)
        for mask in range(self.chips):
            source = self.chip ^ mask
            part = lax.dynamic_slice_in_dim(held, source * rows, rows, 0)
            if mask:
                part = self.between_chips(part, lambda chip: chip ^ mask)
            block = lax.dynamic_update_slice_in_dim(block, part, source * width, 1)
        return block


def turn_head(values, cosine, sine):
    first = values[:, :LANES]
    lane = lax.broadcasted_iota(jnp.int32, first.shape, 1)
    half = ROT // 2
    swapped = jnp.where(
        lane < half, pltpu.roll(first, LANES - half, 1), pltpu.roll(first, half, 1)
    )
    return jnp.concatenate([first * cosine + swapped * sine, values[:, LANES:]], axis=1)


def attend(joined, cosine, sine, mask):
    size = joined.shape[1] // 3
    queries = turn_head(joined[:, :size], cosine, sine).astype(BF16)
    key_rows = turn_head(joined[:, size : 2 * size], cosine, sine).astype(BF16)
    values = joined[:, 2 * size :].astype(BF16)
    scores = contract_cols(queries, key_rows) * (1.0 / math.sqrt(size)) + mask
    powered = jnp.exp(scores - jnp.max(scores, axis=-1, keepdims=True))
    attention = powered / jnp.sum(powered, axis=-1, keepdims=True)
    attended = matmul(attention.astype(BF16), values).astype(BF16)
    return (queries, key_rows, values, attention, attended)


def attend_back(queries, key_rows, values, attention, attended_grad, cosine, sine):
    scale = 1.0 / math.sqrt(queries.shape[1])
    values_grad = contract_rows(attention.astype(BF16), attended_grad)
    attention_grad = contract_cols(attended_grad, values)
    row_dots = jnp.sum(attention_grad * attention, axis=-1, keepdims=True)
    scores_grad = (attention * (attention_grad - row_dots)).astype(BF16)
    queries_grad = turn_head(matmul(scores_grad, key_rows) * scale, cosine, -sine)
    keys_grad = turn_head(contract_rows(scores_grad, queries) * scale, cosine, -sine)
    return jnp.concatenate([queries_grad, keys_grad, values_grad], axis=1).astype(BF16)


def fold_rows(values):
    return jnp.sum(values.reshape(values.shape[0] // 8, 8, values.shape[1]), axis=0)


def forward_kernel(
    n0, n1, wq, bq, wu, bu, wo, wd, cosine, sine, mask, out0, out1, normed, attended, active
):
    length = n0.shape[0]
    normed[:length] = n0[...]
    normed[length:] = n1[...]
    joined = matmul(normed[...], wq[...]) + bq[...]
    for s in range(2):
        rows = slice(s * length, (s + 1) * length)
        attended[rows] = attend(joined[rows], cosine[rows], sine[rows], mask[rows])[4]
    step = min(256, wu.shape[1])
    for at in range(0, wu.shape[1], step):
        hidden = matmul(normed[...], wu[:, at : at + step]) + bu[:, at : at + step]
        active[:, at : at + step] = (
            hidden * (0.5 * (1.0 + lax.erf(hidden * ROOT_HALF)))
        ).astype(BF16)
    for at in range(0, wo.shape[1], step):
        cols = slice(at, at + step)
        total = matmul(attended[...], wo[:, cols]) + matmul(active[...], wd[:, cols])
        out0[:, cols] = total[:length].astype(BF16)
        out1[:, cols] = total[length:].astype(BF16)


def both_kernel(chained, n0, n1, g0, g1, wq, bq, wu, bu, wo, wd, cosine, sine, mask, *refs):
    refs = refs[6:] if chained else refs
    qkv, attention, attended, active, slope, joined_grad, s0, s1, normed, upstream, hidden_grad = (
        refs
    )
    length = n0.shape[0]
    size = wo.shape[0]
    normed[:length] = n0[...]
    normed[length:] = n1[...]
    upstream[:length] = g0[...]
    upstream[length:] = g1[...]
    joined = matmul(normed[...], wq[...]) + bq[...]
    attended_grad = contract_cols(upstream[...], wo[...]).astype(BF16)
    for s in range(2):
        rows = slice(s * length, (s + 1) * length)
        queries, key_rows, values, weights, result = attend(
            joined[rows], cosine[rows], sine[rows], mask[rows]
        )
        qkv[rows, :size] = queries
        qkv[rows, size : 2 * size] = key_rows
        qkv[rows, 2 * size :] = values
        attention[rows] = weights
        attended[rows] = result
        joined_grad[rows] = attend_back(
            queries, key_rows, values, weights, attended_grad[rows], cosine[rows], sine[rows]
        )
    step = min(256, wu.shape[1])
    for at in range(0, wu.shape[1], step):
        cols = slice(at, at + step)
        hidden = matmul(normed[...], wu[:, cols]) + bu[:, cols]
        active_grad = contract_cols(upstream[...], wd[cols])
        normal_cdf = 0.5 * (1.0 + lax.erf(hidden * ROOT_HALF))
        normal_pdf = jnp.exp(-0.5 * hidden * hidden) * DENSITY_SCALE
        active[:, cols] = (hidden * normal_cdf).astype(BF16)
        change = normal_cdf + hidden * normal_pdf
        slope[:, cols] = change.astype(BF16)
        hidden_grad[:, cols] = (active_grad * change).astype(BF16)
    for at in range(0, wq.shape[0], step):
        rows = slice(at, at + step)
        total = contract_cols(joined_grad[...], wq[rows]) + contract_cols(
            hidden_grad[...], wu[rows]
        )
        s0[:, rows] = total[:length].astype(BF16)
        s1[:, rows] = total[length:].astype(BF16)


def backward_kernel(
    chained, n0, n1, g0, g1, wq, wu, wo, wd, cosine, sine, qkv, attention, slope, *refs
):
    refs = refs[2:] if chained else refs
    joined_grad, hidden_grad, norm_sums, joined_sum, hidden_sum, s0, s1, normed, upstream = refs
    length = n0.shape[0]
    size = wo.shape[0]
    normed[:length] = n0[...]
    normed[length:] = n1[...]
    upstream[:length] = g0[...]
    upstream[length:] = g1[...]
    attended_grad = contract_cols(upstream[...], wo[...]).astype(BF16)
    for s in range(2):
        rows = slice(s * length, (s + 1) * length)
        joined_grad[rows] = attend_back(
            qkv[rows, :size],
            qkv[rows, size : 2 * size],
            qkv[rows, 2 * size :],
            attention[rows],
            attended_grad[rows],
            cosine[rows],
            sine[rows],
        )
    joined_sum[...] = fold_rows(joined_grad[...].astype(F32))
    step = min(256, wu.shape[1])
    for at in range(0, wu.shape[1], step):
        cols = slice(at, at + step)
        active_grad = contract_cols(upstream[...], wd[cols])
        grad = (active_grad * slope[:, cols].astype(F32)).astype(BF16)
        hidden_grad[:, cols] = grad
        hidden_sum[:, cols] = fold_rows(grad.astype(F32))
    for at in range(0, wq.shape[0], step):
        rows = slice(at, at + step)
        first = contract_cols(joined_grad[...], wq[rows])
        second = contract_cols(hidden_grad[...], wu[rows])
        part = normed[:, rows].astype(F32)
        norm_sums[0:8, rows] = fold_rows(first * part)
        norm_sums[8:16, rows] = fold_rows(second * part)
        norm_sums[16:24, rows] = fold_rows(first)
        norm_sums[24:32, rows] = fold_rows(second)
        total = first + second
        s0[:, rows] = total[:length].astype(BF16)
        s1[:, rows] = total[length:].astype(BF16)


def whole_spec(array):
    return pl.BlockSpec(
        array.shape, lambda i: (0,) * array.ndim, pipeline_mode=pl.Buffered(buffer_count=1)
    )


def rows_spec(array, count, pair):
    return pl.BlockSpec((count, array.shape[1]), lambda i: (pair, 0))


def call_pair(kernel, whole, by_rows, chain, outs_by_rows, outs_whole, scratch, pair, rows, flops):
    pair_rows = 2 * rows
    out_shape = list(outs_by_rows) + list(outs_whole)
    out_specs = [rows_spec(item, pair_rows, pair) for item in outs_by_rows] + [
        pl.BlockSpec(item.shape, lambda i: (0, 0)) for item in outs_whole
    ]
    operands = list(whole) + list(by_rows)
    in_specs = [whole_spec(item) for item in whole] + [
        rows_spec(item, pair_rows, pair) for item in by_rows
    ]
    aliases = {}
    if chain is not None:
        for at, item in enumerate(chain):
            aliases[len(operands)] = at
            operands.append(item)
            in_specs.append(pl.BlockSpec(memory_space=pl.ANY))
    moved = sum(item.size * item.dtype.itemsize for item in operands[: len(whole)])
    return pl.pallas_call(
        kernel,
        grid=(1,),
        out_shape=out_shape,
        in_specs=in_specs,
        out_specs=out_specs,
        scratch_shapes=scratch,
        input_output_aliases=aliases,
        cost_estimate=pl.CostEstimate(flops=flops, bytes_accessed=moved, transcendentals=0),
        compiler_params=pltpu.CompilerParams(vmem_limit_bytes=40 * 1024 * 1024),
    )(*operands)


def on_device(
    layout,
    tokens,
    segments,
    cotangent,
    norm_gain,
    norm_bias,
    qkv_weight,
    qkv_bias,
    out_weight,
    out_bias,
    up_weight,
    up_bias,
    down_weight,
    down_bias,
):
    layout.place()
    first_section = lax.axis_index("section") == 0
    cores, chips, chip, core = layout.cores, layout.chips, layout.chip, layout.core
    length = segments.shape[1]
    width = tokens.shape[1]
    core_heads, joined_size = qkv_weight.shape[2:]
    head_size = joined_size // 3
    hidden_part = up_weight.shape[2] // chips
    hidden_size = cores * hidden_part
    row_count = chips * length

    def core_rows(block):
        return lax.dynamic_slice_in_dim(block, core * length, length, 0)

    gains = norm_gain[0].astype(F32)
    shifts = norm_bias[0].astype(F32)
    own_tokens = core_rows(tokens).astype(F32)
    own_cotangent = core_rows(cotangent)
    own_normed, _ = normalize(own_tokens)
    gathered = layout.ring_gather(
        jnp.where(first_section, own_normed.astype(BF16), own_cotangent)
    )

    ring = jnp.array(layout.ring, jnp.int32)
    ring_place = jnp.array([layout.ring.index(c) for c in range(chips)], jnp.int32)
    slots = jnp.array(layout.slots, jnp.int32)
    chip_of = ring[(ring_place[chip] + slots) % chips]
    all_segments = layout.gather_chips(segments)
    all_segments = lax.dynamic_index_in_dim(all_segments, core, 1, keepdims=False)
    chosen = (chip_of ^ chip)[:, None] == jnp.arange(chips)[None, :]
    own_segments = jnp.sum(jnp.where(chosen[:, :, None], all_segments[None], 0), axis=1)
    cosine, sine, mask = sequence_tables(own_segments)

    shard = qkv_weight.shape[1]
    at = lax.axis_index("dp") * shard
    gain_rows = lax.dynamic_slice_in_dim(gains, at, shard, 1)
    shift_rows = lax.dynamic_slice_in_dim(shifts, at, shard, 1)
    qkv_scaled = qkv_weight[0].reshape(shard, core_heads * joined_size).astype(F32)
    qkv_scaled = layout.gather_groups((qkv_scaled * gain_rows[0][:, None]).astype(BF16), 0)
    up_scaled = (up_weight[0].astype(F32) * gain_rows[1][:, None]).astype(BF16)
    out_shard = layout.gather_groups(out_weight[0], 1)
    wq = layout.heads_out(
        lambda head: lax.dynamic_slice_in_dim(qkv_scaled, head * joined_size, joined_size, 1)
    )
    wo = layout.heads_out(
        lambda head: lax.dynamic_index_in_dim(out_shard, head, 0, keepdims=False)
    )
    wu = layout.columns_out(layout.gather_groups(up_scaled, 0))
    down_own = layout.gather_groups(down_weight[0], 0)
    wd = jnp.concatenate([down_own, layout.other_core(down_own)], axis=0)

    joined_biases = qkv_bias[0].astype(F32)
    joined_biases = layout.by_core(joined_biases, layout.other_core(joined_biases))
    bq = lax.dynamic_index_in_dim(joined_biases, chip, 0, keepdims=True)
    bu = up_bias[0].astype(F32)[None]
    bu = jnp.concatenate(
        [
            lax.dynamic_slice_in_dim(item, chip * hidden_part, hidden_part, 1)
            for item in (bu, layout.other_core(bu))
        ],
        axis=1,
    )
    ratio = (shifts / gains).astype(BF16)
    bq = bq + matmul(ratio[:1], wq)
    bu = bu + matmul(ratio[1:], wu)
    row_bias = (out_bias[0].astype(F32) + down_bias[0].astype(F32))[None]

    piece = jax.ShapeDtypeStruct((length, width), BF16)
    pair_piece = pltpu.VMEM((2 * length, width), BF16)

    def by_rows(cols, dtype):
        return jax.ShapeDtypeStruct((row_count, cols), dtype)

    matrix_flops = 4 * length * width * (joined_size + head_size + 2 * hidden_size)

    def pair_slots(pair):
        return layout.slots[2 * pair], layout.slots[2 * pair + 1]

    def norm_back(upstream, scaled, normed, inverse):
        return upstream.astype(F32) + inverse * (
            scaled
            - jnp.mean(scaled, axis=-1, keepdims=True)
            - normed * jnp.mean(scaled * normed, axis=-1, keepdims=True)
        )

    pieces = {}
    for pair in range(chips // 2 - 1, -1, -1):
        one, two = pair_slots(pair)
        pieces[one], pieces[two] = call_pair(
            forward_kernel,
            (gathered[one], gathered[two], wq, bq, wu, bu, wo, wd),
            (cosine, sine, mask),
            None,
            (),
            (piece, piece),
            [
                pair_piece,
                pltpu.VMEM((2 * length, head_size), BF16),
                pltpu.VMEM((2 * length, hidden_size), BF16),
            ],
            pair,
            length,
            matrix_flops,
        )
    branch_rows = layout.ring_scatter(pieces, (0,))
    first_out = (own_tokens + branch_rows + row_bias).astype(BF16)

    arrived = lax.ppermute(first_out, "section", [(0, 1)])
    layer_input = jnp.where(first_section, own_tokens, arrived.astype(F32))
    own_normed, own_inverse = normalize(layer_input)
    normed = layout.ring_gather(own_normed.astype(BF16))
    kept_shapes = (
        by_rows(joined_size, BF16),
        by_rows(length, F32),
        by_rows(head_size, BF16),
        by_rows(hidden_size, BF16),
        by_rows(hidden_size, BF16),
        by_rows(joined_size, BF16),
    )
    kept = None
    pieces = {}
    for pair in range(chips // 2):
        one, two = pair_slots(pair)
        *kept, pieces[one], pieces[two] = call_pair(
            functools.partial(both_kernel, kept is not None),
            (normed[one], normed[two], gathered[one], gathered[two], wq, bq, wu, bu, wo, wd),
            (cosine, sine, mask),
            kept,
            kept_shapes,
            (piece, piece),
            [pair_piece, pair_piece, pltpu.VMEM((2 * length, hidden_size), BF16)],
            pair,
            length,
            2 * matrix_flops,
        )
    qkv, attention, attended, active, slope, _ = kept
    scaled_rows = layout.ring_scatter(pieces, (1,))
    second_grad = norm_back(own_cotangent, scaled_rows, own_normed, own_inverse)

    arrived_grad = lax.ppermute(second_grad.astype(BF16), "section", [(1, 0)])
    own_upstream = jnp.where(first_section, arrived_grad, own_cotangent)
    upstream = layout.ring_gather(own_upstream)
    grads = None
    last_pieces = {}
    sums = []
    for pair in range(chips // 2):
        one, two = pair_slots(pair)
        *grads, norm_sums, joined_sum, hidden_sum, last_pieces[one], last_pieces[two] = call_pair(
            functools.partial(backward_kernel, grads is not None),
            (normed[one], normed[two], upstream[one], upstream[two], wq, wu, wo, wd),
            (cosine, sine, qkv, attention, slope),
            grads,
            (by_rows(joined_size, BF16), by_rows(hidden_size, BF16)),
            (
                jax.ShapeDtypeStruct((32, width), F32),
                jax.ShapeDtypeStruct((8, joined_size), F32),
                jax.ShapeDtypeStruct((8, hidden_size), F32),
                piece,
                piece,
            ),
            [pair_piece, pair_piece],
            pair,
            length,
            matrix_flops,
        )
        sums.append((norm_sums, joined_sum, hidden_sum))
    joined_grad, hidden_grad = grads

    normed_rows = jnp.concatenate([normed[slot] for slot in layout.slots], axis=0)
    upstream_rows = jnp.concatenate([upstream[slot] for slot in layout.slots], axis=0)

    def core_sum(own, other):
        return own + layout.other_core(other.astype(BF16)).astype(F32)

    def half(array, which):
        size = array.shape[1] // cores
        return lax.dynamic_slice_in_dim(array, which * size, size, 1)

    out_held = core_sum(
        contract_rows(half(attended, core), upstream_rows),
        contract_rows(half(attended, 1 - core), upstream_rows),
    ).astype(BF16)
    out_blocks = layout.heads_back(
        out_held,
        lambda blocks, head, block: lax.dynamic_update_slice_in_dim(blocks, block[None], head, 0),
        jnp.zeros((core_heads, out_held.shape[0] // core_heads, width), BF16),
    )
    out_weight_grad = layout.scatter_groups(out_blocks, 1)

    hidden_held = core_sum(
        contract_rows(normed_rows, hidden_grad[:, :hidden_part]),
        contract_rows(normed_rows, hidden_grad[:, hidden_part:]),
    ).astype(BF16)
    up_plain = layout.scatter_groups(layout.columns_back(hidden_held), 0)

    joined_held = core_sum(
        contract_rows(half(normed_rows, core), joined_grad),
        contract_rows(half(normed_rows, 1 - core), joined_grad),
    ).astype(BF16)
    joined_blocks = layout.heads_back(
        joined_held,
        lambda blocks, head, block: lax.dynamic_update_slice_in_dim(
            blocks, block, head * joined_size, 1
        ),
        jnp.zeros((joined_held.shape[0] // core_heads, core_heads * joined_size), BF16),
    )
    joined_plain = layout.scatter_groups(joined_blocks, 0)

    down_weight_grad = core_sum(
        contract_rows(active[:, :hidden_part], upstream_rows),
        contract_rows(active[:, hidden_part:], upstream_rows),
    )
    if layout.groups > 1:
        down_weight_grad = layout.scatter_groups(down_weight_grad, 0)

    norm_sums, joined_sum, hidden_sum = (
        functools.reduce(jnp.add, [item[k] for item in sums]) for k in range(3)
    )
    norm_sums = jnp.sum(norm_sums.reshape(2, 2, 8, width), axis=2) / gains
    joined_bias_all = lax.dynamic_update_slice(
        jnp.zeros((chips, joined_size), F32), jnp.sum(joined_sum, axis=0)[None], (chip, 0)
    )
    hidden_sum = jnp.sum(hidden_sum, axis=0)[None, None]
    hidden_bias_all = jnp.zeros((cores, chips, hidden_part), F32)
    hidden_bias_all = lax.dynamic_update_slice(
        hidden_bias_all, hidden_sum[:, :, :hidden_part], (core, chip, 0)
    )
    hidden_bias_all = lax.dynamic_update_slice(
        hidden_bias_all, hidden_sum[:, :, hidden_part:], (1 - core, chip, 0)
    )
    vectors = (
        norm_sums,
        joined_bias_all,
        jnp.sum(own_upstream, axis=0, dtype=F32),
        hidden_bias_all,
    )
    joint = layout.sum_all(jnp.concatenate([item.reshape(-1) for item in vectors]))
    summed, start = [], 0
    for item in vectors:
        summed.append(joint[start : start + item.size].reshape(item.shape))
        start += item.size
    norm_sums, joined_bias_all, out_bias_grad, hidden_bias_all = summed
    joined_bias_grad = lax.dynamic_slice_in_dim(joined_bias_all, core * core_heads, core_heads, 0)
    up_bias_grad = lax.dynamic_index_in_dim(hidden_bias_all, core, 0, keepdims=False).reshape(-1)

    up_weight_grad = up_plain * gain_rows[1][:, None] + shift_rows[1][:, None] * up_bias_grad
    joined_weight_grad = (
        joined_plain * gain_rows[0][:, None]
        + shift_rows[0][:, None] * joined_bias_grad.reshape(-1)
    ).reshape(shard, core_heads, joined_size)

    branch = matmul(attended, wo) + matmul(active, wd)
    pieces = {
        slot: branch[k * length : (k + 1) * length].astype(BF16)
        for k, slot in enumerate(layout.slots)
    }
    branch_rows = layout.ring_scatter(pieces, (1,))
    second_out = (layer_input + branch_rows + row_bias).astype(BF16)
    own_out = jnp.where(first_section, first_out, second_out)
    layer_outputs = layout.by_core(own_out, layout.other_core(own_out))

    scaled_rows = layout.ring_scatter(last_pieces, (0,))
    first_grad = norm_back(own_upstream, scaled_rows, own_normed, own_inverse)
    own_grad = jnp.where(first_section, first_grad, second_grad)
    input_gradients = layout.by_core(own_grad, layout.other_core(own_grad))

    return (
        layer_outputs[None],
        input_gradients[None],
        norm_sums[0][None],
        norm_sums[1][None],
        joined_weight_grad[None],
        joined_bias_grad[None],
        out_weight_grad[None],
        out_bias_grad[None],
        up_weight_grad[None],
        up_bias_grad[None],
        down_weight_grad[None],
        out_bias_grad[None],
    )


def solution(mesh):
    def whole(*arrays):
        layout = Layout(mesh, arrays[5].shape[2])

        def local(*blocks):
            return on_device(layout, *blocks)

        return jax.shard_map(
            local,
            mesh=mesh,
            in_specs=(
                P("dp", None),
                P("dp", None),
                P("dp", None),
                P("section", None, None),
                P("section", None, None),
                P("section", "dp", "tensor", None),
                P("section", "tensor", None),
                P("section", "tensor", "dp", None),
                P("section", None),
                P("section", "dp", "tensor"),
                P("section", "tensor"),
                P("section", ("tensor", "dp"), None),
                P("section", None),
            ),
            out_specs=(
                P("section", "dp", None),
                P("section", "dp", None),
                P("section", None, None),
                P("section", None, None),
                P("section", "dp", "tensor", None),
                P("section", "tensor", None),
                P("section", "tensor", "dp", None),
                P("section", None),
                P("section", "dp", "tensor"),
                P("section", "tensor"),
                P("section", ("tensor", "dp"), None),
                P("section", None),
            ),
            check_vma=False,
        )(*arrays)

    return whole
```

time: 1070 us -> 698 us (0.65)
  the two profiles are of different devices: /device:TPU:16 before, /device:TPU:0 now
where the time goes in v2:
time: 698 us; the launch traced here: 690 us
  waiting for transfers between devices  287 us (41%)
  starting transfers between devices  162 us (23%)
  Pallas kernels  112 us (16%)
  other arithmetic  46.3 us (7%)
  local copies, waits for them, and re-layouts  46.1 us (7%)
  matrix products  32.1 us (5%)
    ppermute x41, waiting for transfers between devices, between_chips(): return lax.ppermute(block, 'dp', pairs)  137 us
    pallas_call x12, Pallas kernels, call_pair(): pl.pallas_call(kernel, grid=(1,), out_shape=out_shape, in_specs=in_specs,...  112 us
    ppermute x1, waiting for transfers between devices, on_device(): arrived_grad = lax.ppermute(second_grad.astype(BF16), 'section', [(1, 0)])  66.8 us
    ppermute x41, starting transfers between devices, between_chips(): return lax.ppermute(block, 'dp', pairs)  61.6 us
    ppermute x28, starting transfers between devices, between_chips(): return lax.ppermute(block, ('section', 'dp'), pairs)  52.9 us
    ppermute x8, waiting for transfers between devices, heads_back(): block = lax.ppermute(block, ('tensor', 'dp'), pairs)  41.2 us
    ppermute x13, starting transfers between devices, other_core(): return lax.ppermute(block, 'tensor', [(0, 1), (1, 0)])  24.8 us
    ppermute x28, waiting for transfers between devices, between_chips(): return lax.ppermute(block, ('section', 'dp'), pairs)  19.6 us
  transfers between devices with their start and end apart: 100, of which 29 were waited for; matrix products, arithmetic and copies ran while one was open for 15% of the time, Pallas kernels for 12%

profile of v2, /device:TPU:0, one launch (start us, length us, event | category | flops | bytes accessed | tf_op | source)
XLA Modules:
  0.0 689.8 jit_solution(10705783098854699733)
XLA Ops:
  7.4 4.5 collective-permute-start.1
  40.1 4.2 collective-permute-done.24
  51.8 5.7 collective-permute-done.17
  57.7 5.7 collective-permute-done.18
  63.4 4.9 collective-permute-done.19
  69.5 12.0 %collective-permute-start.15 = (f32[1,4096]{1,0:T(1,128)S(1)}, f32[1,4096]{1,0:T(1,128)S(1)}, u32[]{:S(2)}, u32[]{:S(2)}) collective-permute-start(f32[1,4096]{1,0:T(1,128)S(1)} %copy-done.103), channel_id=1, source_target_pairs={{0,8},{8,0},{1,9},{9,1},{2,10},{10,2},{3,11},{11,3},{4,12},{12,4},... | collective-permute-start | bytes 49160 | tf_op jit(solution)/shard_map/ppermute | solution.py:112
  83.8 10.0 %collective-permute-start.10 = (bf16[256,512]{1,0:T(8,128)(2,1)S(1)}, bf16[256,512]{1,0:T(8,128)(2,1)S(1)}, u32[]{:S(2)}, u32[]{:S(2)}) collective-permute-start(bf16[256,512]{1,0:T(8,128)(2,1)S(1)} %copy-done.87), channel_id=1, source_target_pairs={{0,4},{1,5},{2,6},{3,7},{4,0},{5,1},{6,2},{7,3},{8,12},{9,13},{10,... | collective-permute-start | bytes 786440 | tf_op jit(solution)/shard_map/ppermute | solution.py:87
  101.4 32.4 %collective-permute-done.10 = bf16[256,512]{1,0:T(8,128)(2,1)S(1)} collective-permute-done((bf16[256,512]{1,0:T(8,128)(2,1)S(1)}, bf16[256,512]{1,0:T(8,128)(2,1)S(1)}, u32[]{:S(2)}, u32[]{:S(2)}) %collective-permute-start.10) | collective-permute-done | bytes 262176 | tf_op jit(solution)/shard_map/ppermute | solution.py:87
  134.5 6.5 collective-permute-start.28
  141.4 6.8 collective-permute-done.25.n0.g0
  148.5 9.5 %collective-permute-done.28.n1.g1 = bf16[128,2048]{1,0:T(8,128)(2,1)S(1)} collective-permute-done((bf16[128,2048]{1,0:T(8,128)(2,1)S(1)}, bf16[128,2048]{1,0:T(8,128)(2,1)S(1)}, u32[]{:S(2)}, u32[]{:S(2)}) %collective-permute-start.28) | collective-permute-done | bytes 524320 | tf_op jit(solution)/shard_map/ppermute | solution.py:87
  158.3 4.3 collective-permute-done.26.n0.g0
  163.3 8.4 %collective-permute-done.29.n1.g1 = bf16[128,2048]{1,0:T(8,128)(2,1)S(1)} collective-permute-done((bf16[128,2048]{1,0:T(8,128)(2,1)S(1)}, bf16[128,2048]{1,0:T(8,128)(2,1)S(1)}, u32[]{:S(2)}, u32[]{:S(2)}) %collective-permute-start.29) | collective-permute-done | bytes 524320 | tf_op jit(solution)/shard_map/ppermute | solution.py:87
  177.6 7.2 %collective-permute-done.30.n1.g1 = bf16[128,2048]{1,0:T(8,128)(2,1)S(1)} collective-permute-done((bf16[128,2048]{1,0:T(8,128)(2,1)S(1)}, bf16[128,2048]{1,0:T(8,128)(2,1)S(1)}, u32[]{:S(2)}, u32[]{:S(2)}) %collective-permute-start.30) | collective-permute-done | bytes 524320 | tf_op jit(solution)/shard_map/ppermute | solution.py:87
  184.8 7.0 %shard_map.248 = (bf16[128,2048]{1,0:T(8,128)(2,1)S(1)}, bf16[128,2048]{1,0:T(8,128)(2,1)S(1)}) custom-call(bf16[128,2048]{1,0:T(8,128)(2,1)S(1)} %collective-permute-done.27.n0.g0, bf16[128,2048]{1,0:T(8,128)(2,1)S(1)} %collective-permute-done.30.n1.g1, bf16[2048,768]{1,0:T(8,128)(2,1)S(1)} %pad_maximum_fusion.2.wq, f32[1,768]{1,0:T(1,128)S(1)} %fusion.44.bq, ...), custom_call_target="tpu_custom_call" | custom-call | flops 3221225472 | bytes 13638656 | tf_op jit(solution)/shard_map/pallas_call | solution.py:436
  197.7 6.8 shard_map.249
  208.9 6.8 shard_map.250
  222.0 6.8 shard_map.247
  235.0 5.8 collective-permute-done.37
  245.6 6.7 collective-permute-done.38
  256.6 10.3 %collective-permute-done.39.n0 = bf16[128,2048]{1,0:T(8,128)(2,1)} collective-permute-done((bf16[128,2048]{1,0:T(8,128)(2,1)S(1)}, bf16[128,2048]{1,0:T(8,128)(2,1)}, u32[]{:S(2)}, u32[]{:S(2)}) %collective-permute-start.39) | collective-permute-done | bytes 524320 | tf_op jit(solution)/shard_map/ppermute | solution.py:87
  274.2 11.2 %shard_map.251 = (bf16[1024,768]{1,0:T(8,128)(2,1)S(1)}, f32[1024,128]{1,0:T(8,128)S(1)}, bf16[1024,256]{1,0:T(8,128)(2,1)S(1)}, bf16[1024,1024]{1,0:T(8,128)(2,...) custom-call(bf16[128,2048]{1,0:T(8,128)(2,1)S(1)} %copy-done.19, ...), custom_call_target="tpu_custom_call" | custom-call | flops 6442450944 | bytes 14687232 | tf_op jit(solution)/shard_map/pallas_call | solution.py:436
  289.2 11.3 %shard_map.252 = (bf16[1024,768]{1,0:T(8,128)(2,1)S(1)}, f32[1024,128]{1,0:T(8,128)S(1)}, bf16[1024,256]{1,0:T(8,128)(2,1)S(1)}, bf16[1024,1024]{1,0:T(8,128)(2,...) custom-call(bf16[128,2048]{1,0:T(8,128)(2,1)} %collective-permute-do, ...), custom_call_target="tpu_custom_call", output_to_operand_aliasing={{0}: (13, {}), {1}: (14, {}), {2}: (15, {}), {3}: (16, {}),... | custom-call | flops 6442450944 | bytes 14687232 | tf_op jit(solution)/shard_map/pallas_call | solution.py:436
  302.1 11.2 %shard_map.253 = (bf16[1024,768]{1,0:T(8,128)(2,1)S(1)}, f32[1024,128]{1,0:T(8,128)S(1)}, bf16[1024,256]{1,0:T(8,128)(2,1)S(1)}, bf16[1024,1024]{1,0:T(8,128)(2,...) custom-call(bf16[128,2048]{1,0:T(8,128)(2,1)S(1)} %collective-permut, ...), custom_call_target="tpu_custom_call", output_to_operand_aliasing={{0}: (13, {}), {1}: (14, {}), {2}: (15, {}), {3}: (16, {}),... | custom-call | flops 6442450944 | bytes 14687232 | tf_op jit(solution)/shard_map/pallas_call | solution.py:436
  313.4 11.2 %shard_map.254 = (bf16[1024,768]{1,0:T(8,128)(2,1)S(1)}, f32[1024,128]{1,0:T(8,128)S(1)}, bf16[1024,256]{1,0:T(8,128)(2,1)S(1)}, bf16[1024,1024]{1,0:T(8,128)(2,...) custom-call(bf16[128,2048]{1,0:T(8,128)(2,1)S(1)} %collective-permut, ...), custom_call_target="tpu_custom_call", output_to_operand_aliasing={{0}: (13, {}), {1}: (14, {}), {2}: (15, {}), {3}: (16, {}),... | custom-call | flops 6442450944 | bytes 14687232 | tf_op jit(solution)/shard_map/pallas_call | solution.py:436
  325.6 6.7 fusion.48
  332.3 4.6 add_convert_fusion
  354.2 66.8 %collective-permute-done.61 = bf16[128,2048]{1,0:T(8,128)(2,1)S(1)} collective-permute-done((bf16[128,2048]{1,0:T(8,128)(2,1)S(1)}, bf16[128,2048]{1,0:T(8,128)(2,1)S(1)}, u32[]{:S(2)}, u32[]{:S(2)}) %collective-permute-start.61) | collective-permute-done | bytes 524320 | tf_op jit(solution)/shard_map/ppermute | solution.py:604
  424.4 9.7 %collective-permute-done.62.g1 = bf16[128,2048]{1,0:T(8,128)(2,1)S(1)} collective-permute-done((bf16[128,2048]{1,0:T(8,128)(2,1)S(1)}, bf16[128,2048]{1,0:T(8,128)(2,1)S(1)}, u32[]{:S(2)}, u32[]{:S(2)}) %collective-permute-start.62) | collective-permute-done | bytes 524320 | tf_op jit(solution)/shard_map/ppermute | solution.py:87
  436.5 9.1 %shard_map.255 = (bf16[1024,768]{1,0:T(8,128)(2,1)S(1)}, bf16[1024,1024]{1,0:T(8,128)(2,1)S(1)}, f32[32,2048]{1,0:T(8,128)S(1)}, f32[8,768]{1,0:T(8,128)S(1)}, f...) custom-call(bf16[128,2048]{1,0:T(8,128)(2,1)S(1)} %copy-done.20, ...), custom_call_target="tpu_custom_call" | custom-call | flops 3221225472 | bytes 14680064 | tf_op jit(solution)/shard_map/pallas_call | solution.py:436
  448.8 9.2 %shard_map.256 = (bf16[1024,768]{1,0:T(8,128)(2,1)S(1)}, bf16[1024,1024]{1,0:T(8,128)(2,1)S(1)}, f32[32,2048]{1,0:T(8,128)S(1)}, f32[8,768]{1,0:T(8,128)S(1)}, f...) custom-call(bf16[128,2048]{1,0:T(8,128)(2,1)} %collective-permute-do, ...), custom_call_target="tpu_custom_call", output_to_operand_aliasing={{0}: (13, {}), {1}: (14, {})} | custom-call | flops 3221225472 | bytes 14680064 | tf_op jit(solution)/shard_map/pallas_call | solution.py:436
  460.7 10.5 %shard_map.257 = (bf16[1024,768]{1,0:T(8,128)(2,1)S(1)}, bf16[1024,1024]{1,0:T(8,128)(2,1)S(1)}, f32[32,2048]{1,0:T(8,128)S(1)}, f32[8,768]{1,0:T(8,128)S(1)}, f...) custom-call(bf16[128,2048]{1,0:T(8,128)(2,1)S(1)} %collective-permut, ...), custom_call_target="tpu_custom_call", output_to_operand_aliasing={{0}: (13, {}), {1}: (14, {})} | custom-call | flops 3221225472 | bytes 14680064 | tf_op jit(solution)/shard_map/pallas_call | solution.py:436
  471.3 10.6 %shard_map.258 = (bf16[1024,768]{1,0:T(8,128)(2,1)S(1)}, bf16[1024,1024]{1,0:T(8,128)(2,1)S(1)}, f32[32,2048]{1,0:T(8,128)S(1)}, f32[8,768]{1,0:T(8,128)S(1)}, f...) custom-call(bf16[128,2048]{1,0:T(8,128)(2,1)S(1)} %collective-permut, ...), custom_call_target="tpu_custom_call", output_to_operand_aliasing={{0}: (13, {}), {1}: (14, {})} | custom-call | flops 3221225472 | bytes 14680064 | tf_op jit(solution)/shard_map/pallas_call | solution.py:436
  492.8 4.1 fusion.6
  514.6 14.6 %collective-permute-done.88 = bf16[32,2048]{1,0:T(8,128)(2,1)S(1)} collective-permute-done((bf16[32,2048]{1,0:T(8,128)(2,1)S(1)}, bf16[32,2048]{1,0:T(8,128)(2,1)S(1)}, u32[]{:S(2)}, u32[]{:S(2)}) %collective-permute-start.88) | collective-permute-done | bytes 131104 | tf_op jit(solution)/shard_map/ppermute | solution.py:229
  529.2 4.9 collective-permute-done.89
  545.2 9.6 %collective-permute-done.71 = bf16[128,2048]{1,0:T(8,128)(2,1)S(1)} collective-permute-done((bf16[128,2048]{1,0:T(8,128)(2,1)S(1)}, bf16[128,2048]{1,0:T(8,128)(2,1)S(1)}, u32[]{:S(2)}, u32[]{:S(2)}) %collective-permute-start.71) | collective-permute-done | bytes 524320 | tf_op jit(solution)/shard_map/ppermute | solution.py:93
  558.8 4.4 collective-permute-start.72
  563.3 8.9 %collective-permute-done.83 = bf16[256,768]{1,0:T(8,128)(2,1)S(1)} collective-permute-done((bf16[256,768]{1,0:T(8,128)(2,1)S(1)}, bf16[256,768]{1,0:T(8,128)(2,1)S(1)}, u32[]{:S(2)}, u32[]{:S(2)}) %collective-permute-start.83) | collective-permute-done | bytes 393248 | tf_op jit(solution)/shard_map/ppermute | solution.py:229
  577.2 10.7 %collective-permute-done.84 = bf16[256,768]{1,0:T(8,128)(2,1)S(1)} collective-permute-done((bf16[256,768]{1,0:T(8,128)(2,1)S(1)}, bf16[256,768]{1,0:T(8,128)(2,1)S(1)}, u32[]{:S(2)}, u32[]{:S(2)}) %collective-permute-start.84) | collective-permute-done | bytes 393248 | tf_op jit(solution)/shard_map/ppermute | solution.py:229
  594.4 9.0 %collective-permute-start.76 = (f32[128,2048]{1,0:T(8,128)}, f32[128,2048]{1,0:T(8,128)}, u32[]{:S(2)}, u32[]{:S(2)}) collective-permute-start(f32[128,2048]{1,0:T(8,128)} %get-tuple-element.197), channel_id=1, source_target_pairs={{0,8},{8,0},{1,9},{9,1},{2,10},{10,2},{3,11},{11,3},{4,12},{12,4},... | collective-permute-start | bytes 3145736 | tf_op jit(solution)/shard_map/ppermute | solution.py:112
  612.7 4.5 add_bitcast_fusion
  617.2 7.6 %collective-permute-done.78 = f32[24576]{0:T(1024)S(1)} collective-permute-done((f32[24576]{0:T(1024)S(1)}, f32[24576]{0:T(1024)S(1)}, u32[]{:S(2)}, u32[]{:S(2)}) %collective-permute-start.78) | collective-permute-done | bytes 98336 | tf_op jit(solution)/shard_map/ppermute | solution.py:87
  628.0 6.4 collective-permute-start.97
  635.8 21.6 %collective-permute-done.95 = bf16[256,512]{1,0:T(8,128)(2,1)S(1)} collective-permute-done((bf16[256,512]{1,0:T(8,128)(2,1)S(1)}, bf16[256,512]{1,0:T(8,128)(2,1)S(1)}, u32[]{:S(2)}, u32[]{:S(2)}) %collective-permute-start.95) | collective-permute-done | bytes 262176 | tf_op jit(solution)/shard_map/ppermute | solution.py:87
  658.1 4.3 collective-permute-done.96
  668.1 5.9 collective-permute-done.80
  681.4 4.4 add_bitcast_fusion.1
  (611 shorter events, 220.6 us)
Async XLA Ops:
  7.4 62.1 %collective-permute-start.1 = (bf16[256,768]{1,0:T(8,128)(2,1)}, bf16[256,768]{1,0:T(8,128)(2,1)}, u32[]{:S(2)}, u32[]{:S(2)}) collective-permute-start(bf16[256,768]{1,0:T(8,128)(2,1)} %get-tuple-element.187), channel_id=1, source_target_pairs={{0,0},{1,1},{2,2},{3,3},{4,8},{5,9},{6,10},{7,11},{8,4},{9,5},{10,... | collective-permute-start | bytes 1179656 | tf_op jit(solution)/shard_map/ppermute | solution.py:215
  11.9 71.9 %collective-permute-start.2 = (bf16[256,768]{1,0:T(8,128)(2,1)}, bf16[256,768]{1,0:T(8,128)(2,1)}, u32[]{:S(2)}, u32[]{:S(2)}) collective-permute-start(bf16[256,768]{1,0:T(8,128)(2,1)} %get-tuple-element.186), channel_id=1, source_target_pairs={{0,1},{1,2},{2,3},{3,0},{4,9},{5,10},{6,11},{7,8},{8,5},{9,6},{10,... | collective-permute-start | bytes 1179656 | tf_op jit(solution)/shard_map/ppermute | solution.py:215
  14.9 79.9 %collective-permute-start.3 = (bf16[256,768]{1,0:T(8,128)(2,1)}, bf16[256,768]{1,0:T(8,128)(2,1)S(1)}, u32[]{:S(2)}, u32[]{:S(2)}) collective-permute-start(bf16[256,768]{1,0:T(8,128)(2,1)} %get-tuple-element.185), channel_id=1, source_target_pairs={{0,2},{1,3},{2,0},{3,1},{4,10},{5,11},{6,8},{7,9},{8,6},{9,7},{10,... | collective-permute-start | bytes 1179656 | tf_op jit(solution)/shard_map/ppermute | solution.py:215
  17.1 32.6 %collective-permute-start.6 = (f32[4,768]{1,0:T(4,128)}, f32[4,768]{1,0:T(4,128)}, u32[]{:S(2)}, u32[]{:S(2)}) collective-permute-start(f32[4,768]{1,0:T(4,128)} %bitcast_convert_fusion), channel_id=1, source_target_pairs={{0,8},{8,0},{1,9},{9,1},{2,10},{10,2},{3,11},{11,3},{4,12},{12,4},... | collective-permute-start | bytes 36872 | tf_op jit(solution)/shard_map/ppermute | solution.py:112
  18.8 16.1 %collective-permute-start.22 = (s32[1,2,128]{2,1,0:T(2,128)}, s32[1,2,128]{2,1,0:T(2,128)}, u32[]{:S(2)}, u32[]{:S(2)}) collective-permute-start(s32[1,2,128]{2,1,0:T(2,128)} %bitcast.15), channel_id=1, source_target_pairs={{0,1},{1,0},{2,3},{3,2},{4,5},{5,4},{6,7},{7,6},{8,9},{9,8},{10,11... | collective-permute-start | bytes 3080 | tf_op jit(solution)/shard_map/ppermute | solution.py:87
  44.3 24.2 %collective-permute-start.7 = (bf16[256,512]{1,0:T(8,128)(2,1)S(1)}, bf16[256,512]{1,0:T(8,128)(2,1)S(1)}, u32[]{:S(2)}, u32[]{:S(2)}) collective-permute-start(bf16[256,512]{1,0:T(8,128)(2,1)S(1)} %get-tuple-element.178), channel_id=1, source_target_pairs={{0,1},{1,0},{2,3},{3,2},{4,5},{5,4},{6,7},{7,6},{8,9},{9,8},{10,11... | collective-permute-start | bytes 786440 | tf_op jit(solution)/shard_map/ppermute | solution.py:87
  68.5 26.4 %collective-permute-start.4 = (bf16[256,768]{1,0:T(8,128)(2,1)S(1)}, bf16[256,768]{1,0:T(8,128)(2,1)S(1)}, u32[]{:S(2)}, u32[]{:S(2)}) collective-permute-start(bf16[256,768]{1,0:T(8,128)(2,1)S(1)} %copy-done.85), channel_id=1, source_target_pairs={{0,3},{1,0},{2,1},{3,2},{4,11},{5,8},{6,9},{7,10},{8,7},{9,4},{10,... | collective-permute-start | bytes 1179656 | tf_op jit(solution)/shard_map/ppermute | solution.py:215
  82.7 51.8 %collective-permute-start = (bf16[128,2048]{1,0:T(8,128)(2,1)S(1)}, bf16[128,2048]{1,0:T(8,128)(2,1)S(1)}, u32[]{:S(2)}, u32[]{:S(2)}) collective-permute-start(bf16[128,2048]{1,0:T(8,128)(2,1)S(1)} %fusion.24.n0.g0), channel_id=1, source_target_pairs={{0,1},{1,3},{2,0},{3,5},{4,2},{5,7},{6,4},{7,6},{8,9},{9,11},{10,8... | collective-permute-start | bytes 1572872 | tf_op jit(solution)/shard_map/ppermute | solution.py:87
  83.8 50.0 %collective-permute-start.10 = (bf16[256,512]{1,0:T(8,128)(2,1)S(1)}, bf16[256,512]{1,0:T(8,128)(2,1)S(1)}, u32[]{:S(2)}, u32[]{:S(2)}) collective-permute-start(bf16[256,512]{1,0:T(8,128)(2,1)S(1)} %copy-done.87), channel_id=1, source_target_pairs={{0,4},{1,5},{2,6},{3,7},{4,0},{5,1},{6,2},{7,3},{8,12},{9,13},{10,... | collective-permute-start | bytes 786440 | tf_op jit(solution)/shard_map/ppermute | solution.py:87
  94.8 39.0 %collective-permute-start.11 = (bf16[256,512]{1,0:T(8,128)(2,1)S(1)}, bf16[256,512]{1,0:T(8,128)(2,1)S(1)}, u32[]{:S(2)}, u32[]{:S(2)}) collective-permute-start(bf16[256,512]{1,0:T(8,128)(2,1)S(1)} %copy-done.86), channel_id=1, source_target_pairs={{0,5},{1,4},{2,7},{3,6},{4,1},{5,0},{6,3},{7,2},{8,13},{9,12},{10,... | collective-permute-start | bytes 786440 | tf_op jit(solution)/shard_map/ppermute | solution.py:87
  94.9 39.0 %collective-permute-start.12 = (bf16[256,512]{1,0:T(8,128)(2,1)S(1)}, bf16[256,512]{1,0:T(8,128)(2,1)S(1)}, u32[]{:S(2)}, u32[]{:S(2)}) collective-permute-start(bf16[256,512]{1,0:T(8,128)(2,1)S(1)} %get-tuple-element.173), channel_id=1, source_target_pairs={{0,6},{1,7},{2,4},{3,5},{4,2},{5,3},{6,0},{7,1},{8,14},{9,15},{10,... | collective-permute-start | bytes 786440 | tf_op jit(solution)/shard_map/ppermute | solution.py:87
  97.5 43.6 %collective-permute-start.13 = (bf16[256,512]{1,0:T(8,128)(2,1)S(1)}, bf16[256,512]{1,0:T(8,128)(2,1)S(1)}, u32[]{:S(2)}, u32[]{:S(2)}) collective-permute-start(bf16[256,512]{1,0:T(8,128)(2,1)S(1)} %get-tuple-element.172), channel_id=1, source_target_pairs={{0,7},{1,6},{2,5},{3,4},{4,3},{5,2},{6,1},{7,0},{8,15},{9,14},{10,... | collective-permute-start | bytes 786440 | tf_op jit(solution)/shard_map/ppermute | solution.py:87
  133.8 38.5 %collective-permute-start.5 = (bf16[1024,768]{1,0:T(8,128)(2,1)S(1)}, bf16[1024,768]{1,0:T(8,128)(2,1)S(1)}, u32[]{:S(2)}, u32[]{:S(2)}) collective-permute-start(bf16[1024,768]{1,0:T(8,128)(2,1)S(1)} %constant_dynamic-update-slice_fusion.38), channel_id=1, source_target_pairs={{0,8},{8,0},{1,9},{9,1},{2,10},{10,2},{3,11},{11,3},{4,12},{12,4},... | collective-permute-start | bytes 4718600 | tf_op jit(solution)/shard_map/ppermute | solution.py:112
  134.5 23.6 %collective-permute-start.28 = (bf16[128,2048]{1,0:T(8,128)(2,1)S(1)}, bf16[128,2048]{1,0:T(8,128)(2,1)S(1)}, u32[]{:S(2)}, u32[]{:S(2)}) collective-permute-start(bf16[128,2048]{1,0:T(8,128)(2,1)S(1)} %collective-permute-done.n1.g1), channel_id=1, source_target_pairs={{0,1},{1,3},{2,0},{3,5},{4,2},{5,7},{6,4},{7,6},{8,9},{9,11},{10,8... | collective-permute-start | bytes 1572872 | tf_op jit(solution)/shard_map/ppermute | solution.py:87
  141.1 32.1 %collective-permute-start.21 = (bf16[512,2048]{1,0:T(8,128)(2,1)S(1)}, bf16[512,2048]{1,0:T(8,128)(2,1)S(1)}, u32[]{:S(2)}, u32[]{:S(2)}) collective-permute-start(bf16[512,2048]{1,0:T(8,128)(2,1)S(1)} %bitcast.106), channel_id=1, source_target_pairs={{0,8},{8,0},{1,9},{9,1},{2,10},{10,2},{3,11},{11,3},{4,12},{12,4},... | collective-permute-start | bytes 6291464 | tf_op jit(solution)/shard_map/ppermute | solution.py:112
  148.2 28.0 %collective-permute-start.14 = (bf16[2048,512]{1,0:T(8,128)(2,1)S(1)}, bf16[2048,512]{1,0:T(8,128)(2,1)S(1)}, u32[]{:S(2)}, u32[]{:S(2)}) collective-permute-start(bf16[2048,512]{1,0:T(8,128)(2,1)S(1)} %constant_dynamic-update-slice_fusion.31), channel_id=1, source_target_pairs={{0,8},{8,0},{1,9},{9,1},{2,10},{10,2},{3,11},{11,3},{4,12},{12,4},... | collective-permute-start | bytes 6291464 | tf_op jit(solution)/shard_map/ppermute | solution.py:112
  162.6 14.9 %collective-permute-start.27 = (bf16[128,2048]{1,0:T(8,128)(2,1)S(1)}, bf16[128,2048]{1,0:T(8,128)(2,1)S(1)}, u32[]{:S(2)}, u32[]{:S(2)}) collective-permute-start(bf16[128,2048]{1,0:T(8,128)(2,1)S(1)} %collective-permute-done.26.n0.g0), channel_id=1, source_target_pairs={{0,2},{1,0},{2,4},{3,1},{4,6},{5,3},{6,7},{7,5},{8,10},{9,8},{10,1... | collective-permute-start | bytes 1572872 | tf_op jit(solution)/shard_map/ppermute | solution.py:87
  195.0 20.8 %collective-permute-start.35 = (bf16[128,2048]{1,0:T(8,128)(2,1)S(1)}, bf16[128,2048]{1,0:T(8,128)(2,1)S(1)}, u32[]{:S(2)}, u32[]{:S(2)}) collective-permute-start(bf16[128,2048]{1,0:T(8,128)(2,1)S(1)} %get-tuple-element.84), channel_id=1, source_target_pairs={{0,1},{1,3},{2,0},{3,5},{4,2},{5,7},{6,4},{7,6},{8,9},{9,11},{10,8... | collective-permute-start | bytes 1572872 | tf_op jit(solution)/shard_map/ppermute | solution.py:93
  266.9 18.5 %collective-permute-start.40 = (bf16[128,2048]{1,0:T(8,128)(2,1)}, bf16[128,2048]{1,0:T(8,128)(2,1)S(1)}, u32[]{:S(2)}, u32[]{:S(2)}) collective-permute-start(bf16[128,2048]{1,0:T(8,128)(2,1)} %collective-permute-done.39.n0), channel_id=1, source_target_pairs={{0,2},{1,0},{2,4},{3,1},{4,6},{5,3},{6,7},{7,5},{8,10},{9,8},{10,1... | collective-permute-start | bytes 1572872 | tf_op jit(solution)/shard_map/ppermute | solution.py:87
  267.8 18.6 %collective-permute-start.43 = (bf16[128,2048]{1,0:T(8,128)(2,1)}, bf16[128,2048]{1,0:T(8,128)(2,1)S(1)}, u32[]{:S(2)}, u32[]{:S(2)}) collective-permute-start(bf16[128,2048]{1,0:T(8,128)(2,1)} %collective-permute-done.42.n1), channel_id=1, source_target_pairs={{0,1},{1,3},{2,0},{3,5},{4,2},{5,7},{6,4},{7,6},{8,9},{9,11},{10,8... | collective-permute-start | bytes 1572872 | tf_op jit(solution)/shard_map/ppermute | solution.py:87
  285.4 27.9 %collective-permute-start.41 = (bf16[128,2048]{1,0:T(8,128)(2,1)S(1)}, bf16[128,2048]{1,0:T(8,128)(2,1)S(1)}, u32[]{:S(2)}, u32[]{:S(2)}) collective-permute-start(bf16[128,2048]{1,0:T(8,128)(2,1)S(1)} %collective-permute-done.40.n0), channel_id=1, source_target_pairs={{0,2},{1,0},{2,4},{3,1},{4,6},{5,3},{6,7},{7,5},{8,10},{9,8},{10,1... | collective-permute-start | bytes 1572872 | tf_op jit(solution)/shard_map/ppermute | solution.py:87
  324.6 15.4 %collective-permute-start.54 = (bf16[128,2048]{1,0:T(8,128)(2,1)S(1)}, bf16[128,2048]{1,0:T(8,128)(2,1)S(1)}, u32[]{:S(2)}, u32[]{:S(2)}) collective-permute-start(bf16[128,2048]{1,0:T(8,128)(2,1)S(1)} %get-tuple-element.108), channel_id=1, source_target_pairs={{16,18},{17,16},{18,20},{19,17},{20,22},{21,19},{22,23},{23,21},{2... | collective-permute-start | bytes 1572872 | tf_op jit(solution)/shard_map/ppermute | solution.py:93
  351.4 69.6 %collective-permute-start.61 = (bf16[128,2048]{1,0:T(8,128)(2,1)S(1)}, bf16[128,2048]{1,0:T(8,128)(2,1)S(1)}, u32[]{:S(2)}, u32[]{:S(2)}) collective-permute-start(bf16[128,2048]{1,0:T(8,128)(2,1)S(1)} %fusion.47), channel_id=1, source_target_pairs={{16,0},{17,1},{18,2},{19,3},{20,4},{21,5},{22,6},{23,7},{24,8},{25... | collective-permute-start | bytes 1572872 | tf_op jit(solution)/shard_map/ppermute | solution.py:604
  353.2 70.0 %collective-permute-start.53 = (bf16[128,2048]{1,0:T(8,128)(2,1)S(1)}, bf16[128,2048]{1,0:T(8,128)(2,1)S(1)}, u32[]{:S(2)}, u32[]{:S(2)}) collective-permute-start(bf16[128,2048]{1,0:T(8,128)(2,1)S(1)} %fusion.23), channel_id=1, source_target_pairs={{0,8},{8,0},{1,9},{9,1},{2,10},{10,2},{3,11},{11,3},{4,12},{12,4},... | collective-permute-start | bytes 1572872 | tf_op jit(solution)/shard_map/ppermute | solution.py:112
  485.1 19.0 %collective-permute-start.73 = (bf16[128,2048]{1,0:T(8,128)(2,1)}, bf16[128,2048]{1,0:T(8,128)(2,1)}, u32[]{:S(2)}, u32[]{:S(2)}) collective-permute-start(bf16[128,2048]{1,0:T(8,128)(2,1)} %get-tuple-element.129), channel_id=1, source_target_pairs={{0,1},{1,3},{2,0},{3,5},{4,2},{5,7},{6,4},{7,6},{8,9},{9,11},{10,8... | collective-permute-start | bytes 1572872 | tf_op jit(solution)/shard_map/ppermute | solution.py:93
  487.4 22.0 %collective-permute-start.69 = (bf16[128,2048]{1,0:T(8,128)(2,1)}, bf16[128,2048]{1,0:T(8,128)(2,1)}, u32[]{:S(2)}, u32[]{:S(2)}) collective-permute-start(bf16[128,2048]{1,0:T(8,128)(2,1)} %get-tuple-element.125), channel_id=1, source_target_pairs={{0,2},{1,0},{2,4},{3,1},{4,6},{5,3},{6,7},{7,5},{8,10},{9,8},{10,1... | collective-permute-start | bytes 1572872 | tf_op jit(solution)/shard_map/ppermute | solution.py:93
  496.8 45.4 %collective-permute-start.81 = (bf16[1024,768]{1,0:T(8,128)(2,1)S(1)}, bf16[1024,768]{1,0:T(8,128)(2,1)S(1)}, u32[]{:S(2)}, u32[]{:S(2)}) collective-permute-start(bf16[1024,768]{1,0:T(8,128)(2,1)S(1)} %fusion.6), channel_id=1, source_target_pairs={{0,8},{8,0},{1,9},{9,1},{2,10},{10,2},{3,11},{11,3},{4,12},{12,4},... | collective-permute-start | bytes 4718600 | tf_op jit(solution)/shard_map/ppermute | solution.py:112
  503.5 99.9 %collective-permute-start.91 = (bf16[2048,512]{1,0:T(8,128)(2,1)S(1)}, bf16[2048,512]{1,0:T(8,128)(2,1)S(1)}, u32[]{:S(2)}, u32[]{:S(2)}) collective-permute-start(bf16[2048,512]{1,0:T(8,128)(2,1)S(1)} %convolution_convert_fusion.1), channel_id=1, source_target_pairs={{0,8},{8,0},{1,9},{9,1},{2,10},{10,2},{3,11},{11,3},{4,12},{12,4},... | collective-permute-start | bytes 6291464 | tf_op jit(solution)/shard_map/ppermute | solution.py:112
  505.3 30.8 %collective-permute-start.74 = (bf16[128,2048]{1,0:T(8,128)(2,1)S(1)}, bf16[128,2048]{1,0:T(8,128)(2,1)S(1)}, u32[]{:S(2)}, u32[]{:S(2)}) collective-permute-start(bf16[128,2048]{1,0:T(8,128)(2,1)S(1)} %add_convert_fusion.4), channel_id=1, source_target_pairs={{0,1},{1,3},{2,0},{3,5},{4,2},{5,7},{6,4},{7,6},{8,9},{9,11},{10,8... | collective-permute-start | bytes 1572872 | tf_op jit(solution)/shard_map/ppermute | solution.py:93
  510.7 27.5 %collective-permute-start.70 = (bf16[128,2048]{1,0:T(8,128)(2,1)S(1)}, bf16[128,2048]{1,0:T(8,128)(2,1)S(1)}, u32[]{:S(2)}, u32[]{:S(2)}) collective-permute-start(bf16[128,2048]{1,0:T(8,128)(2,1)S(1)} %add_convert_fusion.7), channel_id=1, source_target_pairs={{0,2},{1,0},{2,4},{3,1},{4,6},{5,3},{6,7},{7,5},{8,10},{9,8},{10,1... | collective-permute-start | bytes 1572872 | tf_op jit(solution)/shard_map/ppermute | solution.py:93
  514.2 15.0 %collective-permute-start.88 = (bf16[32,2048]{1,0:T(8,128)(2,1)S(1)}, bf16[32,2048]{1,0:T(8,128)(2,1)S(1)}, u32[]{:S(2)}, u32[]{:S(2)}) collective-permute-start(bf16[32,2048]{1,0:T(8,128)(2,1)S(1)} %get-tuple-element.194), channel_id=1, source_target_pairs={{1,0},{2,1},{3,2},{0,3},{9,4},{10,5},{11,6},{8,7},{5,8},{6,9},{7,1... | collective-permute-start | bytes 393224 | tf_op jit(solution)/shard_map/ppermute | solution.py:229
  534.1 24.6 %collective-permute-start.90 = (bf16[32,2048]{1,0:T(8,128)(2,1)S(1)}, bf16[32,2048]{1,0:T(8,128)(2,1)S(1)}, u32[]{:S(2)}, u32[]{:S(2)}) collective-permute-start(bf16[32,2048]{1,0:T(8,128)(2,1)S(1)} %get-tuple-element.192), channel_id=1, source_target_pairs={{3,0},{0,1},{1,2},{2,3},{11,4},{8,5},{9,6},{10,7},{7,8},{4,9},{5,1... | collective-permute-start | bytes 393224 | tf_op jit(solution)/shard_map/ppermute | solution.py:229
  536.2 55.3 %collective-permute-start.75 = (bf16[128,2048]{1,0:T(8,128)(2,1)S(1)}, bf16[128,2048]{1,0:T(8,128)(2,1)S(1)}, u32[]{:S(2)}, u32[]{:S(2)}) collective-permute-start(bf16[128,2048]{1,0:T(8,128)(2,1)S(1)} %add_convert_fusion.3), channel_id=1, source_target_pairs={{0,1},{1,3},{2,0},{3,5},{4,2},{5,7},{6,4},{7,6},{8,9},{9,11},{10,8... | collective-permute-start | bytes 1572872 | tf_op jit(solution)/shard_map/ppermute | solution.py:93
  538.3 16.5 %collective-permute-start.71 = (bf16[128,2048]{1,0:T(8,128)(2,1)S(1)}, bf16[128,2048]{1,0:T(8,128)(2,1)S(1)}, u32[]{:S(2)}, u32[]{:S(2)}) collective-permute-start(bf16[128,2048]{1,0:T(8,128)(2,1)S(1)} %add_convert_fusion.6), channel_id=1, source_target_pairs={{0,2},{1,0},{2,4},{3,1},{4,6},{5,3},{6,7},{7,5},{8,10},{9,8},{10,1... | collective-permute-start | bytes 1572872 | tf_op jit(solution)/shard_map/ppermute | solution.py:93
  544.4 18.8 %collective-permute-start.82 = (bf16[256,768]{1,0:T(8,128)(2,1)S(1)}, bf16[256,768]{1,0:T(8,128)(2,1)S(1)}, u32[]{:S(2)}, u32[]{:S(2)}) collective-permute-start(bf16[256,768]{1,0:T(8,128)(2,1)S(1)} %get-tuple-element.183), channel_id=1, source_target_pairs={{0,0},{1,1},{2,2},{3,3},{8,4},{9,5},{10,6},{11,7},{4,8},{5,9},{6,1... | collective-permute-start | bytes 1179656 | tf_op jit(solution)/shard_map/ppermute | solution.py:229
  554.8 17.3 %collective-permute-start.83 = (bf16[256,768]{1,0:T(8,128)(2,1)S(1)}, bf16[256,768]{1,0:T(8,128)(2,1)S(1)}, u32[]{:S(2)}, u32[]{:S(2)}) collective-permute-start(bf16[256,768]{1,0:T(8,128)(2,1)S(1)} %get-tuple-element.182), channel_id=1, source_target_pairs={{1,0},{2,1},{3,2},{0,3},{9,4},{10,5},{11,6},{8,7},{5,8},{6,9},{7,1... | collective-permute-start | bytes 1179656 | tf_op jit(solution)/shard_map/ppermute | solution.py:229
  558.8 32.7 %collective-permute-start.72 = (bf16[128,2048]{1,0:T(8,128)(2,1)S(1)}, bf16[128,2048]{1,0:T(8,128)(2,1)S(1)}, u32[]{:S(2)}, u32[]{:S(2)}) collective-permute-start(bf16[128,2048]{1,0:T(8,128)(2,1)S(1)} %add_convert_fusion.5), channel_id=1, source_target_pairs={{0,2},{1,0},{2,4},{3,1},{4,6},{5,3},{6,7},{7,5},{8,10},{9,8},{10,1... | collective-permute-start | bytes 1572872 | tf_op jit(solution)/shard_map/ppermute | solution.py:93
  563.2 24.7 %collective-permute-start.84 = (bf16[256,768]{1,0:T(8,128)(2,1)S(1)}, bf16[256,768]{1,0:T(8,128)(2,1)S(1)}, u32[]{:S(2)}, u32[]{:S(2)}) collective-permute-start(bf16[256,768]{1,0:T(8,128)(2,1)S(1)} %get-tuple-element.181), channel_id=1, source_target_pairs={{2,0},{3,1},{0,2},{1,3},{10,4},{11,5},{8,6},{9,7},{6,8},{7,9},{4,1... | collective-permute-start | bytes 1179656 | tf_op jit(solution)/shard_map/ppermute | solution.py:229
  572.2 18.6 %collective-permute-start.85 = (bf16[256,768]{1,0:T(8,128)(2,1)S(1)}, bf16[256,768]{1,0:T(8,128)(2,1)S(1)}, u32[]{:S(2)}, u32[]{:S(2)}) collective-permute-start(bf16[256,768]{1,0:T(8,128)(2,1)S(1)} %get-tuple-element.180), channel_id=1, source_target_pairs={{3,0},{0,1},{1,2},{2,3},{11,4},{8,5},{9,6},{10,7},{7,8},{4,9},{5,1... | collective-permute-start | bytes 1179656 | tf_op jit(solution)/shard_map/ppermute | solution.py:229
  587.9 24.2 %collective-permute-start.99 = (bf16[512,2048]{1,0:T(8,128)(2,1)S(1)}, bf16[512,2048]{1,0:T(8,128)(2,1)S(1)}, u32[]{:S(2)}, u32[]{:S(2)}) collective-permute-start(bf16[512,2048]{1,0:T(8,128)(2,1)S(1)} %convolution_convert_fusion), channel_id=1, source_target_pairs={{0,8},{8,0},{1,9},{9,1},{2,10},{10,2},{3,11},{11,3},{4,12},{12,4},... | collective-permute-start | bytes 6291464 | tf_op jit(solution)/shard_map/ppermute | solution.py:112
  594.4 91.5 %collective-permute-start.76 = (f32[128,2048]{1,0:T(8,128)}, f32[128,2048]{1,0:T(8,128)}, u32[]{:S(2)}, u32[]{:S(2)}) collective-permute-start(f32[128,2048]{1,0:T(8,128)} %get-tuple-element.197), channel_id=1, source_target_pairs={{0,8},{8,0},{1,9},{9,1},{2,10},{10,2},{3,11},{11,3},{4,12},{12,4},... | collective-permute-start | bytes 3145736 | tf_op jit(solution)/shard_map/ppermute | solution.py:112
  608.4 16.4 %collective-permute-start.92 = (bf16[256,512]{1,0:T(8,128)(2,1)S(1)}, bf16[256,512]{1,0:T(8,128)(2,1)S(1)}, u32[]{:S(2)}, u32[]{:S(2)}) collective-permute-start(bf16[256,512]{1,0:T(8,128)(2,1)S(1)} %get-tuple-element.168), channel_id=1, source_target_pairs={{0,1},{1,0},{2,3},{3,2},{4,5},{5,4},{6,7},{7,6},{8,9},{9,8},{10,11... | collective-permute-start | bytes 786440 | tf_op jit(solution)/shard_map/ppermute | solution.py:87
  608.4 19.6 %collective-permute-start.93 = (bf16[256,512]{1,0:T(8,128)(2,1)S(1)}, bf16[256,512]{1,0:T(8,128)(2,1)S(1)}, u32[]{:S(2)}, u32[]{:S(2)}) collective-permute-start(bf16[256,512]{1,0:T(8,128)(2,1)S(1)} %get-tuple-element.167), channel_id=1, source_target_pairs={{0,2},{1,3},{2,0},{3,1},{4,6},{5,7},{6,4},{7,5},{8,10},{9,11},{10,... | collective-permute-start | bytes 786440 | tf_op jit(solution)/shard_map/ppermute | solution.py:87
  610.6 24.5 %collective-permute-start.94 = (bf16[256,512]{1,0:T(8,128)(2,1)S(1)}, bf16[256,512]{1,0:T(8,128)(2,1)S(1)}, u32[]{:S(2)}, u32[]{:S(2)}) collective-permute-start(bf16[256,512]{1,0:T(8,128)(2,1)S(1)} %get-tuple-element.166), channel_id=1, source_target_pairs={{0,3},{1,2},{2,1},{3,0},{4,7},{5,6},{6,5},{7,4},{8,11},{9,10},{10,... | collective-permute-start | bytes 786440 | tf_op jit(solution)/shard_map/ppermute | solution.py:87
  624.8 32.6 %collective-permute-start.95 = (bf16[256,512]{1,0:T(8,128)(2,1)S(1)}, bf16[256,512]{1,0:T(8,128)(2,1)S(1)}, u32[]{:S(2)}, u32[]{:S(2)}) collective-permute-start(bf16[256,512]{1,0:T(8,128)(2,1)S(1)} %get-tuple-element.165), channel_id=1, source_target_pairs={{0,4},{1,5},{2,6},{3,7},{4,0},{5,1},{6,2},{7,3},{8,12},{9,13},{10,... | collective-permute-start | bytes 786440 | tf_op jit(solution)/shard_map/ppermute | solution.py:87
  624.8 37.6 %collective-permute-start.96 = (bf16[256,512]{1,0:T(8,128)(2,1)S(1)}, bf16[256,512]{1,0:T(8,128)(2,1)S(1)}, u32[]{:S(2)}, u32[]{:S(2)}) collective-permute-start(bf16[256,512]{1,0:T(8,128)(2,1)S(1)} %get-tuple-element.164), channel_id=1, source_target_pairs={{0,5},{1,4},{2,7},{3,6},{4,1},{5,0},{6,3},{7,2},{8,13},{9,12},{10,... | collective-permute-start | bytes 786440 | tf_op jit(solution)/shard_map/ppermute | solution.py:87
  628.0 35.2 %collective-permute-start.97 = (bf16[256,512]{1,0:T(8,128)(2,1)S(1)}, bf16[256,512]{1,0:T(8,128)(2,1)S(1)}, u32[]{:S(2)}, u32[]{:S(2)}) collective-permute-start(bf16[256,512]{1,0:T(8,128)(2,1)S(1)} %get-tuple-element.163), channel_id=1, source_target_pairs={{0,6},{1,7},{2,4},{3,5},{4,2},{5,3},{6,0},{7,1},{8,14},{9,15},{10,... | collective-permute-start | bytes 786440 | tf_op jit(solution)/shard_map/ppermute | solution.py:87
  635.1 32.3 %collective-permute-start.98 = (bf16[256,512]{1,0:T(8,128)(2,1)S(1)}, bf16[256,512]{1,0:T(8,128)(2,1)S(1)}, u32[]{:S(2)}, u32[]{:S(2)}) collective-permute-start(bf16[256,512]{1,0:T(8,128)(2,1)S(1)} %get-tuple-element.162), channel_id=1, source_target_pairs={{0,7},{1,6},{2,5},{3,4},{4,3},{5,2},{6,1},{7,0},{8,15},{9,14},{10,... | collective-permute-start | bytes 786440 | tf_op jit(solution)/shard_map/ppermute | solution.py:87
  (179 other events, 3196.0 us)

commit v3 on v2

v3 whole, which is shorter than its diff:
```python
import functools
import math

import jax
import jax.numpy as jnp
from jax import lax
from jax.experimental import pallas as pl
from jax.experimental.layout import Layout as Format
from jax.experimental.layout import with_layout_constraint
from jax.experimental.pallas import tpu as pltpu
from jax.sharding import PartitionSpec as P

ROT = 64
LANES = 128
NORM_EPSILON = 1e-05
MASK_VALUE = -1e30
ROOT_HALF = 0.7071067811865476
DENSITY_SCALE = 0.3989422804014327
F32 = jnp.float32
BF16 = jnp.bfloat16
VMEM_BYTES = 24 * 1024 * 1024


def contract_rows(left_side, right_side):
    return lax.dot_general(
        left_side, right_side, (((0,), (0,)), ((), ())), preferred_element_type=F32
    )


def contract_cols(left_side, right_side):
    return lax.dot_general(
        left_side, right_side, (((1,), (1,)), ((), ())), preferred_element_type=F32
    )


def matmul(left_side, right_side):
    return jnp.dot(left_side, right_side, preferred_element_type=F32)


def normalize(values):
    centered = values - jnp.mean(values, axis=-1, keepdims=True)
    inverse = lax.rsqrt(jnp.mean(centered * centered, axis=-1, keepdims=True) + NORM_EPSILON)
    return (centered * inverse, inverse)


def sequence_tables(segments):
    places = jnp.arange(segments.shape[1], dtype=jnp.int32)
    same_doc = segments[:, :, None] == segments[:, None, :]
    earlier = places[None, :] < places[:, None]
    position = jnp.sum(jnp.where(same_doc & earlier, 1, 0).astype(jnp.int32), axis=2)
    allowed = same_doc & (places[None, :] <= places[:, None])
    exponent = jnp.arange(ROT // 2, dtype=F32) * (2.0 / ROT)
    frequency = 10000.0 ** (-exponent)
    angles = position.astype(F32)[..., None] * frequency
    cosine, sine = jnp.cos(angles), jnp.sin(angles)
    rest = jnp.zeros(angles.shape[:2] + (LANES - ROT,), F32)
    count = segments.shape[0] * segments.shape[1]
    return (
        jnp.concatenate([cosine, cosine, rest + 1.0], axis=-1).reshape(count, LANES),
        jnp.concatenate([-sine, sine, rest], axis=-1).reshape(count, LANES),
        jnp.where(allowed, 0.0, MASK_VALUE).astype(F32).reshape(count, segments.shape[1]),
    )


class Layout:
    def __init__(self, mesh, heads):
        self.cores = mesh.shape["tensor"]
        self.dp = mesh.shape["dp"]
        self.chips = heads
        self.groups = self.dp // heads
        self.core_heads = heads // self.cores
        self.ring = list(range(0, heads, 2)) + list(range(heads - 1, 0, -2))
        self.slots = []
        for k in range(heads // 2):
            self.slots += [-k % heads, k + 1]

    def place(self):
        dp_index = lax.axis_index("dp")
        self.core = lax.axis_index("tensor")
        self.chip = dp_index // self.groups
        self.group = dp_index % self.groups

    def between_chips(self, block, target_of, sections=None):
        pairs = [
            (chip * self.groups + group, target_of(chip) * self.groups + group)
            for chip in range(self.chips)
            for group in range(self.groups)
        ]
        if sections is None:
            return lax.ppermute(block, "dp", pairs)
        pairs = [
            (section * self.dp + source, section * self.dp + target)
            for section in sections
            for source, target in pairs
        ]
        return lax.ppermute(block, ("section", "dp"), pairs)

    def ring_step(self, block, distance, sections=None):
        size = len(self.ring)

        def target_of(chip):
            return self.ring[(self.ring.index(chip) + distance) % size]

        return self.between_chips(block, target_of, sections)

    def between_groups(self, block, distance):
        pairs = [
            (chip * self.groups + group, chip * self.groups + (group + distance) % self.groups)
            for chip in range(self.chips)
            for group in range(self.groups)
        ]
        return lax.ppermute(block, "dp", pairs)

    def other_core(self, block):
        return lax.ppermute(block, "tensor", [(0, 1), (1, 0)])

    def by_core(self, own, other):
        first = self.core == 0
        return jnp.concatenate(
            [jnp.where(first, own, other), jnp.where(first, other, own)], axis=0
        )

    def gather_groups(self, block, axis):
        if self.groups == 1:
            return block
        size = block.shape[axis]
        shape = list(block.shape)
        shape[axis] = size * self.groups
        total = jnp.zeros(shape, block.dtype)
        for distance in range(self.groups):
            part = self.between_groups(block, distance) if distance else block
            source = (self.group - distance) % self.groups
            total = lax.dynamic_update_slice_in_dim(total, part, source * size, axis)
        return total

    def scatter_groups(self, block, axis):
        if self.groups == 1:
            return block.astype(F32)
        size = block.shape[axis] // self.groups
        total = lax.dynamic_slice_in_dim(block, self.group * size, size, axis).astype(F32)
        for distance in range(1, self.groups):
            target = (self.group + distance) % self.groups
            part = lax.dynamic_slice_in_dim(block, target * size, size, axis)
            total = total + self.between_groups(part.astype(BF16), distance).astype(F32)
        return total

    def sum_all(self, block):
        block = block + self.other_core(block)
        mask = 1
        while mask < self.chips:
            block = block + self.between_chips(block, lambda chip: chip ^ mask)
            mask *= 2
        total = block
        for distance in range(1, self.groups):
            total = total + self.between_groups(block, distance)
        return total

    def ring_gather(self, parts, sections=None):
        half = self.chips // 2
        held = [{0: part} for part in parts]
        for step in range(1, half + 1):
            for at, slots in enumerate(held):
                down = half - at % 2
                if step <= down:
                    slots[step] = self.ring_step(slots[step - 1], -1, sections)
                if step <= self.chips - 1 - down:
                    slots[self.chips - step] = self.ring_step(
                        slots[(self.chips - step + 1) % self.chips], 1, sections
                    )
        return {slot: [slots[slot] for slots in held] for slot in range(self.chips)}

    def ring_scatter(self, pieces, sections=None, waits=None):
        half = self.chips // 2
        totals = []
        for at in range(len(pieces[0])):
            parts = [pieces[slot][at] for slot in range(self.chips)]
            up = half - at % 2
            total = parts[0].astype(F32)
            for way, slots in (
                (1, range(up, 0, -1)),
                (-1, range(up + 1, self.chips)),
            ):
                moving = None
                for step, slot in enumerate(slots):
                    if moving is None:
                        moving = parts[slot]
                    else:
                        moving = (moving.astype(F32) + parts[slot].astype(F32)).astype(BF16)
                    if waits and step in waits:
                        moving = ordered(moving, *waits[step])
                    moving = self.ring_step(moving, way, sections)
                total = total + moving.astype(F32)
            totals.append(total)
        return totals

    def head_turn(self, chip, turn):
        return (chip % self.core_heads + turn) % self.core_heads

    def head_route(self, turn):
        pairs = []
        for core in range(self.cores):
            for chip in range(self.chips):
                target_core = chip // self.core_heads
                target = core * self.core_heads + self.head_turn(chip, turn)
                for group in range(self.groups):
                    pairs.append(
                        (
                            core * self.dp + chip * self.groups + group,
                            target_core * self.dp + target * self.groups + group,
                        )
                    )
        return pairs

    def send_head(self, block, turn):
        return lax.ppermute(block, ("tensor", "dp"), self.head_route(turn))

    def return_head(self, block, turn):
        pairs = [(target, source) for source, target in self.head_route(turn)]
        return lax.ppermute(block, ("tensor", "dp"), pairs)

    def swap(self, block, mask):
        return self.between_chips(block, lambda chip: chip ^ mask)


def ordered(block, *earlier):
    return lax.optimization_barrier((block,) + earlier)[0]


class Queue:
    def __init__(self, window, first=()):
        self.window = window
        self.results = [first] * window

    def ready(self, block):
        earlier = self.results[-self.window]
        return ordered(block, *earlier) if earlier else block

    def put(self, *result):
        self.results.append(result)


def turn_head(values, cosine, sine):
    first = values[:, :LANES]
    lane = lax.broadcasted_iota(jnp.int32, first.shape, 1)
    half = ROT // 2
    swapped = jnp.where(
        lane < half, pltpu.roll(first, LANES - half, 1), pltpu.roll(first, half, 1)
    )
    return jnp.concatenate([first * cosine + swapped * sine, values[:, LANES:]], axis=1)


def attend(joined, cosine, sine, mask):
    size = joined.shape[1] // 3
    queries = turn_head(joined[:, :size], cosine, sine).astype(BF16)
    key_rows = turn_head(joined[:, size : 2 * size], cosine, sine).astype(BF16)
    values = joined[:, 2 * size :].astype(BF16)
    scores = contract_cols(queries, key_rows) * (1.0 / math.sqrt(size)) + mask
    powered = jnp.exp(scores - jnp.max(scores, axis=-1, keepdims=True))
    attention = powered / jnp.sum(powered, axis=-1, keepdims=True)
    attended = matmul(attention.astype(BF16), values).astype(BF16)
    return (queries, key_rows, values, attention, attended)


def attend_back(queries, key_rows, values, attention, attended_grad, cosine, sine):
    scale = 1.0 / math.sqrt(queries.shape[1])
    values_grad = contract_rows(attention.astype(BF16), attended_grad)
    attention_grad = contract_cols(attended_grad, values)
    row_dots = jnp.sum(attention_grad * attention, axis=-1, keepdims=True)
    scores_grad = (attention * (attention_grad - row_dots)).astype(BF16)
    queries_grad = turn_head(matmul(scores_grad, key_rows) * scale, cosine, -sine)
    keys_grad = turn_head(contract_rows(scores_grad, queries) * scale, cosine, -sine)
    return jnp.concatenate([queries_grad, keys_grad, values_grad], axis=1).astype(BF16)


def fold_rows(values):
    return jnp.sum(values.reshape(values.shape[0] // 8, 8, values.shape[1]), axis=0)


def store_rows(refs, cols, values):
    rows = values.shape[0] // len(refs)
    for at, ref in enumerate(refs):
        ref[:, cols] = values[at * rows : (at + 1) * rows].astype(BF16)


def steps(size):
    step = min(256, size)
    return [slice(at, at + step) for at in range(0, size, step)]


def load_rows(refs, target, shift=0.0):
    rows = target.shape[0] // len(refs)
    for at, ref in enumerate(refs):
        values = ref[:rows]
        if not isinstance(shift, float):
            values = (values.astype(F32) + shift).astype(BF16)
        target[at * rows : (at + 1) * rows] = values


def split_heads(heads, wo):
    size = wo.shape[0]
    rows = heads.shape[0] // wo.shape[1] * size
    cols = heads.shape[1] - size
    part = size * rows // heads.shape[0]
    for at in range(0, heads.shape[0], rows):
        for k in range(rows // part):
            wo[at // rows * part : (at // rows + 1) * part, k * size : (k + 1) * size] = heads[
                at + k * part : at + (k + 1) * part, cols:
            ]
    return heads.at[:, :cols]


def forward_kernel(count, pieces, *refs):
    blocks, refs = refs[:count], refs[count:]
    heads, wu0, wu1, wd0, wd1, bq, bu, ratio, cosine, sine, mask = refs[:11]
    outs, refs = refs[11 : 11 + pieces], refs[11 + pieces :]
    first_norm, second_norm, attended, active, wo = refs
    wq = split_heads(heads, wo)
    length = mask.shape[1]
    part = wu0.shape[1]
    load_rows(blocks, first_norm, ratio[0:1])
    load_rows(blocks, second_norm, ratio[1:2])
    joined = matmul(first_norm[...], wq[...]) + bq[...]
    for s in range(mask.shape[0] // length):
        rows = slice(s * length, (s + 1) * length)
        attended[rows] = attend(joined[rows], cosine[rows], sine[rows], mask[rows])[4]
    for k, wu in enumerate((wu0, wu1)):
        for cols in steps(part):
            at = slice(k * part + cols.start, k * part + cols.stop)
            hidden = matmul(second_norm[...], wu[:, cols]) + bu[:, at]
            active[:, at] = (hidden * (0.5 * (1.0 + lax.erf(hidden * ROOT_HALF)))).astype(BF16)
    for cols in steps(wo.shape[1]):
        total = (
            matmul(attended[...], wo[:, cols])
            + matmul(active[:, :part], wd0[:, cols])
            + matmul(active[:, part:], wd1[:, cols])
        )
        store_rows(outs, cols, total)


def upstream_kernel(count, *refs):
    grads, refs = refs[:count], refs[count:]
    heads, wd0, wd1, attended_grad, active_grad, upstream, wo = refs
    split_heads(heads, wo)
    part = wd0.shape[0]
    load_rows(grads, upstream)
    attended_grad[...] = contract_cols(upstream[...], wo[...]).astype(BF16)
    for k, wd in enumerate((wd0, wd1)):
        for rows in steps(part):
            at = slice(k * part + rows.start, k * part + rows.stop)
            active_grad[:, at] = contract_cols(upstream[...], wd[rows]).astype(BF16)


def both_kernel(count, pieces, chained, *refs):
    blocks, refs = refs[:count], refs[count:]
    heads, wu0, wu1, bq, bu, ratio, cosine, sine, mask, attended_grad, active_grad = refs[:11]
    refs = refs[11 + chained :]
    first_norm, second_norm, qkv, attention, attended, active, slope = refs[:7]
    outs, (joined_grad, hidden_grad) = refs[7 : 7 + pieces], refs[7 + pieces :]
    length = mask.shape[1]
    size = attended_grad.shape[1]
    wq = heads.at[:, : 3 * size]
    part = wu0.shape[1]
    load_rows(blocks, first_norm, ratio[0:1])
    load_rows(blocks, second_norm, ratio[1:2])
    joined = matmul(first_norm[...], wq[...]) + bq[...]

    def attention_of(s):
        rows = slice(s * length, (s + 1) * length)
        queries, key_rows, values, weights, result = attend(
            joined[rows], cosine[rows], sine[rows], mask[rows]
        )
        qkv[rows, :size] = queries
        qkv[rows, size : 2 * size] = key_rows
        qkv[rows, 2 * size :] = values
        attention[rows] = weights
        attended[rows] = result
        joined_grad[rows] = attend_back(
            queries, key_rows, values, weights, attended_grad[rows], cosine[rows], sine[rows]
        )

    for k, wu in enumerate((wu0, wu1)):
        attention_of(k)
        for cols in steps(part):
            at = slice(k * part + cols.start, k * part + cols.stop)
            hidden = matmul(second_norm[...], wu[:, cols]) + bu[:, at]
            normal_cdf = 0.5 * (1.0 + lax.erf(hidden * ROOT_HALF))
            normal_pdf = jnp.exp(-0.5 * hidden * hidden) * DENSITY_SCALE
            active[:, at] = (hidden * normal_cdf).astype(BF16)
            change = normal_cdf + hidden * normal_pdf
            slope[:, at] = change.astype(BF16)
            hidden_grad[:, at] = (active_grad[:, at].astype(F32) * change).astype(BF16)
    for rows in steps(wq.shape[0]):
        total = (
            contract_cols(joined_grad[...], wq[rows])
            + contract_cols(hidden_grad[:, :part], wu0[rows])
            + contract_cols(hidden_grad[:, part:], wu1[rows])
        )
        store_rows(outs, rows, total)


def backward_kernel(count, pieces, chained, *refs):
    grads, refs = refs[:count], refs[count:]
    second, heads, wu0, wu1, wd0, wd1, cosine, sine = refs[:8]
    first_norm, second_norm, qkv, attention, attended, active, slope = refs[8:15]
    refs = refs[15 + chained :]
    upstream, joined_grad, hidden_grad, norm_sums, joined_sum, hidden_sum = refs[:6]
    outs, wo = refs[6 : 6 + pieces], refs[6 + pieces]
    wq = split_heads(heads, wo)
    length = attention.shape[1]
    size = wo.shape[0]
    part = wu0.shape[1]
    load_rows(grads, upstream)
    attended_grad = contract_cols(upstream[...], wo[...]).astype(BF16)
    for k, wd in enumerate((wd0, wd1)):
        rows = slice(k * length, (k + 1) * length)
        joined_grad[rows] = attend_back(
            qkv[rows, :size],
            qkv[rows, size : 2 * size],
            qkv[rows, 2 * size :],
            attention[rows],
            attended_grad[rows],
            cosine[rows],
            sine[rows],
        )
        for cols in steps(part):
            at = slice(k * part + cols.start, k * part + cols.stop)
            active_grad = contract_cols(upstream[...], wd[cols])
            grad = (active_grad * slope[:, at].astype(F32)).astype(BF16)
            hidden_grad[:, at] = grad
            hidden_sum[:, at] = fold_rows(grad.astype(F32))
    joined_sum[...] = fold_rows(joined_grad[...].astype(F32))
    for rows in steps(wq.shape[0]):
        first = contract_cols(joined_grad[...], wq[rows])
        other = contract_cols(hidden_grad[:, :part], wu0[rows]) + contract_cols(
            hidden_grad[:, part:], wu1[rows]
        )
        norm_sums[0:8, rows] = fold_rows(first * first_norm[:, rows].astype(F32))
        norm_sums[8:16, rows] = fold_rows(other * second_norm[:, rows].astype(F32))
        norm_sums[16:24, rows] = fold_rows(first)
        norm_sums[24:32, rows] = fold_rows(other)
        store_rows(outs, rows, first + other)

    @pl.when(second[0] != 0)
    def _():
        for cols in steps(wq.shape[0]):
            total = (
                matmul(attended[...], wo[:, cols])
                + matmul(active[:, :part], wd0[:, cols])
                + matmul(active[:, part:], wd1[:, cols])
            )
            store_rows(outs, cols, total)


def rows_spec(array, count, pair):
    return pl.BlockSpec((count, array.shape[1]), lambda i: (pair, 0))


def call_rows(
    kernel, whole, by_rows, chain, outs_by_rows, outs_whole, scratch, at, rows, flops
):
    out_shape = list(outs_by_rows) + list(outs_whole)
    out_specs = [rows_spec(item, rows, at) for item in outs_by_rows] + [
        pl.BlockSpec(item.shape, lambda i: (0, 0)) for item in outs_whole
    ]
    operands = [*whole, *by_rows]
    in_specs = [
        pl.BlockSpec(memory_space=pltpu.SMEM if item.ndim == 1 else pltpu.VMEM) for item in whole
    ] + [rows_spec(item, rows, at) for item in by_rows]
    aliases = {}
    for k, item in enumerate(chain or ()):
        aliases[len(operands)] = k
        operands.append(item)
        in_specs.append(pl.BlockSpec(memory_space=pl.ANY))
    return pl.pallas_call(
        kernel,
        grid=(1,),
        out_shape=out_shape,
        in_specs=in_specs,
        out_specs=out_specs,
        scratch_shapes=scratch,
        input_output_aliases=aliases,
        cost_estimate=pl.CostEstimate(flops=flops, bytes_accessed=rows * 8192, transcendentals=0),
        compiler_params=pltpu.CompilerParams(vmem_limit_bytes=VMEM_BYTES),
    )(*operands)


def on_device(
    layout,
    tokens,
    segments,
    cotangent,
    norm_gain,
    norm_bias,
    qkv_weight,
    qkv_bias,
    out_weight,
    out_bias,
    up_weight,
    up_bias,
    down_weight,
    down_bias,
):
    layout.place()
    first_section = lax.axis_index("section") == 0
    cores, chips, chip, core = layout.cores, layout.chips, layout.chip, layout.core
    length = segments.shape[1]
    width = tokens.shape[1]
    core_heads, joined_size = qkv_weight.shape[2:]
    head_size = joined_size // 3
    hidden_part = up_weight.shape[2] // chips
    hidden_size = cores * hidden_part
    row_count = chips * length

    def core_rows(block):
        return lax.dynamic_slice_in_dim(block, core * length, length, 0)

    def parts_of(rows, count=2):
        size = rows.shape[0] // count
        return [rows[k * size : (k + 1) * size] for k in range(count)]

    gains = norm_gain[0].astype(F32)
    shifts = norm_bias[0].astype(F32)
    own_tokens = core_rows(tokens).astype(F32)
    own_cotangent = core_rows(cotangent)
    own_normed, _ = normalize(own_tokens)

    own_segments = lax.dynamic_index_in_dim(segments, core, 0, keepdims=True).astype(BF16)
    own_segments = jnp.pad(own_segments, ((0, 15), (0, width - length)))
    first_block = jnp.where(first_section, own_normed.astype(BF16), own_cotangent)
    first_block = jnp.concatenate([first_block, own_segments], axis=0)
    gathered = layout.ring_gather([first_block])
    all_segments = jnp.concatenate(
        [gathered[slot][0][length : length + 1, :length] for slot in layout.slots], axis=0
    )
    cosine, sine, mask = sequence_tables(all_segments.astype(jnp.int32))

    shard = qkv_weight.shape[1]
    at = lax.axis_index("dp") * shard
    gain_rows = lax.dynamic_slice_in_dim(gains, at, shard, 1)
    qkv_scaled = qkv_weight[0].reshape(shard, core_heads * joined_size).astype(F32)
    qkv_scaled = layout.gather_groups((qkv_scaled * gain_rows[0][:, None]).astype(BF16), 0)
    up_scaled = (up_weight[0].astype(F32) * gain_rows[1][:, None]).astype(BF16)
    up_scaled = layout.gather_groups(up_scaled, 0)
    out_shard = layout.gather_groups(out_weight[0], 1)
    wd0 = layout.gather_groups(down_weight[0], 0)
    wd1 = layout.other_core(wd0)
    block_rows = qkv_scaled.shape[0]

    ratio = shifts / gains
    biases = jnp.concatenate([qkv_bias[0].reshape(-1), up_bias[0]]).astype(F32)[None]
    both = jnp.concatenate([biases, layout.other_core(biases)], axis=0)
    joined_biases = both[:, : core_heads * joined_size]
    joined_biases = jnp.where(
        chip // core_heads == core, joined_biases[0], joined_biases[1]
    ).reshape(core_heads, joined_size)
    bq = lax.dynamic_index_in_dim(joined_biases, chip % core_heads, 0, keepdims=True)
    bu = lax.dynamic_slice_in_dim(
        both, core_heads * joined_size + chip * hidden_part, hidden_part, 1
    ).reshape(1, hidden_size)

    hd_rows = out_shard.shape[1]
    head_blocks = []
    for turn in range(core_heads):
        head = layout.head_turn(chip, turn)
        out_part = lax.dynamic_index_in_dim(out_shard, head, 0, keepdims=False)
        out_part = out_part.reshape(hd_rows, width // head_size, head_size).transpose(1, 0, 2)
        head_blocks.append(
            jnp.concatenate(
                [
                    lax.dynamic_slice_in_dim(qkv_scaled, head * joined_size, joined_size, 1),
                    out_part.reshape(block_rows, head_size),
                ],
                axis=1,
            )
        )
    up_blocks = [
        lax.dynamic_slice_in_dim(up_scaled, (chip ^ up_mask) * hidden_part, hidden_part, 1)
        for up_mask in range(chips)
    ]
    queue = Queue(3)
    heads = jnp.zeros((core_heads * block_rows, joined_size + head_size), BF16)
    for turn, block in enumerate(head_blocks):
        if turn == 2:
            block = ordered(block, *up_blocks)
        block = layout.send_head(queue.ready(block), turn)
        slot = (chip - turn) % core_heads
        heads = lax.dynamic_update_slice_in_dim(heads, block, slot * block_rows, 0)
        queue.put(heads)
    wu0 = jnp.zeros((chips * block_rows, hidden_part), BF16)
    wu0 = lax.dynamic_update_slice_in_dim(wu0, up_blocks[0], chip * block_rows, 0)
    for up_mask in range(chips - 1, 0, -1):
        source = chip ^ up_mask
        block = queue.ready(up_blocks[up_mask])
        if up_mask == 1:
            block = ordered(block, cosine, sine, mask, bq, bu)
        block = layout.swap(block, up_mask)
        wu0 = lax.dynamic_update_slice_in_dim(wu0, block, source * block_rows, 0)
        queue.put(wu0)
    wu1 = layout.other_core(wu0)
    heads = layout.by_core(heads, layout.other_core(ordered(heads, up_blocks[1])))

    row_bias = (out_bias[0].astype(F32) + down_bias[0].astype(F32))[None]

    part_rows = length // 2
    piece = jax.ShapeDtypeStruct((part_rows, width), BF16)

    def by_rows(cols, dtype):
        return jax.ShapeDtypeStruct((row_count, cols), dtype)

    matrix_flops = 4 * length * width * (joined_size + head_size + 2 * hidden_size)

    def pair_blocks(blocks, pair):
        return blocks[layout.slots[2 * pair]] + blocks[layout.slots[2 * pair + 1]]

    def put_pieces(pieces, pair, blocks):
        pieces[layout.slots[2 * pair]] = blocks[:2]
        pieces[layout.slots[2 * pair + 1]] = blocks[2:]

    def norm_back(upstream, scaled, normed, inverse):
        return upstream.astype(F32) + inverse * (
            scaled
            - jnp.mean(scaled, axis=-1, keepdims=True)
            - normed * jnp.mean(scaled * normed, axis=-1, keepdims=True)
        )

    cotangent_blocks = [block for slot in layout.slots for block in gathered[slot]]
    attended_grad, active_grad = call_rows(
        functools.partial(upstream_kernel, len(cotangent_blocks)),
        (*cotangent_blocks, heads, wd0, wd1),
        (),
        None,
        (),
        [by_rows(head_size, BF16), by_rows(hidden_size, BF16)],
        [pltpu.VMEM((row_count, width), BF16), pltpu.VMEM((head_size, width), BF16)],
        0,
        row_count,
        2 * row_count * width * (head_size + hidden_size),
    )

    matrices = (heads, wu0, wu1, wd0, wd1)
    pieces = {}
    for at in (1, 0):
        slots = layout.slots[at * chips // 2 : (at + 1) * chips // 2]
        blocks = [block for slot in slots for block in gathered[slot]]
        rows = row_count // 2
        results = call_rows(
            functools.partial(forward_kernel, len(blocks), 2 * len(slots)),
            (*blocks, *matrices, bq, bu, ratio),
            (cosine, sine, mask),
            None,
            (),
            [piece] * (2 * len(slots)),
            [
                pltpu.VMEM((rows, width), BF16),
                pltpu.VMEM((rows, width), BF16),
                pltpu.VMEM((rows, head_size), BF16),
                pltpu.VMEM((rows, hidden_size), BF16),
                pltpu.VMEM((head_size, width), BF16),
            ],
            at,
            rows,
            2 * matrix_flops,
        )
        for k, slot in enumerate(slots):
            pieces[slot] = results[2 * k : 2 * k + 2]
    branch_rows = layout.ring_scatter(pieces)
    first_out = [
        (rows + branch + row_bias).astype(BF16)
        for rows, branch in zip(parts_of(own_tokens), branch_rows)
    ]

    layer_input = [
        jnp.where(first_section, rows, lax.ppermute(sent, "section", [(0, 1)]).astype(F32))
        for rows, sent in zip(parts_of(own_tokens), first_out)
    ]
    own_normed = [normalize(rows) for rows in layer_input]
    normed_blocks = layout.ring_gather([rows.astype(BF16) for rows, _ in own_normed])
    kept_shapes = (
        by_rows(width, BF16),
        by_rows(width, BF16),
        by_rows(joined_size, BF16),
        by_rows(length, F32),
        by_rows(head_size, BF16),
        by_rows(hidden_size, BF16),
        by_rows(hidden_size, BF16),
    )
    kept = None
    pieces = {}
    for pair in range(chips // 2):
        blocks = pair_blocks(normed_blocks, pair)
        results = call_rows(
            functools.partial(both_kernel, len(blocks), 4, len(kept_shapes) if kept else 0),
            (*blocks, heads, wu0, wu1, bq, bu, ratio),
            (cosine, sine, mask, attended_grad, active_grad),
            kept,
            kept_shapes,
            [piece] * 4,
            [
                pltpu.VMEM((2 * length, joined_size), BF16),
                pltpu.VMEM((2 * length, hidden_size), BF16),
            ],
            pair,
            2 * length,
            2 * matrix_flops,
        )
        kept = results[: len(kept_shapes)]
        put_pieces(pieces, pair, results[len(kept_shapes) :])
    first_norm, second_norm, qkv, attention, attended, active, slope = kept
    scaled_rows = layout.ring_scatter(pieces)
    second_grad = [
        norm_back(given, scaled, *norm)
        for given, scaled, norm in zip(parts_of(own_cotangent), scaled_rows, own_normed)
    ]

    arrived_grad = [
        lax.ppermute(rows.astype(BF16), "section", [(1, 0)]) for rows in second_grad
    ]
    own_upstream = [
        jnp.where(first_section, arrived, given)
        for arrived, given in zip(arrived_grad, parts_of(own_cotangent))
    ]
    upstream_blocks = layout.ring_gather(own_upstream)
    second_section = jnp.where(first_section, 0, 1).astype(jnp.int32).reshape(1)
    grad_shapes = (by_rows(width, BF16), by_rows(joined_size, BF16), by_rows(hidden_size, BF16))
    grads = None
    last_pieces = {}
    sums = []
    for pair in range(chips // 2):
        blocks = pair_blocks(upstream_blocks, pair)
        results = call_rows(
            functools.partial(
                backward_kernel, len(blocks), 4, len(grad_shapes) if grads else 0
            ),
            (*blocks, second_section, *matrices),
            (cosine, sine, first_norm, second_norm, qkv, attention, attended, active, slope),
            grads,
            grad_shapes,
            [
                jax.ShapeDtypeStruct((32, width), F32),
                jax.ShapeDtypeStruct((8, joined_size), F32),
                jax.ShapeDtypeStruct((8, hidden_size), F32),
            ]
            + [piece] * 4,
            [pltpu.VMEM((head_size, width), BF16)],
            pair,
            2 * length,
            matrix_flops,
        )
        grads = results[: len(grad_shapes)]
        sums.append(results[len(grad_shapes) : len(grad_shapes) + 3])
        for k in range(2):
            last_pieces[layout.slots[2 * pair + k]] = results[2 * k - 4 : 2 * k - 2 or None]
    upstream, joined_grad, hidden_grad = grads

    def half_of(array, which):
        size = array.shape[1] // cores
        return lax.dynamic_slice_in_dim(array, which * size, size, 1)

    row_major = Format(major_to_minor=(0, 1))

    def weight_grad(left_side, right_side):
        return with_layout_constraint(contract_rows(left_side, right_side), row_major)

    joined_given = weight_grad(half_of(first_norm, 1 - core), joined_grad).astype(BF16)
    out_given = weight_grad(half_of(attended, 1 - core), upstream).astype(BF16)
    hidden_given = weight_grad(second_norm, hidden_grad[:, hidden_part:]).astype(BF16)
    down_given = weight_grad(active[:, hidden_part:], upstream).astype(BF16)
    given = (joined_given, out_given, hidden_given, down_given)
    joined_taken, out_taken, hidden_taken, down_taken = (
        layout.other_core(item) for item in given
    )

    def core_sum(own, taken):
        return (own + taken.astype(F32)).astype(BF16)

    late_grad, late_attended = ordered(joined_grad, *given), ordered(attended, *given)
    joined_held = core_sum(weight_grad(half_of(first_norm, core), late_grad), joined_taken)
    out_held = core_sum(weight_grad(half_of(late_attended, core), upstream), out_taken)
    late_grad = ordered(hidden_grad, joined_held, out_held)
    hidden_held = core_sum(weight_grad(second_norm, late_grad[:, :hidden_part]), hidden_taken)

    own_given = jnp.concatenate(own_upstream, axis=0)
    norm_sums, joined_sum, hidden_sum = (
        functools.reduce(jnp.add, [item[k] for item in sums]) for k in range(3)
    )
    norm_sums = jnp.sum(norm_sums.reshape(2, 2, 8, width), axis=2)
    norm_sums = jnp.stack([norm_sums[0] - ratio * norm_sums[1], norm_sums[1]]) / gains
    joined_bias_all = lax.dynamic_update_slice(
        jnp.zeros((chips, joined_size), F32), jnp.sum(joined_sum, axis=0)[None], (chip, 0)
    )
    hidden_sum = jnp.sum(hidden_sum, axis=0)[None, None]
    hidden_bias_all = jnp.zeros((cores, chips, hidden_part), F32)
    hidden_bias_all = lax.dynamic_update_slice(
        hidden_bias_all, hidden_sum[:, :, :hidden_part], (core, chip, 0)
    )
    hidden_bias_all = lax.dynamic_update_slice(
        hidden_bias_all, hidden_sum[:, :, hidden_part:], (1 - core, chip, 0)
    )
    vectors = (
        norm_sums,
        joined_bias_all,
        jnp.sum(own_given, axis=0, dtype=F32),
        hidden_bias_all,
    )
    joint = layout.sum_all(
        ordered(jnp.concatenate([item.reshape(-1) for item in vectors]), *given)
    )
    summed, start = [], 0
    for item in vectors:
        summed.append(joint[start : start + item.size].reshape(item.shape))
        start += item.size
    norm_sums, joined_bias_all, out_bias_grad, hidden_bias_all = summed
    joined_bias_grad = lax.dynamic_slice_in_dim(joined_bias_all, core * core_heads, core_heads, 0)
    up_bias_grad = lax.dynamic_index_in_dim(hidden_bias_all, core, 0, keepdims=False).reshape(-1)

    (last_rows,) = layout.ring_scatter(
        {slot: [jnp.concatenate(parts, axis=0)] for slot, parts in last_pieces.items()},
        None,
        {1: (joined_held, out_held)},
    )
    last_normed, last_inverse = (
        jnp.concatenate([norm[k] for norm in own_normed], axis=0) for k in range(2)
    )
    first_grad = norm_back(own_given, last_rows, last_normed, last_inverse)
    own_grad = jnp.where(first_section, first_grad, jnp.concatenate(second_grad, axis=0))
    input_gradients = layout.by_core(own_grad, layout.other_core(own_grad))
    second_out = (jnp.concatenate(layer_input, axis=0) + last_rows + row_bias).astype(BF16)
    own_out = jnp.where(first_section, jnp.concatenate(first_out, axis=0), second_out)
    layer_outputs = layout.by_core(own_out, layout.other_core(own_out))

    up_weight_grad = jnp.zeros((shard, chips * hidden_part), F32)
    qkv_grad = jnp.zeros((shard, core_heads * joined_size), F32)
    out_weight_grad = jnp.zeros((core_heads, head_size // layout.dp, width), F32)
    head_blocks = []
    out_rows = out_held.shape[0] // core_heads
    for turn in range(core_heads):
        slot = (chip - turn) % core_heads
        out_part = lax.dynamic_slice_in_dim(out_held, slot * out_rows, out_rows, 0)
        out_part = out_part.reshape(out_rows, width // head_size, head_size).transpose(1, 0, 2)
        head_blocks.append(
            jnp.concatenate(
                [
                    lax.dynamic_slice_in_dim(joined_held, slot * block_rows, block_rows, 0),
                    out_part.reshape(block_rows, head_size),
                ],
                axis=1,
            )
        )
    queue = Queue(3)
    for turn, block in enumerate(head_blocks):
        head = layout.head_turn(chip, turn)
        if turn == 1:
            block = ordered(block, hidden_held, *head_blocks)
        block = layout.return_head(queue.ready(block), turn)
        out_block = block[:, joined_size:].reshape(width // head_size, out_rows, head_size)
        out_block = out_block.transpose(1, 0, 2).reshape(out_rows, width)
        out_block = layout.scatter_groups(out_block, 0)
        block = layout.scatter_groups(block[:, :joined_size], 0) * gain_rows[0][:, None]
        qkv_grad = lax.dynamic_update_slice_in_dim(qkv_grad, block, head * joined_size, 1)
        out_weight_grad = lax.dynamic_update_slice_in_dim(
            out_weight_grad, out_block[None], head, 0
        )
        queue.put(qkv_grad, out_weight_grad)
    joined_weight_grad = qkv_grad.reshape(shard, core_heads, joined_size)

    late_active = ordered(active, hidden_held)
    down_weight_grad = weight_grad(late_active[:, :hidden_part], upstream) + down_taken.astype(F32)
    if layout.groups > 1:
        down_weight_grad = layout.scatter_groups(down_weight_grad, 0)

    for up_mask in range(chips - 1, -1, -1):
        source = chip ^ up_mask
        block = lax.dynamic_slice_in_dim(hidden_held, source * block_rows, block_rows, 0)
        if up_mask:
            block = queue.ready(block)
            if up_mask == 3:
                block = ordered(block, down_weight_grad, joint)
            if up_mask == 1:
                block = ordered(block, last_rows, joined_weight_grad)
            block = layout.swap(block, up_mask)
        block = layout.scatter_groups(block, 0) * gain_rows[1][:, None]
        up_weight_grad = lax.dynamic_update_slice_in_dim(
            up_weight_grad, block, source * hidden_part, 1
        )
        queue.put(up_weight_grad)

    return (
        layer_outputs[None],
        input_gradients[None],
        norm_sums[0][None],
        norm_sums[1][None],
        joined_weight_grad[None],
        joined_bias_grad[None],
        out_weight_grad[None],
        out_bias_grad[None],
        up_weight_grad[None],
        up_bias_grad[None],
        down_weight_grad[None],
        out_bias_grad[None],
    )


def solution(mesh):
    def whole(*arrays):
        layout = Layout(mesh, arrays[5].shape[2])

        def local(*blocks):
            return on_device(layout, *blocks)

        return jax.shard_map(
            local,
            mesh=mesh,
            in_specs=(
                P("dp", None),
                P("dp", None),
                P("dp", None),
                P("section", None, None),
                P("section", None, None),
                P("section", "dp", "tensor", None),
                P("section", "tensor", None),
                P("section", "tensor", "dp", None),
                P("section", None),
                P("section", "dp", "tensor"),
                P("section", "tensor"),
                P("section", ("tensor", "dp"), None),
                P("section", None),
            ),
            out_specs=(
                P("section", "dp", None),
                P("section", "dp", None),
                P("section", None, None),
                P("section", None, None),
                P("section", "dp", "tensor", None),
                P("section", "tensor", None),
                P("section", "tensor", "dp", None),
                P("section", None),
                P("section", "dp", "tensor"),
                P("section", "tensor"),
                P("section", ("tensor", "dp"), None),
                P("section", None),
            ),
            check_vma=False,
        )(*arrays)

    return whole
```

time: 698 us -> 646 us (0.926)
  the two profiles are of different devices: /device:TPU:0 before, /device:TPU:10 now
where the time goes in v3:
time: 646 us; the launch traced here: 637 us
  starting transfers between devices  193 us (30%)
  waiting for transfers between devices  163 us (25%)
  Pallas kernels  101 us (16%)
  local copies, waits for them, and re-layouts  80.3 us (12%)
  other arithmetic  67 us (10%)
  matrix products  29.2 us (5%)
    ppermute x87, starting transfers between devices, between_chips(): return lax.ppermute(block, 'dp', pairs)  174 us
    ppermute x87, waiting for transfers between devices, between_chips(): return lax.ppermute(block, 'dp', pairs)  143 us
    pallas_call x11, Pallas kernels, call_rows(): pl.pallas_call(kernel, grid=(1,), out_shape=out_shape, in_specs=in_specs,...  101 us
    unnamed x252, local copies, waits for them, and re-layouts  40.4 us
    dot_general x8, matrix products, contract_rows(): lax.dot_general(left_side, right_side, (((0,), (0,)), ((), ())), preferre...  29.2 us
  transfers between devices with their start and end apart: 110, of which 41 were waited for; matrix products, arithmetic and copies ran while one was open for 19% of the time, Pallas kernels for 12%

profile of v3, /device:TPU:10, one launch (start us, length us, event | category | flops | bytes accessed | tf_op | source)
XLA Modules:
  0.0 637.3 jit_solution(8923456554206299395)
XLA Ops:
  16.3 5.3 collective-permute-start.3
  40.8 7.7 %collective-permute-start.8 = (bf16[256,512]{1,0:T(8,128)(2,1)S(1)}, bf16[256,512]{1,0:T(8,128)(2,1)S(1)}, u32[]{:S(2)}, u32[]{:S(2)}) collective-permute-start(bf16[256,512]{1,0:T(8,128)(2,1)S(1)} %copy-done.101), channel_id=1, source_target_pairs={{0,7},{1,6},{2,5},{3,4},{4,3},{5,2},{6,1},{7,0},{8,15},{9,14},{10,... | collective-permute-start | bytes 786440 | tf_op jit(solution)/shard_map/ppermute | solution.py:90
  48.5 12.0 %collective-permute-start.2 = (bf16[144,2048]{1,0:T(8,128)(2,1)}, bf16[144,2048]{1,0:T(8,128)(2,1)S(1)}, u32[]{:S(2)}, u32[]{:S(2)}) collective-permute-start(bf16[144,2048]{1,0:T(8,128)(2,1)} %collective-permute-done.refs_1_), channel_id=1, source_target_pairs={{0,1},{1,3},{2,0},{3,5},{4,2},{5,7},{6,4},{7,6},{8,9},{9,11},{10,8... | collective-permute-start | bytes 1769480 | tf_op jit(solution)/shard_map/ppermute | solution.py:90
  63.2 4.0 collective-permute-start.9
  67.2 7.5 %collective-permute-start.14 = (bf16[144,2048]{1,0:T(8,128)(2,1)}, bf16[144,2048]{1,0:T(8,128)(2,1)S(1)}, u32[]{:S(2)}, u32[]{:S(2)}) collective-permute-start(bf16[144,2048]{1,0:T(8,128)(2,1)} %collective-permute-done.1.refs_2_), channel_id=1, source_target_pairs={{0,2},{1,0},{2,4},{3,1},{4,6},{5,3},{6,7},{7,5},{8,10},{9,8},{10,1... | collective-permute-start | bytes 1769480 | tf_op jit(solution)/shard_map/ppermute | solution.py:90
  77.5 4.6 collective-permute-done.8
  82.1 13.1 %collective-permute-done.2.refs_3_ = bf16[144,2048]{1,0:T(8,128)(2,1)S(1)} collective-permute-done((bf16[144,2048]{1,0:T(8,128)(2,1)}, bf16[144,2048]{1,0:T(8,128)(2,1)S(1)}, u32[]{:S(2)}, u32[]{:S(2)}) %collective-permute-start.2) | collective-permute-done | bytes 589856 | tf_op jit(solution)/shard_map/ppermute | solution.py:90
  95.2 8.4 %collective-permute-done.9 = bf16[256,512]{1,0:T(8,128)(2,1)S(1)} collective-permute-done((bf16[256,512]{1,0:T(8,128)(2,1)S(1)}, bf16[256,512]{1,0:T(8,128)(2,1)S(1)}, u32[]{:S(2)}, u32[]{:S(2)}) %collective-permute-start.9) | collective-permute-done | bytes 262176 | tf_op jit(solution)/shard_map/ppermute | solution.py:90
  106.5 11.6 %collective-permute-start.16 = (bf16[144,2048]{1,0:T(8,128)(2,1)S(1)}, bf16[144,2048]{1,0:T(8,128)(2,1)S(1)}, u32[]{:S(2)}, u32[]{:S(2)}) collective-permute-start(bf16[144,2048]{1,0:T(8,128)(2,1)S(1)} %collective-permute-done.14.refs_0_.refs_4_), channel_id=1, source_target_pairs={{0,2},{1,0},{2,4},{3,1},{4,6},{5,3},{6,7},{7,5},{8,10},{9,8},{10,1... | collective-permute-start | bytes 1769480 | tf_op jit(solution)/shard_map/ppermute | solution.py:90
  118.1 6.4 %collective-permute-done.10 = bf16[256,512]{1,0:T(8,128)(2,1)S(1)} collective-permute-done((bf16[256,512]{1,0:T(8,128)(2,1)S(1)}, bf16[256,512]{1,0:T(8,128)(2,1)S(1)}, u32[]{:S(2)}, u32[]{:S(2)}) %collective-permute-start.10) | collective-permute-done | bytes 262176 | tf_op jit(solution)/shard_map/ppermute | solution.py:90
  124.5 6.8 %collective-permute-done.15.refs_1_.refs_5_ = bf16[144,2048]{1,0:T(8,128)(2,1)S(1)} collective-permute-done((bf16[144,2048]{1,0:T(8,128)(2,1)S(1)}, bf16[144,2048]{1,0:T(8,128)(2,1)S(1)}, u32[]{:S(2)}, u32[]{:S(2)}) %collective-permute-start.15) | collective-permute-done | bytes 589856 | tf_op jit(solution)/shard_map/ppermute | solution.py:90
  131.5 8.7 %collective-permute-start.13 = (bf16[256,512]{1,0:T(8,128)(2,1)}, bf16[256,512]{1,0:T(8,128)(2,1)}, u32[]{:S(2)}, u32[]{:S(2)}) collective-permute-start(bf16[256,512]{1,0:T(8,128)(2,1)} %get-tuple-element.151), channel_id=1, source_target_pairs={{0,2},{1,3},{2,0},{3,1},{4,6},{5,7},{6,4},{7,5},{8,10},{9,11},{10,... | collective-permute-start | bytes 786440 | tf_op jit(solution)/shard_map/ppermute | solution.py:90
  141.9 8.7 %collective-permute-done.17.refs_3_.refs_7_ = bf16[144,2048]{1,0:T(8,128)(2,1)S(1)} collective-permute-done((bf16[144,2048]{1,0:T(8,128)(2,1)S(1)}, bf16[144,2048]{1,0:T(8,128)(2,1)S(1)}, u32[]{:S(2)}, u32[]{:S(2)}) %collective-permute-start.17) | collective-permute-done | bytes 589856 | tf_op jit(solution)/shard_map/ppermute | solution.py:90
  155.9 4.0 collective-permute-start.19
  161.9 3.6 collective-permute-done.19
  171.7 12.2 %shard_map.221 = (bf16[64,2048]{1,0:T(8,128)(2,1)S(1)}, bf16[64,2048]{1,0:T(8,128)(2,1)S(1)}, bf16[64,2048]{1,0:T(8,128)(2,1)S(1)}, bf16[64,2048]{1,0:T(8,128)(2...) custom-call(bf16[144,2048]{1,0:T(8,128)(2,1)S(1)} %copy-done.60, ...), custom_call_target="tpu_custom_call" | custom-call | flops 6442450944 | bytes 4194304 | tf_op jit(solution)/shard_map/pallas_call | solution.py:474
  189.0 12.5 %shard_map.220 = (bf16[64,2048]{1,0:T(8,128)(2,1)S(1)}, bf16[64,2048]{1,0:T(8,128)(2,1)S(1)}, bf16[64,2048]{1,0:T(8,128)(2,1)S(1)}, bf16[64,2048]{1,0:T(8,128)(2...) custom-call(bf16[144,2048]{1,0:T(8,128)(2,1)S(1)} %copy-done.30, ...), custom_call_target="tpu_custom_call" | custom-call | flops 6442450944 | bytes 4194304 | tf_op jit(solution)/shard_map/pallas_call | solution.py:474
  206.1 4.8 collective-permute-done.30
  218.8 5.4 collective-permute-done.34
  229.8 3.7 collective-permute-done.35
  237.2 8.6 %collective-permute-done.36 = bf16[64,2048]{1,0:T(8,128)(2,1)} collective-permute-done((bf16[64,2048]{1,0:T(8,128)(2,1)S(1)}, bf16[64,2048]{1,0:T(8,128)(2,1)}, u32[]{:S(2)}, u32[]{:S(2)}) %collective-permute-start.36) | collective-permute-done | bytes 262176 | tf_op jit(solution)/shard_map/ppermute | solution.py:673
  258.9 8.2 %shard_map.222 = (bf16[1024,256]{1,0:T(8,128)(2,1)S(1)}, bf16[1024,1024]{1,0:T(8,128)(2,1)S(1)}) custom-call(bf16[144,2048]{1,0:T(8,128)(2,1)S(1)} %copy-done.31, bf16[144,2048]{1,0:T(8,128)(2,1)} %collective-permute-done.refs_1_, bf16[144,2048]{1,0:T(8,128)(2,1)} %collective-permute-done.1.refs_2_, bf16[144,2048]{1,0:T(8,128)(2,1)S(1)} %copy-done.58, ...), custom_call_target="tpu_custom_call" | custom-call | flops 5368709120 | bytes 8388608 | tf_op jit(solution)/shard_map/pallas_call | solution.py:474
  271.2 7.2 %shard_map.223 = (bf16[1024,2048]{1,0:T(8,128)(2,1)S(1)}, bf16[1024,2048]{1,0:T(8,128)(2,1)S(1)}, bf16[1024,768]{1,0:T(8,128)(2,1)S(1)}, f32[1024,128]{1,0:T(8,1...) custom-call(bf16[64,2048]{1,0:T(8,128)(2,1)S(1)} %get-tuple-element., ...), custom_call_target="tpu_custom_call" | custom-call | flops 6442450944 | bytes 2097152 | tf_op jit(solution)/shard_map/pallas_call | solution.py:474
  282.7 7.2 %shard_map.224 = (bf16[1024,2048]{1,0:T(8,128)(2,1)S(1)}, bf16[1024,2048]{1,0:T(8,128)(2,1)S(1)}, bf16[1024,768]{1,0:T(8,128)(2,1)S(1)}, f32[1024,128]{1,0:T(8,1...) custom-call(bf16[64,2048]{1,0:T(8,128)(2,1)S(1)} %collective-permute, ...), custom_call_target="tpu_custom_call", output_to_operand_aliasing={{0}: (15, {}), {1}: (16, {}), {2}: (17, {}), {3}: (18, {}),... | custom-call | flops 6442450944 | bytes 2097152 | tf_op jit(solution)/shard_map/pallas_call | solution.py:474
  292.6 7.2 %shard_map.225 = (bf16[1024,2048]{1,0:T(8,128)(2,1)S(1)}, bf16[1024,2048]{1,0:T(8,128)(2,1)S(1)}, bf16[1024,768]{1,0:T(8,128)(2,1)S(1)}, f32[1024,128]{1,0:T(8,1...) custom-call(bf16[64,2048]{1,0:T(8,128)(2,1)S(1)} %collective-permute, ...), custom_call_target="tpu_custom_call", output_to_operand_aliasing={{0}: (15, {}), {1}: (16, {}), {2}: (17, {}), {3}: (18, {}),... | custom-call | flops 6442450944 | bytes 2097152 | tf_op jit(solution)/shard_map/pallas_call | solution.py:474
  301.6 7.2 %shard_map.226 = (bf16[1024,2048]{1,0:T(8,128)(2,1)S(1)}, bf16[1024,2048]{1,0:T(8,128)(2,1)S(1)}, bf16[1024,768]{1,0:T(8,128)(2,1)S(1)}, f32[1024,128]{1,0:T(8,1...) custom-call(bf16[64,2048]{1,0:T(8,128)(2,1)S(1)} %collective-permute, ...), custom_call_target="tpu_custom_call", output_to_operand_aliasing={{0}: (15, {}), {1}: (16, {}), {2}: (17, {}), {3}: (18, {}),... | custom-call | flops 6442450944 | bytes 2097152 | tf_op jit(solution)/shard_map/pallas_call | solution.py:474
  319.6 5.1 collective-permute-done.52
  342.9 4.6 collective-permute-done.65
  349.0 4.9 collective-permute-done.66
  386.6 9.9 %shard_map.227 = (bf16[1024,2048]{1,0:T(8,128)(2,1)S(1)}, bf16[1024,768]{1,0:T(8,128)(2,1)S(1)}, bf16[1024,1024]{1,0:T(8,128)(2,1)S(1)}, f32[32,2048]{1,0:T(8,12...) custom-call(bf16[64,2048]{1,0:T(8,128)(2,1)} %get-tuple-element.330., ...), custom_call_target="tpu_custom_call" | custom-call | flops 3221225472 | bytes 2097152 | tf_op jit(solution)/shard_map/pallas_call | solution.py:474
  403.4 9.8 %shard_map.228 = (bf16[1024,2048]{1,0:T(8,128)(2,1)S(1)}, bf16[1024,768]{1,0:T(8,128)(2,1)S(1)}, bf16[1024,1024]{1,0:T(8,128)(2,1)S(1)}, f32[32,2048]{1,0:T(8,12...) custom-call(bf16[64,2048]{1,0:T(8,128)(2,1)} %collective-permute-don, ...), custom_call_target="tpu_custom_call", output_to_operand_aliasing={{0}: (19, {}), {1}: (20, {}), {2}: (21, {})} | custom-call | flops 3221225472 | bytes 2097152 | tf_op jit(solution)/shard_map/pallas_call | solution.py:474
  417.5 9.6 %shard_map.229 = (bf16[1024,2048]{1,0:T(8,128)(2,1)S(1)}, bf16[1024,768]{1,0:T(8,128)(2,1)S(1)}, bf16[1024,1024]{1,0:T(8,128)(2,1)S(1)}, f32[32,2048]{1,0:T(8,12...) custom-call(bf16[64,2048]{1,0:T(8,128)(2,1)S(1)} %collective-permute, ...), custom_call_target="tpu_custom_call", output_to_operand_aliasing={{0}: (19, {}), {1}: (20, {}), {2}: (21, {})} | custom-call | flops 3221225472 | bytes 2097152 | tf_op jit(solution)/shard_map/pallas_call | solution.py:474
  428.5 10.0 %shard_map.230 = (bf16[1024,2048]{1,0:T(8,128)(2,1)S(1)}, bf16[1024,768]{1,0:T(8,128)(2,1)S(1)}, bf16[1024,1024]{1,0:T(8,128)(2,1)S(1)}, f32[32,2048]{1,0:T(8,12...) custom-call(bf16[64,2048]{1,0:T(8,128)(2,1)S(1)} %collective-permute, ...), custom_call_target="tpu_custom_call", output_to_operand_aliasing={{0}: (19, {}), {1}: (20, {}), {2}: (21, {})} | custom-call | flops 3221225472 | bytes 2097152 | tf_op jit(solution)/shard_map/pallas_call | solution.py:474
  438.6 3.9 convolution_convert_fusion
  443.9 3.7 convolution_convert_fusion.1
  461.0 7.8 %collective-permute-done.82 = bf16[128,2048]{1,0:T(8,128)(2,1)} collective-permute-done((bf16[128,2048]{1,0:T(8,128)(2,1)}, bf16[128,2048]{1,0:T(8,128)(2,1)}, u32[]{:S(2)}, u32[]{:S(2)}) %collective-permute-start.82) | collective-permute-done | bytes 524320 | tf_op jit(solution)/shard_map/ppermute | solution.py:90
  471.8 3.3 add_convert_fusion.1
  483.2 5.5 add_convert_fusion
  500.2 3.7 collective-permute-done.85
  505.9 14.0 %collective-permute-start.86 = (bf16[128,2048]{1,0:T(8,128)(2,1)}, bf16[128,2048]{1,0:T(8,128)(2,1)}, u32[]{:S(2)}, u32[]{:S(2)}) collective-permute-start(bf16[128,2048]{1,0:T(8,128)(2,1)} %add_convert_fusion.5), channel_id=1, source_target_pairs={{0,2},{1,0},{2,4},{3,1},{4,6},{5,3},{6,7},{7,5},{8,10},{9,8},{10,1... | collective-permute-start | bytes 1572872 | tf_op jit(solution)/shard_map/ppermute | solution.py:90
  525.7 6.1 convert_add_fusion
  537.6 3.6 collective-permute-start.102
  547.3 5.2 broadcast_in_dim_reshape.6
  553.2 20.4 %collective-permute-start.104 = (bf16[256,512]{1,0:T(8,128)(2,1)S(1)}, bf16[256,512]{1,0:T(8,128)(2,1)S(1)}, u32[]{:S(2)}, u32[]{:S(2)}) collective-permute-start(bf16[256,512]{1,0:T(8,128)(2,1)S(1)} %copy-done.103), channel_id=1, source_target_pairs={{0,5},{1,4},{2,7},{3,6},{4,1},{5,0},{6,3},{7,2},{8,13},{9,12},{10,... | collective-permute-start | bytes 786440 | tf_op jit(solution)/shard_map/ppermute | solution.py:90
  581.2 11.8 %collective-permute-done.103 = bf16[256,512]{1,0:T(8,128)(2,1)S(1)} collective-permute-done((bf16[256,512]{1,0:T(8,128)(2,1)}, bf16[256,512]{1,0:T(8,128)(2,1)S(1)}, u32[]{:S(2)}, u32[]{:S(2)}) %collective-permute-start.103) | collective-permute-done | bytes 262176 | tf_op jit(solution)/shard_map/ppermute | solution.py:90
  593.9 3.6 collective-permute-start.94
  601.8 10.9 %collective-permute-done.95 = f32[24576]{0:T(1024)S(1)} collective-permute-done((f32[24576]{0:T(1024)S(1)}, f32[24576]{0:T(1024)S(1)}, u32[]{:S(2)}, u32[]{:S(2)}) %collective-permute-start.95) | collective-permute-done | bytes 98336 | tf_op jit(solution)/shard_map/ppermute | solution.py:90
  618.4 3.8 collective-permute-start.107
  (638 shorter events, 276.5 us)
Async XLA Ops:
  6.6 41.9 %collective-permute-start = (bf16[144,2048]{1,0:T(8,128)(2,1)S(1)}, bf16[144,2048]{1,0:T(8,128)(2,1)}, u32[]{:S(2)}, u32[]{:S(2)}) collective-permute-start(bf16[144,2048]{1,0:T(8,128)(2,1)S(1)} %fusion.19.refs_0_), channel_id=1, source_target_pairs={{0,1},{1,3},{2,0},{3,5},{4,2},{5,7},{6,4},{7,6},{8,9},{9,11},{10,8... | collective-permute-start | bytes 1769480 | tf_op jit(solution)/shard_map/ppermute | solution.py:90
  7.1 60.1 %collective-permute-start.1 = (bf16[144,2048]{1,0:T(8,128)(2,1)S(1)}, bf16[144,2048]{1,0:T(8,128)(2,1)}, u32[]{:S(2)}, u32[]{:S(2)}) collective-permute-start(bf16[144,2048]{1,0:T(8,128)(2,1)S(1)} %fusion.19.refs_0_), channel_id=1, source_target_pairs={{0,2},{1,0},{2,4},{3,1},{4,6},{5,3},{6,7},{7,5},{8,10},{9,8},{10,1... | collective-permute-start | bytes 1769480 | tf_op jit(solution)/shard_map/ppermute | solution.py:90
  16.3 19.0 %collective-permute-start.3 = (bf16[256,1024]{1,0:T(8,128)(2,1)}, bf16[256,1024]{1,0:T(8,128)(2,1)}, u32[]{:S(2)}, u32[]{:S(2)}) collective-permute-start(bf16[256,1024]{1,0:T(8,128)(2,1)} %pad_maximum_fusion.2), channel_id=1, source_target_pairs={{0,0},{1,1},{2,2},{3,3},{4,8},{5,9},{6,10},{7,11},{8,4},{9,5},{10,... | collective-permute-start | bytes 1572872 | tf_op jit(solution)/shard_map/ppermute | solution.py:215
  33.3 28.1 %collective-permute-start.5 = (bf16[256,1024]{1,0:T(8,128)(2,1)}, bf16[256,1024]{1,0:T(8,128)(2,1)}, u32[]{:S(2)}, u32[]{:S(2)}) collective-permute-start(bf16[256,1024]{1,0:T(8,128)(2,1)} %get-tuple-element.143), channel_id=1, source_target_pairs={{0,2},{1,3},{2,0},{3,1},{4,10},{5,11},{6,8},{7,9},{8,6},{9,7},{10,... | collective-permute-start | bytes 1572872 | tf_op jit(solution)/shard_map/ppermute | solution.py:215
  40.8 41.3 %collective-permute-start.8 = (bf16[256,512]{1,0:T(8,128)(2,1)S(1)}, bf16[256,512]{1,0:T(8,128)(2,1)S(1)}, u32[]{:S(2)}, u32[]{:S(2)}) collective-permute-start(bf16[256,512]{1,0:T(8,128)(2,1)S(1)} %copy-done.101), channel_id=1, source_target_pairs={{0,7},{1,6},{2,5},{3,4},{4,3},{5,2},{6,1},{7,0},{8,15},{9,14},{10,... | collective-permute-start | bytes 786440 | tf_op jit(solution)/shard_map/ppermute | solution.py:90
  48.5 46.7 %collective-permute-start.2 = (bf16[144,2048]{1,0:T(8,128)(2,1)}, bf16[144,2048]{1,0:T(8,128)(2,1)S(1)}, u32[]{:S(2)}, u32[]{:S(2)}) collective-permute-start(bf16[144,2048]{1,0:T(8,128)(2,1)} %collective-permute-done.refs_1_), channel_id=1, source_target_pairs={{0,1},{1,3},{2,0},{3,5},{4,2},{5,7},{6,4},{7,6},{8,9},{9,11},{10,8... | collective-permute-start | bytes 1769480 | tf_op jit(solution)/shard_map/ppermute | solution.py:90
  63.2 40.4 %collective-permute-start.9 = (bf16[256,512]{1,0:T(8,128)(2,1)S(1)}, bf16[256,512]{1,0:T(8,128)(2,1)S(1)}, u32[]{:S(2)}, u32[]{:S(2)}) collective-permute-start(bf16[256,512]{1,0:T(8,128)(2,1)S(1)} %copy-done.100), channel_id=1, source_target_pairs={{0,6},{1,7},{2,4},{3,5},{4,2},{5,3},{6,0},{7,1},{8,14},{9,15},{10,... | collective-permute-start | bytes 786440 | tf_op jit(solution)/shard_map/ppermute | solution.py:90
  67.2 36.6 %collective-permute-start.6 = (bf16[256,1024]{1,0:T(8,128)(2,1)S(1)}, bf16[256,1024]{1,0:T(8,128)(2,1)S(1)}, u32[]{:S(2)}, u32[]{:S(2)}) collective-permute-start(bf16[256,1024]{1,0:T(8,128)(2,1)S(1)} %copy-done.96), channel_id=1, source_target_pairs={{0,3},{1,0},{2,1},{3,2},{4,11},{5,8},{6,9},{7,10},{8,7},{9,4},{10,... | collective-permute-start | bytes 1572872 | tf_op jit(solution)/shard_map/ppermute | solution.py:215
  67.2 39.3 %collective-permute-start.14 = (bf16[144,2048]{1,0:T(8,128)(2,1)}, bf16[144,2048]{1,0:T(8,128)(2,1)S(1)}, u32[]{:S(2)}, u32[]{:S(2)}) collective-permute-start(bf16[144,2048]{1,0:T(8,128)(2,1)} %collective-permute-done.1.refs_2_), channel_id=1, source_target_pairs={{0,2},{1,0},{2,4},{3,1},{4,6},{5,3},{6,7},{7,5},{8,10},{9,8},{10,1... | collective-permute-start | bytes 1769480 | tf_op jit(solution)/shard_map/ppermute | solution.py:90
  95.2 36.1 %collective-permute-start.15 = (bf16[144,2048]{1,0:T(8,128)(2,1)S(1)}, bf16[144,2048]{1,0:T(8,128)(2,1)S(1)}, u32[]{:S(2)}, u32[]{:S(2)}) collective-permute-start(bf16[144,2048]{1,0:T(8,128)(2,1)S(1)} %collective-permute-done.2.refs_3_), channel_id=1, source_target_pairs={{0,1},{1,3},{2,0},{3,5},{4,2},{5,7},{6,4},{7,6},{8,9},{9,11},{10,8... | collective-permute-start | bytes 1769480 | tf_op jit(solution)/shard_map/ppermute | solution.py:90
  103.6 27.8 %collective-permute-start.11 = (bf16[256,512]{1,0:T(8,128)(2,1)S(1)}, bf16[256,512]{1,0:T(8,128)(2,1)S(1)}, u32[]{:S(2)}, u32[]{:S(2)}) collective-permute-start(bf16[256,512]{1,0:T(8,128)(2,1)S(1)} %get-tuple-element.149), channel_id=1, source_target_pairs={{0,4},{1,5},{2,6},{3,7},{4,0},{5,1},{6,2},{7,3},{8,12},{9,13},{10,... | collective-permute-start | bytes 786440 | tf_op jit(solution)/shard_map/ppermute | solution.py:90
  103.7 56.2 %collective-permute-start.12 = (bf16[256,512]{1,0:T(8,128)(2,1)}, bf16[256,512]{1,0:T(8,128)(2,1)}, u32[]{:S(2)}, u32[]{:S(2)}) collective-permute-start(bf16[256,512]{1,0:T(8,128)(2,1)} %get-tuple-element.150), channel_id=1, source_target_pairs={{0,3},{1,2},{2,1},{3,0},{4,7},{5,6},{6,5},{7,4},{8,11},{9,10},{10,... | collective-permute-start | bytes 786440 | tf_op jit(solution)/shard_map/ppermute | solution.py:90
  104.7 19.9 %collective-permute-start.10 = (bf16[256,512]{1,0:T(8,128)(2,1)S(1)}, bf16[256,512]{1,0:T(8,128)(2,1)S(1)}, u32[]{:S(2)}, u32[]{:S(2)}) collective-permute-start(bf16[256,512]{1,0:T(8,128)(2,1)S(1)} %copy-done.99), channel_id=1, source_target_pairs={{0,5},{1,4},{2,7},{3,6},{4,1},{5,0},{6,3},{7,2},{8,13},{9,12},{10,... | collective-permute-start | bytes 786440 | tf_op jit(solution)/shard_map/ppermute | solution.py:90
  106.5 33.7 %collective-permute-start.16 = (bf16[144,2048]{1,0:T(8,128)(2,1)S(1)}, bf16[144,2048]{1,0:T(8,128)(2,1)S(1)}, u32[]{:S(2)}, u32[]{:S(2)}) collective-permute-start(bf16[144,2048]{1,0:T(8,128)(2,1)S(1)} %collective-permute-done.14.refs_0_.refs_4_), channel_id=1, source_target_pairs={{0,2},{1,0},{2,4},{3,1},{4,6},{5,3},{6,7},{7,5},{8,10},{9,8},{10,1... | collective-permute-start | bytes 1769480 | tf_op jit(solution)/shard_map/ppermute | solution.py:90
  124.5 42.1 %collective-permute-start.7 = (bf16[1024,1024]{1,0:T(8,128)(2,1)}, bf16[1024,1024]{1,0:T(8,128)(2,1)}, u32[]{:S(2)}, u32[]{:S(2)}) collective-permute-start(bf16[1024,1024]{1,0:T(8,128)(2,1)} %constant_dynamic-update-slice_fusion.12), channel_id=1, source_target_pairs={{0,8},{8,0},{1,9},{9,1},{2,10},{10,2},{3,11},{11,3},{4,12},{12,4},... | collective-permute-start | bytes 6291464 | tf_op jit(solution)/shard_map/ppermute | solution.py:115
  131.3 19.4 %collective-permute-start.17 = (bf16[144,2048]{1,0:T(8,128)(2,1)S(1)}, bf16[144,2048]{1,0:T(8,128)(2,1)S(1)}, u32[]{:S(2)}, u32[]{:S(2)}) collective-permute-start(bf16[144,2048]{1,0:T(8,128)(2,1)S(1)} %collective-permute-done.15.refs_1_.refs_5_), channel_id=1, source_target_pairs={{0,1},{1,3},{2,0},{3,5},{4,2},{5,7},{6,4},{7,6},{8,9},{9,11},{10,8... | collective-permute-start | bytes 1769480 | tf_op jit(solution)/shard_map/ppermute | solution.py:90
  131.5 29.4 %collective-permute-start.13 = (bf16[256,512]{1,0:T(8,128)(2,1)}, bf16[256,512]{1,0:T(8,128)(2,1)}, u32[]{:S(2)}, u32[]{:S(2)}) collective-permute-start(bf16[256,512]{1,0:T(8,128)(2,1)} %get-tuple-element.151), channel_id=1, source_target_pairs={{0,2},{1,3},{2,0},{3,1},{4,6},{5,7},{6,4},{7,5},{8,10},{9,11},{10,... | collective-permute-start | bytes 786440 | tf_op jit(solution)/shard_map/ppermute | solution.py:90
  184.0 17.5 %collective-permute-start.29 = (bf16[64,2048]{1,0:T(8,128)(2,1)S(1)}, bf16[64,2048]{1,0:T(8,128)(2,1)S(1)}, u32[]{:S(2)}, u32[]{:S(2)}) collective-permute-start(bf16[64,2048]{1,0:T(8,128)(2,1)S(1)} %get-tuple-element.163), channel_id=1, source_target_pairs={{0,2},{1,0},{2,4},{3,1},{4,6},{5,3},{6,7},{7,5},{8,10},{9,8},{10,1... | collective-permute-start | bytes 786440 | tf_op jit(solution)/shard_map/ppermute | solution.py:90
  186.7 16.9 %collective-permute-start.32 = (bf16[64,2048]{1,0:T(8,128)(2,1)S(1)}, bf16[64,2048]{1,0:T(8,128)(2,1)S(1)}, u32[]{:S(2)}, u32[]{:S(2)}) collective-permute-start(bf16[64,2048]{1,0:T(8,128)(2,1)S(1)} %get-tuple-element.166), channel_id=1, source_target_pairs={{0,1},{1,3},{2,0},{3,5},{4,2},{5,7},{6,4},{7,6},{8,9},{9,11},{10,8... | collective-permute-start | bytes 786440 | tf_op jit(solution)/shard_map/ppermute | solution.py:90
  186.7 17.0 %collective-permute-start.22 = (bf16[64,2048]{1,0:T(8,128)(2,1)S(1)}, bf16[64,2048]{1,0:T(8,128)(2,1)S(1)}, u32[]{:S(2)}, u32[]{:S(2)}) collective-permute-start(bf16[64,2048]{1,0:T(8,128)(2,1)S(1)} %get-tuple-element.155), channel_id=1, source_target_pairs={{0,2},{1,0},{2,4},{3,1},{4,6},{5,3},{6,7},{7,5},{8,10},{9,8},{10,1... | collective-permute-start | bytes 786440 | tf_op jit(solution)/shard_map/ppermute | solution.py:90
  188.8 17.1 %collective-permute-start.26 = (bf16[64,2048]{1,0:T(8,128)(2,1)S(1)}, bf16[64,2048]{1,0:T(8,128)(2,1)S(1)}, u32[]{:S(2)}, u32[]{:S(2)}) collective-permute-start(bf16[64,2048]{1,0:T(8,128)(2,1)S(1)} %get-tuple-element.159), channel_id=1, source_target_pairs={{0,1},{1,3},{2,0},{3,5},{4,2},{5,7},{6,4},{7,6},{8,9},{9,11},{10,8... | collective-permute-start | bytes 786440 | tf_op jit(solution)/shard_map/ppermute | solution.py:90
  211.0 17.2 %collective-permute-start.31 = (bf16[64,2048]{1,0:T(8,128)(2,1)S(1)}, bf16[64,2048]{1,0:T(8,128)(2,1)S(1)}, u32[]{:S(2)}, u32[]{:S(2)}) collective-permute-start(bf16[64,2048]{1,0:T(8,128)(2,1)S(1)} %add_convert_fusion.21), channel_id=1, source_target_pairs={{0,2},{1,0},{2,4},{3,1},{4,6},{5,3},{6,7},{7,5},{8,10},{9,8},{10,1... | collective-permute-start | bytes 786440 | tf_op jit(solution)/shard_map/ppermute | solution.py:90
  251.4 17.4 %collective-permute-start.40 = (bf16[64,2048]{1,0:T(8,128)(2,1)S(1)}, bf16[64,2048]{1,0:T(8,128)(2,1)S(1)}, u32[]{:S(2)}, u32[]{:S(2)}) collective-permute-start(bf16[64,2048]{1,0:T(8,128)(2,1)S(1)} %get-tuple-element.289.refs_0_), channel_id=1, source_target_pairs={{0,2},{1,0},{2,4},{3,1},{4,6},{5,3},{6,7},{7,5},{8,10},{9,8},{10,1... | collective-permute-start | bytes 786440 | tf_op jit(solution)/shard_map/ppermute | solution.py:90
  280.1 21.5 %collective-permute-start.42 = (bf16[64,2048]{1,0:T(8,128)(2,1)S(1)}, bf16[64,2048]{1,0:T(8,128)(2,1)S(1)}, u32[]{:S(2)}, u32[]{:S(2)}) collective-permute-start(bf16[64,2048]{1,0:T(8,128)(2,1)S(1)} %collective-permute-done.41.refs_0_), channel_id=1, source_target_pairs={{0,2},{1,0},{2,4},{3,1},{4,6},{5,3},{6,7},{7,5},{8,10},{9,8},{10,1... | collective-permute-start | bytes 786440 | tf_op jit(solution)/shard_map/ppermute | solution.py:90
  299.8 17.7 %collective-permute-start.60 = (bf16[64,2048]{1,0:T(8,128)(2,1)S(1)}, bf16[64,2048]{1,0:T(8,128)(2,1)S(1)}, u32[]{:S(2)}, u32[]{:S(2)}) collective-permute-start(bf16[64,2048]{1,0:T(8,128)(2,1)S(1)} %get-tuple-element.202), channel_id=1, source_target_pairs={{0,2},{1,0},{2,4},{3,1},{4,6},{5,3},{6,7},{7,5},{8,10},{9,8},{10,1... | collective-permute-start | bytes 786440 | tf_op jit(solution)/shard_map/ppermute | solution.py:90
  330.1 18.9 %collective-permute-start.62 = (bf16[64,2048]{1,0:T(8,128)(2,1)S(1)}, bf16[64,2048]{1,0:T(8,128)(2,1)S(1)}, u32[]{:S(2)}, u32[]{:S(2)}) collective-permute-start(bf16[64,2048]{1,0:T(8,128)(2,1)S(1)} %add_convert_fusion.10), channel_id=1, source_target_pairs={{0,2},{1,0},{2,4},{3,1},{4,6},{5,3},{6,7},{7,5},{8,10},{9,8},{10,1... | collective-permute-start | bytes 786440 | tf_op jit(solution)/shard_map/ppermute | solution.py:90
  371.3 28.1 %collective-permute-start.76 = (bf16[64,2048]{1,0:T(8,128)(2,1)}, bf16[64,2048]{1,0:T(8,128)(2,1)S(1)}, u32[]{:S(2)}, u32[]{:S(2)}) collective-permute-start(bf16[64,2048]{1,0:T(8,128)(2,1)} %collective-permute-done.68.refs_2_), channel_id=1, source_target_pairs={{0,1},{1,3},{2,0},{3,5},{4,2},{5,7},{6,4},{7,6},{8,9},{9,11},{10,8... | collective-permute-start | bytes 786440 | tf_op jit(solution)/shard_map/ppermute | solution.py:90
  374.1 27.0 %collective-permute-start.80 = (bf16[64,2048]{1,0:T(8,128)(2,1)}, bf16[64,2048]{1,0:T(8,128)(2,1)S(1)}, u32[]{:S(2)}, u32[]{:S(2)}) collective-permute-start(bf16[64,2048]{1,0:T(8,128)(2,1)} %collective-permute-done.69.refs_3_), channel_id=1, source_target_pairs={{0,1},{1,3},{2,0},{3,5},{4,2},{5,7},{6,4},{7,6},{8,9},{9,11},{10,8... | collective-permute-start | bytes 786440 | tf_op jit(solution)/shard_map/ppermute | solution.py:90
  375.3 27.9 %collective-permute-start.71 = (bf16[64,2048]{1,0:T(8,128)(2,1)}, bf16[64,2048]{1,0:T(8,128)(2,1)S(1)}, u32[]{:S(2)}, u32[]{:S(2)}) collective-permute-start(bf16[64,2048]{1,0:T(8,128)(2,1)} %collective-permute-done.70.refs_0_), channel_id=1, source_target_pairs={{0,2},{1,0},{2,4},{3,1},{4,6},{5,3},{6,7},{7,5},{8,10},{9,8},{10,1... | collective-permute-start | bytes 786440 | tf_op jit(solution)/shard_map/ppermute | solution.py:90
  377.1 24.6 %collective-permute-start.74 = (bf16[64,2048]{1,0:T(8,128)(2,1)}, bf16[64,2048]{1,0:T(8,128)(2,1)S(1)}, u32[]{:S(2)}, u32[]{:S(2)}) collective-permute-start(bf16[64,2048]{1,0:T(8,128)(2,1)} %collective-permute-done.73.refs_1_), channel_id=1, source_target_pairs={{0,2},{1,0},{2,4},{3,1},{4,6},{5,3},{6,7},{7,5},{8,10},{9,8},{10,1... | collective-permute-start | bytes 786440 | tf_op jit(solution)/shard_map/ppermute | solution.py:90
  401.1 16.4 %collective-permute-start.81 = (bf16[64,2048]{1,0:T(8,128)(2,1)S(1)}, bf16[64,2048]{1,0:T(8,128)(2,1)S(1)}, u32[]{:S(2)}, u32[]{:S(2)}) collective-permute-start(bf16[64,2048]{1,0:T(8,128)(2,1)S(1)} %collective-permute-done.80.refs_3_), channel_id=1, source_target_pairs={{0,1},{1,3},{2,0},{3,5},{4,2},{5,7},{6,4},{7,6},{8,9},{9,11},{10,8... | collective-permute-start | bytes 786440 | tf_op jit(solution)/shard_map/ppermute | solution.py:90
  403.1 25.4 %collective-permute-start.72 = (bf16[64,2048]{1,0:T(8,128)(2,1)S(1)}, bf16[64,2048]{1,0:T(8,128)(2,1)S(1)}, u32[]{:S(2)}, u32[]{:S(2)}) collective-permute-start(bf16[64,2048]{1,0:T(8,128)(2,1)S(1)} %collective-permute-done.71.refs_0_), channel_id=1, source_target_pairs={{0,2},{1,0},{2,4},{3,1},{4,6},{5,3},{6,7},{7,5},{8,10},{9,8},{10,1... | collective-permute-start | bytes 786440 | tf_op jit(solution)/shard_map/ppermute | solution.py:90
  452.8 18.9 %collective-permute-start.83 = (bf16[1024,768]{1,0:T(8,128)(2,1)}, bf16[1024,768]{1,0:T(8,128)(2,1)}, u32[]{:S(2)}, u32[]{:S(2)}) collective-permute-start(bf16[1024,768]{1,0:T(8,128)(2,1)} %fusion.6), channel_id=1, source_target_pairs={{0,8},{8,0},{1,9},{9,1},{2,10},{10,2},{3,11},{11,3},{4,12},{12,4},... | collective-permute-start | bytes 4718600 | tf_op jit(solution)/shard_map/ppermute | solution.py:115
  452.8 30.1 %collective-permute-start.98 = (bf16[2048,512]{1,0:T(8,128)(2,1)}, bf16[2048,512]{1,0:T(8,128)(2,1)}, u32[]{:S(2)}, u32[]{:S(2)}) collective-permute-start(bf16[2048,512]{1,0:T(8,128)(2,1)} %convolution_convert_fusion.1), channel_id=1, source_target_pairs={{0,8},{8,0},{1,9},{9,1},{2,10},{10,2},{3,11},{11,3},{4,12},{12,4},... | collective-permute-start | bytes 6291464 | tf_op jit(solution)/shard_map/ppermute | solution.py:115
  453.3 72.4 %collective-permute-start.106 = (bf16[512,2048]{1,0:T(8,128)(2,1)}, bf16[512,2048]{1,0:T(8,128)(2,1)}, u32[]{:S(2)}, u32[]{:S(2)}) collective-permute-start(bf16[512,2048]{1,0:T(8,128)(2,1)} %convolution_convert_fusion), channel_id=1, source_target_pairs={{0,8},{8,0},{1,9},{9,1},{2,10},{10,2},{3,11},{11,3},{4,12},{12,4},... | collective-permute-start | bytes 6291464 | tf_op jit(solution)/shard_map/ppermute | solution.py:115
  478.0 25.9 %collective-permute-start.85 = (bf16[128,2048]{1,0:T(8,128)(2,1)}, bf16[128,2048]{1,0:T(8,128)(2,1)}, u32[]{:S(2)}, u32[]{:S(2)}) collective-permute-start(bf16[128,2048]{1,0:T(8,128)(2,1)} %add_convert_fusion.6), channel_id=1, source_target_pairs={{0,2},{1,0},{2,4},{3,1},{4,6},{5,3},{6,7},{7,5},{8,10},{9,8},{10,1... | collective-permute-start | bytes 1572872 | tf_op jit(solution)/shard_map/ppermute | solution.py:90
  482.9 38.0 %collective-permute-start.89 = (bf16[128,2048]{1,0:T(8,128)(2,1)}, bf16[128,2048]{1,0:T(8,128)(2,1)}, u32[]{:S(2)}, u32[]{:S(2)}) collective-permute-start(bf16[128,2048]{1,0:T(8,128)(2,1)} %add_convert_fusion.3), channel_id=1, source_target_pairs={{0,1},{1,3},{2,0},{3,5},{4,2},{5,7},{6,4},{7,6},{8,9},{9,11},{10,8... | collective-permute-start | bytes 1572872 | tf_op jit(solution)/shard_map/ppermute | solution.py:90
  488.6 43.1 %collective-permute-start.99 = (bf16[256,1024]{1,0:T(8,128)(2,1)}, bf16[256,1024]{1,0:T(8,128)(2,1)}, u32[]{:S(2)}, u32[]{:S(2)}) collective-permute-start(bf16[256,1024]{1,0:T(8,128)(2,1)} %pad_maximum_fusion.10), channel_id=1, source_target_pairs={{1,0},{2,1},{3,2},{0,3},{9,4},{10,5},{11,6},{8,7},{5,8},{6,9},{7,1... | collective-permute-start | bytes 1572872 | tf_op jit(solution)/shard_map/ppermute | solution.py:219
  497.5 46.6 %collective-permute-start.101 = (bf16[256,1024]{1,0:T(8,128)(2,1)}, bf16[256,1024]{1,0:T(8,128)(2,1)}, u32[]{:S(2)}, u32[]{:S(2)}) collective-permute-start(bf16[256,1024]{1,0:T(8,128)(2,1)} %pad_maximum_fusion.12), channel_id=1, source_target_pairs={{3,0},{0,1},{1,2},{2,3},{11,4},{8,5},{9,6},{10,7},{7,8},{4,9},{5,1... | collective-permute-start | bytes 1572872 | tf_op jit(solution)/shard_map/ppermute | solution.py:219
  505.9 35.3 %collective-permute-start.86 = (bf16[128,2048]{1,0:T(8,128)(2,1)}, bf16[128,2048]{1,0:T(8,128)(2,1)}, u32[]{:S(2)}, u32[]{:S(2)}) collective-permute-start(bf16[128,2048]{1,0:T(8,128)(2,1)} %add_convert_fusion.5), channel_id=1, source_target_pairs={{0,2},{1,0},{2,4},{3,1},{4,6},{5,3},{6,7},{7,5},{8,10},{9,8},{10,1... | collective-permute-start | bytes 1572872 | tf_op jit(solution)/shard_map/ppermute | solution.py:90
  523.0 55.1 %collective-permute-start.90 = (bf16[128,2048]{1,0:T(8,128)(2,1)}, bf16[128,2048]{1,0:T(8,128)(2,1)}, u32[]{:S(2)}, u32[]{:S(2)}) collective-permute-start(bf16[128,2048]{1,0:T(8,128)(2,1)} %add_convert_fusion.2), channel_id=1, source_target_pairs={{0,1},{1,3},{2,0},{3,5},{4,2},{5,7},{6,4},{7,6},{8,9},{9,11},{10,8... | collective-permute-start | bytes 1572872 | tf_op jit(solution)/shard_map/ppermute | solution.py:90
  537.6 36.1 %collective-permute-start.102 = (bf16[256,512]{1,0:T(8,128)(2,1)}, bf16[256,512]{1,0:T(8,128)(2,1)}, u32[]{:S(2)}, u32[]{:S(2)}) collective-permute-start(bf16[256,512]{1,0:T(8,128)(2,1)} %get-tuple-element.264), channel_id=1, source_target_pairs={{0,7},{1,6},{2,5},{3,4},{4,3},{5,2},{6,1},{7,0},{8,15},{9,14},{10,... | collective-permute-start | bytes 786440 | tf_op jit(solution)/shard_map/ppermute | solution.py:90
  542.3 35.8 %collective-permute-start.87 = (bf16[128,2048]{1,0:T(8,128)(2,1)S(1)}, bf16[128,2048]{1,0:T(8,128)(2,1)S(1)}, u32[]{:S(2)}, u32[]{:S(2)}) collective-permute-start(bf16[128,2048]{1,0:T(8,128)(2,1)S(1)} %add_convert_fusion.4), channel_id=1, source_target_pairs={{0,2},{1,0},{2,4},{3,1},{4,6},{5,3},{6,7},{7,5},{8,10},{9,8},{10,1... | collective-permute-start | bytes 1572872 | tf_op jit(solution)/shard_map/ppermute | solution.py:90
  553.2 44.3 %collective-permute-start.104 = (bf16[256,512]{1,0:T(8,128)(2,1)S(1)}, bf16[256,512]{1,0:T(8,128)(2,1)S(1)}, u32[]{:S(2)}, u32[]{:S(2)}) collective-permute-start(bf16[256,512]{1,0:T(8,128)(2,1)S(1)} %copy-done.103), channel_id=1, source_target_pairs={{0,5},{1,4},{2,7},{3,6},{4,1},{5,0},{6,3},{7,2},{8,13},{9,12},{10,... | collective-permute-start | bytes 786440 | tf_op jit(solution)/shard_map/ppermute | solution.py:90
  573.6 19.3 %collective-permute-start.103 = (bf16[256,512]{1,0:T(8,128)(2,1)}, bf16[256,512]{1,0:T(8,128)(2,1)S(1)}, u32[]{:S(2)}, u32[]{:S(2)}) collective-permute-start(bf16[256,512]{1,0:T(8,128)(2,1)} %get-tuple-element.265), channel_id=1, source_target_pairs={{0,6},{1,7},{2,4},{3,5},{4,2},{5,3},{6,0},{7,1},{8,14},{9,15},{10,... | collective-permute-start | bytes 786440 | tf_op jit(solution)/shard_map/ppermute | solution.py:90
  598.4 30.3 %collective-permute-start.108 = (bf16[256,512]{1,0:T(8,128)(2,1)}, bf16[256,512]{1,0:T(8,128)(2,1)S(1)}, u32[]{:S(2)}, u32[]{:S(2)}) collective-permute-start(bf16[256,512]{1,0:T(8,128)(2,1)} %get-tuple-element.271), channel_id=1, source_target_pairs={{0,2},{1,3},{2,0},{3,1},{4,6},{5,7},{6,4},{7,5},{8,10},{9,11},{10,... | collective-permute-start | bytes 786440 | tf_op jit(solution)/shard_map/ppermute | solution.py:90
  601.7 22.9 %collective-permute-start.91 = (bf16[128,2048]{1,0:T(8,128)(2,1)S(1)}, bf16[128,2048]{1,0:T(8,128)(2,1)S(1)}, u32[]{:S(2)}, u32[]{:S(2)}) collective-permute-start(bf16[128,2048]{1,0:T(8,128)(2,1)S(1)} %fusion.21), channel_id=1, source_target_pairs={{0,8},{8,0},{1,9},{9,1},{2,10},{10,2},{3,11},{11,3},{4,12},{12,4},... | collective-permute-start | bytes 1572872 | tf_op jit(solution)/shard_map/ppermute | solution.py:115
  615.4 17.9 %collective-permute-start.92 = (f32[128,2048]{1,0:T(8,128)S(1)}, f32[128,2048]{1,0:T(8,128)}, u32[]{:S(2)}, u32[]{:S(2)}) collective-permute-start(f32[128,2048]{1,0:T(8,128)S(1)} %get-tuple-element.342), channel_id=1, source_target_pairs={{0,8},{8,0},{1,9},{9,1},{2,10},{10,2},{3,11},{11,3},{4,12},{12,4},... | collective-permute-start | bytes 3145736 | tf_op jit(solution)/shard_map/ppermute | solution.py:115
  (177 other events, 2079.9 us)

commit v4 on v3

--- a/solution.py
+++ b/solution.py
@@ -144,16 +144,18 @@
             total = total + self.between_groups(part.astype(BF16), distance).astype(F32)
         return total
 
-    def sum_all(self, block):
-        block = block + self.other_core(block)
+    def sum_steps(self, block):
+        held = [block + self.other_core(block)]
         mask = 1
         while mask < self.chips:
-            block = block + self.between_chips(block, lambda chip: chip ^ mask)
+            held.append(held[-1] + self.between_chips(held[-1], lambda chip: chip ^ mask))
             mask *= 2
-        total = block
-        for distance in range(1, self.groups):
-            total = total + self.between_groups(block, distance)
-        return total
+        if self.groups > 1:
+            total = held[-1]
+            for distance in range(1, self.groups):
+                total = total + self.between_groups(held[-1], distance)
+            held.append(total)
+        return held
 
     def ring_gather(self, parts, sections=None):
         half = self.chips // 2
@@ -220,6 +222,16 @@
 
     def swap(self, block, mask):
         return self.between_chips(block, lambda chip: chip ^ mask)
+
+
+def message_order(chips, core_heads):
+    near = [("up", mask) for mask in range(chips // 2 - 1, 0, -1)]
+    far = [("up", mask) for mask in range(chips - 1, chips // 2 - 1, -1)]
+    heads = [("head", turn) for turn in range(core_heads)]
+    order = []
+    for k, head in enumerate(heads):
+        order += [head] + near[k : k + 1]
+    return order + near[len(heads) :] + far
 
 
 def ordered(block, *earlier):
@@ -449,6 +461,71 @@
                 + matmul(active[:, part:], wd1[:, cols])
             )
             store_rows(outs, cols, total)
+
+
+def sums_kernel(pairs, *refs):
+    where, parts, (given, sums) = refs[0], refs[1 : 1 + 3 * pairs], refs[1 + 3 * pairs :]
+    norm_sums, joined_sum, hidden_sum = (
+        functools.reduce(jnp.add, [parts[3 * pair + k][...] for pair in range(pairs)])
+        for k in range(3)
+    )
+    rows, width = sums.shape[0], given.shape[1]
+    size = joined_sum.shape[1]
+    chip, core = where[0], where[1]
+    upstream = jnp.sum(given[...].astype(F32), axis=0, keepdims=True)
+    for k in range(4):
+        sums[k : k + 1, :width] = jnp.sum(norm_sums[8 * k : 8 * k + 8], axis=0, keepdims=True)
+    sums[4:5, :width] = upstream
+    sums[5:rows, :width] = jnp.zeros((rows - 5, width), F32)
+    mine = lax.broadcasted_iota(jnp.int32, (rows, 1), 0) == chip
+    joined = jnp.sum(joined_sum, axis=0, keepdims=True)
+    sums[:, width : width + size] = jnp.where(mine, joined, 0.0)
+    hidden = jnp.sum(hidden_sum, axis=0, keepdims=True)
+    half = hidden.shape[1] // 2
+    own, other = hidden[:, :half], hidden[:, half:]
+    hidden = jnp.concatenate(
+        [jnp.where(core == 0, own, other), jnp.where(core == 0, other, own)], axis=1
+    )
+    sums[:, width + size :] = jnp.where(mine, hidden, 0.0)
+
+
+def heads_kernel(count, *refs):
+    which, blocks, refs = refs[0], refs[1 : 1 + count], refs[1 + count :]
+    gain, qkv_grad, out_grad, held, signals = refs
+    copies = [
+        pltpu.make_async_copy(block, held.at[which[k]], signals.at[k])
+        for k, block in enumerate(blocks)
+    ]
+    for copy in copies:
+        copy.start()
+    for copy in copies:
+        copy.wait()
+    size = qkv_grad.shape[2]
+    rows, width = out_grad.shape[1:]
+    part = held.shape[2] - size
+    for head in range(count):
+        qkv_grad[:, head] = held[head, :, :size].astype(F32) * gain[...]
+        for k in range(width // part):
+            out_grad[head, :, k * part : (k + 1) * part] = held[
+                head, k * rows : (k + 1) * rows, size:
+            ].astype(F32)
+
+
+def up_kernel(count, chained, *refs):
+    which, blocks, refs = refs[0], refs[1 : 1 + count], refs[1 + count :]
+    gain, refs = refs[0], refs[1 + chained :]
+    up_grad, held, signals = refs
+    size = blocks[0].shape[1]
+    copies = []
+    for k, block in enumerate(blocks):
+        held[k] = block[...].astype(F32) * gain[...]
+        place = pl.multiple_of(which[k] * size, size)
+        copies.append(
+            pltpu.make_async_copy(held.at[k], up_grad.at[:, pl.ds(place, size)], signals.at[k])
+        )
+        copies[-1].start()
+    for copy in copies:
+        copy.wait()
 
 
 def rows_spec(array, count, pair):
@@ -484,6 +561,23 @@
     )(*operands)
 
 
+def call_whole(kernel, operands, outs, scratch, outside=(), aliases=None):
+    spaces = [
+        pltpu.SMEM if item.dtype == jnp.int32 else pl.ANY if k in outside else pltpu.VMEM
+        for k, item in enumerate([*operands, *outs])
+    ]
+    specs = [pl.BlockSpec(memory_space=space) for space in spaces]
+    return pl.pallas_call(
+        kernel,
+        out_shape=outs,
+        in_specs=specs[: len(operands)],
+        out_specs=specs[len(operands) :],
+        scratch_shapes=scratch,
+        input_output_aliases=aliases or {},
+        compiler_params=pltpu.CompilerParams(vmem_limit_bytes=VMEM_BYTES),
+    )(*operands)
+
+
 def on_device(
     layout,
     tokens,
@@ -578,31 +672,35 @@
         for up_mask in range(chips)
     ]
     queue = Queue(3)
+    order = message_order(chips, core_heads)
     heads = jnp.zeros((core_heads * block_rows, joined_size + head_size), BF16)
-    for turn, block in enumerate(head_blocks):
-        if turn == 2:
-            block = ordered(block, *up_blocks)
-        block = layout.send_head(queue.ready(block), turn)
-        slot = (chip - turn) % core_heads
-        heads = lax.dynamic_update_slice_in_dim(heads, block, slot * block_rows, 0)
-        queue.put(heads)
     wu0 = jnp.zeros((chips * block_rows, hidden_part), BF16)
     wu0 = lax.dynamic_update_slice_in_dim(wu0, up_blocks[0], chip * block_rows, 0)
-    for up_mask in range(chips - 1, 0, -1):
-        source = chip ^ up_mask
-        block = queue.ready(up_blocks[up_mask])
-        if up_mask == 1:
+    for k, (kind, which) in enumerate(order):
+        block = head_blocks[which] if kind == "head" else up_blocks[which]
+        if k == 1:
+            block = ordered(block, *head_blocks)
+        if k == 3:
+            block = ordered(block, *up_blocks)
+        if k == len(order) - 1:
             block = ordered(block, cosine, sine, mask, bq, bu)
-        block = layout.swap(block, up_mask)
-        wu0 = lax.dynamic_update_slice_in_dim(wu0, block, source * block_rows, 0)
-        queue.put(wu0)
+        block = queue.ready(block)
+        if kind == "head":
+            block = layout.send_head(block, which)
+            slot = (chip - which) % core_heads
+            heads = lax.dynamic_update_slice_in_dim(heads, block, slot * block_rows, 0)
+        else:
+            block = layout.swap(block, which)
+            wu0 = lax.dynamic_update_slice_in_dim(wu0, block, (chip ^ which) * block_rows, 0)
+        queue.put(block)
     wu1 = layout.other_core(wu0)
-    heads = layout.by_core(heads, layout.other_core(ordered(heads, up_blocks[1])))
+    heads = layout.by_core(heads, layout.other_core(heads))
 
     row_bias = (out_bias[0].astype(F32) + down_bias[0].astype(F32))[None]
 
     part_rows = length // 2
     piece = jax.ShapeDtypeStruct((part_rows, width), BF16)
+    whole_piece = jax.ShapeDtypeStruct((length, width), BF16)
 
     def by_rows(cols, dtype):
         return jax.ShapeDtypeStruct((row_count, cols), dtype)
@@ -729,7 +827,7 @@
         blocks = pair_blocks(upstream_blocks, pair)
         results = call_rows(
             functools.partial(
-                backward_kernel, len(blocks), 4, len(grad_shapes) if grads else 0
+                backward_kernel, len(blocks), 2, len(grad_shapes) if grads else 0
             ),
             (*blocks, second_section, *matrices),
             (cosine, sine, first_norm, second_norm, qkv, attention, attended, active, slope),
@@ -740,7 +838,7 @@
                 jax.ShapeDtypeStruct((8, joined_size), F32),
                 jax.ShapeDtypeStruct((8, hidden_size), F32),
             ]
-            + [piece] * 4,
+            + [whole_piece] * 2,
             [pltpu.VMEM((head_size, width), BF16)],
             pair,
             2 * length,
@@ -749,8 +847,17 @@
         grads = results[: len(grad_shapes)]
         sums.append(results[len(grad_shapes) : len(grad_shapes) + 3])
         for k in range(2):
-            last_pieces[layout.slots[2 * pair + k]] = results[2 * k - 4 : 2 * k - 2 or None]
+            last_pieces[layout.slots[2 * pair + k]] = [results[k - 2]]
     upstream, joined_grad, hidden_grad = grads
+
+    own_given = jnp.concatenate(own_upstream, axis=0)
+    (local_sums,) = call_whole(
+        functools.partial(sums_kernel, len(sums)),
+        [jnp.stack([chip, core]), *[item for pair in sums for item in pair], own_given],
+        [jax.ShapeDtypeStruct((chips, width + joined_size + hidden_size), F32)],
+        [],
+    )
+    joint = layout.sum_steps(local_sums)
 
     def half_of(array, which):
         size = array.shape[1] // cores
@@ -764,60 +871,38 @@
     joined_given = weight_grad(half_of(first_norm, 1 - core), joined_grad).astype(BF16)
     out_given = weight_grad(half_of(attended, 1 - core), upstream).astype(BF16)
     hidden_given = weight_grad(second_norm, hidden_grad[:, hidden_part:]).astype(BF16)
-    down_given = weight_grad(active[:, hidden_part:], upstream).astype(BF16)
-    given = (joined_given, out_given, hidden_given, down_given)
-    joined_taken, out_taken, hidden_taken, down_taken = (
-        layout.other_core(item) for item in given
+    joined_taken, out_taken, hidden_taken = (
+        layout.other_core(item) for item in (joined_given, out_given, hidden_given)
     )
 
     def core_sum(own, taken):
         return (own + taken.astype(F32)).astype(BF16)
 
-    late_grad, late_attended = ordered(joined_grad, *given), ordered(attended, *given)
+    late_grad, late_attended = (
+        ordered(item, joint[0], joined_given, out_given, hidden_given)
+        for item in (joined_grad, attended)
+    )
     joined_held = core_sum(weight_grad(half_of(first_norm, core), late_grad), joined_taken)
     out_held = core_sum(weight_grad(half_of(late_attended, core), upstream), out_taken)
     late_grad = ordered(hidden_grad, joined_held, out_held)
     hidden_held = core_sum(weight_grad(second_norm, late_grad[:, :hidden_part]), hidden_taken)
-
-    own_given = jnp.concatenate(own_upstream, axis=0)
-    norm_sums, joined_sum, hidden_sum = (
-        functools.reduce(jnp.add, [item[k] for item in sums]) for k in range(3)
-    )
-    norm_sums = jnp.sum(norm_sums.reshape(2, 2, 8, width), axis=2)
+    late_active = ordered(active, hidden_held)
+    down_taken = layout.other_core(
+        weight_grad(late_active[:, hidden_part:], upstream).astype(BF16)
+    )
+
+    whole_sums = joint[-1]
+    norm_sums = whole_sums[:4, :width].reshape(2, 2, width)
     norm_sums = jnp.stack([norm_sums[0] - ratio * norm_sums[1], norm_sums[1]]) / gains
-    joined_bias_all = lax.dynamic_update_slice(
-        jnp.zeros((chips, joined_size), F32), jnp.sum(joined_sum, axis=0)[None], (chip, 0)
-    )
-    hidden_sum = jnp.sum(hidden_sum, axis=0)[None, None]
-    hidden_bias_all = jnp.zeros((cores, chips, hidden_part), F32)
-    hidden_bias_all = lax.dynamic_update_slice(
-        hidden_bias_all, hidden_sum[:, :, :hidden_part], (core, chip, 0)
-    )
-    hidden_bias_all = lax.dynamic_update_slice(
-        hidden_bias_all, hidden_sum[:, :, hidden_part:], (1 - core, chip, 0)
-    )
-    vectors = (
-        norm_sums,
-        joined_bias_all,
-        jnp.sum(own_given, axis=0, dtype=F32),
-        hidden_bias_all,
-    )
-    joint = layout.sum_all(
-        ordered(jnp.concatenate([item.reshape(-1) for item in vectors]), *given)
-    )
-    summed, start = [], 0
-    for item in vectors:
-        summed.append(joint[start : start + item.size].reshape(item.shape))
-        start += item.size
-    norm_sums, joined_bias_all, out_bias_grad, hidden_bias_all = summed
-    joined_bias_grad = lax.dynamic_slice_in_dim(joined_bias_all, core * core_heads, core_heads, 0)
-    up_bias_grad = lax.dynamic_index_in_dim(hidden_bias_all, core, 0, keepdims=False).reshape(-1)
-
-    (last_rows,) = layout.ring_scatter(
-        {slot: [jnp.concatenate(parts, axis=0)] for slot, parts in last_pieces.items()},
-        None,
-        {1: (joined_held, out_held)},
-    )
+    out_bias_grad = whole_sums[4, :width]
+    joined_bias_grad = lax.dynamic_slice_in_dim(
+        whole_sums[:, width : width + joined_size], core * core_heads, core_heads, 0
+    )
+    up_bias_grad = lax.dynamic_slice_in_dim(
+        whole_sums[:, width + joined_size :], core * hidden_part, hidden_part, 1
+    ).reshape(-1)
+
+    (last_rows,) = layout.ring_scatter(last_pieces, None, {1: (joined_held, out_held)})
     last_normed, last_inverse = (
         jnp.concatenate([norm[k] for norm in own_normed], axis=0) for k in range(2)
     )
@@ -828,61 +913,92 @@
     own_out = jnp.where(first_section, jnp.concatenate(first_out, axis=0), second_out)
     layer_outputs = layout.by_core(own_out, layout.other_core(own_out))
 
-    up_weight_grad = jnp.zeros((shard, chips * hidden_part), F32)
-    qkv_grad = jnp.zeros((shard, core_heads * joined_size), F32)
-    out_weight_grad = jnp.zeros((core_heads, head_size // layout.dp, width), F32)
+    out_rows = out_held.shape[0] // core_heads
+    share_rows = out_rows // layout.groups
     head_blocks = []
-    out_rows = out_held.shape[0] // core_heads
     for turn in range(core_heads):
         slot = (chip - turn) % core_heads
         out_part = lax.dynamic_slice_in_dim(out_held, slot * out_rows, out_rows, 0)
-        out_part = out_part.reshape(out_rows, width // head_size, head_size).transpose(1, 0, 2)
+        out_part = out_part.reshape(layout.groups, share_rows, width // head_size, head_size)
         head_blocks.append(
             jnp.concatenate(
                 [
                     lax.dynamic_slice_in_dim(joined_held, slot * block_rows, block_rows, 0),
-                    out_part.reshape(block_rows, head_size),
+                    out_part.transpose(0, 2, 1, 3).reshape(block_rows, head_size),
                 ],
                 axis=1,
             )
         )
     queue = Queue(3)
-    for turn, block in enumerate(head_blocks):
-        head = layout.head_turn(chip, turn)
-        if turn == 1:
-            block = ordered(block, hidden_held, *head_blocks)
-        block = layout.return_head(queue.ready(block), turn)
-        out_block = block[:, joined_size:].reshape(width // head_size, out_rows, head_size)
-        out_block = out_block.transpose(1, 0, 2).reshape(out_rows, width)
-        out_block = layout.scatter_groups(out_block, 0)
-        block = layout.scatter_groups(block[:, :joined_size], 0) * gain_rows[0][:, None]
-        qkv_grad = lax.dynamic_update_slice_in_dim(qkv_grad, block, head * joined_size, 1)
-        out_weight_grad = lax.dynamic_update_slice_in_dim(
-            out_weight_grad, out_block[None], head, 0
-        )
-        queue.put(qkv_grad, out_weight_grad)
-    joined_weight_grad = qkv_grad.reshape(shard, core_heads, joined_size)
-
-    late_active = ordered(active, hidden_held)
-    down_weight_grad = weight_grad(late_active[:, :hidden_part], upstream) + down_taken.astype(F32)
-    if layout.groups > 1:
-        down_weight_grad = layout.scatter_groups(down_weight_grad, 0)
-
-    for up_mask in range(chips - 1, -1, -1):
-        source = chip ^ up_mask
-        block = lax.dynamic_slice_in_dim(hidden_held, source * block_rows, block_rows, 0)
-        if up_mask:
-            block = queue.ready(block)
-            if up_mask == 3:
-                block = ordered(block, down_weight_grad, joint)
-            if up_mask == 1:
-                block = ordered(block, last_rows, joined_weight_grad)
-            block = layout.swap(block, up_mask)
-        block = layout.scatter_groups(block, 0) * gain_rows[1][:, None]
-        up_weight_grad = lax.dynamic_update_slice_in_dim(
-            up_weight_grad, block, source * hidden_part, 1
-        )
-        queue.put(up_weight_grad)
+    gain_cols = gain_rows[:, :, None]
+    blocks = {
+        ("up", 0): lax.dynamic_slice_in_dim(hidden_held, chip * block_rows, block_rows, 0)
+    }
+    up_weight_grad = None
+    for k, (kind, which) in enumerate(order):
+        if kind == "head":
+            block = head_blocks[which]
+        else:
+            block = lax.dynamic_slice_in_dim(
+                hidden_held, (chip ^ which) * block_rows, block_rows, 0
+            )
+        if k == 0:
+            block = ordered(block, joint[1], *head_blocks)
+        if k == 2:
+            block = ordered(block, joint[2])
+        if k == 4:
+            block = ordered(block, joint[-1])
+        if k == len(order) - 3:
+            block = ordered(block, down_weight_grad)
+        if k == len(order) - 1:
+            block = ordered(block, last_rows, joined_weight_grad)
+        block = queue.ready(block)
+        block = layout.return_head(block, which) if kind == "head" else layout.swap(block, which)
+        queue.put(block)
+        blocks[kind, which] = block
+        if kind == "head" and which == core_heads - 1:
+            heads_in = [blocks["head", turn] for turn in range(core_heads)]
+            if layout.groups > 1:
+                heads_in = [layout.scatter_groups(item, 0) for item in heads_in]
+            joined_weight_grad, out_weight_grad = call_whole(
+                functools.partial(heads_kernel, core_heads),
+                [
+                    jnp.stack([layout.head_turn(chip, turn) for turn in range(core_heads)]),
+                    *heads_in,
+                    gain_cols[0],
+                ],
+                [
+                    jax.ShapeDtypeStruct((shard, core_heads, joined_size), F32),
+                    jax.ShapeDtypeStruct((core_heads, share_rows, width), F32),
+                ],
+                [
+                    pltpu.VMEM((core_heads, *heads_in[0].shape), heads_in[0].dtype),
+                    pltpu.SemaphoreType.DMA((core_heads,)),
+                ],
+                range(1, 1 + core_heads),
+            )
+            down_weight_grad = weight_grad(
+                late_active[:, :hidden_part], upstream
+            ) + down_taken.astype(F32)
+            if layout.groups > 1:
+                down_weight_grad = layout.scatter_groups(down_weight_grad, 0)
+        if k in (len(order) - 3, len(order) - 1):
+            masks = [mask for mask in range(chips) if ("up", mask) in blocks]
+            columns = [blocks.pop(("up", mask)) for mask in masks]
+            if layout.groups > 1:
+                columns = [layout.scatter_groups(item, 0) for item in columns]
+            chain = [] if up_weight_grad is None else [up_weight_grad]
+            (up_weight_grad,) = call_whole(
+                functools.partial(up_kernel, len(columns), len(chain)),
+                [jnp.stack([chip ^ mask for mask in masks]), *columns, gain_cols[1], *chain],
+                [jax.ShapeDtypeStruct((shard, chips * hidden_part), F32)],
+                [
+                    pltpu.VMEM((len(columns), *columns[0].shape), F32),
+                    pltpu.SemaphoreType.DMA((len(columns),)),
+                ],
+                range(len(columns) + 2, len(columns) + 3 + len(chain)),
+                {len(columns) + 2: 0} if chain else None,
+            )
 
     return (
         layer_outputs[None],

time: 646 us -> 613 us (0.949)
  waiting for transfers between devices: 163 us -> 245 us
  starting transfers between devices: 193 us -> 136 us
  other arithmetic: 67 us -> 35.8 us
  local copies, waits for them, and re-layouts: 80.3 us -> 56.2 us
  matrix products: 29.2 us -> 19.6 us
  Pallas kernels: 101 us -> 109 us
    ppermute x87, starting transfers between devices: 174 us -> 116 us  [between_chips(): return lax.ppermute(block, 'dp', pairs)]
    ppermute x87, waiting for transfers between devices: 143 us -> 201 us  [between_chips(): return lax.ppermute(block, 'dp', pairs)]
    dynamic_update_slice x12 -> x0, other arithmetic: 16.3 us -> none  [the longest x8 11 us: on_device(): lax.dynamic_update_slice_in_dim(up_weight_grad, block, source * hidden_pa...]
    ppermute x4, waiting for transfers between devices: 0.91 us -> 13.1 us  [send_head(): return lax.ppermute(block, ('tensor', 'dp'), self.head_route(turn))]
    ppermute x4, waiting for transfers between devices: 1.33 us -> 13 us  [return_head(): return lax.ppermute(block, ('tensor', 'dp'), pairs)]
    dot_general x8, matrix products: 29.2 us -> 19.6 us  [contract_rows(): lax.dot_general(left_side, right_side, (((0,), (0,)), ((), ())), preferre...]
    pallas_call x0 -> x4, Pallas kernels: none -> 8.32 us  [call_whole(): pl.pallas_call(kernel, out_shape=outs, in_specs=specs[:len(operands)], ou...]
    convert_element_type x25, other arithmetic: 9.43 us -> 1.92 us  [ring_scatter(): moving = (moving.astype(F32) + parts[slot].astype(F32)).astype(BF16)]
  transfers between devices with their start and end apart: 110 -> 110, of which waited for: 41 -> 44; matrix products, arithmetic and copies ran while one was open for 19% -> 11% of each run, Pallas kernels for 12% -> 14%
where the time goes in v4:
time: 613 us; the launch traced here: 605 us
  waiting for transfers between devices  245 us (40%)
  starting transfers between devices  136 us (22%)
  Pallas kernels  109 us (18%)
  local copies, waits for them, and re-layouts  56.2 us (9%)
  other arithmetic  35.8 us (6%)
  matrix products  19.6 us (3%)
    ppermute x87, waiting for transfers between devices, between_chips(): return lax.ppermute(block, 'dp', pairs)  201 us
    ppermute x87, starting transfers between devices, between_chips(): return lax.ppermute(block, 'dp', pairs)  116 us
    pallas_call x11, Pallas kernels, call_rows(): pl.pallas_call(kernel, grid=(1,), out_shape=out_shape, in_specs=in_specs,...  100 us
    unnamed x204, local copies, waits for them, and re-layouts  38 us
    dot_general x8, matrix products, contract_rows(): lax.dot_general(left_side, right_side, (((0,), (0,)), ((), ())), preferre...  19.6 us
    ppermute x4, waiting for transfers between devices, send_head(): return lax.ppermute(block, ('tensor', 'dp'), self.head_route(turn))  13.1 us
    ppermute x4, waiting for transfers between devices, return_head(): return lax.ppermute(block, ('tensor', 'dp'), pairs)  13 us
  transfers between devices with their start and end apart: 110, of which 44 were waited for; matrix products, arithmetic and copies ran while one was open for 11% of the time, Pallas kernels for 14%

profile of v4, /device:TPU:10, one launch (start us, length us, event | category | flops | bytes accessed | tf_op | source)
XLA Modules:
  0.0 604.9 jit_solution(18089361242490392663)
XLA Ops:
  16.6 5.3 collective-permute-start.3
  33.4 13.6 %collective-permute-done.5 = bf16[256,512]{1,0:T(8,128)(2,1)S(1)} collective-permute-done((bf16[256,512]{1,0:T(8,128)(2,1)}, bf16[256,512]{1,0:T(8,128)(2,1)S(1)}, u32[]{:S(2)}, u32[]{:S(2)}) %collective-permute-start.5) | collective-permute-done | bytes 262176 | tf_op jit(solution)/shard_map/ppermute | solution.py:90
  59.9 19.8 %collective-permute-done.2.refs_3_ = bf16[144,2048]{1,0:T(8,128)(2,1)S(1)} collective-permute-done((bf16[144,2048]{1,0:T(8,128)(2,1)}, bf16[144,2048]{1,0:T(8,128)(2,1)S(1)}, u32[]{:S(2)}, u32[]{:S(2)}) %collective-permute-start.2) | collective-permute-done | bytes 589856 | tf_op jit(solution)/shard_map/ppermute | solution.py:90
  87.7 13.9 %collective-permute-done.15.refs_1_.refs_5_ = bf16[144,2048]{1,0:T(8,128)(2,1)S(1)} collective-permute-done((bf16[144,2048]{1,0:T(8,128)(2,1)S(1)}, bf16[144,2048]{1,0:T(8,128)(2,1)S(1)}, u32[]{:S(2)}, u32[]{:S(2)}) %collective-permute-start.15) | collective-permute-done | bytes 589856 | tf_op jit(solution)/shard_map/ppermute | solution.py:90
  101.8 13.1 %collective-permute-done.8 = bf16[256,1024]{1,0:T(8,128)(2,1)S(1)} collective-permute-done((bf16[256,1024]{1,0:T(8,128)(2,1)S(1)}, bf16[256,1024]{1,0:T(8,128)(2,1)S(1)}, u32[]{:S(2)}, u32[]{:S(2)}) %collective-permute-start.8) | collective-permute-done | bytes 524320 | tf_op jit(solution)/shard_map/ppermute | solution.py:217
  114.9 4.5 collective-permute-start.12
  123.4 14.0 %collective-permute-done.17.refs_3_.refs_7_ = bf16[144,2048]{1,0:T(8,128)(2,1)S(1)} collective-permute-done((bf16[144,2048]{1,0:T(8,128)(2,1)S(1)}, bf16[144,2048]{1,0:T(8,128)(2,1)S(1)}, u32[]{:S(2)}, u32[]{:S(2)}) %collective-permute-start.17) | collective-permute-done | bytes 589856 | tf_op jit(solution)/shard_map/ppermute | solution.py:90
  142.6 5.1 collective-permute-start.19
  150.7 6.1 %collective-permute-done.19 = bf16[256,512]{1,0:T(8,128)(2,1)S(1)} collective-permute-done((bf16[256,512]{1,0:T(8,128)(2,1)S(1)}, bf16[256,512]{1,0:T(8,128)(2,1)S(1)}, u32[]{:S(2)}, u32[]{:S(2)}) %collective-permute-start.19) | collective-permute-done | bytes 262176 | tf_op jit(solution)/shard_map/ppermute | solution.py:90
  162.3 12.2 %shard_map.221 = (bf16[64,2048]{1,0:T(8,128)(2,1)S(1)}, bf16[64,2048]{1,0:T(8,128)(2,1)S(1)}, bf16[64,2048]{1,0:T(8,128)(2,1)S(1)}, bf16[64,2048]{1,0:T(8,128)(2...) custom-call(bf16[144,2048]{1,0:T(8,128)(2,1)S(1)} %copy-done.46, ...), custom_call_target="tpu_custom_call" | custom-call | flops 6442450944 | bytes 4194304 | tf_op jit(solution)/shard_map/pallas_call | solution.py:551
  181.1 12.5 %shard_map.220 = (bf16[64,2048]{1,0:T(8,128)(2,1)S(1)}, bf16[64,2048]{1,0:T(8,128)(2,1)S(1)}, bf16[64,2048]{1,0:T(8,128)(2,1)S(1)}, bf16[64,2048]{1,0:T(8,128)(2...) custom-call(bf16[144,2048]{1,0:T(8,128)(2,1)S(1)} %copy-done.28, ...), custom_call_target="tpu_custom_call" | custom-call | flops 6442450944 | bytes 4194304 | tf_op jit(solution)/shard_map/pallas_call | solution.py:551
  198.1 4.8 collective-permute-done.30
  205.2 3.3 collective-permute-done.23
  210.8 3.5 collective-permute-done.34
  219.9 4.2 collective-permute-done.35
  229.1 8.2 %collective-permute-done.36 = bf16[64,2048]{1,0:T(8,128)(2,1)} collective-permute-done((bf16[64,2048]{1,0:T(8,128)(2,1)S(1)}, bf16[64,2048]{1,0:T(8,128)(2,1)}, u32[]{:S(2)}, u32[]{:S(2)}) %collective-permute-start.36) | collective-permute-done | bytes 262176 | tf_op jit(solution)/shard_map/ppermute | solution.py:771
  237.3 2.8 collective-permute-done.37
  250.5 8.2 %shard_map.222 = (bf16[1024,256]{1,0:T(8,128)(2,1)S(1)}, bf16[1024,1024]{1,0:T(8,128)(2,1)S(1)}) custom-call(bf16[144,2048]{1,0:T(8,128)(2,1)S(1)} %copy-done.29, bf16[144,2048]{1,0:T(8,128)(2,1)} %collective-permute-done.refs_1_, bf16[144,2048]{1,0:T(8,128)(2,1)} %collective-permute-done.1.refs_2_, bf16[144,2048]{1,0:T(8,128)(2,1)S(1)} %copy-done.44, ...), custom_call_target="tpu_custom_call" | custom-call | flops 5368709120 | bytes 8388608 | tf_op jit(solution)/shard_map/pallas_call | solution.py:551
  262.8 7.2 %shard_map.223 = (bf16[1024,2048]{1,0:T(8,128)(2,1)S(1)}, bf16[1024,2048]{1,0:T(8,128)(2,1)S(1)}, bf16[1024,768]{1,0:T(8,128)(2,1)S(1)}, f32[1024,128]{1,0:T(8,1...) custom-call(bf16[64,2048]{1,0:T(8,128)(2,1)S(1)} %get-tuple-element., ...), custom_call_target="tpu_custom_call" | custom-call | flops 6442450944 | bytes 2097152 | tf_op jit(solution)/shard_map/pallas_call | solution.py:551
  274.2 7.2 %shard_map.224 = (bf16[1024,2048]{1,0:T(8,128)(2,1)S(1)}, bf16[1024,2048]{1,0:T(8,128)(2,1)S(1)}, bf16[1024,768]{1,0:T(8,128)(2,1)S(1)}, f32[1024,128]{1,0:T(8,1...) custom-call(bf16[64,2048]{1,0:T(8,128)(2,1)S(1)} %collective-permute, ...), custom_call_target="tpu_custom_call", output_to_operand_aliasing={{0}: (15, {}), {1}: (16, {}), {2}: (17, {}), {3}: (18, {}),... | custom-call | flops 6442450944 | bytes 2097152 | tf_op jit(solution)/shard_map/pallas_call | solution.py:551
  285.1 7.2 %shard_map.225 = (bf16[1024,2048]{1,0:T(8,128)(2,1)S(1)}, bf16[1024,2048]{1,0:T(8,128)(2,1)S(1)}, bf16[1024,768]{1,0:T(8,128)(2,1)S(1)}, f32[1024,128]{1,0:T(8,1...) custom-call(bf16[64,2048]{1,0:T(8,128)(2,1)S(1)} %collective-permute, ...), custom_call_target="tpu_custom_call", output_to_operand_aliasing={{0}: (15, {}), {1}: (16, {}), {2}: (17, {}), {3}: (18, {}),... | custom-call | flops 6442450944 | bytes 2097152 | tf_op jit(solution)/shard_map/pallas_call | solution.py:551
  293.4 7.2 %shard_map.226 = (bf16[1024,2048]{1,0:T(8,128)(2,1)S(1)}, bf16[1024,2048]{1,0:T(8,128)(2,1)S(1)}, bf16[1024,768]{1,0:T(8,128)(2,1)S(1)}, f32[1024,128]{1,0:T(8,1...) custom-call(bf16[64,2048]{1,0:T(8,128)(2,1)S(1)} %collective-permute, ...), custom_call_target="tpu_custom_call", output_to_operand_aliasing={{0}: (15, {}), {1}: (16, {}), {2}: (17, {}), {3}: (18, {}),... | custom-call | flops 6442450944 | bytes 2097152 | tf_op jit(solution)/shard_map/pallas_call | solution.py:551
  311.5 5.1 collective-permute-done.52
  328.3 3.0 collective-permute-done.64
  333.6 4.6 collective-permute-done.65
  339.8 4.9 collective-permute-done.66
  351.7 2.8 collective-permute-done.67
  377.4 9.8 %shard_map.227 = (bf16[1024,2048]{1,0:T(8,128)(2,1)S(1)}, bf16[1024,768]{1,0:T(8,128)(2,1)S(1)}, bf16[1024,1024]{1,0:T(8,128)(2,1)S(1)}, f32[32,2048]{1,0:T(8,12...) custom-call(bf16[64,2048]{1,0:T(8,128)(2,1)} %get-tuple-element.321., ...), custom_call_target="tpu_custom_call" | custom-call | flops 3221225472 | bytes 2097152 | tf_op jit(solution)/shard_map/pallas_call | solution.py:551
  392.9 9.7 %shard_map.228 = (bf16[1024,2048]{1,0:T(8,128)(2,1)S(1)}, bf16[1024,768]{1,0:T(8,128)(2,1)S(1)}, bf16[1024,1024]{1,0:T(8,128)(2,1)S(1)}, f32[32,2048]{1,0:T(8,12...) custom-call(bf16[64,2048]{1,0:T(8,128)(2,1)} %collective-permute-don, ...), custom_call_target="tpu_custom_call", output_to_operand_aliasing={{0}: (19, {}), {1}: (20, {}), {2}: (21, {})} | custom-call | flops 3221225472 | bytes 2097152 | tf_op jit(solution)/shard_map/pallas_call | solution.py:551
  406.4 9.5 %shard_map.229 = (bf16[1024,2048]{1,0:T(8,128)(2,1)S(1)}, bf16[1024,768]{1,0:T(8,128)(2,1)S(1)}, bf16[1024,1024]{1,0:T(8,128)(2,1)S(1)}, f32[32,2048]{1,0:T(8,12...) custom-call(bf16[64,2048]{1,0:T(8,128)(2,1)S(1)} %collective-permute, ...), custom_call_target="tpu_custom_call", output_to_operand_aliasing={{0}: (19, {}), {1}: (20, {}), {2}: (21, {})} | custom-call | flops 3221225472 | bytes 2097152 | tf_op jit(solution)/shard_map/pallas_call | solution.py:551
  417.5 9.8 %shard_map.230 = (bf16[1024,2048]{1,0:T(8,128)(2,1)S(1)}, bf16[1024,768]{1,0:T(8,128)(2,1)S(1)}, bf16[1024,1024]{1,0:T(8,128)(2,1)S(1)}, f32[32,2048]{1,0:T(8,12...) custom-call(bf16[64,2048]{1,0:T(8,128)(2,1)S(1)} %collective-permute, ...), custom_call_target="tpu_custom_call", output_to_operand_aliasing={{0}: (19, {}), {1}: (20, {}), {2}: (21, {})} | custom-call | flops 3221225472 | bytes 2097152 | tf_op jit(solution)/shard_map/pallas_call | solution.py:551
  435.8 4.8 convolution_convert_fusion.1
  441.8 4.0 collective-permute-done.95
  450.8 2.6 collective-permute-done.96
  457.4 7.3 %collective-permute-done.82 = bf16[128,2048]{1,0:T(8,128)(2,1)S(1)} collective-permute-done((bf16[128,2048]{1,0:T(8,128)(2,1)S(1)}, bf16[128,2048]{1,0:T(8,128)(2,1)S(1)}, u32[]{:S(2)}, u32[]{:S(2)}) %collective-permute-start.82) | collective-permute-done | bytes 524320 | tf_op jit(solution)/shard_map/ppermute | solution.py:90
  473.3 15.2 %collective-permute-done.86 = bf16[128,2048]{1,0:T(8,128)(2,1)S(1)} collective-permute-done((bf16[128,2048]{1,0:T(8,128)(2,1)S(1)}, bf16[128,2048]{1,0:T(8,128)(2,1)S(1)}, u32[]{:S(2)}, u32[]{:S(2)}) %collective-permute-start.86) | collective-permute-done | bytes 524320 | tf_op jit(solution)/shard_map/ppermute | solution.py:90
  488.7 3.3 collective-permute-start.87
  494.9 12.4 %collective-permute-done.90 = bf16[128,2048]{1,0:T(8,128)(2,1)S(1)} collective-permute-done((bf16[128,2048]{1,0:T(8,128)(2,1)S(1)}, bf16[128,2048]{1,0:T(8,128)(2,1)S(1)}, u32[]{:S(2)}, u32[]{:S(2)}) %collective-permute-start.90) | collective-permute-done | bytes 524320 | tf_op jit(solution)/shard_map/ppermute | solution.py:90
  507.5 3.4 collective-permute-start.101
  510.9 5.8 collective-permute-done.102.refs_3_
  516.8 5.6 collective-permute-start.88
  525.1 8.4 %collective-permute-done.101.refs_3_ = bf16[256,1024]{1,0:T(8,128)(2,1)S(1)} collective-permute-done((bf16[256,1024]{1,0:T(8,128)(2,1)S(1)}, bf16[256,1024]{1,0:T(8,128)(2,1)S(1)}, u32[]{:S(2)}, u32[]{:S(2)}) %collective-permute-start.101) | collective-permute-done | bytes 524320 | tf_op jit(solution)/shard_map/ppermute | solution.py:221
  533.5 4.5 collective-permute-done.103.refs_4_
  538.0 10.1 %collective-permute-start.104 = (bf16[256,512]{1,0:T(8,128)(2,1)S(1)}, bf16[256,512]{1,0:T(8,128)(2,1)S(1)}, u32[]{:S(2)}, u32[]{:S(2)}) collective-permute-start(bf16[256,512]{1,0:T(8,128)(2,1)S(1)} %get-tuple-element.257), channel_id=1, source_target_pairs={{0,7},{1,6},{2,5},{3,4},{4,3},{5,2},{6,1},{7,0},{8,15},{9,14},{10,... | collective-permute-start | bytes 786440 | tf_op jit(solution)/shard_map/ppermute | solution.py:90
  548.1 3.6 shard_map.232
  553.7 23.0 %collective-permute-done.104.refs_6_ = bf16[256,512]{1,0:T(8,128)(2,1)S(1)} collective-permute-done((bf16[256,512]{1,0:T(8,128)(2,1)S(1)}, bf16[256,512]{1,0:T(8,128)(2,1)S(1)}, u32[]{:S(2)}, u32[]{:S(2)}) %collective-permute-start.104) | collective-permute-done | bytes 262176 | tf_op jit(solution)/shard_map/ppermute | solution.py:90
  581.1 4.5 convert_add_fusion
  587.3 12.5 %collective-permute-done.109.refs_5_ = bf16[256,512]{1,0:T(8,128)(2,1)S(1)} collective-permute-done((bf16[256,512]{1,0:T(8,128)(2,1)S(1)}, bf16[256,512]{1,0:T(8,128)(2,1)S(1)}, u32[]{:S(2)}, u32[]{:S(2)}) %collective-permute-start.109) | collective-permute-done | bytes 262176 | tf_op jit(solution)/shard_map/ppermute | solution.py:90
  (553 shorter events, 227.8 us)
Async XLA Ops:
  6.6 42.8 %collective-permute-start = (bf16[144,2048]{1,0:T(8,128)(2,1)S(1)}, bf16[144,2048]{1,0:T(8,128)(2,1)}, u32[]{:S(2)}, u32[]{:S(2)}) collective-permute-start(bf16[144,2048]{1,0:T(8,128)(2,1)S(1)} %fusion.18.refs_0_), channel_id=1, source_target_pairs={{0,1},{1,3},{2,0},{3,5},{4,2},{5,7},{6,4},{7,6},{8,9},{9,11},{10,8... | collective-permute-start | bytes 1769480 | tf_op jit(solution)/shard_map/ppermute | solution.py:90
  7.1 51.2 %collective-permute-start.1 = (bf16[144,2048]{1,0:T(8,128)(2,1)S(1)}, bf16[144,2048]{1,0:T(8,128)(2,1)}, u32[]{:S(2)}, u32[]{:S(2)}) collective-permute-start(bf16[144,2048]{1,0:T(8,128)(2,1)S(1)} %fusion.18.refs_0_), channel_id=1, source_target_pairs={{0,2},{1,0},{2,4},{3,1},{4,6},{5,3},{6,7},{7,5},{8,10},{9,8},{10,1... | collective-permute-start | bytes 1769480 | tf_op jit(solution)/shard_map/ppermute | solution.py:90
  8.8 21.6 %collective-permute-start.18 = (f32[1,7168]{1,0:T(1,128)S(1)}, f32[1,7168]{1,0:T(1,128)}, u32[]{:S(2)}, u32[]{:S(2)}) collective-permute-start(f32[1,7168]{1,0:T(1,128)S(1)} %maximum_convert_fusion), channel_id=1, source_target_pairs={{0,8},{8,0},{1,9},{9,1},{2,10},{10,2},{3,11},{11,3},{4,12},{12,4},... | collective-permute-start | bytes 86024 | tf_op jit(solution)/shard_map/ppermute | solution.py:115
  16.6 32.8 %collective-permute-start.3 = (bf16[256,1024]{1,0:T(8,128)(2,1)}, bf16[256,1024]{1,0:T(8,128)(2,1)}, u32[]{:S(2)}, u32[]{:S(2)}) collective-permute-start(bf16[256,1024]{1,0:T(8,128)(2,1)} %pad_maximum_fusion.2), channel_id=1, source_target_pairs={{0,0},{1,1},{2,2},{3,3},{4,8},{5,9},{6,10},{7,11},{8,4},{9,5},{10,... | collective-permute-start | bytes 1572872 | tf_op jit(solution)/shard_map/ppermute | solution.py:217
  22.9 28.1 %collective-permute-start.4 = (bf16[256,1024]{1,0:T(8,128)(2,1)}, bf16[256,1024]{1,0:T(8,128)(2,1)}, u32[]{:S(2)}, u32[]{:S(2)}) collective-permute-start(bf16[256,1024]{1,0:T(8,128)(2,1)} %pad_maximum_fusion.3), channel_id=1, source_target_pairs={{0,1},{1,2},{2,3},{3,0},{4,9},{5,10},{6,11},{7,8},{8,5},{9,6},{10,... | collective-permute-start | bytes 1572872 | tf_op jit(solution)/shard_map/ppermute | solution.py:217
  47.0 37.1 %collective-permute-start.6 = (bf16[256,1024]{1,0:T(8,128)(2,1)}, bf16[256,1024]{1,0:T(8,128)(2,1)S(1)}, u32[]{:S(2)}, u32[]{:S(2)}) collective-permute-start(bf16[256,1024]{1,0:T(8,128)(2,1)} %pad_maximum_fusion.4), channel_id=1, source_target_pairs={{0,2},{1,3},{2,0},{3,1},{4,10},{5,11},{6,8},{7,9},{8,6},{9,7},{10,... | collective-permute-start | bytes 1572872 | tf_op jit(solution)/shard_map/ppermute | solution.py:217
  49.4 30.4 %collective-permute-start.2 = (bf16[144,2048]{1,0:T(8,128)(2,1)}, bf16[144,2048]{1,0:T(8,128)(2,1)S(1)}, u32[]{:S(2)}, u32[]{:S(2)}) collective-permute-start(bf16[144,2048]{1,0:T(8,128)(2,1)} %collective-permute-done.refs_1_), channel_id=1, source_target_pairs={{0,1},{1,3},{2,0},{3,5},{4,2},{5,7},{6,4},{7,6},{8,9},{9,11},{10,8... | collective-permute-start | bytes 1769480 | tf_op jit(solution)/shard_map/ppermute | solution.py:90
  49.4 35.9 %collective-permute-start.7 = (bf16[256,512]{1,0:T(8,128)(2,1)}, bf16[256,512]{1,0:T(8,128)(2,1)S(1)}, u32[]{:S(2)}, u32[]{:S(2)}) collective-permute-start(bf16[256,512]{1,0:T(8,128)(2,1)} %get-tuple-element.141), channel_id=1, source_target_pairs={{0,2},{1,3},{2,0},{3,1},{4,6},{5,7},{6,4},{7,5},{8,10},{9,11},{10,... | collective-permute-start | bytes 786440 | tf_op jit(solution)/shard_map/ppermute | solution.py:90
  51.0 36.6 %collective-permute-start.10 = (bf16[256,512]{1,0:T(8,128)(2,1)}, bf16[256,512]{1,0:T(8,128)(2,1)S(1)}, u32[]{:S(2)}, u32[]{:S(2)}) collective-permute-start(bf16[256,512]{1,0:T(8,128)(2,1)} %get-tuple-element.143), channel_id=1, source_target_pairs={{0,1},{1,0},{2,3},{3,2},{4,5},{5,4},{6,7},{7,6},{8,9},{9,8},{10,11... | collective-permute-start | bytes 786440 | tf_op jit(solution)/shard_map/ppermute | solution.py:90
  58.4 29.2 %collective-permute-start.14 = (bf16[144,2048]{1,0:T(8,128)(2,1)}, bf16[144,2048]{1,0:T(8,128)(2,1)S(1)}, u32[]{:S(2)}, u32[]{:S(2)}) collective-permute-start(bf16[144,2048]{1,0:T(8,128)(2,1)} %collective-permute-done.1.refs_2_), channel_id=1, source_target_pairs={{0,2},{1,0},{2,4},{3,1},{4,6},{5,3},{6,7},{7,5},{8,10},{9,8},{10,1... | collective-permute-start | bytes 1769480 | tf_op jit(solution)/shard_map/ppermute | solution.py:90
  79.7 21.9 %collective-permute-start.15 = (bf16[144,2048]{1,0:T(8,128)(2,1)S(1)}, bf16[144,2048]{1,0:T(8,128)(2,1)S(1)}, u32[]{:S(2)}, u32[]{:S(2)}) collective-permute-start(bf16[144,2048]{1,0:T(8,128)(2,1)S(1)} %collective-permute-done.2.refs_3_), channel_id=1, source_target_pairs={{0,1},{1,3},{2,0},{3,5},{4,2},{5,7},{6,4},{7,6},{8,9},{9,11},{10,8... | collective-permute-start | bytes 1769480 | tf_op jit(solution)/shard_map/ppermute | solution.py:90
  84.1 76.1 %collective-permute-start.21 = (bf16[512,2048]{1,0:T(8,128)(2,1)}, bf16[512,2048]{1,0:T(8,128)(2,1)}, u32[]{:S(2)}, u32[]{:S(2)}) collective-permute-start(bf16[512,2048]{1,0:T(8,128)(2,1)} %bitcast.23.refs_7_.refs_9_.refs_8_), channel_id=1, source_target_pairs={{0,8},{8,0},{1,9},{9,1},{2,10},{10,2},{3,11},{11,3},{4,12},{12,4},... | collective-permute-start | bytes 6291464 | tf_op jit(solution)/shard_map/ppermute | solution.py:115
  85.3 57.3 %collective-permute-start.11 = (bf16[256,512]{1,0:T(8,128)(2,1)}, bf16[256,512]{1,0:T(8,128)(2,1)}, u32[]{:S(2)}, u32[]{:S(2)}) collective-permute-start(bf16[256,512]{1,0:T(8,128)(2,1)} %get-tuple-element.144), channel_id=1, source_target_pairs={{0,7},{1,6},{2,5},{3,4},{4,3},{5,2},{6,1},{7,0},{8,15},{9,14},{10,... | collective-permute-start | bytes 786440 | tf_op jit(solution)/shard_map/ppermute | solution.py:90
  87.6 27.3 %collective-permute-start.8 = (bf16[256,1024]{1,0:T(8,128)(2,1)S(1)}, bf16[256,1024]{1,0:T(8,128)(2,1)S(1)}, u32[]{:S(2)}, u32[]{:S(2)}) collective-permute-start(bf16[256,1024]{1,0:T(8,128)(2,1)S(1)} %copy-done.78), channel_id=1, source_target_pairs={{0,3},{1,0},{2,1},{3,2},{4,11},{5,8},{6,9},{7,10},{8,7},{9,4},{10,... | collective-permute-start | bytes 1572872 | tf_op jit(solution)/shard_map/ppermute | solution.py:217
  87.6 32.7 %collective-permute-start.16 = (bf16[144,2048]{1,0:T(8,128)(2,1)S(1)}, bf16[144,2048]{1,0:T(8,128)(2,1)S(1)}, u32[]{:S(2)}, u32[]{:S(2)}) collective-permute-start(bf16[144,2048]{1,0:T(8,128)(2,1)S(1)} %collective-permute-done.14.refs_0_.refs_4_), channel_id=1, source_target_pairs={{0,2},{1,0},{2,4},{3,1},{4,6},{5,3},{6,7},{7,5},{8,10},{9,8},{10,1... | collective-permute-start | bytes 1769480 | tf_op jit(solution)/shard_map/ppermute | solution.py:90
  101.6 35.8 %collective-permute-start.17 = (bf16[144,2048]{1,0:T(8,128)(2,1)S(1)}, bf16[144,2048]{1,0:T(8,128)(2,1)S(1)}, u32[]{:S(2)}, u32[]{:S(2)}) collective-permute-start(bf16[144,2048]{1,0:T(8,128)(2,1)S(1)} %collective-permute-done.15.refs_1_.refs_5_), channel_id=1, source_target_pairs={{0,1},{1,3},{2,0},{3,5},{4,2},{5,7},{6,4},{7,6},{8,9},{9,11},{10,8... | collective-permute-start | bytes 1769480 | tf_op jit(solution)/shard_map/ppermute | solution.py:90
  114.9 33.8 %collective-permute-start.12 = (bf16[256,512]{1,0:T(8,128)(2,1)}, bf16[256,512]{1,0:T(8,128)(2,1)}, u32[]{:S(2)}, u32[]{:S(2)}) collective-permute-start(bf16[256,512]{1,0:T(8,128)(2,1)} %get-tuple-element.145), channel_id=1, source_target_pairs={{0,6},{1,7},{2,4},{3,5},{4,2},{5,3},{6,0},{7,1},{8,14},{9,15},{10,... | collective-permute-start | bytes 786440 | tf_op jit(solution)/shard_map/ppermute | solution.py:90
  120.3 29.4 %collective-permute-start.13 = (bf16[256,512]{1,0:T(8,128)(2,1)}, bf16[256,512]{1,0:T(8,128)(2,1)}, u32[]{:S(2)}, u32[]{:S(2)}) collective-permute-start(bf16[256,512]{1,0:T(8,128)(2,1)} %get-tuple-element.146), channel_id=1, source_target_pairs={{0,5},{1,4},{2,7},{3,6},{4,1},{5,0},{6,3},{7,2},{8,13},{9,12},{10,... | collective-permute-start | bytes 786440 | tf_op jit(solution)/shard_map/ppermute | solution.py:90
  137.4 19.8 %collective-permute-start.9 = (bf16[1024,1024]{1,0:T(8,128)(2,1)}, bf16[1024,1024]{1,0:T(8,128)(2,1)}, u32[]{:S(2)}, u32[]{:S(2)}) collective-permute-start(bf16[1024,1024]{1,0:T(8,128)(2,1)} %constant_dynamic-update-slice_fusion.16), channel_id=1, source_target_pairs={{0,8},{8,0},{1,9},{9,1},{2,10},{10,2},{3,11},{11,3},{4,12},{12,4},... | collective-permute-start | bytes 6291464 | tf_op jit(solution)/shard_map/ppermute | solution.py:115
  174.5 19.0 %collective-permute-start.29 = (bf16[64,2048]{1,0:T(8,128)(2,1)S(1)}, bf16[64,2048]{1,0:T(8,128)(2,1)S(1)}, u32[]{:S(2)}, u32[]{:S(2)}) collective-permute-start(bf16[64,2048]{1,0:T(8,128)(2,1)S(1)} %get-tuple-element.158), channel_id=1, source_target_pairs={{0,2},{1,0},{2,4},{3,1},{4,6},{5,3},{6,7},{7,5},{8,10},{9,8},{10,1... | collective-permute-start | bytes 786440 | tf_op jit(solution)/shard_map/ppermute | solution.py:90
  176.8 16.9 %collective-permute-start.32 = (bf16[64,2048]{1,0:T(8,128)(2,1)S(1)}, bf16[64,2048]{1,0:T(8,128)(2,1)S(1)}, u32[]{:S(2)}, u32[]{:S(2)}) collective-permute-start(bf16[64,2048]{1,0:T(8,128)(2,1)S(1)} %get-tuple-element.161), channel_id=1, source_target_pairs={{0,1},{1,3},{2,0},{3,5},{4,2},{5,7},{6,4},{7,6},{8,9},{9,11},{10,8... | collective-permute-start | bytes 786440 | tf_op jit(solution)/shard_map/ppermute | solution.py:90
  178.8 17.0 %collective-permute-start.22 = (bf16[64,2048]{1,0:T(8,128)(2,1)S(1)}, bf16[64,2048]{1,0:T(8,128)(2,1)S(1)}, u32[]{:S(2)}, u32[]{:S(2)}) collective-permute-start(bf16[64,2048]{1,0:T(8,128)(2,1)S(1)} %get-tuple-element.150), channel_id=1, source_target_pairs={{0,2},{1,0},{2,4},{3,1},{4,6},{5,3},{6,7},{7,5},{8,10},{9,8},{10,1... | collective-permute-start | bytes 786440 | tf_op jit(solution)/shard_map/ppermute | solution.py:90
  178.9 17.1 %collective-permute-start.26 = (bf16[64,2048]{1,0:T(8,128)(2,1)S(1)}, bf16[64,2048]{1,0:T(8,128)(2,1)S(1)}, u32[]{:S(2)}, u32[]{:S(2)}) collective-permute-start(bf16[64,2048]{1,0:T(8,128)(2,1)S(1)} %get-tuple-element.154), channel_id=1, source_target_pairs={{0,1},{1,3},{2,0},{3,5},{4,2},{5,7},{6,4},{7,6},{8,9},{9,11},{10,8... | collective-permute-start | bytes 786440 | tf_op jit(solution)/shard_map/ppermute | solution.py:90
  243.4 17.7 %collective-permute-start.40 = (bf16[64,2048]{1,0:T(8,128)(2,1)S(1)}, bf16[64,2048]{1,0:T(8,128)(2,1)S(1)}, u32[]{:S(2)}, u32[]{:S(2)}) collective-permute-start(bf16[64,2048]{1,0:T(8,128)(2,1)S(1)} %get-tuple-element.279.refs_0_), channel_id=1, source_target_pairs={{0,2},{1,0},{2,4},{3,1},{4,6},{5,3},{6,7},{7,5},{8,10},{9,8},{10,1... | collective-permute-start | bytes 786440 | tf_op jit(solution)/shard_map/ppermute | solution.py:90
  272.5 21.0 %collective-permute-start.42 = (bf16[64,2048]{1,0:T(8,128)(2,1)S(1)}, bf16[64,2048]{1,0:T(8,128)(2,1)S(1)}, u32[]{:S(2)}, u32[]{:S(2)}) collective-permute-start(bf16[64,2048]{1,0:T(8,128)(2,1)S(1)} %collective-permute-done.41.refs_0_), channel_id=1, source_target_pairs={{0,2},{1,0},{2,4},{3,1},{4,6},{5,3},{6,7},{7,5},{8,10},{9,8},{10,1... | collective-permute-start | bytes 786440 | tf_op jit(solution)/shard_map/ppermute | solution.py:90
  292.3 17.0 %collective-permute-start.60 = (bf16[64,2048]{1,0:T(8,128)(2,1)S(1)}, bf16[64,2048]{1,0:T(8,128)(2,1)S(1)}, u32[]{:S(2)}, u32[]{:S(2)}) collective-permute-start(bf16[64,2048]{1,0:T(8,128)(2,1)S(1)} %get-tuple-element.197), channel_id=1, source_target_pairs={{0,2},{1,0},{2,4},{3,1},{4,6},{5,3},{6,7},{7,5},{8,10},{9,8},{10,1... | collective-permute-start | bytes 786440 | tf_op jit(solution)/shard_map/ppermute | solution.py:90
  320.9 18.9 %collective-permute-start.62 = (bf16[64,2048]{1,0:T(8,128)(2,1)S(1)}, bf16[64,2048]{1,0:T(8,128)(2,1)S(1)}, u32[]{:S(2)}, u32[]{:S(2)}) collective-permute-start(bf16[64,2048]{1,0:T(8,128)(2,1)S(1)} %add_convert_fusion.10), channel_id=1, source_target_pairs={{0,2},{1,0},{2,4},{3,1},{4,6},{5,3},{6,7},{7,5},{8,10},{9,8},{10,1... | collective-permute-start | bytes 786440 | tf_op jit(solution)/shard_map/ppermute | solution.py:90
  362.1 26.8 %collective-permute-start.76 = (bf16[64,2048]{1,0:T(8,128)(2,1)}, bf16[64,2048]{1,0:T(8,128)(2,1)S(1)}, u32[]{:S(2)}, u32[]{:S(2)}) collective-permute-start(bf16[64,2048]{1,0:T(8,128)(2,1)} %collective-permute-done.68.refs_2_), channel_id=1, source_target_pairs={{0,1},{1,3},{2,0},{3,5},{4,2},{5,7},{6,4},{7,6},{8,9},{9,11},{10,8... | collective-permute-start | bytes 786440 | tf_op jit(solution)/shard_map/ppermute | solution.py:90
  364.9 25.2 %collective-permute-start.80 = (bf16[64,2048]{1,0:T(8,128)(2,1)}, bf16[64,2048]{1,0:T(8,128)(2,1)S(1)}, u32[]{:S(2)}, u32[]{:S(2)}) collective-permute-start(bf16[64,2048]{1,0:T(8,128)(2,1)} %collective-permute-done.69.refs_3_), channel_id=1, source_target_pairs={{0,1},{1,3},{2,0},{3,5},{4,2},{5,7},{6,4},{7,6},{8,9},{9,11},{10,8... | collective-permute-start | bytes 786440 | tf_op jit(solution)/shard_map/ppermute | solution.py:90
  366.1 26.0 %collective-permute-start.71 = (bf16[64,2048]{1,0:T(8,128)(2,1)}, bf16[64,2048]{1,0:T(8,128)(2,1)S(1)}, u32[]{:S(2)}, u32[]{:S(2)}) collective-permute-start(bf16[64,2048]{1,0:T(8,128)(2,1)} %collective-permute-done.70.refs_0_), channel_id=1, source_target_pairs={{0,2},{1,0},{2,4},{3,1},{4,6},{5,3},{6,7},{7,5},{8,10},{9,8},{10,1... | collective-permute-start | bytes 786440 | tf_op jit(solution)/shard_map/ppermute | solution.py:90
  367.3 23.5 %collective-permute-start.74 = (bf16[64,2048]{1,0:T(8,128)(2,1)}, bf16[64,2048]{1,0:T(8,128)(2,1)S(1)}, u32[]{:S(2)}, u32[]{:S(2)}) collective-permute-start(bf16[64,2048]{1,0:T(8,128)(2,1)} %collective-permute-done.73.refs_1_), channel_id=1, source_target_pairs={{0,2},{1,0},{2,4},{3,1},{4,6},{5,3},{6,7},{7,5},{8,10},{9,8},{10,1... | collective-permute-start | bytes 786440 | tf_op jit(solution)/shard_map/ppermute | solution.py:90
  392.1 25.4 %collective-permute-start.72 = (bf16[64,2048]{1,0:T(8,128)(2,1)S(1)}, bf16[64,2048]{1,0:T(8,128)(2,1)S(1)}, u32[]{:S(2)}, u32[]{:S(2)}) collective-permute-start(bf16[64,2048]{1,0:T(8,128)(2,1)S(1)} %collective-permute-done.71.refs_0_), channel_id=1, source_target_pairs={{0,2},{1,0},{2,4},{3,1},{4,6},{5,3},{6,7},{7,5},{8,10},{9,8},{10,1... | collective-permute-start | bytes 786440 | tf_op jit(solution)/shard_map/ppermute | solution.py:90
  450.3 41.7 %collective-permute-start.99 = (bf16[2048,512]{1,0:T(8,128)(2,1)S(1)}, bf16[2048,512]{1,0:T(8,128)(2,1)S(1)}, u32[]{:S(2)}, u32[]{:S(2)}) collective-permute-start(bf16[2048,512]{1,0:T(8,128)(2,1)S(1)} %convolution_convert_fusion.1), channel_id=1, source_target_pairs={{0,8},{8,0},{1,9},{9,1},{2,10},{10,2},{3,11},{11,3},{4,12},{12,4},... | collective-permute-start | bytes 6291464 | tf_op jit(solution)/shard_map/ppermute | solution.py:115
  468.0 20.6 %collective-permute-start.86 = (bf16[128,2048]{1,0:T(8,128)(2,1)S(1)}, bf16[128,2048]{1,0:T(8,128)(2,1)S(1)}, u32[]{:S(2)}, u32[]{:S(2)}) collective-permute-start(bf16[128,2048]{1,0:T(8,128)(2,1)S(1)} %add_convert_fusion.6), channel_id=1, source_target_pairs={{0,2},{1,0},{2,4},{3,1},{4,6},{5,3},{6,7},{7,5},{8,10},{9,8},{10,1... | collective-permute-start | bytes 1572872 | tf_op jit(solution)/shard_map/ppermute | solution.py:90
  470.5 54.4 %collective-permute-start.98 = (bf16[256,1024]{1,0:T(8,128)(2,1)S(1)}, bf16[256,1024]{1,0:T(8,128)(2,1)S(1)}, u32[]{:S(2)}, u32[]{:S(2)}) collective-permute-start(bf16[256,1024]{1,0:T(8,128)(2,1)S(1)} %pad_maximum_fusion.8), channel_id=1, source_target_pairs={{1,0},{2,1},{3,2},{0,3},{9,4},{10,5},{11,6},{8,7},{5,8},{6,9},{7,1... | collective-permute-start | bytes 1572872 | tf_op jit(solution)/shard_map/ppermute | solution.py:221
  470.7 24.1 %collective-permute-start.97 = (bf16[256,1024]{1,0:T(8,128)(2,1)S(1)}, bf16[256,1024]{1,0:T(8,128)(2,1)S(1)}, u32[]{:S(2)}, u32[]{:S(2)}) collective-permute-start(bf16[256,1024]{1,0:T(8,128)(2,1)S(1)} %pad_maximum_fusion.7), channel_id=1, source_target_pairs={{0,0},{1,1},{2,2},{3,3},{8,4},{9,5},{10,6},{11,7},{4,8},{5,9},{6,1... | collective-permute-start | bytes 1572872 | tf_op jit(solution)/shard_map/ppermute | solution.py:221
  471.6 35.7 %collective-permute-start.90 = (bf16[128,2048]{1,0:T(8,128)(2,1)S(1)}, bf16[128,2048]{1,0:T(8,128)(2,1)S(1)}, u32[]{:S(2)}, u32[]{:S(2)}) collective-permute-start(bf16[128,2048]{1,0:T(8,128)(2,1)S(1)} %add_convert_fusion.3), channel_id=1, source_target_pairs={{0,1},{1,3},{2,0},{3,5},{4,2},{5,7},{6,4},{7,6},{8,9},{9,11},{10,8... | collective-permute-start | bytes 1572872 | tf_op jit(solution)/shard_map/ppermute | solution.py:90
  488.7 27.9 %collective-permute-start.87 = (bf16[128,2048]{1,0:T(8,128)(2,1)S(1)}, bf16[128,2048]{1,0:T(8,128)(2,1)S(1)}, u32[]{:S(2)}, u32[]{:S(2)}) collective-permute-start(bf16[128,2048]{1,0:T(8,128)(2,1)S(1)} %add_convert_fusion.5), channel_id=1, source_target_pairs={{0,2},{1,0},{2,4},{3,1},{4,6},{5,3},{6,7},{7,5},{8,10},{9,8},{10,1... | collective-permute-start | bytes 1572872 | tf_op jit(solution)/shard_map/ppermute | solution.py:90
  494.9 21.8 %collective-permute-start.102 = (bf16[256,512]{1,0:T(8,128)(2,1)S(1)}, bf16[256,512]{1,0:T(8,128)(2,1)S(1)}, u32[]{:S(2)}, u32[]{:S(2)}) collective-permute-start(bf16[256,512]{1,0:T(8,128)(2,1)S(1)} %get-tuple-element.252), channel_id=1, source_target_pairs={{0,2},{1,3},{2,0},{3,1},{4,6},{5,7},{6,4},{7,5},{8,10},{9,11},{10,... | collective-permute-start | bytes 786440 | tf_op jit(solution)/shard_map/ppermute | solution.py:90
  507.4 44.3 %collective-permute-start.91 = (bf16[128,2048]{1,0:T(8,128)(2,1)S(1)}, bf16[128,2048]{1,0:T(8,128)(2,1)S(1)}, u32[]{:S(2)}, u32[]{:S(2)}) collective-permute-start(bf16[128,2048]{1,0:T(8,128)(2,1)S(1)} %add_convert_fusion.2), channel_id=1, source_target_pairs={{0,1},{1,3},{2,0},{3,5},{4,2},{5,7},{6,4},{7,6},{8,9},{9,11},{10,8... | collective-permute-start | bytes 1572872 | tf_op jit(solution)/shard_map/ppermute | solution.py:90
  507.5 26.0 %collective-permute-start.101 = (bf16[256,1024]{1,0:T(8,128)(2,1)S(1)}, bf16[256,1024]{1,0:T(8,128)(2,1)S(1)}, u32[]{:S(2)}, u32[]{:S(2)}) collective-permute-start(bf16[256,1024]{1,0:T(8,128)(2,1)S(1)} %pad_maximum_fusion.9), channel_id=1, source_target_pairs={{2,0},{3,1},{0,2},{1,3},{10,4},{11,5},{8,6},{9,7},{6,8},{7,9},{4,1... | collective-permute-start | bytes 1572872 | tf_op jit(solution)/shard_map/ppermute | solution.py:221
  516.6 21.4 %collective-permute-start.103 = (bf16[256,1024]{1,0:T(8,128)(2,1)S(1)}, bf16[256,1024]{1,0:T(8,128)(2,1)S(1)}, u32[]{:S(2)}, u32[]{:S(2)}) collective-permute-start(bf16[256,1024]{1,0:T(8,128)(2,1)S(1)} %pad_maximum_fusion.10), channel_id=1, source_target_pairs={{3,0},{0,1},{1,2},{2,3},{11,4},{8,5},{9,6},{10,7},{7,8},{4,9},{5,1... | collective-permute-start | bytes 1572872 | tf_op jit(solution)/shard_map/ppermute | solution.py:221
  516.8 36.5 %collective-permute-start.88 = (bf16[128,2048]{1,0:T(8,128)(2,1)S(1)}, bf16[128,2048]{1,0:T(8,128)(2,1)S(1)}, u32[]{:S(2)}, u32[]{:S(2)}) collective-permute-start(bf16[128,2048]{1,0:T(8,128)(2,1)S(1)} %add_convert_fusion.4), channel_id=1, source_target_pairs={{0,2},{1,0},{2,4},{3,1},{4,6},{5,3},{6,7},{7,5},{8,10},{9,8},{10,1... | collective-permute-start | bytes 1572872 | tf_op jit(solution)/shard_map/ppermute | solution.py:90
  524.9 56.2 %collective-permute-start.108 = (bf16[512,2048]{1,0:T(8,128)(2,1)S(1)}, bf16[512,2048]{1,0:T(8,128)(2,1)S(1)}, u32[]{:S(2)}, u32[]{:S(2)}) collective-permute-start(bf16[512,2048]{1,0:T(8,128)(2,1)S(1)} %convolution_convert_fusion), channel_id=1, source_target_pairs={{0,8},{8,0},{1,9},{9,1},{2,10},{10,2},{3,11},{11,3},{4,12},{12,4},... | collective-permute-start | bytes 6291464 | tf_op jit(solution)/shard_map/ppermute | solution.py:115
  533.5 52.1 %collective-permute-start.107 = (bf16[256,512]{1,0:T(8,128)(2,1)S(1)}, bf16[256,512]{1,0:T(8,128)(2,1)S(1)}, u32[]{:S(2)}, u32[]{:S(2)}) collective-permute-start(bf16[256,512]{1,0:T(8,128)(2,1)S(1)} %get-tuple-element.260), channel_id=1, source_target_pairs={{0,1},{1,0},{2,3},{3,2},{4,5},{5,4},{6,7},{7,6},{8,9},{9,8},{10,11... | collective-permute-start | bytes 786440 | tf_op jit(solution)/shard_map/ppermute | solution.py:90
  538.0 38.6 %collective-permute-start.104 = (bf16[256,512]{1,0:T(8,128)(2,1)S(1)}, bf16[256,512]{1,0:T(8,128)(2,1)S(1)}, u32[]{:S(2)}, u32[]{:S(2)}) collective-permute-start(bf16[256,512]{1,0:T(8,128)(2,1)S(1)} %get-tuple-element.257), channel_id=1, source_target_pairs={{0,7},{1,6},{2,5},{3,4},{4,3},{5,2},{6,1},{7,0},{8,15},{9,14},{10,... | collective-permute-start | bytes 786440 | tf_op jit(solution)/shard_map/ppermute | solution.py:90
  551.7 50.5 %collective-permute-start.106 = (bf16[256,512]{1,0:T(8,128)(2,1)S(1)}, bf16[256,512]{1,0:T(8,128)(2,1)S(1)}, u32[]{:S(2)}, u32[]{:S(2)}) collective-permute-start(bf16[256,512]{1,0:T(8,128)(2,1)S(1)} %get-tuple-element.259), channel_id=1, source_target_pairs={{0,5},{1,4},{2,7},{3,6},{4,1},{5,0},{6,3},{7,2},{8,13},{9,12},{10,... | collective-permute-start | bytes 786440 | tf_op jit(solution)/shard_map/ppermute | solution.py:90
  576.6 25.6 %collective-permute-start.105 = (bf16[256,512]{1,0:T(8,128)(2,1)S(1)}, bf16[256,512]{1,0:T(8,128)(2,1)S(1)}, u32[]{:S(2)}, u32[]{:S(2)}) collective-permute-start(bf16[256,512]{1,0:T(8,128)(2,1)S(1)} %get-tuple-element.258), channel_id=1, source_target_pairs={{0,4},{1,5},{2,6},{3,7},{4,0},{5,1},{6,2},{7,3},{8,12},{9,13},{10,... | collective-permute-start | bytes 786440 | tf_op jit(solution)/shard_map/ppermute | solution.py:90
  (154 other events, 1928.1 us)

commit v5 on v4

--- a/solution.py
+++ b/solution.py
@@ -196,7 +196,7 @@
         return totals
 
     def head_turn(self, chip, turn):
-        return (chip % self.core_heads + turn) % self.core_heads
+        return (chip % self.core_heads) ^ turn
 
     def head_route(self, turn):
         pairs = []
@@ -323,55 +323,45 @@
 
 def forward_kernel(count, pieces, *refs):
     blocks, refs = refs[:count], refs[count:]
-    heads, wu0, wu1, wd0, wd1, bq, bu, ratio, cosine, sine, mask = refs[:11]
-    outs, refs = refs[11 : 11 + pieces], refs[11 + pieces :]
+    heads, wu, wd, bq, bu, ratio, cosine, sine, mask = refs[:9]
+    outs, refs = refs[9 : 9 + pieces], refs[9 + pieces :]
     first_norm, second_norm, attended, active, wo = refs
     wq = split_heads(heads, wo)
     length = mask.shape[1]
-    part = wu0.shape[1]
     load_rows(blocks, first_norm, ratio[0:1])
     load_rows(blocks, second_norm, ratio[1:2])
     joined = matmul(first_norm[...], wq[...]) + bq[...]
     for s in range(mask.shape[0] // length):
         rows = slice(s * length, (s + 1) * length)
         attended[rows] = attend(joined[rows], cosine[rows], sine[rows], mask[rows])[4]
-    for k, wu in enumerate((wu0, wu1)):
-        for cols in steps(part):
-            at = slice(k * part + cols.start, k * part + cols.stop)
-            hidden = matmul(second_norm[...], wu[:, cols]) + bu[:, at]
-            active[:, at] = (hidden * (0.5 * (1.0 + lax.erf(hidden * ROOT_HALF)))).astype(BF16)
+    for cols in steps(wu.shape[1]):
+        hidden = matmul(second_norm[...], wu[:, cols]) + bu[:, cols]
+        active[:, cols] = (hidden * (0.5 * (1.0 + lax.erf(hidden * ROOT_HALF)))).astype(BF16)
     for cols in steps(wo.shape[1]):
-        total = (
-            matmul(attended[...], wo[:, cols])
-            + matmul(active[:, :part], wd0[:, cols])
-            + matmul(active[:, part:], wd1[:, cols])
-        )
+        total = matmul(attended[...], wo[:, cols]) + matmul(active[...], wd[:, cols])
         store_rows(outs, cols, total)
 
 
 def upstream_kernel(count, *refs):
     grads, refs = refs[:count], refs[count:]
-    heads, wd0, wd1, attended_grad, active_grad, upstream, wo = refs
+    heads, wd, attended_grad, active_grad, upstream, wo = refs
     split_heads(heads, wo)
-    part = wd0.shape[0]
     load_rows(grads, upstream)
     attended_grad[...] = contract_cols(upstream[...], wo[...]).astype(BF16)
-    for k, wd in enumerate((wd0, wd1)):
-        for rows in steps(part):
-            at = slice(k * part + rows.start, k * part + rows.stop)
-            active_grad[:, at] = contract_cols(upstream[...], wd[rows]).astype(BF16)
+    for rows in steps(wd.shape[0]):
+        active_grad[:, rows] = contract_cols(upstream[...], wd[rows]).astype(BF16)
 
 
 def both_kernel(count, pieces, chained, *refs):
     blocks, refs = refs[:count], refs[count:]
-    heads, wu0, wu1, bq, bu, ratio, cosine, sine, mask, attended_grad, active_grad = refs[:11]
-    refs = refs[11 + chained :]
+    heads, wu, bq, bu, ratio, cosine, sine, mask, attended_grad, active_grad = refs[:10]
+    refs = refs[10 + chained :]
     first_norm, second_norm, qkv, attention, attended, active, slope = refs[:7]
     outs, (joined_grad, hidden_grad) = refs[7 : 7 + pieces], refs[7 + pieces :]
     length = mask.shape[1]
     size = attended_grad.shape[1]
     wq = heads.at[:, : 3 * size]
-    part = wu0.shape[1]
+    part = wu.shape[1] // 2
     load_rows(blocks, first_norm, ratio[0:1])
     load_rows(blocks, second_norm, ratio[1:2])
     joined = matmul(first_norm[...], wq[...]) + bq[...]
@@ -390,11 +380,11 @@
             queries, key_rows, values, weights, attended_grad[rows], cosine[rows], sine[rows]
         )
 
-    for k, wu in enumerate((wu0, wu1)):
+    for k in range(2):
         attention_of(k)
         for cols in steps(part):
             at = slice(k * part + cols.start, k * part + cols.stop)
-            hidden = matmul(second_norm[...], wu[:, cols]) + bu[:, at]
+            hidden = matmul(second_norm[...], wu[:, at]) + bu[:, at]
             normal_cdf = 0.5 * (1.0 + lax.erf(hidden * ROOT_HALF))
             normal_pdf = jnp.exp(-0.5 * hidden * hidden) * DENSITY_SCALE
             active[:, at] = (hidden * normal_cdf).astype(BF16)
@@ -402,28 +392,26 @@
             slope[:, at] = change.astype(BF16)
             hidden_grad[:, at] = (active_grad[:, at].astype(F32) * change).astype(BF16)
     for rows in steps(wq.shape[0]):
-        total = (
-            contract_cols(joined_grad[...], wq[rows])
-            + contract_cols(hidden_grad[:, :part], wu0[rows])
-            + contract_cols(hidden_grad[:, part:], wu1[rows])
+        total = contract_cols(joined_grad[...], wq[rows]) + contract_cols(
+            hidden_grad[...], wu[rows]
         )
         store_rows(outs, rows, total)
 
 
 def backward_kernel(count, pieces, chained, *refs):
     grads, refs = refs[:count], refs[count:]
-    second, heads, wu0, wu1, wd0, wd1, cosine, sine = refs[:8]
-    first_norm, second_norm, qkv, attention, attended, active, slope = refs[8:15]
-    refs = refs[15 + chained :]
+    second, heads, wu, wd, cosine, sine = refs[:6]
+    first_norm, second_norm, qkv, attention, attended, active, slope = refs[6:13]
+    refs = refs[13 + chained :]
     upstream, joined_grad, hidden_grad, norm_sums, joined_sum, hidden_sum = refs[:6]
     outs, wo = refs[6 : 6 + pieces], refs[6 + pieces]
     wq = split_heads(heads, wo)
     length = attention.shape[1]
     size = wo.shape[0]
-    part = wu0.shape[1]
+    part = wu.shape[1] // 2
     load_rows(grads, upstream)
     attended_grad = contract_cols(upstream[...], wo[...]).astype(BF16)
-    for k, wd in enumerate((wd0, wd1)):
+    for k in range(2):
         rows = slice(k * length, (k + 1) * length)
         joined_grad[rows] = attend_back(
             qkv[rows, :size],
@@ -436,16 +424,14 @@
         )
         for cols in steps(part):
             at = slice(k * part + cols.start, k * part + cols.stop)
-            active_grad = contract_cols(upstream[...], wd[cols])
+            active_grad = contract_cols(upstream[...], wd[at])
             grad = (active_grad * slope[:, at].astype(F32)).astype(BF16)
             hidden_grad[:, at] = grad
             hidden_sum[:, at] = fold_rows(grad.astype(F32))
     joined_sum[...] = fold_rows(joined_grad[...].astype(F32))
     for rows in steps(wq.shape[0]):
         first = contract_cols(joined_grad[...], wq[rows])
-        other = contract_cols(hidden_grad[:, :part], wu0[rows]) + contract_cols(
-            hidden_grad[:, part:], wu1[rows]
-        )
+        other = contract_cols(hidden_grad[...], wu[rows])
         norm_sums[0:8, rows] = fold_rows(first * first_norm[:, rows].astype(F32))
         norm_sums[8:16, rows] = fold_rows(other * second_norm[:, rows].astype(F32))
         norm_sums[16:24, rows] = fold_rows(first)
@@ -455,11 +441,7 @@
     @pl.when(second[0] != 0)
     def _():
         for cols in steps(wq.shape[0]):
-            total = (
-                matmul(attended[...], wo[:, cols])
-                + matmul(active[:, :part], wd0[:, cols])
-                + matmul(active[:, part:], wd1[:, cols])
-            )
+            total = matmul(attended[...], wo[:, cols]) + matmul(active[...], wd[:, cols])
             store_rows(outs, cols, total)
 
 
@@ -637,7 +619,7 @@
     up_scaled = layout.gather_groups(up_scaled, 0)
     out_shard = layout.gather_groups(out_weight[0], 1)
     wd0 = layout.gather_groups(down_weight[0], 0)
-    wd1 = layout.other_core(wd0)
+    wd = jnp.concatenate([wd0, layout.other_core(wd0)], axis=0)
     block_rows = qkv_scaled.shape[0]
 
     ratio = shifts / gains
@@ -683,17 +665,17 @@
         if k == 3:
             block = ordered(block, *up_blocks)
         if k == len(order) - 1:
-            block = ordered(block, cosine, sine, mask, bq, bu)
+            block = ordered(block, cosine, sine, mask, bq, bu, wd)
         block = queue.ready(block)
         if kind == "head":
             block = layout.send_head(block, which)
-            slot = (chip - which) % core_heads
+            slot = layout.head_turn(chip, which)
             heads = lax.dynamic_update_slice_in_dim(heads, block, slot * block_rows, 0)
         else:
             block = layout.swap(block, which)
             wu0 = lax.dynamic_update_slice_in_dim(wu0, block, (chip ^ which) * block_rows, 0)
         queue.put(block)
-    wu1 = layout.other_core(wu0)
+    wu = jnp.concatenate([wu0, layout.other_core(wu0)], axis=1)
     heads = layout.by_core(heads, layout.other_core(heads))
 
     row_bias = (out_bias[0].astype(F32) + down_bias[0].astype(F32))[None]
@@ -724,7 +706,7 @@
     cotangent_blocks = [block for slot in layout.slots for block in gathered[slot]]
     attended_grad, active_grad = call_rows(
         functools.partial(upstream_kernel, len(cotangent_blocks)),
-        (*cotangent_blocks, heads, wd0, wd1),
+        (*cotangent_blocks, heads, wd),
         (),
         None,
         (),
@@ -735,7 +717,7 @@
         2 * row_count * width * (head_size + hidden_size),
     )
 
-    matrices = (heads, wu0, wu1, wd0, wd1)
+    matrices = (heads, wu, wd)
     pieces = {}
     for at in (1, 0):
         slots = layout.slots[at * chips // 2 : (at + 1) * chips // 2]
@@ -768,7 +750,7 @@
     ]
 
     layer_input = [
-        jnp.where(first_section, rows, lax.ppermute(sent, "section", [(0, 1)]).astype(F32))
+        jnp.where(first_section, rows, lax.ppermute(sent, "section", [(0, 1), (1, 0)]).astype(F32))
         for rows, sent in zip(parts_of(own_tokens), first_out)
     ]
     own_normed = [normalize(rows) for rows in layer_input]
@@ -788,7 +770,7 @@
         blocks = pair_blocks(normed_blocks, pair)
         results = call_rows(
             functools.partial(both_kernel, len(blocks), 4, len(kept_shapes) if kept else 0),
-            (*blocks, heads, wu0, wu1, bq, bu, ratio),
+            (*blocks, heads, wu, bq, bu, ratio),
             (cosine, sine, mask, attended_grad, active_grad),
             kept,
             kept_shapes,
@@ -811,7 +793,7 @@
     ]
 
     arrived_grad = [
-        lax.ppermute(rows.astype(BF16), "section", [(1, 0)]) for rows in second_grad
+        lax.ppermute(rows.astype(BF16), "section", [(0, 1), (1, 0)]) for rows in second_grad
     ]
     own_upstream = [
         jnp.where(first_section, arrived, given)
@@ -917,7 +899,7 @@
     share_rows = out_rows // layout.groups
     head_blocks = []
     for turn in range(core_heads):
-        slot = (chip - turn) % core_heads
+        slot = layout.head_turn(chip, turn)
         out_part = lax.dynamic_slice_in_dim(out_held, slot * out_rows, out_rows, 0)
         out_part = out_part.reshape(layout.groups, share_rows, width // head_size, head_size)
         head_blocks.append(

time: 613 us -> 593 us (0.967)
  Pallas kernels: 109 us -> 86.3 us
    pallas_call x11, Pallas kernels: 100 us -> 78 us  [call_rows(): pl.pallas_call(kernel, grid=(1,), out_shape=out_shape, in_specs=in_specs,...]
    ppermute x87, waiting for transfers between devices: 201 us -> 188 us  [between_chips(): return lax.ppermute(block, 'dp', pairs)]
    ppermute x87, starting transfers between devices: 116 us -> 107 us  [between_chips(): return lax.ppermute(block, 'dp', pairs)]
    ppermute x4, waiting for transfers between devices: 13.1 us -> 21.5 us  [send_head(): return lax.ppermute(block, ('tensor', 'dp'), self.head_route(turn))]
    ppermute x4, starting transfers between devices: 9.22 us -> 16.2 us  [send_head(): return lax.ppermute(block, ('tensor', 'dp'), self.head_route(turn))]
    concatenate x0 -> x2, other arithmetic: none -> 6.64 us  [the longest x1 4.04 us: on_device(): wu = jnp.concatenate([wu0, layout.other_core(wu0)], axis=1)]
    unnamed x204 -> x218, local copies, waits for them, and re-layouts: 38 us -> 36.6 us
  transfers between devices with their start and end apart: 110 -> 110, of which waited for: 44 -> 44; matrix products, arithmetic and copies ran while one was open for 11% -> 12% of each run, Pallas kernels for 14% -> 11%
where the time goes in v5:
time: 593 us; the launch traced here: 588 us
  waiting for transfers between devices  241 us (41%)
  starting transfers between devices  138 us (23%)
  Pallas kernels  86.3 us (15%)
  local copies, waits for them, and re-layouts  58.8 us (10%)
  other arithmetic  40.5 us (7%)
  matrix products  19.8 us (3%)
    ppermute x87, waiting for transfers between devices, between_chips(): return lax.ppermute(block, 'dp', pairs)  188 us
    ppermute x87, starting transfers between devices, between_chips(): return lax.ppermute(block, 'dp', pairs)  107 us
    pallas_call x11, Pallas kernels, call_rows(): pl.pallas_call(kernel, grid=(1,), out_shape=out_shape, in_specs=in_specs,...  78 us
    unnamed x218, local copies, waits for them, and re-layouts  36.6 us
    ppermute x4, waiting for transfers between devices, send_head(): return lax.ppermute(block, ('tensor', 'dp'), self.head_route(turn))  21.5 us
    dot_general x8, matrix products, contract_rows(): lax.dot_general(left_side, right_side, (((0,), (0,)), ((), ())), preferre...  19.8 us
    ppermute x4, starting transfers between devices, send_head(): return lax.ppermute(block, ('tensor', 'dp'), self.head_route(turn))  16.2 us
  transfers between devices with their start and end apart: 110, of which 44 were waited for; matrix products, arithmetic and copies ran while one was open for 12% of the time, Pallas kernels for 11%

profile of v5, /device:TPU:10, one launch (start us, length us, event | category | flops | bytes accessed | tf_op | source)
XLA Modules:
  0.0 587.7 jit_solution(17894686728967049132)
XLA Ops:
  8.8 3.5 copy.79
  15.9 5.4 collective-permute-start.3
  32.7 14.7 %collective-permute-done.5 = bf16[256,512]{1,0:T(8,128)(2,1)S(1)} collective-permute-done((bf16[256,512]{1,0:T(8,128)(2,1)S(1)}, bf16[256,512]{1,0:T(8,128)(2,1)S(1)}, u32[]{:S(2)}, u32[]{:S(2)}) %collective-permute-start.5) | collective-permute-done | bytes 262176 | tf_op jit(solution)/shard_map/ppermute | solution.py:90
  47.4 3.4 collective-permute-start.6
  60.4 5.2 collective-permute-done.6
  66.1 5.3 collective-permute-done.7
  73.9 5.9 %collective-permute-start.8 = (bf16[256,1024]{1,0:T(8,128)(2,1)S(1)}, bf16[256,1024]{1,0:T(8,128)(2,1)S(1)}, u32[]{:S(2)}, u32[]{:S(2)}) collective-permute-start(bf16[256,1024]{1,0:T(8,128)(2,1)S(1)} %copy-done.85), channel_id=1, source_target_pairs={{0,3},{1,2},{2,1},{3,0},{4,11},{5,10},{6,9},{7,8},{8,7},{9,6},{10,... | collective-permute-start | bytes 1572872 | tf_op jit(solution)/shard_map/ppermute | solution.py:217
  85.8 16.3 %collective-permute-done.8 = bf16[256,1024]{1,0:T(8,128)(2,1)S(1)} collective-permute-done((bf16[256,1024]{1,0:T(8,128)(2,1)S(1)}, bf16[256,1024]{1,0:T(8,128)(2,1)S(1)}, u32[]{:S(2)}, u32[]{:S(2)}) %collective-permute-start.8) | collective-permute-done | bytes 524320 | tf_op jit(solution)/shard_map/ppermute | solution.py:217
  102.1 5.3 collective-permute-start.12
  108.2 12.7 %collective-permute-done.15.refs_1_.refs_5_ = bf16[144,2048]{1,0:T(8,128)(2,1)S(1)} collective-permute-done((bf16[144,2048]{1,0:T(8,128)(2,1)S(1)}, bf16[144,2048]{1,0:T(8,128)(2,1)S(1)}, u32[]{:S(2)}, u32[]{:S(2)}) %collective-permute-start.15) | collective-permute-done | bytes 589856 | tf_op jit(solution)/shard_map/ppermute | solution.py:90
  126.3 21.3 %collective-permute-done.17.refs_3_.refs_7_ = bf16[144,2048]{1,0:T(8,128)(2,1)S(1)} collective-permute-done((bf16[144,2048]{1,0:T(8,128)(2,1)S(1)}, bf16[144,2048]{1,0:T(8,128)(2,1)S(1)}, u32[]{:S(2)}, u32[]{:S(2)}) %collective-permute-start.17) | collective-permute-done | bytes 589856 | tf_op jit(solution)/shard_map/ppermute | solution.py:90
  164.7 4.0 pad_maximum_fusion.2.refs_5_.refs_6_
  168.8 9.3 %shard_map.221 = (bf16[64,2048]{1,0:T(8,128)(2,1)S(1)}, bf16[64,2048]{1,0:T(8,128)(2,1)S(1)}, bf16[64,2048]{1,0:T(8,128)(2,1)S(1)}, bf16[64,2048]{1,0:T(8,128)(2...) custom-call(bf16[144,2048]{1,0:T(8,128)(2,1)S(1)} %copy-done.52, ...), custom_call_target="tpu_custom_call" | custom-call | flops 6442450944 | bytes 4194304 | tf_op jit(solution)/shard_map/pallas_call | solution.py:533
  182.4 9.3 %shard_map.220 = (bf16[64,2048]{1,0:T(8,128)(2,1)S(1)}, bf16[64,2048]{1,0:T(8,128)(2,1)S(1)}, bf16[64,2048]{1,0:T(8,128)(2,1)S(1)}, bf16[64,2048]{1,0:T(8,128)(2...) custom-call(bf16[144,2048]{1,0:T(8,128)(2,1)S(1)} %fusion.18.refs_0_, ...), custom_call_target="tpu_custom_call" | custom-call | flops 6442450944 | bytes 4194304 | tf_op jit(solution)/shard_map/pallas_call | solution.py:533
  196.2 4.8 collective-permute-done.30
  203.4 3.3 collective-permute-done.23
  209.0 4.9 collective-permute-done.34
  219.5 4.0 collective-permute-done.35
  225.9 7.2 %collective-permute-done.36 = bf16[64,2048]{1,0:T(8,128)(2,1)S(1)} collective-permute-done((bf16[64,2048]{1,0:T(8,128)(2,1)S(1)}, bf16[64,2048]{1,0:T(8,128)(2,1)S(1)}, u32[]{:S(2)}, u32[]{:S(2)}) %collective-permute-start.36) | collective-permute-done | bytes 262176 | tf_op jit(solution)/shard_map/ppermute | solution.py:753
  233.1 3.0 collective-permute-done.37
  249.6 5.6 shard_map.222
  259.3 5.5 shard_map.223
  265.0 3.2 collective-permute-done.50.refs_3_
  271.5 5.5 shard_map.224
  282.2 5.5 shard_map.225
  289.1 5.5 shard_map.226
  304.1 5.1 collective-permute-done.52
  326.5 5.1 collective-permute-done.65
  332.8 5.2 collective-permute-done.66
  341.8 4.3 collective-permute-done.59
  375.3 8.0 %shard_map.227 = (bf16[1024,2048]{1,0:T(8,128)(2,1)S(1)}, bf16[1024,768]{1,0:T(8,128)(2,1)S(1)}, bf16[1024,1024]{1,0:T(8,128)(2,1)S(1)}, f32[32,2048]{1,0:T(8,12...) custom-call(bf16[64,2048]{1,0:T(8,128)(2,1)} %get-tuple-element.321., ...), custom_call_target="tpu_custom_call" | custom-call | flops 3221225472 | bytes 2097152 | tf_op jit(solution)/shard_map/pallas_call | solution.py:533
  388.9 7.9 %shard_map.228 = (bf16[1024,2048]{1,0:T(8,128)(2,1)S(1)}, bf16[1024,768]{1,0:T(8,128)(2,1)S(1)}, bf16[1024,1024]{1,0:T(8,128)(2,1)S(1)}, f32[32,2048]{1,0:T(8,12...) custom-call(bf16[64,2048]{1,0:T(8,128)(2,1)} %collective-permute-don, ...), custom_call_target="tpu_custom_call", output_to_operand_aliasing={{0}: (17, {}), {1}: (18, {}), {2}: (19, {})} | custom-call | flops 3221225472 | bytes 2097152 | tf_op jit(solution)/shard_map/pallas_call | solution.py:533
  399.1 7.8 %shard_map.229 = (bf16[1024,2048]{1,0:T(8,128)(2,1)S(1)}, bf16[1024,768]{1,0:T(8,128)(2,1)S(1)}, bf16[1024,1024]{1,0:T(8,128)(2,1)S(1)}, f32[32,2048]{1,0:T(8,12...) custom-call(bf16[64,2048]{1,0:T(8,128)(2,1)S(1)} %collective-permute, ...), custom_call_target="tpu_custom_call", output_to_operand_aliasing={{0}: (17, {}), {1}: (18, {}), {2}: (19, {})} | custom-call | flops 3221225472 | bytes 2097152 | tf_op jit(solution)/shard_map/pallas_call | solution.py:533
  407.8 8.2 %shard_map.230 = (bf16[1024,2048]{1,0:T(8,128)(2,1)S(1)}, bf16[1024,768]{1,0:T(8,128)(2,1)S(1)}, bf16[1024,1024]{1,0:T(8,128)(2,1)S(1)}, f32[32,2048]{1,0:T(8,12...) custom-call(bf16[64,2048]{1,0:T(8,128)(2,1)S(1)} %collective-permute, ...), custom_call_target="tpu_custom_call", output_to_operand_aliasing={{0}: (17, {}), {1}: (18, {}), {2}: (19, {})} | custom-call | flops 3221225472 | bytes 2097152 | tf_op jit(solution)/shard_map/pallas_call | solution.py:533
  423.5 5.0 convolution_convert_fusion.1
  430.7 3.0 collective-permute-done.95
  446.0 5.6 collective-permute-done.82
  461.5 19.2 %collective-permute-done.86 = bf16[128,2048]{1,0:T(8,128)(2,1)S(1)} collective-permute-done((bf16[128,2048]{1,0:T(8,128)(2,1)S(1)}, bf16[128,2048]{1,0:T(8,128)(2,1)S(1)}, u32[]{:S(2)}, u32[]{:S(2)}) %collective-permute-start.86) | collective-permute-done | bytes 524320 | tf_op jit(solution)/shard_map/ppermute | solution.py:90
  486.5 7.8 %collective-permute-done.90 = bf16[128,2048]{1,0:T(8,128)(2,1)S(1)} collective-permute-done((bf16[128,2048]{1,0:T(8,128)(2,1)S(1)}, bf16[128,2048]{1,0:T(8,128)(2,1)S(1)}, u32[]{:S(2)}, u32[]{:S(2)}) %collective-permute-start.90) | collective-permute-done | bytes 524320 | tf_op jit(solution)/shard_map/ppermute | solution.py:90
  494.6 4.5 collective-permute-start.101
  499.1 3.5 collective-permute-done.102.refs_3_
  502.9 9.2 %collective-permute-start.88 = (bf16[128,2048]{1,0:T(8,128)(2,1)S(1)}, bf16[128,2048]{1,0:T(8,128)(2,1)S(1)}, u32[]{:S(2)}, u32[]{:S(2)}) collective-permute-start(bf16[128,2048]{1,0:T(8,128)(2,1)S(1)} %add_convert_fusion.4), channel_id=1, source_target_pairs={{0,2},{1,0},{2,4},{3,1},{4,6},{5,3},{6,7},{7,5},{8,10},{9,8},{10,1... | collective-permute-start | bytes 1572872 | tf_op jit(solution)/shard_map/ppermute | solution.py:90
  514.7 5.1 collective-permute-start.107
  519.9 11.3 %collective-permute-done.103.refs_4_ = bf16[256,1024]{1,0:T(8,128)(2,1)S(1)} collective-permute-done((bf16[256,1024]{1,0:T(8,128)(2,1)S(1)}, bf16[256,1024]{1,0:T(8,128)(2,1)S(1)}, u32[]{:S(2)}, u32[]{:S(2)}) %collective-permute-start.103) | collective-permute-done | bytes 524320 | tf_op jit(solution)/shard_map/ppermute | solution.py:221
  533.6 3.6 shard_map.232
  537.7 22.6 %collective-permute-done.104.refs_6_ = bf16[256,512]{1,0:T(8,128)(2,1)S(1)} collective-permute-done((bf16[256,512]{1,0:T(8,128)(2,1)S(1)}, bf16[256,512]{1,0:T(8,128)(2,1)S(1)}, u32[]{:S(2)}, u32[]{:S(2)}) %collective-permute-start.104) | collective-permute-done | bytes 262176 | tf_op jit(solution)/shard_map/ppermute | solution.py:90
  563.9 4.5 convert_add_fusion
  570.1 12.5 %collective-permute-done.109.refs_5_ = bf16[256,512]{1,0:T(8,128)(2,1)S(1)} collective-permute-done((bf16[256,512]{1,0:T(8,128)(2,1)S(1)}, bf16[256,512]{1,0:T(8,128)(2,1)S(1)}, u32[]{:S(2)}, u32[]{:S(2)}) %collective-permute-start.109) | collective-permute-done | bytes 262176 | tf_op jit(solution)/shard_map/ppermute | solution.py:90
  (569 shorter events, 235.7 us)
Async XLA Ops:
  6.5 50.7 %collective-permute-start = (bf16[144,2048]{1,0:T(8,128)(2,1)S(1)}, bf16[144,2048]{1,0:T(8,128)(2,1)S(1)}, u32[]{:S(2)}, u32[]{:S(2)}) collective-permute-start(bf16[144,2048]{1,0:T(8,128)(2,1)S(1)} %fusion.18.refs_0_), channel_id=1, source_target_pairs={{0,1},{1,3},{2,0},{3,5},{4,2},{5,7},{6,4},{7,6},{8,9},{9,11},{10,8... | collective-permute-start | bytes 1769480 | tf_op jit(solution)/shard_map/ppermute | solution.py:90
  7.0 52.2 %collective-permute-start.1 = (bf16[144,2048]{1,0:T(8,128)(2,1)S(1)}, bf16[144,2048]{1,0:T(8,128)(2,1)S(1)}, u32[]{:S(2)}, u32[]{:S(2)}) collective-permute-start(bf16[144,2048]{1,0:T(8,128)(2,1)S(1)} %fusion.18.refs_0_), channel_id=1, source_target_pairs={{0,2},{1,0},{2,4},{3,1},{4,6},{5,3},{6,7},{7,5},{8,10},{9,8},{10,1... | collective-permute-start | bytes 1769480 | tf_op jit(solution)/shard_map/ppermute | solution.py:90
  8.6 23.5 %collective-permute-start.18 = (f32[1,7168]{1,0:T(1,128)S(1)}, f32[1,7168]{1,0:T(1,128)S(1)}, u32[]{:S(2)}, u32[]{:S(2)}) collective-permute-start(f32[1,7168]{1,0:T(1,128)S(1)} %maximum_convert_fusion), channel_id=1, source_target_pairs={{0,8},{8,0},{1,9},{9,1},{2,10},{10,2},{3,11},{11,3},{4,12},{12,4},... | collective-permute-start | bytes 86024 | tf_op jit(solution)/shard_map/ppermute | solution.py:115
  15.9 31.5 %collective-permute-start.3 = (bf16[256,1024]{1,0:T(8,128)(2,1)}, bf16[256,1024]{1,0:T(8,128)(2,1)}, u32[]{:S(2)}, u32[]{:S(2)}) collective-permute-start(bf16[256,1024]{1,0:T(8,128)(2,1)} %pad_maximum_fusion.4), channel_id=1, source_target_pairs={{0,0},{1,1},{2,2},{3,3},{4,8},{5,9},{6,10},{7,11},{8,4},{9,5},{10,... | collective-permute-start | bytes 1572872 | tf_op jit(solution)/shard_map/ppermute | solution.py:217
  22.2 29.4 %collective-permute-start.4 = (bf16[256,1024]{1,0:T(8,128)(2,1)}, bf16[256,1024]{1,0:T(8,128)(2,1)}, u32[]{:S(2)}, u32[]{:S(2)}) collective-permute-start(bf16[256,1024]{1,0:T(8,128)(2,1)} %pad_maximum_fusion.5), channel_id=1, source_target_pairs={{0,1},{1,0},{2,3},{3,2},{4,9},{5,8},{6,11},{7,10},{8,5},{9,4},{10,... | collective-permute-start | bytes 1572872 | tf_op jit(solution)/shard_map/ppermute | solution.py:217
  32.1 15.3 %collective-permute-start.5 = (bf16[256,512]{1,0:T(8,128)(2,1)S(1)}, bf16[256,512]{1,0:T(8,128)(2,1)S(1)}, u32[]{:S(2)}, u32[]{:S(2)}) collective-permute-start(bf16[256,512]{1,0:T(8,128)(2,1)S(1)} %get-tuple-element.138), channel_id=1, source_target_pairs={{0,3},{1,2},{2,1},{3,0},{4,7},{5,6},{6,5},{7,4},{8,11},{9,10},{10,... | collective-permute-start | bytes 786440 | tf_op jit(solution)/shard_map/ppermute | solution.py:90
  47.4 73.9 %collective-permute-start.19 = (bf16[512,2048]{1,0:T(8,128)(2,1)}, bf16[512,2048]{1,0:T(8,128)(2,1)S(1)}, u32[]{:S(2)}, u32[]{:S(2)}) collective-permute-start(bf16[512,2048]{1,0:T(8,128)(2,1)} %bitcast.169), channel_id=1, source_target_pairs={{0,8},{8,0},{1,9},{9,1},{2,10},{10,2},{3,11},{11,3},{4,12},{12,4},... | collective-permute-start | bytes 6291464 | tf_op jit(solution)/shard_map/ppermute | solution.py:115
  47.4 18.1 %collective-permute-start.6 = (bf16[256,1024]{1,0:T(8,128)(2,1)S(1)}, bf16[256,1024]{1,0:T(8,128)(2,1)S(1)}, u32[]{:S(2)}, u32[]{:S(2)}) collective-permute-start(bf16[256,1024]{1,0:T(8,128)(2,1)S(1)} %copy-done.86), channel_id=1, source_target_pairs={{0,2},{1,3},{2,0},{3,1},{4,10},{5,11},{6,8},{7,9},{8,6},{9,7},{10,... | collective-permute-start | bytes 1572872 | tf_op jit(solution)/shard_map/ppermute | solution.py:217
  51.6 19.8 %collective-permute-start.7 = (bf16[256,512]{1,0:T(8,128)(2,1)}, bf16[256,512]{1,0:T(8,128)(2,1)S(1)}, u32[]{:S(2)}, u32[]{:S(2)}) collective-permute-start(bf16[256,512]{1,0:T(8,128)(2,1)} %get-tuple-element.141), channel_id=1, source_target_pairs={{0,2},{1,3},{2,0},{3,1},{4,6},{5,7},{6,4},{7,5},{8,10},{9,11},{10,... | collective-permute-start | bytes 786440 | tf_op jit(solution)/shard_map/ppermute | solution.py:90
  57.1 24.3 %collective-permute-start.2 = (bf16[144,2048]{1,0:T(8,128)(2,1)S(1)}, bf16[144,2048]{1,0:T(8,128)(2,1)S(1)}, u32[]{:S(2)}, u32[]{:S(2)}) collective-permute-start(bf16[144,2048]{1,0:T(8,128)(2,1)S(1)} %collective-permute-done.refs_1_), channel_id=1, source_target_pairs={{0,1},{1,3},{2,0},{3,5},{4,2},{5,7},{6,4},{7,6},{8,9},{9,11},{10,8... | collective-permute-start | bytes 1769480 | tf_op jit(solution)/shard_map/ppermute | solution.py:90
  59.2 25.5 %collective-permute-start.14 = (bf16[144,2048]{1,0:T(8,128)(2,1)S(1)}, bf16[144,2048]{1,0:T(8,128)(2,1)S(1)}, u32[]{:S(2)}, u32[]{:S(2)}) collective-permute-start(bf16[144,2048]{1,0:T(8,128)(2,1)S(1)} %collective-permute-done.1.refs_2_), channel_id=1, source_target_pairs={{0,2},{1,0},{2,4},{3,1},{4,6},{5,3},{6,7},{7,5},{8,10},{9,8},{10,1... | collective-permute-start | bytes 1769480 | tf_op jit(solution)/shard_map/ppermute | solution.py:90
  71.4 80.7 %collective-permute-start.11 = (bf16[256,512]{1,0:T(8,128)(2,1)}, bf16[256,512]{1,0:T(8,128)(2,1)}, u32[]{:S(2)}, u32[]{:S(2)}) collective-permute-start(bf16[256,512]{1,0:T(8,128)(2,1)} %get-tuple-element.144), channel_id=1, source_target_pairs={{0,7},{1,6},{2,5},{3,4},{4,3},{5,2},{6,1},{7,0},{8,15},{9,14},{10,... | collective-permute-start | bytes 786440 | tf_op jit(solution)/shard_map/ppermute | solution.py:90
  73.9 28.2 %collective-permute-start.8 = (bf16[256,1024]{1,0:T(8,128)(2,1)S(1)}, bf16[256,1024]{1,0:T(8,128)(2,1)S(1)}, u32[]{:S(2)}, u32[]{:S(2)}) collective-permute-start(bf16[256,1024]{1,0:T(8,128)(2,1)S(1)} %copy-done.85), channel_id=1, source_target_pairs={{0,3},{1,2},{2,1},{3,0},{4,11},{5,10},{6,9},{7,8},{8,7},{9,6},{10,... | collective-permute-start | bytes 1572872 | tf_op jit(solution)/shard_map/ppermute | solution.py:217
  81.4 39.5 %collective-permute-start.15 = (bf16[144,2048]{1,0:T(8,128)(2,1)S(1)}, bf16[144,2048]{1,0:T(8,128)(2,1)S(1)}, u32[]{:S(2)}, u32[]{:S(2)}) collective-permute-start(bf16[144,2048]{1,0:T(8,128)(2,1)S(1)} %collective-permute-done.2.refs_3_), channel_id=1, source_target_pairs={{0,1},{1,3},{2,0},{3,5},{4,2},{5,7},{6,4},{7,6},{8,9},{9,11},{10,8... | collective-permute-start | bytes 1769480 | tf_op jit(solution)/shard_map/ppermute | solution.py:90
  84.6 36.5 %collective-permute-start.16 = (bf16[144,2048]{1,0:T(8,128)(2,1)S(1)}, bf16[144,2048]{1,0:T(8,128)(2,1)S(1)}, u32[]{:S(2)}, u32[]{:S(2)}) collective-permute-start(bf16[144,2048]{1,0:T(8,128)(2,1)S(1)} %collective-permute-done.14.refs_0_.refs_4_), channel_id=1, source_target_pairs={{0,2},{1,0},{2,4},{3,1},{4,6},{5,3},{6,7},{7,5},{8,10},{9,8},{10,1... | collective-permute-start | bytes 1769480 | tf_op jit(solution)/shard_map/ppermute | solution.py:90
  102.1 51.9 %collective-permute-start.12 = (bf16[256,512]{1,0:T(8,128)(2,1)}, bf16[256,512]{1,0:T(8,128)(2,1)}, u32[]{:S(2)}, u32[]{:S(2)}) collective-permute-start(bf16[256,512]{1,0:T(8,128)(2,1)} %get-tuple-element.145), channel_id=1, source_target_pairs={{0,6},{1,7},{2,4},{3,5},{4,2},{5,3},{6,0},{7,1},{8,14},{9,15},{10,... | collective-permute-start | bytes 786440 | tf_op jit(solution)/shard_map/ppermute | solution.py:90
  120.9 26.7 %collective-permute-start.17 = (bf16[144,2048]{1,0:T(8,128)(2,1)S(1)}, bf16[144,2048]{1,0:T(8,128)(2,1)S(1)}, u32[]{:S(2)}, u32[]{:S(2)}) collective-permute-start(bf16[144,2048]{1,0:T(8,128)(2,1)S(1)} %collective-permute-done.15.refs_1_.refs_5_), channel_id=1, source_target_pairs={{0,1},{1,3},{2,0},{3,5},{4,2},{5,7},{6,4},{7,6},{8,9},{9,11},{10,8... | collective-permute-start | bytes 1769480 | tf_op jit(solution)/shard_map/ppermute | solution.py:90
  121.1 34.5 %collective-permute-start.13 = (bf16[256,512]{1,0:T(8,128)(2,1)}, bf16[256,512]{1,0:T(8,128)(2,1)}, u32[]{:S(2)}, u32[]{:S(2)}) collective-permute-start(bf16[256,512]{1,0:T(8,128)(2,1)} %get-tuple-element.146), channel_id=1, source_target_pairs={{0,5},{1,4},{2,7},{3,6},{4,1},{5,0},{6,3},{7,2},{8,13},{9,12},{10,... | collective-permute-start | bytes 786440 | tf_op jit(solution)/shard_map/ppermute | solution.py:90
  121.3 38.9 %collective-permute-start.9 = (bf16[1024,1024]{1,0:T(8,128)(2,1)}, bf16[1024,1024]{1,0:T(8,128)(2,1)}, u32[]{:S(2)}, u32[]{:S(2)}) collective-permute-start(bf16[1024,1024]{1,0:T(8,128)(2,1)} %constant_dynamic-update-slice_fusion.16), channel_id=1, source_target_pairs={{0,8},{8,0},{1,9},{9,1},{2,10},{10,2},{3,11},{11,3},{4,12},{12,4},... | collective-permute-start | bytes 6291464 | tf_op jit(solution)/shard_map/ppermute | solution.py:115
  178.1 15.1 %collective-permute-start.32 = (bf16[64,2048]{1,0:T(8,128)(2,1)S(1)}, bf16[64,2048]{1,0:T(8,128)(2,1)S(1)}, u32[]{:S(2)}, u32[]{:S(2)}) collective-permute-start(bf16[64,2048]{1,0:T(8,128)(2,1)S(1)} %get-tuple-element.161), channel_id=1, source_target_pairs={{0,1},{1,3},{2,0},{3,5},{4,2},{5,7},{6,4},{7,6},{8,9},{9,11},{10,8... | collective-permute-start | bytes 786440 | tf_op jit(solution)/shard_map/ppermute | solution.py:90
  201.2 17.0 %collective-permute-start.31 = (bf16[64,2048]{1,0:T(8,128)(2,1)S(1)}, bf16[64,2048]{1,0:T(8,128)(2,1)S(1)}, u32[]{:S(2)}, u32[]{:S(2)}) collective-permute-start(bf16[64,2048]{1,0:T(8,128)(2,1)S(1)} %add_convert_fusion.21), channel_id=1, source_target_pairs={{0,2},{1,0},{2,4},{3,1},{4,6},{5,3},{6,7},{7,5},{8,10},{9,8},{10,1... | collective-permute-start | bytes 786440 | tf_op jit(solution)/shard_map/ppermute | solution.py:90
  238.2 17.0 %collective-permute-start.38 = (bf16[64,2048]{1,0:T(8,128)(2,1)S(1)}, bf16[64,2048]{1,0:T(8,128)(2,1)S(1)}, u32[]{:S(2)}, u32[]{:S(2)}) collective-permute-start(bf16[64,2048]{1,0:T(8,128)(2,1)S(1)} %get-tuple-element.279.refs_0_), channel_id=1, source_target_pairs={{0,1},{1,3},{2,0},{3,5},{4,2},{5,7},{6,4},{7,6},{8,9},{9,11},{10,8... | collective-permute-start | bytes 786440 | tf_op jit(solution)/shard_map/ppermute | solution.py:90
  238.3 18.1 %collective-permute-start.40 = (bf16[64,2048]{1,0:T(8,128)(2,1)S(1)}, bf16[64,2048]{1,0:T(8,128)(2,1)S(1)}, u32[]{:S(2)}, u32[]{:S(2)}) collective-permute-start(bf16[64,2048]{1,0:T(8,128)(2,1)S(1)} %get-tuple-element.279.refs_0_), channel_id=1, source_target_pairs={{0,2},{1,0},{2,4},{3,1},{4,6},{5,3},{6,7},{7,5},{8,10},{9,8},{10,1... | collective-permute-start | bytes 786440 | tf_op jit(solution)/shard_map/ppermute | solution.py:90
  240.8 16.6 %collective-permute-start.43 = (bf16[64,2048]{1,0:T(8,128)(2,1)S(1)}, bf16[64,2048]{1,0:T(8,128)(2,1)S(1)}, u32[]{:S(2)}, u32[]{:S(2)}) collective-permute-start(bf16[64,2048]{1,0:T(8,128)(2,1)S(1)} %get-tuple-element.275.refs_1_), channel_id=1, source_target_pairs={{0,2},{1,0},{2,4},{3,1},{4,6},{5,3},{6,7},{7,5},{8,10},{9,8},{10,1... | collective-permute-start | bytes 786440 | tf_op jit(solution)/shard_map/ppermute | solution.py:90
  268.5 20.6 %collective-permute-start.42 = (bf16[64,2048]{1,0:T(8,128)(2,1)S(1)}, bf16[64,2048]{1,0:T(8,128)(2,1)S(1)}, u32[]{:S(2)}, u32[]{:S(2)}) collective-permute-start(bf16[64,2048]{1,0:T(8,128)(2,1)S(1)} %collective-permute-done.41.refs_0_), channel_id=1, source_target_pairs={{0,2},{1,0},{2,4},{3,1},{4,6},{5,3},{6,7},{7,5},{8,10},{9,8},{10,1... | collective-permute-start | bytes 786440 | tf_op jit(solution)/shard_map/ppermute | solution.py:90
  314.1 18.8 %collective-permute-start.62 = (bf16[64,2048]{1,0:T(8,128)(2,1)S(1)}, bf16[64,2048]{1,0:T(8,128)(2,1)S(1)}, u32[]{:S(2)}, u32[]{:S(2)}) collective-permute-start(bf16[64,2048]{1,0:T(8,128)(2,1)S(1)} %add_convert_fusion.10), channel_id=1, source_target_pairs={{0,2},{1,0},{2,4},{3,1},{4,6},{5,3},{6,7},{7,5},{8,10},{9,8},{10,1... | collective-permute-start | bytes 786440 | tf_op jit(solution)/shard_map/ppermute | solution.py:90
  356.4 28.4 %collective-permute-start.76 = (bf16[64,2048]{1,0:T(8,128)(2,1)}, bf16[64,2048]{1,0:T(8,128)(2,1)S(1)}, u32[]{:S(2)}, u32[]{:S(2)}) collective-permute-start(bf16[64,2048]{1,0:T(8,128)(2,1)} %collective-permute-done.68.refs_2_), channel_id=1, source_target_pairs={{0,1},{1,3},{2,0},{3,5},{4,2},{5,7},{6,4},{7,6},{8,9},{9,11},{10,8... | collective-permute-start | bytes 786440 | tf_op jit(solution)/shard_map/ppermute | solution.py:90
  359.2 26.5 %collective-permute-start.80 = (bf16[64,2048]{1,0:T(8,128)(2,1)}, bf16[64,2048]{1,0:T(8,128)(2,1)S(1)}, u32[]{:S(2)}, u32[]{:S(2)}) collective-permute-start(bf16[64,2048]{1,0:T(8,128)(2,1)} %collective-permute-done.69.refs_3_), channel_id=1, source_target_pairs={{0,1},{1,3},{2,0},{3,5},{4,2},{5,7},{6,4},{7,6},{8,9},{9,11},{10,8... | collective-permute-start | bytes 786440 | tf_op jit(solution)/shard_map/ppermute | solution.py:90
  360.1 27.6 %collective-permute-start.71 = (bf16[64,2048]{1,0:T(8,128)(2,1)}, bf16[64,2048]{1,0:T(8,128)(2,1)S(1)}, u32[]{:S(2)}, u32[]{:S(2)}) collective-permute-start(bf16[64,2048]{1,0:T(8,128)(2,1)} %collective-permute-done.70.refs_0_), channel_id=1, source_target_pairs={{0,2},{1,0},{2,4},{3,1},{4,6},{5,3},{6,7},{7,5},{8,10},{9,8},{10,1... | collective-permute-start | bytes 786440 | tf_op jit(solution)/shard_map/ppermute | solution.py:90
  362.1 24.8 %collective-permute-start.74 = (bf16[64,2048]{1,0:T(8,128)(2,1)}, bf16[64,2048]{1,0:T(8,128)(2,1)S(1)}, u32[]{:S(2)}, u32[]{:S(2)}) collective-permute-start(bf16[64,2048]{1,0:T(8,128)(2,1)} %collective-permute-done.73.refs_1_), channel_id=1, source_target_pairs={{0,2},{1,0},{2,4},{3,1},{4,6},{5,3},{6,7},{7,5},{8,10},{9,8},{10,1... | collective-permute-start | bytes 786440 | tf_op jit(solution)/shard_map/ppermute | solution.py:90
  387.7 20.0 %collective-permute-start.72 = (bf16[64,2048]{1,0:T(8,128)(2,1)S(1)}, bf16[64,2048]{1,0:T(8,128)(2,1)S(1)}, u32[]{:S(2)}, u32[]{:S(2)}) collective-permute-start(bf16[64,2048]{1,0:T(8,128)(2,1)S(1)} %collective-permute-done.71.refs_0_), channel_id=1, source_target_pairs={{0,2},{1,0},{2,4},{3,1},{4,6},{5,3},{6,7},{7,5},{8,10},{9,8},{10,1... | collective-permute-start | bytes 786440 | tf_op jit(solution)/shard_map/ppermute | solution.py:90
  437.1 16.6 %collective-permute-start.84 = (bf16[1024,768]{1,0:T(8,128)(2,1)S(1)}, bf16[1024,768]{1,0:T(8,128)(2,1)S(1)}, u32[]{:S(2)}, u32[]{:S(2)}) collective-permute-start(bf16[1024,768]{1,0:T(8,128)(2,1)S(1)} %fusion.6), channel_id=1, source_target_pairs={{0,8},{8,0},{1,9},{9,1},{2,10},{10,2},{3,11},{11,3},{4,12},{12,4},... | collective-permute-start | bytes 4718600 | tf_op jit(solution)/shard_map/ppermute | solution.py:115
  437.2 46.5 %collective-permute-start.99 = (bf16[2048,512]{1,0:T(8,128)(2,1)S(1)}, bf16[2048,512]{1,0:T(8,128)(2,1)S(1)}, u32[]{:S(2)}, u32[]{:S(2)}) collective-permute-start(bf16[2048,512]{1,0:T(8,128)(2,1)S(1)} %convolution_convert_fusion.1), channel_id=1, source_target_pairs={{0,8},{8,0},{1,9},{9,1},{2,10},{10,2},{3,11},{11,3},{4,12},{12,4},... | collective-permute-start | bytes 6291464 | tf_op jit(solution)/shard_map/ppermute | solution.py:115
  455.6 25.1 %collective-permute-start.86 = (bf16[128,2048]{1,0:T(8,128)(2,1)S(1)}, bf16[128,2048]{1,0:T(8,128)(2,1)S(1)}, u32[]{:S(2)}, u32[]{:S(2)}) collective-permute-start(bf16[128,2048]{1,0:T(8,128)(2,1)S(1)} %add_convert_fusion.6), channel_id=1, source_target_pairs={{0,2},{1,0},{2,4},{3,1},{4,6},{5,3},{6,7},{7,5},{8,10},{9,8},{10,1... | collective-permute-start | bytes 1572872 | tf_op jit(solution)/shard_map/ppermute | solution.py:90
  457.3 57.3 %collective-permute-start.98 = (bf16[256,1024]{1,0:T(8,128)(2,1)S(1)}, bf16[256,1024]{1,0:T(8,128)(2,1)S(1)}, u32[]{:S(2)}, u32[]{:S(2)}) collective-permute-start(bf16[256,1024]{1,0:T(8,128)(2,1)S(1)} %pad_maximum_fusion.10), channel_id=1, source_target_pairs={{1,0},{0,1},{3,2},{2,3},{9,4},{8,5},{11,6},{10,7},{5,8},{4,9},{7,1... | collective-permute-start | bytes 1572872 | tf_op jit(solution)/shard_map/ppermute | solution.py:221
  459.4 27.1 %collective-permute-start.97 = (bf16[256,1024]{1,0:T(8,128)(2,1)S(1)}, bf16[256,1024]{1,0:T(8,128)(2,1)S(1)}, u32[]{:S(2)}, u32[]{:S(2)}) collective-permute-start(bf16[256,1024]{1,0:T(8,128)(2,1)S(1)} %pad_maximum_fusion.9), channel_id=1, source_target_pairs={{0,0},{1,1},{2,2},{3,3},{8,4},{9,5},{10,6},{11,7},{4,8},{5,9},{6,1... | collective-permute-start | bytes 1572872 | tf_op jit(solution)/shard_map/ppermute | solution.py:221
  460.2 34.2 %collective-permute-start.90 = (bf16[128,2048]{1,0:T(8,128)(2,1)S(1)}, bf16[128,2048]{1,0:T(8,128)(2,1)S(1)}, u32[]{:S(2)}, u32[]{:S(2)}) collective-permute-start(bf16[128,2048]{1,0:T(8,128)(2,1)S(1)} %add_convert_fusion.3), channel_id=1, source_target_pairs={{0,1},{1,3},{2,0},{3,5},{4,2},{5,7},{6,4},{7,6},{8,9},{9,11},{10,8... | collective-permute-start | bytes 1572872 | tf_op jit(solution)/shard_map/ppermute | solution.py:90
  480.9 21.9 %collective-permute-start.87 = (bf16[128,2048]{1,0:T(8,128)(2,1)S(1)}, bf16[128,2048]{1,0:T(8,128)(2,1)S(1)}, u32[]{:S(2)}, u32[]{:S(2)}) collective-permute-start(bf16[128,2048]{1,0:T(8,128)(2,1)S(1)} %add_convert_fusion.5), channel_id=1, source_target_pairs={{0,2},{1,0},{2,4},{3,1},{4,6},{5,3},{6,7},{7,5},{8,10},{9,8},{10,1... | collective-permute-start | bytes 1572872 | tf_op jit(solution)/shard_map/ppermute | solution.py:90
  486.5 16.1 %collective-permute-start.102 = (bf16[256,512]{1,0:T(8,128)(2,1)S(1)}, bf16[256,512]{1,0:T(8,128)(2,1)S(1)}, u32[]{:S(2)}, u32[]{:S(2)}) collective-permute-start(bf16[256,512]{1,0:T(8,128)(2,1)S(1)} %get-tuple-element.252), channel_id=1, source_target_pairs={{0,2},{1,3},{2,0},{3,1},{4,6},{5,7},{6,4},{7,5},{8,10},{9,11},{10,... | collective-permute-start | bytes 786440 | tf_op jit(solution)/shard_map/ppermute | solution.py:90
  494.5 42.7 %collective-permute-start.91 = (bf16[128,2048]{1,0:T(8,128)(2,1)S(1)}, bf16[128,2048]{1,0:T(8,128)(2,1)S(1)}, u32[]{:S(2)}, u32[]{:S(2)}) collective-permute-start(bf16[128,2048]{1,0:T(8,128)(2,1)S(1)} %add_convert_fusion.2), channel_id=1, source_target_pairs={{0,1},{1,3},{2,0},{3,5},{4,2},{5,7},{6,4},{7,6},{8,9},{9,11},{10,8... | collective-permute-start | bytes 1572872 | tf_op jit(solution)/shard_map/ppermute | solution.py:90
  494.6 20.1 %collective-permute-start.101 = (bf16[256,1024]{1,0:T(8,128)(2,1)S(1)}, bf16[256,1024]{1,0:T(8,128)(2,1)S(1)}, u32[]{:S(2)}, u32[]{:S(2)}) collective-permute-start(bf16[256,1024]{1,0:T(8,128)(2,1)S(1)} %pad_maximum_fusion.11), channel_id=1, source_target_pairs={{2,0},{3,1},{0,2},{1,3},{10,4},{11,5},{8,6},{9,7},{6,8},{7,9},{4,1... | collective-permute-start | bytes 1572872 | tf_op jit(solution)/shard_map/ppermute | solution.py:221
  502.6 28.6 %collective-permute-start.103 = (bf16[256,1024]{1,0:T(8,128)(2,1)S(1)}, bf16[256,1024]{1,0:T(8,128)(2,1)S(1)}, u32[]{:S(2)}, u32[]{:S(2)}) collective-permute-start(bf16[256,1024]{1,0:T(8,128)(2,1)S(1)} %pad_maximum_fusion.12), channel_id=1, source_target_pairs={{3,0},{2,1},{1,2},{0,3},{11,4},{10,5},{9,6},{8,7},{7,8},{6,9},{5,1... | collective-permute-start | bytes 1572872 | tf_op jit(solution)/shard_map/ppermute | solution.py:221
  502.9 34.4 %collective-permute-start.88 = (bf16[128,2048]{1,0:T(8,128)(2,1)S(1)}, bf16[128,2048]{1,0:T(8,128)(2,1)S(1)}, u32[]{:S(2)}, u32[]{:S(2)}) collective-permute-start(bf16[128,2048]{1,0:T(8,128)(2,1)S(1)} %add_convert_fusion.4), channel_id=1, source_target_pairs={{0,2},{1,0},{2,4},{3,1},{4,6},{5,3},{6,7},{7,5},{8,10},{9,8},{10,1... | collective-permute-start | bytes 1572872 | tf_op jit(solution)/shard_map/ppermute | solution.py:90
  514.6 49.3 %collective-permute-start.108 = (bf16[512,2048]{1,0:T(8,128)(2,1)S(1)}, bf16[512,2048]{1,0:T(8,128)(2,1)S(1)}, u32[]{:S(2)}, u32[]{:S(2)}) collective-permute-start(bf16[512,2048]{1,0:T(8,128)(2,1)S(1)} %convolution_convert_fusion), channel_id=1, source_target_pairs={{0,8},{8,0},{1,9},{9,1},{2,10},{10,2},{3,11},{11,3},{4,12},{12,4},... | collective-permute-start | bytes 6291464 | tf_op jit(solution)/shard_map/ppermute | solution.py:115
  514.7 53.7 %collective-permute-start.107 = (bf16[256,512]{1,0:T(8,128)(2,1)S(1)}, bf16[256,512]{1,0:T(8,128)(2,1)S(1)}, u32[]{:S(2)}, u32[]{:S(2)}) collective-permute-start(bf16[256,512]{1,0:T(8,128)(2,1)S(1)} %get-tuple-element.260), channel_id=1, source_target_pairs={{0,1},{1,0},{2,3},{3,2},{4,5},{5,4},{6,7},{7,6},{8,9},{9,8},{10,11... | collective-permute-start | bytes 786440 | tf_op jit(solution)/shard_map/ppermute | solution.py:90
  531.2 29.1 %collective-permute-start.104 = (bf16[256,512]{1,0:T(8,128)(2,1)S(1)}, bf16[256,512]{1,0:T(8,128)(2,1)S(1)}, u32[]{:S(2)}, u32[]{:S(2)}) collective-permute-start(bf16[256,512]{1,0:T(8,128)(2,1)S(1)} %get-tuple-element.257), channel_id=1, source_target_pairs={{0,7},{1,6},{2,5},{3,4},{4,3},{5,2},{6,1},{7,0},{8,15},{9,14},{10,... | collective-permute-start | bytes 786440 | tf_op jit(solution)/shard_map/ppermute | solution.py:90
  537.2 47.8 %collective-permute-start.106 = (bf16[256,512]{1,0:T(8,128)(2,1)S(1)}, bf16[256,512]{1,0:T(8,128)(2,1)S(1)}, u32[]{:S(2)}, u32[]{:S(2)}) collective-permute-start(bf16[256,512]{1,0:T(8,128)(2,1)S(1)} %get-tuple-element.259), channel_id=1, source_target_pairs={{0,5},{1,4},{2,7},{3,6},{4,1},{5,0},{6,3},{7,2},{8,13},{9,12},{10,... | collective-permute-start | bytes 786440 | tf_op jit(solution)/shard_map/ppermute | solution.py:90
  560.3 24.7 %collective-permute-start.105 = (bf16[256,512]{1,0:T(8,128)(2,1)S(1)}, bf16[256,512]{1,0:T(8,128)(2,1)S(1)}, u32[]{:S(2)}, u32[]{:S(2)}) collective-permute-start(bf16[256,512]{1,0:T(8,128)(2,1)S(1)} %get-tuple-element.258), channel_id=1, source_target_pairs={{0,4},{1,5},{2,6},{3,7},{4,0},{5,1},{6,2},{7,3},{8,12},{9,13},{10,... | collective-permute-start | bytes 786440 | tf_op jit(solution)/shard_map/ppermute | solution.py:90
  (161 other events, 2189.5 us)

commit v6 on v5

--- a/solution.py
+++ b/solution.py
@@ -224,14 +224,19 @@
         return self.between_chips(block, lambda chip: chip ^ mask)
 
 
-def message_order(chips, core_heads):
+def message_orders(chips, core_heads):
     near = [("up", mask) for mask in range(chips // 2 - 1, 0, -1)]
     far = [("up", mask) for mask in range(chips - 1, chips // 2 - 1, -1)]
     heads = [("head", turn) for turn in range(core_heads)]
-    order = []
-    for k, head in enumerate(heads):
-        order += [head] + near[k : k + 1]
-    return order + near[len(heads) :] + far
+    out = heads[:1]
+    for k, head in enumerate(heads[1:]):
+        out += [head] + near[k : k + 1]
+    out += near[len(heads) - 1 :] + far
+    mixed = [item for pair in zip(near, far) for item in pair][: len(heads)]
+    back = [item for pair in zip(heads, mixed) for item in pair]
+    rest = [item for item in far if item not in back]
+    back += rest[:-1] + [item for item in near if item not in back] + rest[-1:]
+    return (out, back)
 
 
 def ordered(block, *earlier):
@@ -398,17 +403,14 @@
         store_rows(outs, rows, total)
 
 
-def backward_kernel(count, pieces, chained, *refs):
+def backward_kernel(count, chained, *refs):
     grads, refs = refs[:count], refs[count:]
-    second, heads, wu, wd, cosine, sine = refs[:6]
-    first_norm, second_norm, qkv, attention, attended, active, slope = refs[6:13]
-    refs = refs[13 + chained :]
-    upstream, joined_grad, hidden_grad, norm_sums, joined_sum, hidden_sum = refs[:6]
-    outs, wo = refs[6 : 6 + pieces], refs[6 + pieces]
-    wq = split_heads(heads, wo)
+    heads, wd, cosine, sine, qkv, attention, slope = refs[:7]
+    upstream, joined_grad, hidden_grad, joined_sum, hidden_sum, wo = refs[7 + chained :]
+    split_heads(heads, wo)
     length = attention.shape[1]
     size = wo.shape[0]
-    part = wu.shape[1] // 2
+    part = wd.shape[0] // 2
     load_rows(grads, upstream)
     attended_grad = contract_cols(upstream[...], wo[...]).astype(BF16)
     for k in range(2):
@@ -429,27 +431,39 @@
             hidden_grad[:, at] = grad
             hidden_sum[:, at] = fold_rows(grad.astype(F32))
     joined_sum[...] = fold_rows(joined_grad[...].astype(F32))
-    for rows in steps(wq.shape[0]):
-        first = contract_cols(joined_grad[...], wq[rows])
-        other = contract_cols(hidden_grad[...], wu[rows])
-        norm_sums[0:8, rows] = fold_rows(first * first_norm[:, rows].astype(F32))
-        norm_sums[8:16, rows] = fold_rows(other * second_norm[:, rows].astype(F32))
-        norm_sums[16:24, rows] = fold_rows(first)
-        norm_sums[24:32, rows] = fold_rows(other)
-        store_rows(outs, rows, first + other)
+
+
+def scaled_kernel(second, heads, wu, wd, *refs):
+    first_norm, second_norm, attended, active, joined_grad, hidden_grad = refs[:6]
+    out, norm_sums, wo = refs[6:]
+    wq = split_heads(heads, wo)
+
+    @pl.when(pl.program_id(0) == 0)
+    def _():
+        norm_sums[...] = jnp.zeros_like(norm_sums)
+
+    for cols in steps(wq.shape[0]):
+        first = contract_cols(joined_grad[...], wq[cols])
+        other = contract_cols(hidden_grad[...], wu[cols])
+        norm_sums[0:8, cols] += fold_rows(first * first_norm[:, cols].astype(F32))
+        norm_sums[8:16, cols] += fold_rows(other * second_norm[:, cols].astype(F32))
+        norm_sums[16:24, cols] += fold_rows(first)
+        norm_sums[24:32, cols] += fold_rows(other)
+        out[:, cols] = (first + other).astype(BF16)
 
     @pl.when(second[0] != 0)
     def _():
         for cols in steps(wq.shape[0]):
             total = matmul(attended[...], wo[:, cols]) + matmul(active[...], wd[:, cols])
-            store_rows(outs, cols, total)
+            out[:, cols] = total.astype(BF16)
 
 
 def sums_kernel(pairs, *refs):
-    where, parts, (given, sums) = refs[0], refs[1 : 1 + 3 * pairs], refs[1 + 3 * pairs :]
-    norm_sums, joined_sum, hidden_sum = (
-        functools.reduce(jnp.add, [parts[3 * pair + k][...] for pair in range(pairs)])
-        for k in range(3)
+    where, norm_sums, parts = refs[0], refs[1], refs[2 : 2 + 2 * pairs]
+    given, sums = refs[2 + 2 * pairs :]
+    joined_sum, hidden_sum = (
+        functools.reduce(jnp.add, [parts[2 * pair + k][...] for pair in range(pairs)])
+        for k in range(2)
     )
     rows, width = sums.shape[0], given.shape[1]
     size = joined_sum.shape[1]
@@ -654,7 +668,7 @@
         for up_mask in range(chips)
     ]
     queue = Queue(3)
-    order = message_order(chips, core_heads)
+    order, back_order = message_orders(chips, core_heads)
     heads = jnp.zeros((core_heads * block_rows, joined_size + head_size), BF16)
     wu0 = jnp.zeros((chips * block_rows, hidden_part), BF16)
     wu0 = lax.dynamic_update_slice_in_dim(wu0, up_blocks[0], chip * block_rows, 0)
@@ -682,7 +696,6 @@
 
     part_rows = length // 2
     piece = jax.ShapeDtypeStruct((part_rows, width), BF16)
-    whole_piece = jax.ShapeDtypeStruct((length, width), BF16)
 
     def by_rows(cols, dtype):
         return jax.ShapeDtypeStruct((row_count, cols), dtype)
@@ -803,43 +816,29 @@
     second_section = jnp.where(first_section, 0, 1).astype(jnp.int32).reshape(1)
     grad_shapes = (by_rows(width, BF16), by_rows(joined_size, BF16), by_rows(hidden_size, BF16))
     grads = None
-    last_pieces = {}
     sums = []
     for pair in range(chips // 2):
         blocks = pair_blocks(upstream_blocks, pair)
         results = call_rows(
             functools.partial(
-                backward_kernel, len(blocks), 2, len(grad_shapes) if grads else 0
+                backward_kernel, len(blocks), len(grad_shapes) if grads else 0
             ),
-            (*blocks, second_section, *matrices),
-            (cosine, sine, first_norm, second_norm, qkv, attention, attended, active, slope),
+            (*blocks, heads, wd),
+            (cosine, sine, qkv, attention, slope),
             grads,
             grad_shapes,
             [
-                jax.ShapeDtypeStruct((32, width), F32),
                 jax.ShapeDtypeStruct((8, joined_size), F32),
                 jax.ShapeDtypeStruct((8, hidden_size), F32),
-            ]
-            + [whole_piece] * 2,
+            ],
             [pltpu.VMEM((head_size, width), BF16)],
             pair,
             2 * length,
-            matrix_flops,
+            matrix_flops // 2,
         )
         grads = results[: len(grad_shapes)]
-        sums.append(results[len(grad_shapes) : len(grad_shapes) + 3])
-        for k in range(2):
-            last_pieces[layout.slots[2 * pair + k]] = [results[k - 2]]
+        sums.append(results[len(grad_shapes) :])
     upstream, joined_grad, hidden_grad = grads
-
-    own_given = jnp.concatenate(own_upstream, axis=0)
-    (local_sums,) = call_whole(
-        functools.partial(sums_kernel, len(sums)),
-        [jnp.stack([chip, core]), *[item for pair in sums for item in pair], own_given],
-        [jax.ShapeDtypeStruct((chips, width + joined_size + hidden_size), F32)],
-        [],
-    )
-    joint = layout.sum_steps(local_sums)
 
     def half_of(array, which):
         size = array.shape[1] // cores
@@ -861,8 +860,7 @@
         return (own + taken.astype(F32)).astype(BF16)
 
     late_grad, late_attended = (
-        ordered(item, joint[0], joined_given, out_given, hidden_given)
-        for item in (joined_grad, attended)
+        ordered(item, joined_given, out_given, hidden_given) for item in (joined_grad, attended)
     )
     joined_held = core_sum(weight_grad(half_of(first_norm, core), late_grad), joined_taken)
     out_held = core_sum(weight_grad(half_of(late_attended, core), upstream), out_taken)
@@ -873,6 +871,48 @@
         weight_grad(late_active[:, hidden_part:], upstream).astype(BF16)
     )
 
+    late_grad = ordered(joined_grad, joined_held, out_held, hidden_held)
+    pair_rows = 2 * length
+
+    def by_pair(item):
+        return pl.BlockSpec((pair_rows, item.shape[1]), lambda i: (i, 0))
+
+    row_items = (first_norm, second_norm, attended, active, late_grad, hidden_grad)
+    last_rows, norm_parts = pl.pallas_call(
+        scaled_kernel,
+        grid=(row_count // pair_rows,),
+        out_shape=[by_rows(width, BF16), jax.ShapeDtypeStruct((32, width), F32)],
+        in_specs=[pl.BlockSpec(memory_space=pltpu.SMEM)]
+        + [pl.BlockSpec(memory_space=pltpu.VMEM)] * 3
+        + [by_pair(item) for item in row_items],
+        out_specs=[
+            by_pair(by_rows(width, BF16)),
+            pl.BlockSpec((32, width), lambda i: (0, 0)),
+        ],
+        scratch_shapes=[pltpu.VMEM((head_size, width), BF16)],
+        cost_estimate=pl.CostEstimate(
+            flops=2 * matrix_flops, bytes_accessed=row_count * 8192, transcendentals=0
+        ),
+        compiler_params=pltpu.CompilerParams(vmem_limit_bytes=VMEM_BYTES),
+    )(second_section, heads, wu, wd, *row_items)
+    last_pieces = {
+        slot: [last_rows[k * length : (k + 1) * length]] for k, slot in enumerate(layout.slots)
+    }
+
+    own_given = jnp.concatenate(own_upstream, axis=0)
+    (local_sums,) = call_whole(
+        functools.partial(sums_kernel, len(sums)),
+        [
+            jnp.stack([chip, core]),
+            norm_parts,
+            *[item for pair in sums for item in pair],
+            own_given,
+        ],
+        [jax.ShapeDtypeStruct((chips, width + joined_size + hidden_size), F32)],
+        [],
+    )
+    joint = layout.sum_steps(local_sums)
+
     whole_sums = joint[-1]
     norm_sums = whole_sums[:4, :width].reshape(2, 2, width)
     norm_sums = jnp.stack([norm_sums[0] - ratio * norm_sums[1], norm_sums[1]]) / gains
@@ -884,7 +924,7 @@
         whole_sums[:, width + joined_size :], core * hidden_part, hidden_part, 1
     ).reshape(-1)
 
-    (last_rows,) = layout.ring_scatter(last_pieces, None, {1: (joined_held, out_held)})
+    (last_rows,) = layout.ring_scatter(last_pieces)
     last_normed, last_inverse = (
         jnp.concatenate([norm[k] for norm in own_normed], axis=0) for k in range(2)
     )
@@ -917,7 +957,7 @@
         ("up", 0): lax.dynamic_slice_in_dim(hidden_held, chip * block_rows, block_rows, 0)
     }
     up_weight_grad = None
-    for k, (kind, which) in enumerate(order):
+    for k, (kind, which) in enumerate(back_order):
         if kind == "head":
             block = head_blocks[which]
         else:
@@ -925,14 +965,16 @@
                 hidden_held, (chip ^ which) * block_rows, block_rows, 0
             )
         if k == 0:
-            block = ordered(block, joint[1], *head_blocks)
-        if k == 2:
+            block = ordered(block, *head_blocks)
+        if k == 6:
+            block = ordered(block, joint[0])
+        if k == 8:
+            block = ordered(block, joint[1])
+        if k == 10:
             block = ordered(block, joint[2])
-        if k == 4:
-            block = ordered(block, joint[-1])
-        if k == len(order) - 3:
+        if k == len(back_order) - 3:
             block = ordered(block, down_weight_grad)
-        if k == len(order) - 1:
+        if k == len(back_order) - 1:
             block = ordered(block, last_rows, joined_weight_grad)
         block = queue.ready(block)
         block = layout.return_head(block, which) if kind == "head" else layout.swap(block, which)
@@ -964,7 +1006,7 @@
             ) + down_taken.astype(F32)
             if layout.groups > 1:
                 down_weight_grad = layout.scatter_groups(down_weight_grad, 0)
-        if k in (len(order) - 3, len(order) - 1):
+        if k in (len(back_order) - 3, len(back_order) - 1):
             masks = [mask for mask in range(chips) if ("up", mask) in blocks]
             columns = [blocks.pop(("up", mask)) for mask in masks]
             if layout.groups > 1:

time: 593 us -> 583 us (0.983)
  waiting for transfers between devices: 241 us -> 229 us
  local copies, waits for them, and re-layouts: 58.8 us -> 52.4 us
    pallas_call x11, Pallas kernels: 78 us -> 59.9 us  [call_rows(): pl.pallas_call(kernel, grid=(1,), out_shape=out_shape, in_specs=in_specs,...]
    pallas_call x0 -> x1, Pallas kernels: none -> 17.3 us  [on_device(): pl.pallas_call(scaled_kernel, grid=(row_count // pair_rows,), out_shape=[...]
    ppermute x4, waiting for transfers between devices: 21.5 us -> 8.49 us  [send_head(): return lax.ppermute(block, ('tensor', 'dp'), self.head_route(turn))]
    ppermute x87, starting transfers between devices: 107 us -> 120 us  [between_chips(): return lax.ppermute(block, 'dp', pairs)]
    ppermute x4, starting transfers between devices: 16.2 us -> 4.47 us  [send_head(): return lax.ppermute(block, ('tensor', 'dp'), self.head_route(turn))]
    unnamed x218 -> x186, local copies, waits for them, and re-layouts: 36.6 us -> 27.6 us
  transfers between devices with their start and end apart: 110 -> 110, of which waited for: 44 -> 42; matrix products, arithmetic and copies ran while one was open for 12% -> 13% of each run, Pallas kernels for 11% -> 13%
where the time goes in v6:
time: 583 us; the launch traced here: 574 us
  waiting for transfers between devices  229 us (39%)
  starting transfers between devices  143 us (25%)
  Pallas kernels  85.5 us (15%)
  local copies, waits for them, and re-layouts  52.4 us (9%)
  other arithmetic  42.7 us (7%)
  matrix products  18.7 us (3%)
    ppermute x87, waiting for transfers between devices, between_chips(): return lax.ppermute(block, 'dp', pairs)  189 us
    ppermute x87, starting transfers between devices, between_chips(): return lax.ppermute(block, 'dp', pairs)  120 us
    pallas_call x11, Pallas kernels, call_rows(): pl.pallas_call(kernel, grid=(1,), out_shape=out_shape, in_specs=in_specs,...  59.9 us
    unnamed x186, local copies, waits for them, and re-layouts  27.6 us
    dot_general x8, matrix products, contract_rows(): lax.dot_general(left_side, right_side, (((0,), (0,)), ((), ())), preferre...  18.7 us
    pallas_call x1, Pallas kernels, on_device(): pl.pallas_call(scaled_kernel, grid=(row_count // pair_rows,), out_shape=[...  17.3 us
  transfers between devices with their start and end apart: 110, of which 42 were waited for; matrix products, arithmetic and copies ran while one was open for 13% of the time, Pallas kernels for 13%

profile of v6, /device:TPU:10, one launch (start us, length us, event | category | flops | bytes accessed | tf_op | source)
XLA Modules:
  0.0 574.3 jit_solution(9995517099097810207)
XLA Ops:
  25.1 9.8 %collective-permute-done.6 = bf16[256,512]{1,0:T(8,128)(2,1)} collective-permute-done((bf16[256,512]{1,0:T(8,128)(2,1)}, bf16[256,512]{1,0:T(8,128)(2,1)}, u32[]{:S(2)}, u32[]{:S(2)}) %collective-permute-start.6) | collective-permute-done | bytes 262176 | tf_op jit(solution)/shard_map/ppermute | solution.py:90
  35.0 6.9 %collective-permute-start.19 = (bf16[512,2048]{1,0:T(8,128)(2,1)}, bf16[512,2048]{1,0:T(8,128)(2,1)S(1)}, u32[]{:S(2)}, u32[]{:S(2)}) collective-permute-start(bf16[512,2048]{1,0:T(8,128)(2,1)} %bitcast.169), channel_id=1, source_target_pairs={{0,8},{8,0},{1,9},{9,1},{2,10},{10,2},{3,11},{11,3},{4,12},{12,4},... | collective-permute-start | bytes 6291464 | tf_op jit(solution)/shard_map/ppermute | solution.py:115
  50.6 11.9 %collective-permute-done.9 = bf16[256,512]{1,0:T(8,128)(2,1)S(1)} collective-permute-done((bf16[256,512]{1,0:T(8,128)(2,1)}, bf16[256,512]{1,0:T(8,128)(2,1)S(1)}, u32[]{:S(2)}, u32[]{:S(2)}) %collective-permute-start.9) | collective-permute-done | bytes 262176 | tf_op jit(solution)/shard_map/ppermute | solution.py:90
  62.5 5.0 collective-permute-start.14
  70.6 8.5 %collective-permute-done.5 = bf16[256,1024]{1,0:T(8,128)(2,1)S(1)} collective-permute-done((bf16[256,1024]{1,0:T(8,128)(2,1)S(1)}, bf16[256,1024]{1,0:T(8,128)(2,1)S(1)}, u32[]{:S(2)}, u32[]{:S(2)}) %collective-permute-start.5) | collective-permute-done | bytes 524320 | tf_op jit(solution)/shard_map/ppermute | solution.py:217
  79.9 13.5 %collective-permute-done.2.refs_3_ = bf16[144,2048]{1,0:T(8,128)(2,1)S(1)} collective-permute-done((bf16[144,2048]{1,0:T(8,128)(2,1)S(1)}, bf16[144,2048]{1,0:T(8,128)(2,1)S(1)}, u32[]{:S(2)}, u32[]{:S(2)}) %collective-permute-start.2) | collective-permute-done | bytes 589856 | tf_op jit(solution)/shard_map/ppermute | solution.py:90
  97.9 20.9 %collective-permute-done.15.refs_1_.refs_5_ = bf16[144,2048]{1,0:T(8,128)(2,1)S(1)} collective-permute-done((bf16[144,2048]{1,0:T(8,128)(2,1)S(1)}, bf16[144,2048]{1,0:T(8,128)(2,1)S(1)}, u32[]{:S(2)}, u32[]{:S(2)}) %collective-permute-start.15) | collective-permute-done | bytes 589856 | tf_op jit(solution)/shard_map/ppermute | solution.py:90
  122.6 22.7 %collective-permute-done.17.refs_3_.refs_7_ = bf16[144,2048]{1,0:T(8,128)(2,1)S(1)} collective-permute-done((bf16[144,2048]{1,0:T(8,128)(2,1)S(1)}, bf16[144,2048]{1,0:T(8,128)(2,1)S(1)}, u32[]{:S(2)}, u32[]{:S(2)}) %collective-permute-start.17) | collective-permute-done | bytes 589856 | tf_op jit(solution)/shard_map/ppermute | solution.py:90
  162.2 4.0 pad_maximum_fusion.2.refs_5_.wu
  166.4 9.3 %shard_map.221 = (bf16[64,2048]{1,0:T(8,128)(2,1)S(1)}, bf16[64,2048]{1,0:T(8,128)(2,1)S(1)}, bf16[64,2048]{1,0:T(8,128)(2,1)S(1)}, bf16[64,2048]{1,0:T(8,128)(2...) custom-call(bf16[144,2048]{1,0:T(8,128)(2,1)S(1)} %copy-done.41, ...), custom_call_target="tpu_custom_call" | custom-call | flops 6442450944 | bytes 4194304 | tf_op jit(solution)/shard_map/pallas_call | solution.py:547
  180.2 9.3 %shard_map.220 = (bf16[64,2048]{1,0:T(8,128)(2,1)S(1)}, bf16[64,2048]{1,0:T(8,128)(2,1)S(1)}, bf16[64,2048]{1,0:T(8,128)(2,1)S(1)}, bf16[64,2048]{1,0:T(8,128)(2...) custom-call(bf16[144,2048]{1,0:T(8,128)(2,1)S(1)} %fusion.18.refs_0_, ...), custom_call_target="tpu_custom_call" | custom-call | flops 6442450944 | bytes 4194304 | tf_op jit(solution)/shard_map/pallas_call | solution.py:547
  194.0 4.8 collective-permute-done.30
  201.1 3.3 collective-permute-done.23
  206.7 4.9 collective-permute-done.34
  217.2 4.0 collective-permute-done.35
  223.6 7.3 %collective-permute-done.36 = bf16[64,2048]{1,0:T(8,128)(2,1)} collective-permute-done((bf16[64,2048]{1,0:T(8,128)(2,1)S(1)}, bf16[64,2048]{1,0:T(8,128)(2,1)}, u32[]{:S(2)}, u32[]{:S(2)}) %collective-permute-start.36) | collective-permute-done | bytes 262176 | tf_op jit(solution)/shard_map/ppermute | solution.py:766
  245.2 5.6 shard_map.222
  255.0 5.5 shard_map.223
  267.2 5.5 shard_map.224
  277.8 5.5 shard_map.225
  285.0 5.5 shard_map.226
  298.8 5.1 collective-permute-done.52
  306.2 3.3 collective-permute-done.64
  322.3 5.3 collective-permute-done.68
  328.7 5.4 collective-permute-done.69
  337.9 4.3 collective-permute-done.59
  349.9 5.5 collective-permute-done.74.refs_2_
  357.4 3.6 collective-permute-done.79.refs_3_
  366.2 4.0 collective-permute-done.80.refs_3_
  377.8 3.7 shard_map.227
  385.0 3.8 shard_map.228
  388.9 3.6 shard_map.229
  396.1 3.4 copy-done.16
  413.5 3.9 add_convert_fusion
  418.9 17.3 %shard_map.231 = (bf16[1024,2048]{1,0:T(8,128)(2,1)S(1)}, f32[32,2048]{1,0:T(8,128)S(1)}) custom-call(s32[1]{0:T(128)} %bitcast.26.second, bf16[2048,1024]{1,0:T(8,128)(2,1)S(1)} %copy-done.3, bf16[2048,1024]{1,0:T(8,128)(2,1)S(1)} %copy-done.12, bf16[1024,2048]{1,0:T(8,128)(2,1)S(1)} %copy-done.7, bf16[1024,2048]{1,0:T(8,128)(2,1)S(1)} %copy-done.16, ...), custom_call_target="tpu_custom_call" | custom-call | flops 6442450944 | bytes 8388608 | tf_op jit(solution)/shard_map/pallas_call | solution.py:881
  448.3 8.0 %collective-permute-start.96 = (f32[8,3840]{1,0:T(8,128)S(1)}, f32[8,3840]{1,0:T(8,128)S(1)}, u32[]{:S(2)}, u32[]{:S(2)}) collective-permute-start(f32[8,3840]{1,0:T(8,128)S(1)} %add.476), channel_id=1, source_target_pairs={{0,2},{1,3},{2,0},{3,1},{4,6},{5,7},{6,4},{7,5},{8,10},{9,11},{10,... | collective-permute-start | bytes 368648 | tf_op jit(solution)/shard_map/ppermute | solution.py:90
  458.0 3.8 collective-permute-start.102
  463.6 3.5 collective-permute-start.97
  474.2 5.0 collective-permute-done.102.refs_6_
  482.0 7.7 %collective-permute-done.97 = f32[8,3840]{1,0:T(8,128)S(1)} collective-permute-done((f32[8,3840]{1,0:T(8,128)S(1)}, f32[8,3840]{1,0:T(8,128)S(1)}, u32[]{:S(2)}, u32[]{:S(2)}) %collective-permute-start.97) | collective-permute-done | bytes 122912 | tf_op jit(solution)/shard_map/ppermute | solution.py:90
  489.8 7.5 %collective-permute-done.86 = bf16[128,2048]{1,0:T(8,128)(2,1)S(1)} collective-permute-done((bf16[128,2048]{1,0:T(8,128)(2,1)S(1)}, bf16[128,2048]{1,0:T(8,128)(2,1)S(1)}, u32[]{:S(2)}, u32[]{:S(2)}) %collective-permute-start.86) | collective-permute-done | bytes 524320 | tf_op jit(solution)/shard_map/ppermute | solution.py:90
  500.3 11.3 %collective-permute-done.103.refs_4_ = bf16[256,1024]{1,0:T(8,128)(2,1)S(1)} collective-permute-done((bf16[256,1024]{1,0:T(8,128)(2,1)S(1)}, bf16[256,1024]{1,0:T(8,128)(2,1)S(1)}, u32[]{:S(2)}, u32[]{:S(2)}) %collective-permute-start.103) | collective-permute-done | bytes 524320 | tf_op jit(solution)/shard_map/ppermute | solution.py:221
  511.7 7.4 %collective-permute-start.105 = (bf16[256,512]{1,0:T(8,128)(2,1)S(1)}, bf16[256,512]{1,0:T(8,128)(2,1)S(1)}, u32[]{:S(2)}, u32[]{:S(2)}) collective-permute-start(bf16[256,512]{1,0:T(8,128)(2,1)S(1)} %get-tuple-element.237), channel_id=1, source_target_pairs={{0,6},{1,7},{2,4},{3,5},{4,2},{5,3},{6,0},{7,1},{8,14},{9,15},{10,... | collective-permute-start | bytes 786440 | tf_op jit(solution)/shard_map/ppermute | solution.py:90
  519.1 3.6 shard_map.233
  522.7 11.4 %collective-permute-start.104 = (bf16[256,512]{1,0:T(8,128)(2,1)S(1)}, bf16[256,512]{1,0:T(8,128)(2,1)S(1)}, u32[]{:S(2)}, u32[]{:S(2)}) collective-permute-start(bf16[256,512]{1,0:T(8,128)(2,1)S(1)} %get-tuple-element.234), channel_id=1, source_target_pairs={{0,1},{1,0},{2,3},{3,2},{4,5},{5,4},{6,7},{7,6},{8,9},{9,8},{10,11... | collective-permute-start | bytes 786440 | tf_op jit(solution)/shard_map/ppermute | solution.py:90
  536.6 4.5 convert_add_fusion
  541.1 11.3 %collective-permute-done.88 = bf16[128,2048]{1,0:T(8,128)(2,1)S(1)} collective-permute-done((bf16[128,2048]{1,0:T(8,128)(2,1)S(1)}, bf16[128,2048]{1,0:T(8,128)(2,1)S(1)}, u32[]{:S(2)}, u32[]{:S(2)}) %collective-permute-start.88) | collective-permute-done | bytes 524320 | tf_op jit(solution)/shard_map/ppermute | solution.py:90
  552.4 5.4 collective-permute-done.91
  (536 shorter events, 235.1 us)
Async XLA Ops:
  6.6 41.9 %collective-permute-start = (bf16[144,2048]{1,0:T(8,128)(2,1)S(1)}, bf16[144,2048]{1,0:T(8,128)(2,1)S(1)}, u32[]{:S(2)}, u32[]{:S(2)}) collective-permute-start(bf16[144,2048]{1,0:T(8,128)(2,1)S(1)} %fusion.18.refs_0_), channel_id=1, source_target_pairs={{0,1},{1,3},{2,0},{3,5},{4,2},{5,7},{6,4},{7,6},{8,9},{9,11},{10,8... | collective-permute-start | bytes 1769480 | tf_op jit(solution)/shard_map/ppermute | solution.py:90
  7.1 42.9 %collective-permute-start.1 = (bf16[144,2048]{1,0:T(8,128)(2,1)S(1)}, bf16[144,2048]{1,0:T(8,128)(2,1)S(1)}, u32[]{:S(2)}, u32[]{:S(2)}) collective-permute-start(bf16[144,2048]{1,0:T(8,128)(2,1)S(1)} %fusion.18.refs_0_), channel_id=1, source_target_pairs={{0,2},{1,0},{2,4},{3,1},{4,6},{5,3},{6,7},{7,5},{8,10},{9,8},{10,1... | collective-permute-start | bytes 1769480 | tf_op jit(solution)/shard_map/ppermute | solution.py:90
  8.8 15.7 %collective-permute-start.18 = (f32[1,7168]{1,0:T(1,128)S(1)}, f32[1,7168]{1,0:T(1,128)S(1)}, u32[]{:S(2)}, u32[]{:S(2)}) collective-permute-start(f32[1,7168]{1,0:T(1,128)S(1)} %maximum_convert_fusion), channel_id=1, source_target_pairs={{0,8},{8,0},{1,9},{9,1},{2,10},{10,2},{3,11},{11,3},{4,12},{12,4},... | collective-permute-start | bytes 86024 | tf_op jit(solution)/shard_map/ppermute | solution.py:115
  14.8 28.8 %collective-permute-start.3 = (bf16[256,1024]{1,0:T(8,128)(2,1)S(1)}, bf16[256,1024]{1,0:T(8,128)(2,1)}, u32[]{:S(2)}, u32[]{:S(2)}) collective-permute-start(bf16[256,1024]{1,0:T(8,128)(2,1)S(1)} %pad_maximum_fusion.4), channel_id=1, source_target_pairs={{0,0},{1,1},{2,2},{3,3},{4,8},{5,9},{6,10},{7,11},{8,4},{9,5},{10,... | collective-permute-start | bytes 1572872 | tf_op jit(solution)/shard_map/ppermute | solution.py:217
  17.6 25.9 %collective-permute-start.4 = (bf16[256,1024]{1,0:T(8,128)(2,1)}, bf16[256,1024]{1,0:T(8,128)(2,1)S(1)}, u32[]{:S(2)}, u32[]{:S(2)}) collective-permute-start(bf16[256,1024]{1,0:T(8,128)(2,1)} %get-tuple-element.128), channel_id=1, source_target_pairs={{0,1},{1,0},{2,3},{3,2},{4,9},{5,8},{6,11},{7,10},{8,5},{9,4},{10,... | collective-permute-start | bytes 1572872 | tf_op jit(solution)/shard_map/ppermute | solution.py:217
  35.0 85.0 %collective-permute-start.19 = (bf16[512,2048]{1,0:T(8,128)(2,1)}, bf16[512,2048]{1,0:T(8,128)(2,1)S(1)}, u32[]{:S(2)}, u32[]{:S(2)}) collective-permute-start(bf16[512,2048]{1,0:T(8,128)(2,1)} %bitcast.169), channel_id=1, source_target_pairs={{0,8},{8,0},{1,9},{9,1},{2,10},{10,2},{3,11},{11,3},{4,12},{12,4},... | collective-permute-start | bytes 6291464 | tf_op jit(solution)/shard_map/ppermute | solution.py:115
  43.5 23.9 %collective-permute-start.7 = (bf16[256,1024]{1,0:T(8,128)(2,1)S(1)}, bf16[256,1024]{1,0:T(8,128)(2,1)S(1)}, u32[]{:S(2)}, u32[]{:S(2)}) collective-permute-start(bf16[256,1024]{1,0:T(8,128)(2,1)S(1)} %pad_maximum_fusion.7), channel_id=1, source_target_pairs={{0,3},{1,2},{2,1},{3,0},{4,11},{5,10},{6,9},{7,8},{8,7},{9,6},{10,... | collective-permute-start | bytes 1572872 | tf_op jit(solution)/shard_map/ppermute | solution.py:217
  43.6 18.9 %collective-permute-start.9 = (bf16[256,512]{1,0:T(8,128)(2,1)}, bf16[256,512]{1,0:T(8,128)(2,1)S(1)}, u32[]{:S(2)}, u32[]{:S(2)}) collective-permute-start(bf16[256,512]{1,0:T(8,128)(2,1)} %get-tuple-element.132), channel_id=1, source_target_pairs={{0,2},{1,3},{2,0},{3,1},{4,6},{5,7},{6,4},{7,5},{8,10},{9,11},{10,... | collective-permute-start | bytes 786440 | tf_op jit(solution)/shard_map/ppermute | solution.py:90
  48.5 30.5 %collective-permute-start.5 = (bf16[256,1024]{1,0:T(8,128)(2,1)S(1)}, bf16[256,1024]{1,0:T(8,128)(2,1)S(1)}, u32[]{:S(2)}, u32[]{:S(2)}) collective-permute-start(bf16[256,1024]{1,0:T(8,128)(2,1)S(1)} %copy-done.72), channel_id=1, source_target_pairs={{0,2},{1,3},{2,0},{3,1},{4,10},{5,11},{6,8},{7,9},{8,6},{9,7},{10,... | collective-permute-start | bytes 1572872 | tf_op jit(solution)/shard_map/ppermute | solution.py:217
  50.0 43.4 %collective-permute-start.2 = (bf16[144,2048]{1,0:T(8,128)(2,1)S(1)}, bf16[144,2048]{1,0:T(8,128)(2,1)S(1)}, u32[]{:S(2)}, u32[]{:S(2)}) collective-permute-start(bf16[144,2048]{1,0:T(8,128)(2,1)S(1)} %collective-permute-done.refs_1_), channel_id=1, source_target_pairs={{0,1},{1,3},{2,0},{3,5},{4,2},{5,7},{6,4},{7,6},{8,9},{9,11},{10,8... | collective-permute-start | bytes 1769480 | tf_op jit(solution)/shard_map/ppermute | solution.py:90
  62.5 33.8 %collective-permute-start.14 = (bf16[144,2048]{1,0:T(8,128)(2,1)S(1)}, bf16[144,2048]{1,0:T(8,128)(2,1)S(1)}, u32[]{:S(2)}, u32[]{:S(2)}) collective-permute-start(bf16[144,2048]{1,0:T(8,128)(2,1)S(1)} %collective-permute-done.1.refs_2_), channel_id=1, source_target_pairs={{0,2},{1,0},{2,4},{3,1},{4,6},{5,3},{6,7},{7,5},{8,10},{9,8},{10,1... | collective-permute-start | bytes 1769480 | tf_op jit(solution)/shard_map/ppermute | solution.py:90
  67.4 82.2 %collective-permute-start.11 = (bf16[256,512]{1,0:T(8,128)(2,1)}, bf16[256,512]{1,0:T(8,128)(2,1)}, u32[]{:S(2)}, u32[]{:S(2)}) collective-permute-start(bf16[256,512]{1,0:T(8,128)(2,1)} %get-tuple-element.134), channel_id=1, source_target_pairs={{0,7},{1,6},{2,5},{3,4},{4,3},{5,2},{6,1},{7,0},{8,15},{9,14},{10,... | collective-permute-start | bytes 786440 | tf_op jit(solution)/shard_map/ppermute | solution.py:90
  79.1 18.1 %collective-permute-start.10 = (bf16[256,512]{1,0:T(8,128)(2,1)S(1)}, bf16[256,512]{1,0:T(8,128)(2,1)S(1)}, u32[]{:S(2)}, u32[]{:S(2)}) collective-permute-start(bf16[256,512]{1,0:T(8,128)(2,1)S(1)} %copy-done.75), channel_id=1, source_target_pairs={{0,1},{1,0},{2,3},{3,2},{4,5},{5,4},{6,7},{7,6},{8,9},{9,8},{10,11... | collective-permute-start | bytes 786440 | tf_op jit(solution)/shard_map/ppermute | solution.py:90
  93.4 25.3 %collective-permute-start.15 = (bf16[144,2048]{1,0:T(8,128)(2,1)S(1)}, bf16[144,2048]{1,0:T(8,128)(2,1)S(1)}, u32[]{:S(2)}, u32[]{:S(2)}) collective-permute-start(bf16[144,2048]{1,0:T(8,128)(2,1)S(1)} %collective-permute-done.2.refs_3_), channel_id=1, source_target_pairs={{0,1},{1,3},{2,0},{3,5},{4,2},{5,7},{6,4},{7,6},{8,9},{9,11},{10,8... | collective-permute-start | bytes 1769480 | tf_op jit(solution)/shard_map/ppermute | solution.py:90
  96.3 22.7 %collective-permute-start.16 = (bf16[144,2048]{1,0:T(8,128)(2,1)S(1)}, bf16[144,2048]{1,0:T(8,128)(2,1)S(1)}, u32[]{:S(2)}, u32[]{:S(2)}) collective-permute-start(bf16[144,2048]{1,0:T(8,128)(2,1)S(1)} %collective-permute-done.14.refs_0_.refs_4_), channel_id=1, source_target_pairs={{0,2},{1,0},{2,4},{3,1},{4,6},{5,3},{6,7},{7,5},{8,10},{9,8},{10,1... | collective-permute-start | bytes 1769480 | tf_op jit(solution)/shard_map/ppermute | solution.py:90
  97.2 54.3 %collective-permute-start.12 = (bf16[256,512]{1,0:T(8,128)(2,1)}, bf16[256,512]{1,0:T(8,128)(2,1)}, u32[]{:S(2)}, u32[]{:S(2)}) collective-permute-start(bf16[256,512]{1,0:T(8,128)(2,1)} %get-tuple-element.135), channel_id=1, source_target_pairs={{0,6},{1,7},{2,4},{3,5},{4,2},{5,3},{6,0},{7,1},{8,14},{9,15},{10,... | collective-permute-start | bytes 786440 | tf_op jit(solution)/shard_map/ppermute | solution.py:90
  118.8 26.5 %collective-permute-start.17 = (bf16[144,2048]{1,0:T(8,128)(2,1)S(1)}, bf16[144,2048]{1,0:T(8,128)(2,1)S(1)}, u32[]{:S(2)}, u32[]{:S(2)}) collective-permute-start(bf16[144,2048]{1,0:T(8,128)(2,1)S(1)} %collective-permute-done.15.refs_1_.refs_5_), channel_id=1, source_target_pairs={{0,1},{1,3},{2,0},{3,5},{4,2},{5,7},{6,4},{7,6},{8,9},{9,11},{10,8... | collective-permute-start | bytes 1769480 | tf_op jit(solution)/shard_map/ppermute | solution.py:90
  119.0 38.8 %collective-permute-start.8 = (bf16[1024,1024]{1,0:T(8,128)(2,1)}, bf16[1024,1024]{1,0:T(8,128)(2,1)}, u32[]{:S(2)}, u32[]{:S(2)}) collective-permute-start(bf16[1024,1024]{1,0:T(8,128)(2,1)} %constant_dynamic-update-slice_fusion.16), channel_id=1, source_target_pairs={{0,8},{8,0},{1,9},{9,1},{2,10},{10,2},{3,11},{11,3},{4,12},{12,4},... | collective-permute-start | bytes 6291464 | tf_op jit(solution)/shard_map/ppermute | solution.py:115
  119.9 33.3 %collective-permute-start.13 = (bf16[256,512]{1,0:T(8,128)(2,1)}, bf16[256,512]{1,0:T(8,128)(2,1)}, u32[]{:S(2)}, u32[]{:S(2)}) collective-permute-start(bf16[256,512]{1,0:T(8,128)(2,1)} %get-tuple-element.136), channel_id=1, source_target_pairs={{0,5},{1,4},{2,7},{3,6},{4,1},{5,0},{6,3},{7,2},{8,13},{9,12},{10,... | collective-permute-start | bytes 786440 | tf_op jit(solution)/shard_map/ppermute | solution.py:90
  175.7 15.3 %collective-permute-start.32 = (bf16[64,2048]{1,0:T(8,128)(2,1)S(1)}, bf16[64,2048]{1,0:T(8,128)(2,1)S(1)}, u32[]{:S(2)}, u32[]{:S(2)}) collective-permute-start(bf16[64,2048]{1,0:T(8,128)(2,1)S(1)} %get-tuple-element.151), channel_id=1, source_target_pairs={{0,1},{1,3},{2,0},{3,5},{4,2},{5,7},{6,4},{7,6},{8,9},{9,11},{10,8... | collective-permute-start | bytes 786440 | tf_op jit(solution)/shard_map/ppermute | solution.py:90
  198.9 16.9 %collective-permute-start.31 = (bf16[64,2048]{1,0:T(8,128)(2,1)S(1)}, bf16[64,2048]{1,0:T(8,128)(2,1)S(1)}, u32[]{:S(2)}, u32[]{:S(2)}) collective-permute-start(bf16[64,2048]{1,0:T(8,128)(2,1)S(1)} %add_convert_fusion.21), channel_id=1, source_target_pairs={{0,2},{1,0},{2,4},{3,1},{4,6},{5,3},{6,7},{7,5},{8,10},{9,8},{10,1... | collective-permute-start | bytes 786440 | tf_op jit(solution)/shard_map/ppermute | solution.py:90
  236.2 14.7 %collective-permute-start.44 = (bf16[64,2048]{1,0:T(8,128)(2,1)S(1)}, bf16[64,2048]{1,0:T(8,128)(2,1)S(1)}, u32[]{:S(2)}, u32[]{:S(2)}) collective-permute-start(bf16[64,2048]{1,0:T(8,128)(2,1)S(1)} %get-tuple-element.259.refs_0_), channel_id=1, source_target_pairs={{0,1},{1,3},{2,0},{3,5},{4,2},{5,7},{6,4},{7,6},{8,9},{9,11},{10,8... | collective-permute-start | bytes 786440 | tf_op jit(solution)/shard_map/ppermute | solution.py:90
  236.3 15.7 %collective-permute-start.38 = (bf16[64,2048]{1,0:T(8,128)(2,1)S(1)}, bf16[64,2048]{1,0:T(8,128)(2,1)S(1)}, u32[]{:S(2)}, u32[]{:S(2)}) collective-permute-start(bf16[64,2048]{1,0:T(8,128)(2,1)S(1)} %get-tuple-element.259.refs_0_), channel_id=1, source_target_pairs={{0,2},{1,0},{2,4},{3,1},{4,6},{5,3},{6,7},{7,5},{8,10},{9,8},{10,1... | collective-permute-start | bytes 786440 | tf_op jit(solution)/shard_map/ppermute | solution.py:90
  264.2 20.8 %collective-permute-start.40 = (bf16[64,2048]{1,0:T(8,128)(2,1)S(1)}, bf16[64,2048]{1,0:T(8,128)(2,1)S(1)}, u32[]{:S(2)}, u32[]{:S(2)}) collective-permute-start(bf16[64,2048]{1,0:T(8,128)(2,1)S(1)} %collective-permute-done.39.refs_0_), channel_id=1, source_target_pairs={{0,2},{1,0},{2,4},{3,1},{4,6},{5,3},{6,7},{7,5},{8,10},{9,8},{10,1... | collective-permute-start | bytes 786440 | tf_op jit(solution)/shard_map/ppermute | solution.py:90
  309.6 19.1 %collective-permute-start.65 = (bf16[64,2048]{1,0:T(8,128)(2,1)S(1)}, bf16[64,2048]{1,0:T(8,128)(2,1)S(1)}, u32[]{:S(2)}, u32[]{:S(2)}) collective-permute-start(bf16[64,2048]{1,0:T(8,128)(2,1)S(1)} %add_convert_fusion.10), channel_id=1, source_target_pairs={{0,2},{1,0},{2,4},{3,1},{4,6},{5,3},{6,7},{7,5},{8,10},{9,8},{10,1... | collective-permute-start | bytes 786440 | tf_op jit(solution)/shard_map/ppermute | solution.py:90
  361.6 20.0 %collective-permute-start.61 = (bf16[64,2048]{1,0:T(8,128)(2,1)}, bf16[64,2048]{1,0:T(8,128)(2,1)S(1)}, u32[]{:S(2)}, u32[]{:S(2)}) collective-permute-start(bf16[64,2048]{1,0:T(8,128)(2,1)} %collective-permute-done.60.refs_0_), channel_id=1, source_target_pairs={{0,2},{1,0},{2,4},{3,1},{4,6},{5,3},{6,7},{7,5},{8,10},{9,8},{10,1... | collective-permute-start | bytes 786440 | tf_op jit(solution)/shard_map/ppermute | solution.py:90
  364.1 18.7 %collective-permute-start.76 = (bf16[64,2048]{1,0:T(8,128)(2,1)}, bf16[64,2048]{1,0:T(8,128)(2,1)S(1)}, u32[]{:S(2)}, u32[]{:S(2)}) collective-permute-start(bf16[64,2048]{1,0:T(8,128)(2,1)} %collective-permute-done.75.refs_2_), channel_id=1, source_target_pairs={{0,1},{1,3},{2,0},{3,5},{4,2},{5,7},{6,4},{7,6},{8,9},{9,11},{10,8... | collective-permute-start | bytes 786440 | tf_op jit(solution)/shard_map/ppermute | solution.py:90
  364.4 19.3 %collective-permute-start.73 = (bf16[64,2048]{1,0:T(8,128)(2,1)}, bf16[64,2048]{1,0:T(8,128)(2,1)S(1)}, u32[]{:S(2)}, u32[]{:S(2)}) collective-permute-start(bf16[64,2048]{1,0:T(8,128)(2,1)} %collective-permute-done.72.refs_1_), channel_id=1, source_target_pairs={{0,2},{1,0},{2,4},{3,1},{4,6},{5,3},{6,7},{7,5},{8,10},{9,8},{10,1... | collective-permute-start | bytes 786440 | tf_op jit(solution)/shard_map/ppermute | solution.py:90
  370.2 18.7 %collective-permute-start.81 = (bf16[64,2048]{1,0:T(8,128)(2,1)}, bf16[64,2048]{1,0:T(8,128)(2,1)S(1)}, u32[]{:S(2)}, u32[]{:S(2)}) collective-permute-start(bf16[64,2048]{1,0:T(8,128)(2,1)} %collective-permute-done.80.refs_3_), channel_id=1, source_target_pairs={{0,1},{1,3},{2,0},{3,5},{4,2},{5,7},{6,4},{7,6},{8,9},{9,11},{10,8... | collective-permute-start | bytes 786440 | tf_op jit(solution)/shard_map/ppermute | solution.py:90
  411.4 46.6 %collective-permute-start.98 = (bf16[256,1024]{1,0:T(8,128)(2,1)}, bf16[256,1024]{1,0:T(8,128)(2,1)S(1)}, u32[]{:S(2)}, u32[]{:S(2)}) collective-permute-start(bf16[256,1024]{1,0:T(8,128)(2,1)} %pad_maximum_fusion.9), channel_id=1, source_target_pairs={{0,0},{1,1},{2,2},{3,3},{8,4},{9,5},{10,6},{11,7},{4,8},{5,9},{6,1... | collective-permute-start | bytes 1572872 | tf_op jit(solution)/shard_map/ppermute | solution.py:221
  437.5 26.1 %collective-permute-start.85 = (bf16[128,2048]{1,0:T(8,128)(2,1)}, bf16[128,2048]{1,0:T(8,128)(2,1)}, u32[]{:S(2)}, u32[]{:S(2)}) collective-permute-start(bf16[128,2048]{1,0:T(8,128)(2,1)} %get-tuple-element.271), channel_id=1, source_target_pairs={{0,2},{1,0},{2,4},{3,1},{4,6},{5,3},{6,7},{7,5},{8,10},{9,8},{10,1... | collective-permute-start | bytes 1572872 | tf_op jit(solution)/shard_map/ppermute | solution.py:90
  444.0 24.5 %collective-permute-start.99 = (bf16[256,1024]{1,0:T(8,128)(2,1)}, bf16[256,1024]{1,0:T(8,128)(2,1)S(1)}, u32[]{:S(2)}, u32[]{:S(2)}) collective-permute-start(bf16[256,1024]{1,0:T(8,128)(2,1)} %pad_maximum_fusion.10), channel_id=1, source_target_pairs={{1,0},{0,1},{3,2},{2,3},{9,4},{8,5},{11,6},{10,7},{5,8},{4,9},{7,1... | collective-permute-start | bytes 1572872 | tf_op jit(solution)/shard_map/ppermute | solution.py:221
  457.9 16.2 %collective-permute-start.100 = (bf16[256,512]{1,0:T(8,128)(2,1)S(1)}, bf16[256,512]{1,0:T(8,128)(2,1)S(1)}, u32[]{:S(2)}, u32[]{:S(2)}) collective-permute-start(bf16[256,512]{1,0:T(8,128)(2,1)S(1)} %get-tuple-element.282), channel_id=1, source_target_pairs={{0,3},{1,2},{2,1},{3,0},{4,7},{5,6},{6,5},{7,4},{8,11},{9,10},{10,... | collective-permute-start | bytes 786440 | tf_op jit(solution)/shard_map/ppermute | solution.py:90
  458.0 21.2 %collective-permute-start.102 = (bf16[256,512]{1,0:T(8,128)(2,1)S(1)}, bf16[256,512]{1,0:T(8,128)(2,1)S(1)}, u32[]{:S(2)}, u32[]{:S(2)}) collective-permute-start(bf16[256,512]{1,0:T(8,128)(2,1)S(1)} %get-tuple-element.230), channel_id=1, source_target_pairs={{0,7},{1,6},{2,5},{3,4},{4,3},{5,2},{6,1},{7,0},{8,15},{9,14},{10,... | collective-permute-start | bytes 786440 | tf_op jit(solution)/shard_map/ppermute | solution.py:90
  461.7 28.0 %collective-permute-start.89 = (bf16[128,2048]{1,0:T(8,128)(2,1)S(1)}, bf16[128,2048]{1,0:T(8,128)(2,1)S(1)}, u32[]{:S(2)}, u32[]{:S(2)}) collective-permute-start(bf16[128,2048]{1,0:T(8,128)(2,1)S(1)} %copy-done.73), channel_id=1, source_target_pairs={{0,1},{1,3},{2,0},{3,5},{4,2},{5,7},{6,4},{7,6},{8,9},{9,11},{10,8... | collective-permute-start | bytes 1572872 | tf_op jit(solution)/shard_map/ppermute | solution.py:90
  463.6 26.1 %collective-permute-start.97 = (f32[8,3840]{1,0:T(8,128)S(1)}, f32[8,3840]{1,0:T(8,128)S(1)}, u32[]{:S(2)}, u32[]{:S(2)}) collective-permute-start(f32[8,3840]{1,0:T(8,128)S(1)} %add.477), channel_id=1, source_target_pairs={{0,4},{1,5},{2,6},{3,7},{4,0},{5,1},{6,2},{7,3},{8,12},{9,13},{10,... | collective-permute-start | bytes 368648 | tf_op jit(solution)/shard_map/ppermute | solution.py:90
  468.5 28.8 %collective-permute-start.86 = (bf16[128,2048]{1,0:T(8,128)(2,1)S(1)}, bf16[128,2048]{1,0:T(8,128)(2,1)S(1)}, u32[]{:S(2)}, u32[]{:S(2)}) collective-permute-start(bf16[128,2048]{1,0:T(8,128)(2,1)S(1)} %add_convert_fusion.6), channel_id=1, source_target_pairs={{0,2},{1,0},{2,4},{3,1},{4,6},{5,3},{6,7},{7,5},{8,10},{9,8},{10,1... | collective-permute-start | bytes 1572872 | tf_op jit(solution)/shard_map/ppermute | solution.py:90
  474.1 60.5 %collective-permute-start.108 = (bf16[512,2048]{1,0:T(8,128)(2,1)S(1)}, bf16[512,2048]{1,0:T(8,128)(2,1)S(1)}, u32[]{:S(2)}, u32[]{:S(2)}) collective-permute-start(bf16[512,2048]{1,0:T(8,128)(2,1)S(1)} %convolution_convert_fusion), channel_id=1, source_target_pairs={{0,8},{8,0},{1,9},{9,1},{2,10},{10,2},{3,11},{11,3},{4,12},{12,4},... | collective-permute-start | bytes 6291464 | tf_op jit(solution)/shard_map/ppermute | solution.py:115
  479.1 21.1 %collective-permute-start.101 = (bf16[256,1024]{1,0:T(8,128)(2,1)S(1)}, bf16[256,1024]{1,0:T(8,128)(2,1)S(1)}, u32[]{:S(2)}, u32[]{:S(2)}) collective-permute-start(bf16[256,1024]{1,0:T(8,128)(2,1)S(1)} %copy-done.71), channel_id=1, source_target_pairs={{2,0},{3,1},{0,2},{1,3},{10,4},{11,5},{8,6},{9,7},{6,8},{7,9},{4,1... | collective-permute-start | bytes 1572872 | tf_op jit(solution)/shard_map/ppermute | solution.py:221
  489.7 22.0 %collective-permute-start.103 = (bf16[256,1024]{1,0:T(8,128)(2,1)S(1)}, bf16[256,1024]{1,0:T(8,128)(2,1)S(1)}, u32[]{:S(2)}, u32[]{:S(2)}) collective-permute-start(bf16[256,1024]{1,0:T(8,128)(2,1)S(1)} %copy-done.70), channel_id=1, source_target_pairs={{3,0},{2,1},{1,2},{0,3},{11,4},{10,5},{9,6},{8,7},{7,8},{6,9},{5,1... | collective-permute-start | bytes 1572872 | tf_op jit(solution)/shard_map/ppermute | solution.py:221
  497.7 25.0 %collective-permute-start.87 = (bf16[128,2048]{1,0:T(8,128)(2,1)S(1)}, bf16[128,2048]{1,0:T(8,128)(2,1)S(1)}, u32[]{:S(2)}, u32[]{:S(2)}) collective-permute-start(bf16[128,2048]{1,0:T(8,128)(2,1)S(1)} %get-tuple-element.269), channel_id=1, source_target_pairs={{0,2},{1,0},{2,4},{3,1},{4,6},{5,3},{6,7},{7,5},{8,10},{9,8},{10,1... | collective-permute-start | bytes 1572872 | tf_op jit(solution)/shard_map/ppermute | solution.py:90
  500.2 33.9 %collective-permute-start.90 = (bf16[128,2048]{1,0:T(8,128)(2,1)S(1)}, bf16[128,2048]{1,0:T(8,128)(2,1)S(1)}, u32[]{:S(2)}, u32[]{:S(2)}) collective-permute-start(bf16[128,2048]{1,0:T(8,128)(2,1)S(1)} %get-tuple-element.270), channel_id=1, source_target_pairs={{0,1},{1,3},{2,0},{3,5},{4,2},{5,7},{6,4},{7,6},{8,9},{9,11},{10,8... | collective-permute-start | bytes 1572872 | tf_op jit(solution)/shard_map/ppermute | solution.py:90
  500.3 40.8 %collective-permute-start.107 = (bf16[256,512]{1,0:T(8,128)(2,1)S(1)}, bf16[256,512]{1,0:T(8,128)(2,1)S(1)}, u32[]{:S(2)}, u32[]{:S(2)}) collective-permute-start(bf16[256,512]{1,0:T(8,128)(2,1)S(1)} %get-tuple-element.239), channel_id=1, source_target_pairs={{0,2},{1,3},{2,0},{3,1},{4,6},{5,7},{6,4},{7,5},{8,10},{9,11},{10,... | collective-permute-start | bytes 786440 | tf_op jit(solution)/shard_map/ppermute | solution.py:90
  511.7 46.8 %collective-permute-start.105 = (bf16[256,512]{1,0:T(8,128)(2,1)S(1)}, bf16[256,512]{1,0:T(8,128)(2,1)S(1)}, u32[]{:S(2)}, u32[]{:S(2)}) collective-permute-start(bf16[256,512]{1,0:T(8,128)(2,1)S(1)} %get-tuple-element.237), channel_id=1, source_target_pairs={{0,6},{1,7},{2,4},{3,5},{4,2},{5,3},{6,0},{7,1},{8,14},{9,15},{10,... | collective-permute-start | bytes 786440 | tf_op jit(solution)/shard_map/ppermute | solution.py:90
  522.7 43.1 %collective-permute-start.104 = (bf16[256,512]{1,0:T(8,128)(2,1)S(1)}, bf16[256,512]{1,0:T(8,128)(2,1)S(1)}, u32[]{:S(2)}, u32[]{:S(2)}) collective-permute-start(bf16[256,512]{1,0:T(8,128)(2,1)S(1)} %get-tuple-element.234), channel_id=1, source_target_pairs={{0,1},{1,0},{2,3},{3,2},{4,5},{5,4},{6,7},{7,6},{8,9},{9,8},{10,11... | collective-permute-start | bytes 786440 | tf_op jit(solution)/shard_map/ppermute | solution.py:90
  534.5 17.9 %collective-permute-start.88 = (bf16[128,2048]{1,0:T(8,128)(2,1)S(1)}, bf16[128,2048]{1,0:T(8,128)(2,1)S(1)}, u32[]{:S(2)}, u32[]{:S(2)}) collective-permute-start(bf16[128,2048]{1,0:T(8,128)(2,1)S(1)} %get-tuple-element.267), channel_id=1, source_target_pairs={{0,2},{1,0},{2,4},{3,1},{4,6},{5,3},{6,7},{7,5},{8,10},{9,8},{10,1... | collective-permute-start | bytes 1572872 | tf_op jit(solution)/shard_map/ppermute | solution.py:90
  534.6 23.3 %collective-permute-start.91 = (bf16[128,2048]{1,0:T(8,128)(2,1)S(1)}, bf16[128,2048]{1,0:T(8,128)(2,1)S(1)}, u32[]{:S(2)}, u32[]{:S(2)}) collective-permute-start(bf16[128,2048]{1,0:T(8,128)(2,1)S(1)} %get-tuple-element.268), channel_id=1, source_target_pairs={{0,1},{1,3},{2,0},{3,5},{4,2},{5,7},{6,4},{7,6},{8,9},{9,11},{10,8... | collective-permute-start | bytes 1572872 | tf_op jit(solution)/shard_map/ppermute | solution.py:90
  541.0 22.5 %collective-permute-start.109 = (bf16[256,512]{1,0:T(8,128)(2,1)S(1)}, bf16[256,512]{1,0:T(8,128)(2,1)S(1)}, u32[]{:S(2)}, u32[]{:S(2)}) collective-permute-start(bf16[256,512]{1,0:T(8,128)(2,1)S(1)} %get-tuple-element.243), channel_id=1, source_target_pairs={{0,5},{1,4},{2,7},{3,6},{4,1},{5,0},{6,3},{7,2},{8,13},{9,12},{10,... | collective-permute-start | bytes 786440 | tf_op jit(solution)/shard_map/ppermute | solution.py:90
  (145 other events, 1811.2 us)

commit v7 on v6

--- a/solution.py
+++ b/solution.py
@@ -676,7 +676,7 @@
         block = head_blocks[which] if kind == "head" else up_blocks[which]
         if k == 1:
             block = ordered(block, *head_blocks)
-        if k == 3:
+        if k == 2:
             block = ordered(block, *up_blocks)
         if k == len(order) - 1:
             block = ordered(block, cosine, sine, mask, bq, bu, wd)
@@ -732,10 +732,10 @@
 
     matrices = (heads, wu, wd)
     pieces = {}
-    for at in (1, 0):
-        slots = layout.slots[at * chips // 2 : (at + 1) * chips // 2]
+    for at in range(chips // 2 - 1, -1, -1):
+        slots = layout.slots[2 * at : 2 * at + 2]
         blocks = [block for slot in slots for block in gathered[slot]]
-        rows = row_count // 2
+        rows = 2 * length
         results = call_rows(
             functools.partial(forward_kernel, len(blocks), 2 * len(slots)),
             (*blocks, *matrices, bq, bu, ratio),
@@ -752,7 +752,7 @@
             ],
             at,
             rows,
-            2 * matrix_flops,
+            matrix_flops,
         )
         for k, slot in enumerate(slots):
             pieces[slot] = results[2 * k : 2 * k + 2]

time: 583 us -> 581 us (level)
    unnamed x186 -> x174, local copies, waits for them, and re-layouts: 27.6 us -> 28.1 us
    pallas_call x11 -> x13, Pallas kernels: 59.9 us -> 59.9 us  [call_rows(): pl.pallas_call(kernel, grid=(1,), out_shape=out_shape, in_specs=in_specs,...]
  transfers between devices with their start and end apart: 110 -> 110, of which waited for: 42 -> 42; matrix products, arithmetic and copies ran while one was open for 13% -> 13% of each run, Pallas kernels for 13% -> 14%
where the time goes in v7:
time: 581 us; the launch traced here: 575 us
  waiting for transfers between devices  231 us (40%)
  starting transfers between devices  141 us (24%)
  Pallas kernels  85.5 us (15%)
  local copies, waits for them, and re-layouts  53 us (9%)
  other arithmetic  41.8 us (7%)
  matrix products  18.7 us (3%)
    ppermute x87, waiting for transfers between devices, between_chips(): return lax.ppermute(block, 'dp', pairs)  192 us
    ppermute x87, starting transfers between devices, between_chips(): return lax.ppermute(block, 'dp', pairs)  119 us
    pallas_call x13, Pallas kernels, call_rows(): pl.pallas_call(kernel, grid=(1,), out_shape=out_shape, in_specs=in_specs,...  59.9 us
    unnamed x174, local copies, waits for them, and re-layouts  28.1 us
    dot_general x8, matrix products, contract_rows(): lax.dot_general(left_side, right_side, (((0,), (0,)), ((), ())), preferre...  18.7 us
    pallas_call x1, Pallas kernels, on_device(): pl.pallas_call(scaled_kernel, grid=(row_count // pair_rows,), out_shape=[...  17.3 us
  transfers between devices with their start and end apart: 110, of which 42 were waited for; matrix products, arithmetic and copies ran while one was open for 13% of the time, Pallas kernels for 14%

profile of v7, /device:TPU:10, one launch (start us, length us, event | category | flops | bytes accessed | tf_op | source)
XLA Modules:
  0.0 574.8 jit_solution(12891669996706063426)
XLA Ops:
  25.1 9.8 %collective-permute-done.4 = bf16[256,512]{1,0:T(8,128)(2,1)} collective-permute-done((bf16[256,512]{1,0:T(8,128)(2,1)}, bf16[256,512]{1,0:T(8,128)(2,1)}, u32[]{:S(2)}, u32[]{:S(2)}) %collective-permute-start.4) | collective-permute-done | bytes 262176 | tf_op jit(solution)/shard_map/ppermute | solution.py:90
  35.0 6.9 %collective-permute-start.19 = (bf16[512,2048]{1,0:T(8,128)(2,1)}, bf16[512,2048]{1,0:T(8,128)(2,1)S(1)}, u32[]{:S(2)}, u32[]{:S(2)}) collective-permute-start(bf16[512,2048]{1,0:T(8,128)(2,1)} %bitcast.171), channel_id=1, source_target_pairs={{0,8},{8,0},{1,9},{9,1},{2,10},{10,2},{3,11},{11,3},{4,12},{12,4},... | collective-permute-start | bytes 6291464 | tf_op jit(solution)/shard_map/ppermute | solution.py:115
  50.6 11.9 %collective-permute-done.7 = bf16[256,512]{1,0:T(8,128)(2,1)S(1)} collective-permute-done((bf16[256,512]{1,0:T(8,128)(2,1)}, bf16[256,512]{1,0:T(8,128)(2,1)S(1)}, u32[]{:S(2)}, u32[]{:S(2)}) %collective-permute-start.7) | collective-permute-done | bytes 262176 | tf_op jit(solution)/shard_map/ppermute | solution.py:90
  62.5 5.0 collective-permute-start.14
  70.6 8.5 %collective-permute-done.3 = bf16[256,1024]{1,0:T(8,128)(2,1)S(1)} collective-permute-done((bf16[256,1024]{1,0:T(8,128)(2,1)S(1)}, bf16[256,1024]{1,0:T(8,128)(2,1)S(1)}, u32[]{:S(2)}, u32[]{:S(2)}) %collective-permute-start.3) | collective-permute-done | bytes 524320 | tf_op jit(solution)/shard_map/ppermute | solution.py:217
  79.9 13.5 %collective-permute-done.13.refs_1_.refs_3_ = bf16[144,2048]{1,0:T(8,128)(2,1)S(1)} collective-permute-done((bf16[144,2048]{1,0:T(8,128)(2,1)S(1)}, bf16[144,2048]{1,0:T(8,128)(2,1)S(1)}, u32[]{:S(2)}, u32[]{:S(2)}) %collective-permute-start.13) | collective-permute-done | bytes 589856 | tf_op jit(solution)/shard_map/ppermute | solution.py:90
  97.9 20.9 %collective-permute-done.15.refs_1_.refs_5_ = bf16[144,2048]{1,0:T(8,128)(2,1)S(1)} collective-permute-done((bf16[144,2048]{1,0:T(8,128)(2,1)S(1)}, bf16[144,2048]{1,0:T(8,128)(2,1)S(1)}, u32[]{:S(2)}, u32[]{:S(2)}) %collective-permute-start.15) | collective-permute-done | bytes 589856 | tf_op jit(solution)/shard_map/ppermute | solution.py:90
  122.6 22.7 %collective-permute-done.17.refs_1_.refs_7_ = bf16[144,2048]{1,0:T(8,128)(2,1)S(1)} collective-permute-done((bf16[144,2048]{1,0:T(8,128)(2,1)S(1)}, bf16[144,2048]{1,0:T(8,128)(2,1)S(1)}, u32[]{:S(2)}, u32[]{:S(2)}) %collective-permute-start.17) | collective-permute-done | bytes 589856 | tf_op jit(solution)/shard_map/ppermute | solution.py:90
  166.1 4.6 shard_map.222
  171.3 4.6 shard_map.221
  180.0 4.6 shard_map.223
  184.7 4.6 shard_map.220
  194.0 4.6 collective-permute-done.30
  206.6 4.9 collective-permute-done.34
  217.1 4.0 collective-permute-done.35
  223.5 7.3 %collective-permute-done.36 = bf16[64,2048]{1,0:T(8,128)(2,1)} collective-permute-done((bf16[64,2048]{1,0:T(8,128)(2,1)S(1)}, bf16[64,2048]{1,0:T(8,128)(2,1)}, u32[]{:S(2)}, u32[]{:S(2)}) %collective-permute-start.36) | collective-permute-done | bytes 262176 | tf_op jit(solution)/shard_map/ppermute | solution.py:766
  245.0 5.6 shard_map.224
  254.8 5.5 shard_map.225
  267.1 5.5 shard_map.226
  278.0 5.5 shard_map.227
  285.0 5.5 shard_map.228
  298.9 5.1 collective-permute-done.52
  306.3 3.3 collective-permute-done.64
  322.4 5.3 collective-permute-done.68
  328.8 5.3 collective-permute-done.69
  337.9 4.3 collective-permute-done.59
  349.9 5.5 collective-permute-done.74.refs_2_
  357.4 3.6 collective-permute-done.79.refs_3_
  366.3 3.7 collective-permute-done.80.refs_3_
  377.8 3.7 shard_map.229
  384.9 3.8 shard_map.230
  388.7 3.6 shard_map.231
  395.9 3.4 copy-done.16
  413.5 3.9 add_convert_fusion
  418.9 17.3 %shard_map.233 = (bf16[1024,2048]{1,0:T(8,128)(2,1)S(1)}, f32[32,2048]{1,0:T(8,128)S(1)}) custom-call(s32[1]{0:T(128)} %bitcast.26.second, bf16[2048,1024]{1,0:T(8,128)(2,1)S(1)} %copy-done.3, bf16[2048,1024]{1,0:T(8,128)(2,1)S(1)} %copy-done.10, bf16[1024,2048]{1,0:T(8,128)(2,1)S(1)} %copy-done.7, bf16[1024,2048]{1,0:T(8,128)(2,1)S(1)} %copy-done.16, ...), custom_call_target="tpu_custom_call" | custom-call | flops 6442450944 | bytes 8388608 | tf_op jit(solution)/shard_map/pallas_call | solution.py:881
  448.3 8.0 %collective-permute-start.96 = (f32[8,3840]{1,0:T(8,128)S(1)}, f32[8,3840]{1,0:T(8,128)S(1)}, u32[]{:S(2)}, u32[]{:S(2)}) collective-permute-start(f32[8,3840]{1,0:T(8,128)S(1)} %add.476), channel_id=1, source_target_pairs={{0,2},{1,3},{2,0},{3,1},{4,6},{5,7},{6,4},{7,5},{8,10},{9,11},{10,... | collective-permute-start | bytes 368648 | tf_op jit(solution)/shard_map/ppermute | solution.py:90
  458.0 3.6 collective-permute-start.102
  463.5 3.4 collective-permute-start.97
  471.7 8.3 %collective-permute-done.102.refs_6_ = bf16[256,512]{1,0:T(8,128)(2,1)S(1)} collective-permute-done((bf16[256,512]{1,0:T(8,128)(2,1)S(1)}, bf16[256,512]{1,0:T(8,128)(2,1)S(1)}, u32[]{:S(2)}, u32[]{:S(2)}) %collective-permute-start.102) | collective-permute-done | bytes 262176 | tf_op jit(solution)/shard_map/ppermute | solution.py:90
  482.4 6.6 %collective-permute-done.97 = f32[8,3840]{1,0:T(8,128)S(1)} collective-permute-done((f32[8,3840]{1,0:T(8,128)S(1)}, f32[8,3840]{1,0:T(8,128)S(1)}, u32[]{:S(2)}, u32[]{:S(2)}) %collective-permute-start.97) | collective-permute-done | bytes 122912 | tf_op jit(solution)/shard_map/ppermute | solution.py:90
  489.0 8.6 %collective-permute-done.86 = bf16[128,2048]{1,0:T(8,128)(2,1)S(1)} collective-permute-done((bf16[128,2048]{1,0:T(8,128)(2,1)S(1)}, bf16[128,2048]{1,0:T(8,128)(2,1)S(1)}, u32[]{:S(2)}, u32[]{:S(2)}) %collective-permute-start.86) | collective-permute-done | bytes 524320 | tf_op jit(solution)/shard_map/ppermute | solution.py:90
  501.9 9.8 %collective-permute-done.103.refs_4_ = bf16[256,1024]{1,0:T(8,128)(2,1)S(1)} collective-permute-done((bf16[256,1024]{1,0:T(8,128)(2,1)S(1)}, bf16[256,1024]{1,0:T(8,128)(2,1)S(1)}, u32[]{:S(2)}, u32[]{:S(2)}) %collective-permute-start.103) | collective-permute-done | bytes 524320 | tf_op jit(solution)/shard_map/ppermute | solution.py:221
  511.8 7.7 %collective-permute-start.105 = (bf16[256,512]{1,0:T(8,128)(2,1)S(1)}, bf16[256,512]{1,0:T(8,128)(2,1)S(1)}, u32[]{:S(2)}, u32[]{:S(2)}) collective-permute-start(bf16[256,512]{1,0:T(8,128)(2,1)S(1)} %get-tuple-element.237), channel_id=1, source_target_pairs={{0,6},{1,7},{2,4},{3,5},{4,2},{5,3},{6,0},{7,1},{8,14},{9,15},{10,... | collective-permute-start | bytes 786440 | tf_op jit(solution)/shard_map/ppermute | solution.py:90
  519.4 3.6 shard_map.235
  523.0 11.1 %collective-permute-start.104 = (bf16[256,512]{1,0:T(8,128)(2,1)S(1)}, bf16[256,512]{1,0:T(8,128)(2,1)S(1)}, u32[]{:S(2)}, u32[]{:S(2)}) collective-permute-start(bf16[256,512]{1,0:T(8,128)(2,1)S(1)} %get-tuple-element.234), channel_id=1, source_target_pairs={{0,1},{1,0},{2,3},{3,2},{4,5},{5,4},{6,7},{7,6},{8,9},{9,8},{10,11... | collective-permute-start | bytes 786440 | tf_op jit(solution)/shard_map/ppermute | solution.py:90
  536.6 4.5 convert_add_fusion
  541.2 11.4 %collective-permute-done.88 = bf16[128,2048]{1,0:T(8,128)(2,1)S(1)} collective-permute-done((bf16[128,2048]{1,0:T(8,128)(2,1)S(1)}, bf16[128,2048]{1,0:T(8,128)(2,1)S(1)}, u32[]{:S(2)}, u32[]{:S(2)}) %collective-permute-start.88) | collective-permute-done | bytes 524320 | tf_op jit(solution)/shard_map/ppermute | solution.py:90
  560.1 3.7 collective-permute-done.109.refs_4_
  (526 shorter events, 243.4 us)
Async XLA Ops:
  6.6 41.9 %collective-permute-start = (bf16[144,2048]{1,0:T(8,128)(2,1)S(1)}, bf16[144,2048]{1,0:T(8,128)(2,1)S(1)}, u32[]{:S(2)}, u32[]{:S(2)}) collective-permute-start(bf16[144,2048]{1,0:T(8,128)(2,1)S(1)} %fusion.18.refs_0_), channel_id=1, source_target_pairs={{0,1},{1,3},{2,0},{3,5},{4,2},{5,7},{6,4},{7,6},{8,9},{9,11},{10,8... | collective-permute-start | bytes 1769480 | tf_op jit(solution)/shard_map/ppermute | solution.py:90
  7.1 42.9 %collective-permute-start.12 = (bf16[144,2048]{1,0:T(8,128)(2,1)S(1)}, bf16[144,2048]{1,0:T(8,128)(2,1)S(1)}, u32[]{:S(2)}, u32[]{:S(2)}) collective-permute-start(bf16[144,2048]{1,0:T(8,128)(2,1)S(1)} %fusion.18.refs_0_), channel_id=1, source_target_pairs={{0,2},{1,0},{2,4},{3,1},{4,6},{5,3},{6,7},{7,5},{8,10},{9,8},{10,1... | collective-permute-start | bytes 1769480 | tf_op jit(solution)/shard_map/ppermute | solution.py:90
  8.8 15.7 %collective-permute-start.18 = (f32[1,7168]{1,0:T(1,128)S(1)}, f32[1,7168]{1,0:T(1,128)S(1)}, u32[]{:S(2)}, u32[]{:S(2)}) collective-permute-start(f32[1,7168]{1,0:T(1,128)S(1)} %maximum_convert_fusion), channel_id=1, source_target_pairs={{0,8},{8,0},{1,9},{9,1},{2,10},{10,2},{3,11},{11,3},{4,12},{12,4},... | collective-permute-start | bytes 86024 | tf_op jit(solution)/shard_map/ppermute | solution.py:115
  14.8 28.8 %collective-permute-start.1 = (bf16[256,1024]{1,0:T(8,128)(2,1)S(1)}, bf16[256,1024]{1,0:T(8,128)(2,1)}, u32[]{:S(2)}, u32[]{:S(2)}) collective-permute-start(bf16[256,1024]{1,0:T(8,128)(2,1)S(1)} %pad_maximum_fusion.4), channel_id=1, source_target_pairs={{0,0},{1,1},{2,2},{3,3},{4,8},{5,9},{6,10},{7,11},{8,4},{9,5},{10,... | collective-permute-start | bytes 1572872 | tf_op jit(solution)/shard_map/ppermute | solution.py:217
  17.6 25.9 %collective-permute-start.2 = (bf16[256,1024]{1,0:T(8,128)(2,1)}, bf16[256,1024]{1,0:T(8,128)(2,1)S(1)}, u32[]{:S(2)}, u32[]{:S(2)}) collective-permute-start(bf16[256,1024]{1,0:T(8,128)(2,1)} %get-tuple-element.128), channel_id=1, source_target_pairs={{0,1},{1,0},{2,3},{3,2},{4,9},{5,8},{6,11},{7,10},{8,5},{9,4},{10,... | collective-permute-start | bytes 1572872 | tf_op jit(solution)/shard_map/ppermute | solution.py:217
  35.0 85.0 %collective-permute-start.19 = (bf16[512,2048]{1,0:T(8,128)(2,1)}, bf16[512,2048]{1,0:T(8,128)(2,1)S(1)}, u32[]{:S(2)}, u32[]{:S(2)}) collective-permute-start(bf16[512,2048]{1,0:T(8,128)(2,1)} %bitcast.171), channel_id=1, source_target_pairs={{0,8},{8,0},{1,9},{9,1},{2,10},{10,2},{3,11},{11,3},{4,12},{12,4},... | collective-permute-start | bytes 6291464 | tf_op jit(solution)/shard_map/ppermute | solution.py:115
  43.5 23.9 %collective-permute-start.5 = (bf16[256,1024]{1,0:T(8,128)(2,1)S(1)}, bf16[256,1024]{1,0:T(8,128)(2,1)S(1)}, u32[]{:S(2)}, u32[]{:S(2)}) collective-permute-start(bf16[256,1024]{1,0:T(8,128)(2,1)S(1)} %pad_maximum_fusion.7), channel_id=1, source_target_pairs={{0,3},{1,2},{2,1},{3,0},{4,11},{5,10},{6,9},{7,8},{8,7},{9,6},{10,... | collective-permute-start | bytes 1572872 | tf_op jit(solution)/shard_map/ppermute | solution.py:217
  43.6 18.9 %collective-permute-start.7 = (bf16[256,512]{1,0:T(8,128)(2,1)}, bf16[256,512]{1,0:T(8,128)(2,1)S(1)}, u32[]{:S(2)}, u32[]{:S(2)}) collective-permute-start(bf16[256,512]{1,0:T(8,128)(2,1)} %get-tuple-element.132), channel_id=1, source_target_pairs={{0,2},{1,3},{2,0},{3,1},{4,6},{5,7},{6,4},{7,5},{8,10},{9,11},{10,... | collective-permute-start | bytes 786440 | tf_op jit(solution)/shard_map/ppermute | solution.py:90
  48.5 30.5 %collective-permute-start.3 = (bf16[256,1024]{1,0:T(8,128)(2,1)S(1)}, bf16[256,1024]{1,0:T(8,128)(2,1)S(1)}, u32[]{:S(2)}, u32[]{:S(2)}) collective-permute-start(bf16[256,1024]{1,0:T(8,128)(2,1)S(1)} %copy-done.66), channel_id=1, source_target_pairs={{0,2},{1,3},{2,0},{3,1},{4,10},{5,11},{6,8},{7,9},{8,6},{9,7},{10,... | collective-permute-start | bytes 1572872 | tf_op jit(solution)/shard_map/ppermute | solution.py:217
  50.0 43.5 %collective-permute-start.13 = (bf16[144,2048]{1,0:T(8,128)(2,1)S(1)}, bf16[144,2048]{1,0:T(8,128)(2,1)S(1)}, u32[]{:S(2)}, u32[]{:S(2)}) collective-permute-start(bf16[144,2048]{1,0:T(8,128)(2,1)S(1)} %collective-permute-done.refs_1_), channel_id=1, source_target_pairs={{0,1},{1,3},{2,0},{3,5},{4,2},{5,7},{6,4},{7,6},{8,9},{9,11},{10,8... | collective-permute-start | bytes 1769480 | tf_op jit(solution)/shard_map/ppermute | solution.py:90
  62.5 33.8 %collective-permute-start.14 = (bf16[144,2048]{1,0:T(8,128)(2,1)S(1)}, bf16[144,2048]{1,0:T(8,128)(2,1)S(1)}, u32[]{:S(2)}, u32[]{:S(2)}) collective-permute-start(bf16[144,2048]{1,0:T(8,128)(2,1)S(1)} %collective-permute-done.12.refs_0_.refs_2_), channel_id=1, source_target_pairs={{0,2},{1,0},{2,4},{3,1},{4,6},{5,3},{6,7},{7,5},{8,10},{9,8},{10,1... | collective-permute-start | bytes 1769480 | tf_op jit(solution)/shard_map/ppermute | solution.py:90
  67.4 82.3 %collective-permute-start.9 = (bf16[256,512]{1,0:T(8,128)(2,1)}, bf16[256,512]{1,0:T(8,128)(2,1)}, u32[]{:S(2)}, u32[]{:S(2)}) collective-permute-start(bf16[256,512]{1,0:T(8,128)(2,1)} %get-tuple-element.134), channel_id=1, source_target_pairs={{0,7},{1,6},{2,5},{3,4},{4,3},{5,2},{6,1},{7,0},{8,15},{9,14},{10,... | collective-permute-start | bytes 786440 | tf_op jit(solution)/shard_map/ppermute | solution.py:90
  79.1 18.1 %collective-permute-start.8 = (bf16[256,512]{1,0:T(8,128)(2,1)S(1)}, bf16[256,512]{1,0:T(8,128)(2,1)S(1)}, u32[]{:S(2)}, u32[]{:S(2)}) collective-permute-start(bf16[256,512]{1,0:T(8,128)(2,1)S(1)} %copy-done.69), channel_id=1, source_target_pairs={{0,1},{1,0},{2,3},{3,2},{4,5},{5,4},{6,7},{7,6},{8,9},{9,8},{10,11... | collective-permute-start | bytes 786440 | tf_op jit(solution)/shard_map/ppermute | solution.py:90
  93.4 25.3 %collective-permute-start.15 = (bf16[144,2048]{1,0:T(8,128)(2,1)S(1)}, bf16[144,2048]{1,0:T(8,128)(2,1)S(1)}, u32[]{:S(2)}, u32[]{:S(2)}) collective-permute-start(bf16[144,2048]{1,0:T(8,128)(2,1)S(1)} %collective-permute-done.13.refs_1_.refs_3_), channel_id=1, source_target_pairs={{0,1},{1,3},{2,0},{3,5},{4,2},{5,7},{6,4},{7,6},{8,9},{9,11},{10,8... | collective-permute-start | bytes 1769480 | tf_op jit(solution)/shard_map/ppermute | solution.py:90
  96.3 22.7 %collective-permute-start.16 = (bf16[144,2048]{1,0:T(8,128)(2,1)S(1)}, bf16[144,2048]{1,0:T(8,128)(2,1)S(1)}, u32[]{:S(2)}, u32[]{:S(2)}) collective-permute-start(bf16[144,2048]{1,0:T(8,128)(2,1)S(1)} %collective-permute-done.14.refs_0_.refs_4_), channel_id=1, source_target_pairs={{0,2},{1,0},{2,4},{3,1},{4,6},{5,3},{6,7},{7,5},{8,10},{9,8},{10,1... | collective-permute-start | bytes 1769480 | tf_op jit(solution)/shard_map/ppermute | solution.py:90
  97.1 54.4 %collective-permute-start.10 = (bf16[256,512]{1,0:T(8,128)(2,1)}, bf16[256,512]{1,0:T(8,128)(2,1)}, u32[]{:S(2)}, u32[]{:S(2)}) collective-permute-start(bf16[256,512]{1,0:T(8,128)(2,1)} %get-tuple-element.135), channel_id=1, source_target_pairs={{0,6},{1,7},{2,4},{3,5},{4,2},{5,3},{6,0},{7,1},{8,14},{9,15},{10,... | collective-permute-start | bytes 786440 | tf_op jit(solution)/shard_map/ppermute | solution.py:90
  118.8 26.5 %collective-permute-start.17 = (bf16[144,2048]{1,0:T(8,128)(2,1)S(1)}, bf16[144,2048]{1,0:T(8,128)(2,1)S(1)}, u32[]{:S(2)}, u32[]{:S(2)}) collective-permute-start(bf16[144,2048]{1,0:T(8,128)(2,1)S(1)} %collective-permute-done.15.refs_1_.refs_5_), channel_id=1, source_target_pairs={{0,1},{1,3},{2,0},{3,5},{4,2},{5,7},{6,4},{7,6},{8,9},{9,11},{10,8... | collective-permute-start | bytes 1769480 | tf_op jit(solution)/shard_map/ppermute | solution.py:90
  119.0 38.8 %collective-permute-start.6 = (bf16[1024,1024]{1,0:T(8,128)(2,1)}, bf16[1024,1024]{1,0:T(8,128)(2,1)}, u32[]{:S(2)}, u32[]{:S(2)}) collective-permute-start(bf16[1024,1024]{1,0:T(8,128)(2,1)} %constant_dynamic-update-slice_fusion.16), channel_id=1, source_target_pairs={{0,8},{8,0},{1,9},{9,1},{2,10},{10,2},{3,11},{11,3},{4,12},{12,4},... | collective-permute-start | bytes 6291464 | tf_op jit(solution)/shard_map/ppermute | solution.py:115
  120.0 33.3 %collective-permute-start.11 = (bf16[256,512]{1,0:T(8,128)(2,1)}, bf16[256,512]{1,0:T(8,128)(2,1)}, u32[]{:S(2)}, u32[]{:S(2)}) collective-permute-start(bf16[256,512]{1,0:T(8,128)(2,1)} %get-tuple-element.136), channel_id=1, source_target_pairs={{0,5},{1,4},{2,7},{3,6},{4,1},{5,0},{6,3},{7,2},{8,13},{9,12},{10,... | collective-permute-start | bytes 786440 | tf_op jit(solution)/shard_map/ppermute | solution.py:90
  170.8 18.5 %collective-permute-start.29 = (bf16[64,2048]{1,0:T(8,128)(2,1)S(1)}, bf16[64,2048]{1,0:T(8,128)(2,1)S(1)}, u32[]{:S(2)}, u32[]{:S(2)}) collective-permute-start(bf16[64,2048]{1,0:T(8,128)(2,1)S(1)} %get-tuple-element.148), channel_id=1, source_target_pairs={{0,2},{1,0},{2,4},{3,1},{4,6},{5,3},{6,7},{7,5},{8,10},{9,8},{10,1... | collective-permute-start | bytes 786440 | tf_op jit(solution)/shard_map/ppermute | solution.py:90
  175.9 14.9 %collective-permute-start.32 = (bf16[64,2048]{1,0:T(8,128)(2,1)S(1)}, bf16[64,2048]{1,0:T(8,128)(2,1)S(1)}, u32[]{:S(2)}, u32[]{:S(2)}) collective-permute-start(bf16[64,2048]{1,0:T(8,128)(2,1)S(1)} %get-tuple-element.151), channel_id=1, source_target_pairs={{0,1},{1,3},{2,0},{3,5},{4,2},{5,7},{6,4},{7,6},{8,9},{9,11},{10,8... | collective-permute-start | bytes 786440 | tf_op jit(solution)/shard_map/ppermute | solution.py:90
  198.8 17.0 %collective-permute-start.31 = (bf16[64,2048]{1,0:T(8,128)(2,1)S(1)}, bf16[64,2048]{1,0:T(8,128)(2,1)S(1)}, u32[]{:S(2)}, u32[]{:S(2)}) collective-permute-start(bf16[64,2048]{1,0:T(8,128)(2,1)S(1)} %add_convert_fusion.21), channel_id=1, source_target_pairs={{0,2},{1,0},{2,4},{3,1},{4,6},{5,3},{6,7},{7,5},{8,10},{9,8},{10,1... | collective-permute-start | bytes 786440 | tf_op jit(solution)/shard_map/ppermute | solution.py:90
  236.1 14.5 %collective-permute-start.44 = (bf16[64,2048]{1,0:T(8,128)(2,1)S(1)}, bf16[64,2048]{1,0:T(8,128)(2,1)S(1)}, u32[]{:S(2)}, u32[]{:S(2)}) collective-permute-start(bf16[64,2048]{1,0:T(8,128)(2,1)S(1)} %get-tuple-element.259.refs_0_), channel_id=1, source_target_pairs={{0,1},{1,3},{2,0},{3,5},{4,2},{5,7},{6,4},{7,6},{8,9},{9,11},{10,8... | collective-permute-start | bytes 786440 | tf_op jit(solution)/shard_map/ppermute | solution.py:90
  236.2 15.5 %collective-permute-start.38 = (bf16[64,2048]{1,0:T(8,128)(2,1)S(1)}, bf16[64,2048]{1,0:T(8,128)(2,1)S(1)}, u32[]{:S(2)}, u32[]{:S(2)}) collective-permute-start(bf16[64,2048]{1,0:T(8,128)(2,1)S(1)} %get-tuple-element.259.refs_0_), channel_id=1, source_target_pairs={{0,2},{1,0},{2,4},{3,1},{4,6},{5,3},{6,7},{7,5},{8,10},{9,8},{10,1... | collective-permute-start | bytes 786440 | tf_op jit(solution)/shard_map/ppermute | solution.py:90
  264.3 20.7 %collective-permute-start.40 = (bf16[64,2048]{1,0:T(8,128)(2,1)S(1)}, bf16[64,2048]{1,0:T(8,128)(2,1)S(1)}, u32[]{:S(2)}, u32[]{:S(2)}) collective-permute-start(bf16[64,2048]{1,0:T(8,128)(2,1)S(1)} %collective-permute-done.39.refs_0_), channel_id=1, source_target_pairs={{0,2},{1,0},{2,4},{3,1},{4,6},{5,3},{6,7},{7,5},{8,10},{9,8},{10,1... | collective-permute-start | bytes 786440 | tf_op jit(solution)/shard_map/ppermute | solution.py:90
  309.7 19.2 %collective-permute-start.65 = (bf16[64,2048]{1,0:T(8,128)(2,1)S(1)}, bf16[64,2048]{1,0:T(8,128)(2,1)S(1)}, u32[]{:S(2)}, u32[]{:S(2)}) collective-permute-start(bf16[64,2048]{1,0:T(8,128)(2,1)S(1)} %add_convert_fusion.10), channel_id=1, source_target_pairs={{0,2},{1,0},{2,4},{3,1},{4,6},{5,3},{6,7},{7,5},{8,10},{9,8},{10,1... | collective-permute-start | bytes 786440 | tf_op jit(solution)/shard_map/ppermute | solution.py:90
  361.7 19.9 %collective-permute-start.61 = (bf16[64,2048]{1,0:T(8,128)(2,1)}, bf16[64,2048]{1,0:T(8,128)(2,1)S(1)}, u32[]{:S(2)}, u32[]{:S(2)}) collective-permute-start(bf16[64,2048]{1,0:T(8,128)(2,1)} %collective-permute-done.60.refs_0_), channel_id=1, source_target_pairs={{0,2},{1,0},{2,4},{3,1},{4,6},{5,3},{6,7},{7,5},{8,10},{9,8},{10,1... | collective-permute-start | bytes 786440 | tf_op jit(solution)/shard_map/ppermute | solution.py:90
  364.2 18.5 %collective-permute-start.76 = (bf16[64,2048]{1,0:T(8,128)(2,1)}, bf16[64,2048]{1,0:T(8,128)(2,1)S(1)}, u32[]{:S(2)}, u32[]{:S(2)}) collective-permute-start(bf16[64,2048]{1,0:T(8,128)(2,1)} %collective-permute-done.75.refs_2_), channel_id=1, source_target_pairs={{0,1},{1,3},{2,0},{3,5},{4,2},{5,7},{6,4},{7,6},{8,9},{9,11},{10,8... | collective-permute-start | bytes 786440 | tf_op jit(solution)/shard_map/ppermute | solution.py:90
  364.5 19.2 %collective-permute-start.73 = (bf16[64,2048]{1,0:T(8,128)(2,1)}, bf16[64,2048]{1,0:T(8,128)(2,1)S(1)}, u32[]{:S(2)}, u32[]{:S(2)}) collective-permute-start(bf16[64,2048]{1,0:T(8,128)(2,1)} %collective-permute-done.72.refs_1_), channel_id=1, source_target_pairs={{0,2},{1,0},{2,4},{3,1},{4,6},{5,3},{6,7},{7,5},{8,10},{9,8},{10,1... | collective-permute-start | bytes 786440 | tf_op jit(solution)/shard_map/ppermute | solution.py:90
  370.0 18.7 %collective-permute-start.81 = (bf16[64,2048]{1,0:T(8,128)(2,1)}, bf16[64,2048]{1,0:T(8,128)(2,1)S(1)}, u32[]{:S(2)}, u32[]{:S(2)}) collective-permute-start(bf16[64,2048]{1,0:T(8,128)(2,1)} %collective-permute-done.80.refs_3_), channel_id=1, source_target_pairs={{0,1},{1,3},{2,0},{3,5},{4,2},{5,7},{6,4},{7,6},{8,9},{9,11},{10,8... | collective-permute-start | bytes 786440 | tf_op jit(solution)/shard_map/ppermute | solution.py:90
  411.3 46.7 %collective-permute-start.98 = (bf16[256,1024]{1,0:T(8,128)(2,1)}, bf16[256,1024]{1,0:T(8,128)(2,1)S(1)}, u32[]{:S(2)}, u32[]{:S(2)}) collective-permute-start(bf16[256,1024]{1,0:T(8,128)(2,1)} %pad_maximum_fusion.9), channel_id=1, source_target_pairs={{0,0},{1,1},{2,2},{3,3},{8,4},{9,5},{10,6},{11,7},{4,8},{5,9},{6,1... | collective-permute-start | bytes 1572872 | tf_op jit(solution)/shard_map/ppermute | solution.py:221
  437.4 26.1 %collective-permute-start.85 = (bf16[128,2048]{1,0:T(8,128)(2,1)}, bf16[128,2048]{1,0:T(8,128)(2,1)}, u32[]{:S(2)}, u32[]{:S(2)}) collective-permute-start(bf16[128,2048]{1,0:T(8,128)(2,1)} %get-tuple-element.271), channel_id=1, source_target_pairs={{0,2},{1,0},{2,4},{3,1},{4,6},{5,3},{6,7},{7,5},{8,10},{9,8},{10,1... | collective-permute-start | bytes 1572872 | tf_op jit(solution)/shard_map/ppermute | solution.py:90
  443.9 24.3 %collective-permute-start.99 = (bf16[256,1024]{1,0:T(8,128)(2,1)}, bf16[256,1024]{1,0:T(8,128)(2,1)S(1)}, u32[]{:S(2)}, u32[]{:S(2)}) collective-permute-start(bf16[256,1024]{1,0:T(8,128)(2,1)} %pad_maximum_fusion.10), channel_id=1, source_target_pairs={{1,0},{0,1},{3,2},{2,3},{9,4},{8,5},{11,6},{10,7},{5,8},{4,9},{7,1... | collective-permute-start | bytes 1572872 | tf_op jit(solution)/shard_map/ppermute | solution.py:221
  458.0 22.0 %collective-permute-start.102 = (bf16[256,512]{1,0:T(8,128)(2,1)S(1)}, bf16[256,512]{1,0:T(8,128)(2,1)S(1)}, u32[]{:S(2)}, u32[]{:S(2)}) collective-permute-start(bf16[256,512]{1,0:T(8,128)(2,1)S(1)} %get-tuple-element.230), channel_id=1, source_target_pairs={{0,7},{1,6},{2,5},{3,4},{4,3},{5,2},{6,1},{7,0},{8,15},{9,14},{10,... | collective-permute-start | bytes 786440 | tf_op jit(solution)/shard_map/ppermute | solution.py:90
  461.6 27.4 %collective-permute-start.89 = (bf16[128,2048]{1,0:T(8,128)(2,1)S(1)}, bf16[128,2048]{1,0:T(8,128)(2,1)S(1)}, u32[]{:S(2)}, u32[]{:S(2)}) collective-permute-start(bf16[128,2048]{1,0:T(8,128)(2,1)S(1)} %copy-done.67), channel_id=1, source_target_pairs={{0,1},{1,3},{2,0},{3,5},{4,2},{5,7},{6,4},{7,6},{8,9},{9,11},{10,8... | collective-permute-start | bytes 1572872 | tf_op jit(solution)/shard_map/ppermute | solution.py:90
  463.5 25.5 %collective-permute-start.97 = (f32[8,3840]{1,0:T(8,128)S(1)}, f32[8,3840]{1,0:T(8,128)S(1)}, u32[]{:S(2)}, u32[]{:S(2)}) collective-permute-start(f32[8,3840]{1,0:T(8,128)S(1)} %add.477), channel_id=1, source_target_pairs={{0,4},{1,5},{2,6},{3,7},{4,0},{5,1},{6,2},{7,3},{8,12},{9,13},{10,... | collective-permute-start | bytes 368648 | tf_op jit(solution)/shard_map/ppermute | solution.py:90
  468.3 29.4 %collective-permute-start.86 = (bf16[128,2048]{1,0:T(8,128)(2,1)S(1)}, bf16[128,2048]{1,0:T(8,128)(2,1)S(1)}, u32[]{:S(2)}, u32[]{:S(2)}) collective-permute-start(bf16[128,2048]{1,0:T(8,128)(2,1)S(1)} %add_convert_fusion.6), channel_id=1, source_target_pairs={{0,2},{1,0},{2,4},{3,1},{4,6},{5,3},{6,7},{7,5},{8,10},{9,8},{10,1... | collective-permute-start | bytes 1572872 | tf_op jit(solution)/shard_map/ppermute | solution.py:90
  471.6 63.0 %collective-permute-start.108 = (bf16[512,2048]{1,0:T(8,128)(2,1)S(1)}, bf16[512,2048]{1,0:T(8,128)(2,1)S(1)}, u32[]{:S(2)}, u32[]{:S(2)}) collective-permute-start(bf16[512,2048]{1,0:T(8,128)(2,1)S(1)} %convolution_convert_fusion), channel_id=1, source_target_pairs={{0,8},{8,0},{1,9},{9,1},{2,10},{10,2},{3,11},{11,3},{4,12},{12,4},... | collective-permute-start | bytes 6291464 | tf_op jit(solution)/shard_map/ppermute | solution.py:115
  480.0 20.6 %collective-permute-start.101 = (bf16[256,1024]{1,0:T(8,128)(2,1)S(1)}, bf16[256,1024]{1,0:T(8,128)(2,1)S(1)}, u32[]{:S(2)}, u32[]{:S(2)}) collective-permute-start(bf16[256,1024]{1,0:T(8,128)(2,1)S(1)} %copy-done.65), channel_id=1, source_target_pairs={{2,0},{3,1},{0,2},{1,3},{10,4},{11,5},{8,6},{9,7},{6,8},{7,9},{4,1... | collective-permute-start | bytes 1572872 | tf_op jit(solution)/shard_map/ppermute | solution.py:221
  489.0 22.8 %collective-permute-start.103 = (bf16[256,1024]{1,0:T(8,128)(2,1)S(1)}, bf16[256,1024]{1,0:T(8,128)(2,1)S(1)}, u32[]{:S(2)}, u32[]{:S(2)}) collective-permute-start(bf16[256,1024]{1,0:T(8,128)(2,1)S(1)} %copy-done.64), channel_id=1, source_target_pairs={{3,0},{2,1},{1,2},{0,3},{11,4},{10,5},{9,6},{8,7},{7,8},{6,9},{5,1... | collective-permute-start | bytes 1572872 | tf_op jit(solution)/shard_map/ppermute | solution.py:221
  498.1 24.9 %collective-permute-start.87 = (bf16[128,2048]{1,0:T(8,128)(2,1)S(1)}, bf16[128,2048]{1,0:T(8,128)(2,1)S(1)}, u32[]{:S(2)}, u32[]{:S(2)}) collective-permute-start(bf16[128,2048]{1,0:T(8,128)(2,1)S(1)} %get-tuple-element.269), channel_id=1, source_target_pairs={{0,2},{1,0},{2,4},{3,1},{4,6},{5,3},{6,7},{7,5},{8,10},{9,8},{10,1... | collective-permute-start | bytes 1572872 | tf_op jit(solution)/shard_map/ppermute | solution.py:90
  500.6 33.5 %collective-permute-start.90 = (bf16[128,2048]{1,0:T(8,128)(2,1)S(1)}, bf16[128,2048]{1,0:T(8,128)(2,1)S(1)}, u32[]{:S(2)}, u32[]{:S(2)}) collective-permute-start(bf16[128,2048]{1,0:T(8,128)(2,1)S(1)} %get-tuple-element.270), channel_id=1, source_target_pairs={{0,1},{1,3},{2,0},{3,5},{4,2},{5,7},{6,4},{7,6},{8,9},{9,11},{10,8... | collective-permute-start | bytes 1572872 | tf_op jit(solution)/shard_map/ppermute | solution.py:90
  500.7 40.4 %collective-permute-start.107 = (bf16[256,512]{1,0:T(8,128)(2,1)S(1)}, bf16[256,512]{1,0:T(8,128)(2,1)S(1)}, u32[]{:S(2)}, u32[]{:S(2)}) collective-permute-start(bf16[256,512]{1,0:T(8,128)(2,1)S(1)} %get-tuple-element.239), channel_id=1, source_target_pairs={{0,2},{1,3},{2,0},{3,1},{4,6},{5,7},{6,4},{7,5},{8,10},{9,11},{10,... | collective-permute-start | bytes 786440 | tf_op jit(solution)/shard_map/ppermute | solution.py:90
  511.8 43.6 %collective-permute-start.105 = (bf16[256,512]{1,0:T(8,128)(2,1)S(1)}, bf16[256,512]{1,0:T(8,128)(2,1)S(1)}, u32[]{:S(2)}, u32[]{:S(2)}) collective-permute-start(bf16[256,512]{1,0:T(8,128)(2,1)S(1)} %get-tuple-element.237), channel_id=1, source_target_pairs={{0,6},{1,7},{2,4},{3,5},{4,2},{5,3},{6,0},{7,1},{8,14},{9,15},{10,... | collective-permute-start | bytes 786440 | tf_op jit(solution)/shard_map/ppermute | solution.py:90
  523.0 43.1 %collective-permute-start.104 = (bf16[256,512]{1,0:T(8,128)(2,1)S(1)}, bf16[256,512]{1,0:T(8,128)(2,1)S(1)}, u32[]{:S(2)}, u32[]{:S(2)}) collective-permute-start(bf16[256,512]{1,0:T(8,128)(2,1)S(1)} %get-tuple-element.234), channel_id=1, source_target_pairs={{0,1},{1,0},{2,3},{3,2},{4,5},{5,4},{6,7},{7,6},{8,9},{9,8},{10,11... | collective-permute-start | bytes 786440 | tf_op jit(solution)/shard_map/ppermute | solution.py:90
  534.5 18.1 %collective-permute-start.88 = (bf16[128,2048]{1,0:T(8,128)(2,1)S(1)}, bf16[128,2048]{1,0:T(8,128)(2,1)S(1)}, u32[]{:S(2)}, u32[]{:S(2)}) collective-permute-start(bf16[128,2048]{1,0:T(8,128)(2,1)S(1)} %get-tuple-element.267), channel_id=1, source_target_pairs={{0,2},{1,0},{2,4},{3,1},{4,6},{5,3},{6,7},{7,5},{8,10},{9,8},{10,1... | collective-permute-start | bytes 1572872 | tf_op jit(solution)/shard_map/ppermute | solution.py:90
  534.6 20.1 %collective-permute-start.91 = (bf16[128,2048]{1,0:T(8,128)(2,1)S(1)}, bf16[128,2048]{1,0:T(8,128)(2,1)S(1)}, u32[]{:S(2)}, u32[]{:S(2)}) collective-permute-start(bf16[128,2048]{1,0:T(8,128)(2,1)S(1)} %get-tuple-element.268), channel_id=1, source_target_pairs={{0,1},{1,3},{2,0},{3,5},{4,2},{5,7},{6,4},{7,6},{8,9},{9,11},{10,8... | collective-permute-start | bytes 1572872 | tf_op jit(solution)/shard_map/ppermute | solution.py:90
  541.1 22.7 %collective-permute-start.109 = (bf16[256,512]{1,0:T(8,128)(2,1)S(1)}, bf16[256,512]{1,0:T(8,128)(2,1)S(1)}, u32[]{:S(2)}, u32[]{:S(2)}) collective-permute-start(bf16[256,512]{1,0:T(8,128)(2,1)S(1)} %get-tuple-element.243), channel_id=1, source_target_pairs={{0,5},{1,4},{2,7},{3,6},{4,1},{5,0},{6,3},{7,2},{8,13},{9,12},{10,... | collective-permute-start | bytes 786440 | tf_op jit(solution)/shard_map/ppermute | solution.py:90
  (139 other events, 1596.4 us)
